TPU v7x, 256 devices: a whole 4x4x8 slice. The times are simulated.
256 devices in a mesh: span: 8 (over z_lo, core), dom: 32 (over x, y, z_hi).
Axes of the slice: x: 4, y: 4, z: 8 (z_hi: 2, z_lo: 4; z = z_hi * 4 + z_lo), core: 2. Of those that a mesh axis runs over, the one named last changes fastest.
Arguments:
- velocity_modes: float32 [3, 512, 20736], P(None, 'span', 'dom'), may hold values from -1.4 to 1.4
- metric: float32 [4, 20736], P(None, 'dom'), may hold values from -0.375 to 0.375
- pair_table: int32 [320, 4], P('dom'), may hold values from 0 to 7, as said below
- bound_table: int32 [256, 2], P('dom'), may hold values from 0 to 7, as said below
Outputs:
- advection: float32 [3, 512, 20736], P(None, 'span', 'dom')
Inputs may be any that keep to these rules, and one draw needn't show every extreme that they name: Each partition's elements form a patch of 4 x 2 elements; every edge between two elements of the patch is listed once, with local element numbers, and no edge is listed twice in pair_table and bound_table together. `bound_table`: local element numbers and edge numbers.
All inputs are finite; a program needn't handle non-finite values.
Results may differ from a plain program's by a relative error of at most 0.00014.
Values sent between devices are 32-bit elements; how exact they have to be, the bound alone decides.
No kernel may reach another device: no remote copies, remote signals or barrier semaphores. Data moves between devices by JAX's collectives and lax.ppermute only.
A program may use at most 64 MiB of HBM per device.

v0:
```python
import math

import jax
import jax.numpy as jnp
import numpy as np
from jax import lax
from jax.sharding import PartitionSpec as P

NZ = 512


SPAN_RATE = 1.0 / 32.0


def padded(block, sides, width):
    for axis, dim in sides:
        count = lax.axis_size(axis)
        forward = [(i, i + 1) for i in range(count - 1)]
        forward.append((count - 1, 0))
        backward = [(target, source) for source, target in forward]
        low = lax.ppermute(
            lax.slice_in_dim(block, block.shape[dim] - width, None, axis=dim), axis, forward
        )
        high = lax.ppermute(lax.slice_in_dim(block, 0, width, axis=dim), axis, backward)
        block = jnp.concatenate([low, block, high], axis=dim)
    return block


def legendre_rows(abscissa, node_count):
    legendre = np.zeros((node_count, node_count))
    legendre[:, 0] = 1.0
    legendre[:, 1] = abscissa
    for degree in range(2, node_count):
        legendre[:, degree] = (
            (2 * degree - 1) * abscissa * legendre[:, degree - 1]
            - (degree - 1) * legendre[:, degree - 2]
        ) / degree
    return legendre


def lobatto_matrix(order):
    node_count = order + 1
    abscissa = -np.cos(np.pi * np.arange(node_count) / order)
    for iteration in range(60):
        legendre = legendre_rows(abscissa, node_count)
        abscissa = abscissa - (abscissa * legendre[:, order] - legendre[:, order - 1]) / (
            node_count * legendre[:, order]
        )
    legendre = legendre_rows(abscissa, node_count)
    end_values = legendre[:, order]
    spacing = abscissa[:, None] - abscissa[None, :] + np.eye(node_count)
    matrix = end_values[:, None] / (end_values[None, :] * spacing)
    matrix = matrix * (1.0 - np.eye(node_count))
    matrix[0, 0] = -order * node_count / 4.0
    matrix[order, order] = order * node_count / 4.0
    return matrix


def grad_table():
    lobatto = lobatto_matrix(8)
    return np.concatenate([np.kron(np.eye(9), lobatto).T, np.kron(lobatto, np.eye(9)).T], axis=1)


def edge_table():
    positions = np.arange(9)
    outline = [positions, positions * 9 + 8, 72 + (8 - positions), (8 - positions) * 9]
    return np.stack(outline)[:, 1:8]


def spectral_tables(length):
    plane_ids = jnp.arange(length, dtype=jnp.int32)[:, None]
    slot_ids = jnp.arange(length, dtype=jnp.int32)[None, :]
    wavenum = jnp.where(slot_ids == 1, length // 2, slot_ids // 2)
    phases = plane_ids * wavenum % length
    angles = phases.astype(jnp.float32) * (2.0 * math.pi / length)
    sine_slot = (slot_ids % 2 == 1) & (slot_ids > 1)
    inverse_table = jnp.where(sine_slot, jnp.sin(angles), jnp.cos(angles))
    wave_rate = jnp.where(slot_ids == 1, 0, wavenum).astype(jnp.float32) * SPAN_RATE
    slope_table = wave_rate * jnp.where(sine_slot, jnp.cos(angles), -jnp.sin(angles))
    weight = jnp.where(slot_ids <= 1, 1.0 / length, 2.0 / length)
    forward_table = (inverse_table * weight).T
    return (inverse_table, slope_table, forward_table)


def plane_gradients(signal, metric):
    components, extent, points = signal.shape
    elements = points // 81
    flat_rows = signal.reshape(components * extent * elements, 81)
    table = jnp.asarray(grad_table(), jnp.float32)
    pair_grad = jnp.dot(flat_rows, table, precision=lax.Precision.HIGHEST)
    pair_grad = pair_grad.reshape(components, extent, elements, 162)
    along_xi = pair_grad[..., :81]
    along_eta = pair_grad[..., 81:]
    metrics = metric.reshape(4, 1, 1, elements, 81)
    dudx = metrics[0] * along_xi + metrics[2] * along_eta
    dudy = metrics[1] * along_xi + metrics[3] * along_eta
    return jnp.concatenate([dudx, dudy], 0).reshape(2 * components, extent, points)


def edge_inner(elements, edges):
    inner = jnp.asarray(edge_table(), jnp.int32)
    return elements[:, None] * 81 + jnp.take(inner, edges, axis=0)


def make_settle(first_side, second_side, lower_flat, upper_flat, side_count):

    def flipped(rims):
        components, extent, width = rims.shape
        return rims.reshape(components, extent, side_count, 7)[..., ::-1].reshape(
            components, extent, width
        )

    def edge_rims(signal):
        return jnp.stack([signal[..., lower_flat], signal[..., upper_flat]])

    def settle(signal, extended):
        own_side = signal[..., first_side]
        far_side = signal[..., second_side]
        average = (own_side + far_side) * 0.5
        signal = signal.at[..., first_side].set(average).at[..., second_side].set(average)
        lower_mean = (extended[1] + flipped(extended[0])) * 0.5
        upper_mean = (extended[2] + flipped(extended[3])) * 0.5
        return signal.at[..., lower_flat].set(lower_mean).at[..., upper_flat].set(upper_mean)

    return (edge_rims, settle)


def on_device(velocity_modes, metric, pair_table, bound_table):
    highest = lax.Precision.HIGHEST
    side_count = bound_table.shape[0] // 2
    first_side = edge_inner(pair_table[:, 0], pair_table[:, 1])
    second_side = edge_inner(pair_table[:, 2], pair_table[:, 3])[:, ::-1]
    lower_flat = edge_inner(bound_table[:side_count, 0], bound_table[:side_count, 1]).reshape(-1)
    upper_flat = edge_inner(bound_table[side_count:, 0], bound_table[side_count:, 1]).reshape(-1)
    edge_rims, settle = make_settle(first_side, second_side, lower_flat, upper_flat, side_count)
    inverse_table, slope_table, forward_table = spectral_tables(NZ)
    arrived = lax.all_to_all(velocity_modes, "span", split_axis=2, concat_axis=1, tiled=True)
    physical = jnp.einsum("zm,fmp->fzp", inverse_table, arrived, precision=highest)
    span_slope = jnp.einsum("zm,fmp->fzp", slope_table, arrived, precision=highest)
    plane_data = lax.all_to_all(
        jnp.concatenate([physical, span_slope], 0), "span", split_axis=1, concat_axis=2, tiled=True
    )
    gradient = plane_gradients(plane_data[:3], metric)
    extended = padded(edge_rims(gradient), (("dom", 0),), 1)
    gradient = settle(gradient, extended)
    advect = (
        plane_data[0] * gradient[0:3]
        + plane_data[1] * gradient[3:6]
        + plane_data[2] * plane_data[3:6]
    )
    spectra = jnp.einsum(
        "mz,fzp->fmp",
        forward_table,
        lax.all_to_all(advect, "span", split_axis=2, concat_axis=1, tiled=True),
        precision=highest,
    )
    returned = lax.all_to_all(spectra, "span", split_axis=1, concat_axis=2, tiled=True)
    extended = padded(edge_rims(returned), (("dom", 0),), 1)
    return settle(returned, extended)


def solution(mesh):
    return jax.shard_map(
        on_device,
        mesh=mesh,
        in_specs=(P(None, "span", "dom"), P(None, "dom"), P("dom", None), P("dom", None)),
        out_specs=P(None, "span", "dom"),
        check_vma=False,
    )
```

profile of v0, /device:TPU:1, one launch (start us, length us, event | category | flops | bytes accessed | tf_op | source)
XLA Modules:
  0.0 209.0 jit_solution(3187426187291905189)
XLA Ops:
  0.0 1.9 copy.39
  1.9 1.8 reshape.404
  3.7 7.4 %all-to-all-start = ((f32[8,1,15552]{2,1,0:T(1,128)}), f32[8,1,15552]{2,1,0:T(1,128)S(1)}, u32[]{:S(2)}, u32[]{:S(2)}) async-start(f32[8,1,15552]{2,1,0:T(1,128)} %reshape.404), calls=%async_computation | async-start | bytes 999424 | tf_op jit(solution)/shard_map/all_to_all | solution.py:137
  12.6 12.5 %all-to-all-done = f32[8,1,15552]{2,1,0:T(1,128)S(1)} async-done(((f32[8,1,15552]{2,1,0:T(1,128)}), f32[8,1,15552]{2,1,0:T(1,128)S(1)}, u32[]{:S(2)}, u32[]{:S(2)}) %all-to-all-start) | async-done | bytes 497696 | tf_op jit(solution)/shard_map/all_to_all | solution.py:137
  25.6 1.9 reduce.8
  28.8 5.7 %convolution_bitcast_fusion.2 = f32[3,512,81]{1,2,0:T(8,128)S(1)} fusion(f32[3,512,81]{2,1,0:T(8,128)S(1)} %bitcast.148, s32[512]{0:T(512)S(1)} %fusion.34, pred[512]{0:T(512)(128)(4,1)S(1)} %fusion.40), kind=kOutput, calls=%fused_computation.32 | convolution fusion | flops 768344064 | bytes 997888 | tf_op jit(solution)/shard_map/zm,fmp->fzp/dot_general | solution.py:138
  34.6 5.8 %convolution_bitcast_fusion.1 = f32[3,512,81]{1,2,0:T(8,128)S(1)} fusion(f32[3,512,81]{2,1,0:T(8,128)S(1)} %bitcast.149, f32[512]{0:T(512)S(1)} %fusion.36, s32[512]{0:T(512)S(1)} %fusion.34, pred[512]{0:T(512)(128)(4,1)S(1)} %fusion.40), kind=kOutput, calls=%fused_computation.31 | convolution fusion | flops 768868352 | bytes 999936 | tf_op jit(solution)/shard_map/zm,fmp->fzp/dot_general | solution.py:139
  40.4 1.4 copy.43
  41.9 3.1 %reshape.406 = f32[8,1,31104]{2,1,0:T(1,128)} reshape(f32[512,6,81]{2,1,0:T(8,128)S(1)} %bitcast.136) | data formatting | bytes 1990656
  45.0 4.5 %all-to-all-start.1 = ((f32[8,1,31104]{2,1,0:T(1,128)}), f32[8,1,31104]{2,1,0:T(1,128)S(1)}, u32[]{:S(2)}, u32[]{:S(2)}) async-start(f32[8,1,31104]{2,1,0:T(1,128)} %reshape.406), calls=%async_computation.1 | async-start | bytes 1990656 | tf_op jit(solution)/shard_map/all_to_all | solution.py:140
  52.7 21.3 %all-to-all-done.1 = f32[8,1,31104]{2,1,0:T(1,128)S(1)} async-done(((f32[8,1,31104]{2,1,0:T(1,128)}), f32[8,1,31104]{2,1,0:T(1,128)S(1)}, u32[]{:S(2)}, u32[]{:S(2)}) %all-to-all-start.1) | async-done | bytes 995360 | tf_op jit(solution)/shard_map/all_to_all | solution.py:140
  74.1 3.0 %reduce.9 = f32[8,31104]{1,0:T(8,128)S(1)} reduce(f32[8,1,31104]{2,1,0:T(1,128)S(1)} %all-to-all-done.1, f32[]{:T(128)} %broadcast.372), dimensions={1}, to_apply=%all_to_all.54.reduce_sub_computation | reduce | bytes 1990660 | tf_op jit(solution)/shard_map/all_to_all | solution.py:140
  77.1 1.4 reshape.407
  80.4 1.4 fusion.58
  82.1 1.3 pad_maximum_fusion
  83.4 2.4 %copy.68 = f32[6,64,8,81]{1,0,3,2:T(8,128)S(1)} copy(f32[6,64,8,81]{3,2,1,0:T(8,128)} %pad_maximum_fusion) | data formatting | bytes 1990656 | tf_op jit(solution)/shard_map/reshape | solution.py:97
  88.4 4.4 %collective-permute-start = (f32[1,6,64,28]{2,1,3,0:T(8,128)}, f32[1,6,64,28]{2,1,3,0:T(8,128)}, u32[]{:S(2)}, u32[]{:S(2)}) collective-permute-start(f32[1,6,64,28]{2,1,3,0:T(8,128)} %bitcast.24), channel_id=1, source_target_pairs={{0,1},{1,2},{2,3},{3,4},{4,5},{5,6},{6,7},{7,8},{8,9},{9,10},{10,1... | collective-permute-start | bytes 129032 | tf_op jit(solution)/shard_map/ppermute | solution.py:21
  92.8 2.1 slice.127
  95.6 3.1 %scatter_fusion = f32[6,64,648]{1,0,2:T(8,128)S(1)} fusion(f32[6,64,648]{1,0,2:T(8,128)S(1)} %bitcast.126, s32[70]{0:T(128)} %copy-done.8, f32[70,6,64]{2,1,0:T(8,128)S(1)} %add_multiply_fusion), kind=kCustom, calls=%fused_computation.12 | custom fusion | bytes 322840 | tf_op jit(solution)/shard_map/scatter | solution.py:120
  98.7 2.9 %scatter_fusion.1 = f32[6,64,648]{1,0,2:T(8,128)S(1)} fusion(f32[6,64,648]{1,0,2:T(8,128)S(1)} %scatter_fusion, s32[70]{0:T(128)S(1)} %copy-done.6, f32[70,6,64]{2,1,0:T(8,128)S(1)} %add_multiply_fusion), kind=kCustom, calls=%fused_computation.13 | custom fusion | bytes 322840 | tf_op jit(solution)/shard_map/scatter | solution.py:120
  101.7 5.2 %collective-permute-start.1 = (f32[1,6,64,28]{2,1,3,0:T(8,128)S(1)}, f32[1,6,64,28]{2,1,3,0:T(8,128)}, u32[]{:S(2)}, u32[]{:S(2)}) collective-permute-start(f32[1,6,64,28]{2,1,3,0:T(8,128)S(1)} %bitcast.144), channel_id=1, source_target_pairs={{1,0},{2,1},{3,2},{4,3},{5,4},{6,5},{7,6},{8,7},{9,8},{10,9},{11,1... | collective-permute-start | bytes 129032 | tf_op jit(solution)/shard_map/ppermute | solution.py:24
  106.9 1.8 mul.177
  108.7 1.8 copy.46
  110.5 1.8 mul.200
  112.2 1.8 copy.52
  114.1 1.7 mul.203
  115.8 1.8 copy.53
  117.7 1.6 copy.67
  119.3 1.6 rev.16
  121.8 1.6 rev.17
  124.4 1.7 scatter_fusion.2
  126.0 1.7 scatter_fusion.3
  127.7 3.4 %fusion.1 = f32[3,64,648]{1,0,2:T(4,128)} fusion(f32[6,64,648]{1,0,2:T(8,128)S(1)} %scatter_fusion.3, f32[3,64,8,81]{1,0,3,2:T(4,128)} %copy.67, f32[64,648]{0,1:T(8,128)} %copy.53, f32[64,648]{0,1:T(8,128)S(1)} %copy-done.4, f32[64,648]{0,1:T(8,128)S(1)} %copy-done.3), kind=kLoop, calls=%fused_computation.27 | loop fusion | flops 622080 | bytes 2488320 | tf_op jit(solution)/shard_map/add | solution.py:147
  131.1 2.9 %reshape.408 = f32[8,1,15552]{2,1,0:T(1,128)} reshape(f32[648,3,64]{2,1,0:T(4,128)} %bitcast.139) | data formatting | bytes 995328
  134.0 5.0 %all-to-all-start.2 = ((f32[8,1,15552]{2,1,0:T(1,128)}), f32[8,1,15552]{2,1,0:T(1,128)S(1)}, u32[]{:S(2)}, u32[]{:S(2)}) async-start(f32[8,1,15552]{2,1,0:T(1,128)} %reshape.408), calls=%async_computation.2 | async-start | bytes 999424 | tf_op jit(solution)/shard_map/all_to_all | solution.py:154
  139.0 13.9 %all-to-all-done.2 = f32[8,1,15552]{2,1,0:T(1,128)S(1)} async-done(((f32[8,1,15552]{2,1,0:T(1,128)}), f32[8,1,15552]{2,1,0:T(1,128)S(1)}, u32[]{:S(2)}, u32[]{:S(2)}) %all-to-all-start.2) | async-done | bytes 497696 | tf_op jit(solution)/shard_map/all_to_all | solution.py:154
  153.0 1.8 reduce.10
  155.9 6.7 %convolution_bitcast_fusion = f32[3,512,81]{1,2,0:T(8,128)S(1)} fusion(f32[3,512,81]{2,1,0:T(8,128)S(1)} %bitcast.147, f32[512]{0:T(512)S(1)} %fusion.42, s32[512]{0:T(512)S(1)} %copy-done.24, pred[512]{0:T(512)(128)(4,1)S(1)} %copy-done.26), kind=kOutput, calls=%fused_computation.30 | convolution fusion | flops 768606208 | bytes 999936 | tf_op jit(solution)/shard_map/mz,fzp->fmp/dot_general | solution.py:151
  163.1 1.4 reshape.410
  164.4 17.1 %all_to_all.69 = f32[8,1,15552]{2,1,0:T(1,128)S(1)} all-to-all(f32[8,1,15552]{2,1,0:T(1,128)S(1)} %reshape.410), channel_id=1, replica_groups=mesh['span'=8,'dom'=32] {'span'}, dimensions={0} | all-to-all | bytes 995328 | tf_op jit(solution)/shard_map/all_to_all | solution.py:157
  181.5 1.8 reduce.11
  188.0 4.9 %collective-permute-start.3 = (f32[1,3,64,28]{2,1,3,0:T(4,128)S(1)}, f32[1,3,64,28]{2,1,3,0:T(4,128)S(1)}, u32[]{:S(2)}, u32[]{:S(2)}) collective-permute-start(f32[1,3,64,28]{2,1,3,0:T(4,128)S(1)} %bitcast.150), channel_id=1, source_target_pairs={{1,0},{2,1},{3,2},{4,3},{5,4},{6,5},{7,6},{8,7},{9,8},{10,9},{11,1... | collective-permute-start | bytes 64520 | tf_op jit(solution)/shard_map/ppermute | solution.py:24
  193.5 3.0 %scatter_fusion.4 = f32[3,64,648]{1,0,2:T(4,128)S(1)} fusion(f32[3,64,648]{1,0,2:T(4,128)S(1)} %bitcast.131, s32[70]{0:T(128)S(1)} %copy-done.9, f32[70,3,64]{2,1,0:T(4,128)S(1)} %add_multiply_fusion.1), kind=kCustom, calls=%fused_computation.16 | custom fusion | bytes 161560 | tf_op jit(solution)/shard_map/scatter | solution.py:120
  196.5 3.0 %scatter_fusion.5 = f32[3,64,648]{1,0,2:T(4,128)S(1)} fusion(f32[3,64,648]{1,0,2:T(4,128)S(1)} %scatter_fusion.4, s32[70]{0:T(128)S(1)} %copy-done.7, f32[70,3,64]{2,1,0:T(4,128)S(1)} %add_multiply_fusion.1), kind=kCustom, calls=%fused_computation.17 | custom fusion | bytes 161560 | tf_op jit(solution)/shard_map/scatter | solution.py:120
  199.5 4.5 %collective-permute-done.2 = f32[1,3,64,28]{2,1,3,0:T(4,128)S(1)} collective-permute-done((f32[1,3,64,28]{2,1,3,0:T(4,128)S(1)}, f32[1,3,64,28]{2,1,3,0:T(4,128)S(1)}, u32[]{:S(2)}, u32[]{:S(2)}) %collective-permute-start.2) | collective-permute-done | bytes 21536 | tf_op jit(solution)/shard_map/ppermute | solution.py:21
  204.1 1.6 scatter_fusion.6
  205.7 1.6 scatter_fusion.7
  207.3 1.5 copy.60
  (122 shorter events, 20.7 us)
Async XLA Ops:
  1.9 9.3 %copy-start.22 = (s32[10,4]{0,1:T(4,128)S(1)}, s32[10,4]{0,1:T(4,128)}, u32[]{:S(2)}) copy-start(s32[10,4]{0,1:T(4,128)} %param.15) | copy-start | bytes 484
  1.9 9.3 %copy-start = (s32[4,7]{1,0:T(4,128)S(1)}, s32[4,7]{1,0:T(4,128)}, u32[]{:S(2)}) copy-start(s32[4,7]{1,0:T(4,128)} %constant.94.clone2.4) | copy-start | bytes 340
  1.9 10.6 %copy-start.21 = (s32[8,2]{0,1:T(2,128)S(1)}, s32[8,2]{0,1:T(2,128)}, u32[]{:S(2)}) copy-start(s32[8,2]{0,1:T(2,128)} %param.16) | copy-start | bytes 196
  3.7 21.4 %all-to-all-start = ((f32[8,1,15552]{2,1,0:T(1,128)}), f32[8,1,15552]{2,1,0:T(1,128)S(1)}, u32[]{:S(2)}, u32[]{:S(2)}) async-start(f32[8,1,15552]{2,1,0:T(1,128)} %reshape.404), calls=%async_computation | async-start | bytes 999424 | tf_op jit(solution)/shard_map/all_to_all | solution.py:137
  12.5 22.1 %copy-start.25 = (pred[512]{0:T(512)(128)(4,1)}, pred[512]{0:T(512)(128)(4,1)S(1)}, u32[]{:S(2)}) copy-start(pred[512]{0:T(512)(128)(4,1)S(1)} %fusion.40) | copy-start | bytes 1540
  12.5 22.1 %copy-start.23 = (s32[512]{0:T(512)}, s32[512]{0:T(512)S(1)}, u32[]{:S(2)}) copy-start(s32[512]{0:T(512)S(1)} %fusion.34) | copy-start | bytes 6148
  45.0 4.5 %copy-start.15 = (f32[4,648]{1,0:T(4,128)S(1)}, f32[4,648]{1,0:T(4,128)}, u32[]{:S(2)}) copy-start(f32[4,648]{1,0:T(4,128)} %param.14) | copy-start | bytes 31108
  45.0 29.1 %all-to-all-start.1 = ((f32[8,1,31104]{2,1,0:T(1,128)}), f32[8,1,31104]{2,1,0:T(1,128)S(1)}, u32[]{:S(2)}, u32[]{:S(2)}) async-start(f32[8,1,31104]{2,1,0:T(1,128)} %reshape.406), calls=%async_computation.1 | async-start | bytes 1990656 | tf_op jit(solution)/shard_map/all_to_all | solution.py:140
  49.9 24.2 %copy-start.5 = (s32[70]{0:T(128)}, s32[70]{0:T(128)S(1)}, u32[]{:S(2)}) copy-start(s32[70]{0:T(128)S(1)} %reshape.242) | copy-start | bytes 844
  49.9 24.1 %copy-start.8 = (s32[70]{0:T(128)}, s32[70]{0:T(128)S(1)}, u32[]{:S(2)}) copy-start(s32[70]{0:T(128)S(1)} %reshape.298) | copy-start | bytes 844
  51.5 34.3 %copy-start.12 = (s32[1024]{0:T(1024)}, s32[1024]{0:T(1024)S(1)}, u32[]{:S(2)}) copy-start(s32[1024]{0:T(1024)S(1)} %pad_clamp_fusion.4) | copy-start | bytes 12292
  51.5 34.9 %copy-start.10 = (s32[1024]{0:T(1024)}, s32[1024]{0:T(1024)S(1)}, u32[]{:S(2)}) copy-start(s32[1024]{0:T(1024)S(1)} %pad_clamp_fusion.6) | copy-start | bytes 12292
  51.5 0.6 copy-start.19
  52.7 21.4 %copy-start.17 = (s32[28]{0:T(128)}, s32[28]{0:T(128)S(1)}, u32[]{:S(2)}) copy-start(s32[28]{0:T(128)S(1)} %fusion.44) | copy-start | bytes 340
  52.7 34.4 %copy-start.16 = (s32[1024]{0:T(1024)}, s32[1024]{0:T(1024)S(1)}, u32[]{:S(2)}) copy-start(s32[1024]{0:T(1024)S(1)} %pad_clamp_fusion) | copy-start | bytes 12292
  79.4 2.4 %copy-start.1 = (f32[6,8,64,81]{3,1,2,0:T(8,128)}, f32[6,8,64,81]{3,1,2,0:T(8,128)S(1)}, u32[]{:S(2)}) copy-start(f32[6,8,64,81]{3,1,2,0:T(8,128)S(1)} %copy.70) | copy-start | bytes 2985988
  79.4 1.0 copy-start.14
  88.4 30.9 %collective-permute-start = (f32[1,6,64,28]{2,1,3,0:T(8,128)}, f32[1,6,64,28]{2,1,3,0:T(8,128)}, u32[]{:S(2)}, u32[]{:S(2)}) collective-permute-start(f32[1,6,64,28]{2,1,3,0:T(8,128)} %bitcast.24), channel_id=1, source_target_pairs={{0,1},{1,2},{2,3},{3,4},{4,5},{5,6},{6,7},{7,8},{8,9},{9,10},{10,1... | collective-permute-start | bytes 129032 | tf_op jit(solution)/shard_map/ppermute | solution.py:21
  95.6 3.1 %copy-start.6 = (s32[70]{0:T(128)S(1)}, s32[70]{0:T(128)}, u32[]{:S(2)}) copy-start(s32[70]{0:T(128)} %copy-done.5) | copy-start | bytes 844
  101.6 16.0 %copy-start.2 = (f32[3,64,8,81]{3,2,1,0:T(8,128)S(1)}, f32[3,64,8,81]{3,2,1,0:T(8,128)}, u32[]{:S(2)}) copy-start(f32[3,64,8,81]{3,2,1,0:T(8,128)} %slice.127) | copy-start | bytes 1492996
  101.7 20.2 %collective-permute-start.1 = (f32[1,6,64,28]{2,1,3,0:T(8,128)S(1)}, f32[1,6,64,28]{2,1,3,0:T(8,128)}, u32[]{:S(2)}, u32[]{:S(2)}) collective-permute-start(f32[1,6,64,28]{2,1,3,0:T(8,128)S(1)} %bitcast.144), channel_id=1, source_target_pairs={{1,0},{2,1},{3,2},{4,3},{5,4},{6,5},{7,6},{8,7},{9,8},{10,9},{11,1... | collective-permute-start | bytes 129032 | tf_op jit(solution)/shard_map/ppermute | solution.py:24
  119.3 8.4 %copy-start.3 = (f32[64,648]{0,1:T(8,128)S(1)}, f32[64,648]{0,1:T(8,128)}, u32[]{:S(2)}) copy-start(f32[64,648]{0,1:T(8,128)} %copy.46) | copy-start | bytes 497668
  119.3 8.4 %copy-start.4 = (f32[64,648]{0,1:T(8,128)S(1)}, f32[64,648]{0,1:T(8,128)}, u32[]{:S(2)}) copy-start(f32[64,648]{0,1:T(8,128)} %copy.52) | copy-start | bytes 497668
  134.0 19.0 %all-to-all-start.2 = ((f32[8,1,15552]{2,1,0:T(1,128)}), f32[8,1,15552]{2,1,0:T(1,128)S(1)}, u32[]{:S(2)}, u32[]{:S(2)}) async-start(f32[8,1,15552]{2,1,0:T(1,128)} %reshape.408), calls=%async_computation.2 | async-start | bytes 999424 | tf_op jit(solution)/shard_map/all_to_all | solution.py:154
  154.8 1.1 copy-start.24
  154.8 1.1 copy-start.26
  184.4 2.2 %copy-start.13 = (s32[1024]{0:T(1024)S(1)}, s32[1024]{0:T(1024)}, u32[]{:S(2)}) copy-start(s32[1024]{0:T(1024)} %copy-done.12) | copy-start | bytes 12292
  186.6 0.7 copy-start.11
  187.3 6.2 %copy-start.9 = (s32[70]{0:T(128)S(1)}, s32[70]{0:T(128)}, u32[]{:S(2)}) copy-start(s32[70]{0:T(128)} %copy-done.8) | copy-start | bytes 844
  188.0 11.5 %collective-permute-start.3 = (f32[1,3,64,28]{2,1,3,0:T(4,128)S(1)}, f32[1,3,64,28]{2,1,3,0:T(4,128)S(1)}, u32[]{:S(2)}, u32[]{:S(2)}) collective-permute-start(f32[1,3,64,28]{2,1,3,0:T(4,128)S(1)} %bitcast.150), channel_id=1, source_target_pairs={{1,0},{2,1},{3,2},{4,3},{5,4},{6,5},{7,6},{8,7},{9,8},{10,9},{11,1... | collective-permute-start | bytes 64520 | tf_op jit(solution)/shard_map/ppermute | solution.py:24
  192.9 11.2 %collective-permute-start.2 = (f32[1,3,64,28]{2,1,3,0:T(4,128)S(1)}, f32[1,3,64,28]{2,1,3,0:T(4,128)S(1)}, u32[]{:S(2)}, u32[]{:S(2)}) collective-permute-start(f32[1,3,64,28]{2,1,3,0:T(4,128)S(1)} %bitcast.151), channel_id=1, source_target_pairs={{0,1},{1,2},{2,3},{3,4},{4,5},{5,6},{6,7},{7,8},{8,9},{9,10},{10,1... | collective-permute-start | bytes 64520 | tf_op jit(solution)/shard_map/ppermute | solution.py:21
  193.5 3.0 %copy-start.7 = (s32[70]{0:T(128)S(1)}, s32[70]{0:T(128)}, u32[]{:S(2)}) copy-start(s32[70]{0:T(128)} %copy-done.5) | copy-start | bytes 844
  196.5 7.6 %copy-start.20 = (s32[28]{0:T(128)S(1)}, s32[28]{0:T(128)}, u32[]{:S(2)}) copy-start(s32[28]{0:T(128)} %copy-done.19) | copy-start | bytes 340
  196.5 9.2 %copy-start.18 = (s32[28]{0:T(128)S(1)}, s32[28]{0:T(128)}, u32[]{:S(2)}) copy-start(s32[28]{0:T(128)} %copy-done.17) | copy-start | bytes 340
where the time goes:
time: 213 us; the launch traced here: 209 us
  local copies, waits for them, and re-layouts  70.4 us (33%)
  waiting for transfers between devices  52.3 us (25%)
  starting transfers between devices  32 us (15%)
  matrix products  19.6 us (9%)
  blocking collectives  17.1 us (8%)
  other arithmetic  16.6 us (8%)
    all_to_all x1, waiting for transfers between devices, on_device(): lax.all_to_all(jnp.concatenate([physical, span_slope], 0), 'span', split_...  21.3 us
    all_to_all x1, blocking collectives, on_device(): lax.all_to_all(spectra, 'span', split_axis=1, concat_axis=2, tiled=True)  17.1 us
    unnamed x63, local copies, waits for them, and re-layouts  15.3 us
    all_to_all x1, waiting for transfers between devices, on_device(): lax.all_to_all(advect, 'span', split_axis=2, concat_axis=1, tiled=True)  13.9 us
    all_to_all x1, waiting for transfers between devices, on_device(): lax.all_to_all(velocity_modes, 'span', split_axis=2, concat_axis=1, tiled...  12.5 us
    scatter x4, local copies, waits for them, and re-layouts, settle(): signal.at[..., first_side].set(average).at[..., second_side].set(average)  11.9 us
    ppermute x2, starting transfers between devices, padded(): lax.ppermute(lax.slice_in_dim(block, 0, width, axis=dim), axis, backward)  10.2 us
    scatter x5, local copies, waits for them, and re-layouts, settle(): signal.at[..., lower_flat].set(lower_mean).at[..., upper_flat]  7.96 us
  transfers between devices with their start and end apart: 7, of which 4 were waited for; matrix products, arithmetic and copies ran while one was open for 16% of the time, Pallas kernels for 0%

commit v1 on v0

v1 whole, which is shorter than its diff:
```python
import jax
import jax.numpy as jnp
import ml_dtypes
import numpy as np
from jax import lax
from jax.experimental import pallas as pl
from jax.experimental.pallas import tpu as pltpu
from jax.sharding import PartitionSpec as P

NZ = 512
PTS = 81
ELEMS = 8
ROWS = 4
PAIRS = 10
SPAN = 8
MODES = NZ // SPAN
SPAN_RATE = 1.0 / 32.0
BF = jnp.bfloat16
F32 = jnp.float32
LIMIT = 48 * 1024 * 1024


def legendre_rows(abscissa, node_count):
    legendre = np.zeros((node_count, node_count))
    legendre[:, 0] = 1.0
    legendre[:, 1] = abscissa
    for degree in range(2, node_count):
        legendre[:, degree] = (
            (2 * degree - 1) * abscissa * legendre[:, degree - 1]
            - (degree - 1) * legendre[:, degree - 2]
        ) / degree
    return legendre


def lobatto_matrix(order):
    node_count = order + 1
    abscissa = -np.cos(np.pi * np.arange(node_count) / order)
    for _ in range(60):
        legendre = legendre_rows(abscissa, node_count)
        abscissa = abscissa - (abscissa * legendre[:, order] - legendre[:, order - 1]) / (
            node_count * legendre[:, order]
        )
    legendre = legendre_rows(abscissa, node_count)
    end_values = legendre[:, order]
    spacing = abscissa[:, None] - abscissa[None, :] + np.eye(node_count)
    matrix = end_values[:, None] / (end_values[None, :] * spacing)
    matrix = matrix * (1.0 - np.eye(node_count))
    matrix[0, 0] = -order * node_count / 4.0
    matrix[order, order] = order * node_count / 4.0
    return matrix


def edge_points():
    positions = np.arange(9)
    outline = [positions, positions * 9 + 8, 72 + (8 - positions), (8 - positions) * 9]
    return np.stack(outline)[:, 1:8]


def halves(table):
    high = table.astype(np.float32).astype(ml_dtypes.bfloat16)
    low = (table - high.astype(np.float64)).astype(np.float32).astype(ml_dtypes.bfloat16)
    return high, low


def span_tables():
    planes = np.arange(NZ)[None, :]
    slots = np.arange(NZ)[:, None]
    waves = np.where(slots == 1, NZ // 2, slots // 2)
    angles = (planes * waves % NZ) * (2.0 * np.pi / NZ)
    sine = (slots % 2 == 1) & (slots > 1)
    value = np.where(sine, np.sin(angles), np.cos(angles))
    rate = np.where(slots == 1, 0, waves) * SPAN_RATE
    slope = rate * np.where(sine, np.cos(angles), -np.sin(angles))
    return value, slope


def point_matrices():
    lobatto = lobatto_matrix(8)
    return np.kron(np.eye(9), lobatto), np.kron(lobatto, np.eye(9))


def gradient_table():
    along_xi, along_eta = point_matrices()
    table = np.zeros((176, 96))
    table[:81, :81] = along_xi
    table[88:169, :81] = along_eta
    return table


def edge_tables():
    edges = edge_points()
    mats = point_matrices()
    table = np.zeros((256, 1024))
    pick = np.zeros((256, 512))
    for s in range(4):
        for t in range(3):
            for c in range(3):
                for xy in range(2):
                    for i in range(7):
                        lane = s * 128 + t * 42 + c * 14 + xy * 7 + i
                        for h in range(2):
                            table[c * 81 : c * 81 + 81, h * 512 + lane] = mats[h][edges[s, i]]
                        pick[xy * 128 + edges[s, i], lane] = 1.0
    return table, pick


def settle_tables():
    edges = edge_points()
    take = np.zeros((256, 128))
    give = np.zeros((128, 256))
    where = np.zeros((8, 256))
    for s in range(4):
        for c in range(3):
            for i in range(7):
                lane = s * 21 + c * 7 + i
                take[c * 81 + edges[s, 6 - i], lane] = 1.0
                give[lane, c * 81 + edges[s, i]] = 0.5
                where[s, c * 81 + edges[s, i]] = 0.5
    return take, give, where


def row_of(place, part):
    return (place & 1) * ROWS + ((place >> 1) ^ (3 * (part & 1)))


def split(x):
    high = x.astype(BF)
    return high, (x - high.astype(F32)).astype(BF)


def dot(a, b, dims=((1,), (0,))):
    return lax.dot_general(a, b, (dims, ((), ())), preferred_element_type=F32)


def edge_start(edge):
    base = jnp.where(edge == 0, 1, jnp.where(edge == 1, 17, jnp.where(edge == 2, 79, 63)))
    step = jnp.where(edge == 0, 1, jnp.where(edge == 1, 9, jnp.where(edge == 2, -1, -9)))
    return base, step


def list_pairs(pair, count, own, other, other_edge):
    for e in range(ELEMS):
        count[e] = 0
    for n in range(ELEMS * 4):
        own[n] = -1
        other[n] = 0
        other_edge[n] = 0
    for row in range(PAIRS):
        for first, second in ((0, 2), (2, 0)):
            e = pair[row, first]
            slot = e * 4 + count[e]
            own[slot] = pair[row, first + 1]
            other[slot] = pair[row, second]
            other_edge[slot] = pair[row, second + 1]
            count[e] = count[e] + 1


def pack_kernel(bound, v, packed, *outs):
    me, part = lax.axis_index("span"), lax.axis_index("dom")
    for e in range(ELEMS):
        for c in range(3):
            packed[e, :, c * 81 : c * 81 + 81] = v[c, :, e * 81 : e * 81 + 81]
        packed[e, :, 243:256] = jnp.zeros((MODES, 13), F32)
    for k in range(SPAN):
        outs[k][...] = packed[bound[row_of(me ^ k, part), 0]]


def edge_kernel(bound, pair, packed, metric, high, low, pick, columns, *rest):
    outs = rest[:SPAN]
    grads, rows, lines, square, count, own, other, other_edge = rest[SPAN:]
    me, part = lax.axis_index("span"), lax.axis_index("dom")
    list_pairs(pair, count, own, other, other_edge)
    rows[...] = jnp.zeros((16, 256), F32)
    for e in range(ELEMS):
        for j in range(4):
            at = e + 8 * (j // 2)
            lane = 128 * (j % 2)
            rows[at : at + 1, lane : lane + 81] = metric[j : j + 1, e * 81 : e * 81 + 81]
    rows_high, rows_low = split(rows[...])
    scale = dot(rows_high, pick[...]) + dot(rows_low, pick[...])
    values_high, values_low = split(packed[...].reshape(ELEMS * MODES, 256))
    for s in range(4):
        lanes = pl.ds(s * 128, 128)
        parts = []
        for h in range(2):
            at = pl.ds(h * 512 + s * 128, 128)
            parts.append(
                dot(values_high, high[:, at])
                + dot(values_low, high[:, at])
                + dot(values_high, low[:, at])
            )
        for e in range(ELEMS):
            span = slice(e * MODES, (e + 1) * MODES)
            grads[e, s] = (
                parts[0][span] * scale[e : e + 1, s * 128 : s * 128 + 128]
                + parts[1][span] * scale[8 + e : 9 + e, s * 128 : s * 128 + 128]
            )
    lane = lax.broadcasted_iota(jnp.int32, (MODES, 128), 1)
    for k in range(SPAN):
        e = bound[row_of(me ^ k, part), 0]
        picked = [grads[other[e * 4 + t], other_edge[e * 4 + t]] for t in range(3)]
        outs[k][...] = jnp.where(lane < 42, picked[0], jnp.where(lane < 84, picked[1], picked[2]))
    mine = bound[row_of(me, part), 0]
    for n in range(16):
        lines[n] = rows[n : n + 1, :]
    square[...] = jnp.zeros((128, 128), F32)
    for j in range(4):
        line = lines[mine + 8 * (j // 2)]
        square[j : j + 1, :] = line[:, 128 * (j % 2) : 128 * (j % 2) + 128]
    columns[...] = square[...].T


def element_kernel(bound, *rest):
    blocks = rest[:SPAN]
    columns, th, tl, dh, dl, gh, gl = rest[SPAN : SPAN + 7]
    send, mine, u, q, g, modes, value, slope, fields = rest[SPAN + 7 :]
    me, part = lax.axis_index("span"), lax.axis_index("dom")
    for k in range(SPAN):
        modes[pl.ds(pl.multiple_of((me ^ k) * MODES, MODES), MODES), :] = blocks[k][...]
    vh, vl = split(modes[...].T)
    value[0:256] = dot(vh, th[...]) + dot(vl, th[...]) + dot(vh, tl[...])
    slope[0:256] = dot(vh, dh[...]) + dot(vl, dh[...]) + dot(vh, dl[...])
    value[256:264] = jnp.zeros((8, NZ), F32)
    slope[256:264] = jnp.zeros((8, NZ), F32)
    third = value[162:250]
    for c in range(3):
        uh, ul = split(value[81 * c : 81 * c + 96])
        both = dot(gh[...], uh) + dot(gh[...], ul) + dot(gl[...], uh)
        fx, fe = both[:88], both[88:]
        g[c] = columns[0:88, 0:1] * fx + columns[0:88, 2:3] * fe
        g[3 + c] = columns[0:88, 1:2] * fx + columns[0:88, 3:4] * fe
        u[c] = value[81 * c : 81 * c + 88]
        q[c] = third * slope[81 * c : 81 * c + 88]
    base, step = edge_start(bound[row_of(me, part), 1])
    send[...] = jnp.zeros((88, NZ), F32)
    mine[...] = jnp.zeros((88, NZ), F32)
    order = [(g, f) for f in range(6)] + [(u, 0), (u, 1)] + [(q, c) for c in range(3)]
    for f, (ref, at) in enumerate(order):
        for i in range(7):
            line = ref[at, pl.ds(base + step * i, 1), :]
            mine[f * 8 + i : f * 8 + i + 1, :] = line
            send[f * 8 + 6 - i : f * 8 + 7 - i, :] = line


def term_kernel(bound, pair, *rest):
    blocks = rest[:SPAN]
    th, tl, u, q, g, term, modes, count, own, other, other_edge = rest[SPAN:]
    me, part = lax.axis_index("span"), lax.axis_index("dom")
    list_pairs(pair, count, own, other, other_edge)
    for k in range(SPAN):
        modes[pl.ds(pl.multiple_of((me ^ k) * MODES, MODES), MODES), :] = blocks[k][...]
    eh, el = split(modes[...].T)
    planes = dot(eh, th[...]) + dot(el, th[...]) + dot(eh, tl[...])
    ph, pw = split(planes)
    e = bound[row_of(me, part), 0]
    lane = lax.broadcasted_iota(jnp.int32, (88, 128), 1)
    point = lax.broadcasted_iota(jnp.int32, (88, 128), 0)
    slot = jnp.where(lane < 42, 0, jnp.where(lane < 84, 1, 2))
    starts = []
    for t in range(3):
        edge = own[e * 4 + t]
        base, step = edge_start(edge)
        starts.append((jnp.where(edge < 0, -1000, base), step))
    base = jnp.where(slot == 0, starts[0][0], jnp.where(slot == 1, starts[1][0], starts[2][0]))
    step = jnp.where(slot == 0, starts[0][1], jnp.where(slot == 1, starts[1][1], starts[2][1]))
    place = lane - slot * 42
    takes = []
    for f in range(6):
        xy, c = f // 3, f % 3
        i = 6 - (place - (c * 14 + xy * 7))
        hit = (i >= 0) & (i <= 6) & (lane < 126) & (point == base + step * i)
        takes.append(jnp.where(hit, 0.5, 0.0))
    keep = 1.0 - jnp.sum(takes[0], axis=1, keepdims=True)
    take = jnp.concatenate(takes, axis=0).astype(BF)
    far = dot(take, ph) + dot(take, pw)
    for c in range(3):
        value = (
            u[0] * (g[c] * keep + far[c * 88 : c * 88 + 88])
            + u[1] * (g[3 + c] * keep + far[(3 + c) * 88 : (3 + c) * 88 + 88])
            + q[c]
        )
        term[81 * c : 81 * c + 81, :] = value[:81]
    term[243:256, :] = jnp.zeros((13, NZ), F32)


def spectra_kernel(bound, term, mine, other, th, tl, *rest):
    outs = rest[:SPAN]
    work, spec = rest[SPAN:]
    me, part = lax.axis_index("span"), lax.axis_index("dom")
    work[...] = term[...]
    m = [mine[f * 8 : f * 8 + 8, :] for f in range(11)]
    r = [other[f * 8 : f * 8 + 8, :] for f in range(11)]
    base, step = edge_start(bound[row_of(me, part), 1])
    for c in range(3):
        gx = (m[c] + r[c]) * 0.5
        gy = (m[3 + c] + r[3 + c]) * 0.5
        value = (
            (m[6] * gx + m[7] * gy + m[8 + c]) + (r[6] * gx + r[7] * gy + r[8 + c])
        ) * 0.5
        for i in range(7):
            work[pl.ds(81 * c + base + step * i, 1), :] = value[i : i + 1, :]
    wh, wl = split(work[...])
    along = ((1,), (1,))
    total = dot(th[...], wh, along) + dot(th[...], wl, along) + dot(tl[...], wh, along)
    slot = lax.broadcasted_iota(jnp.int32, (NZ, 256), 0)
    spec[...] = total * jnp.where(slot < 2, 1.0 / NZ, 2.0 / NZ)
    for k in range(SPAN):
        outs[k][...] = spec[pl.ds(pl.multiple_of((me ^ k) * MODES, MODES), MODES), :]


def settle_kernel(bound, pair, *rest):
    blocks = rest[:SPAN]
    take, give, where, out, packed, edges, far, count, own, other, other_edge = rest[SPAN:]
    me, part = lax.axis_index("span"), lax.axis_index("dom")
    list_pairs(pair, count, own, other, other_edge)
    for k in range(SPAN):
        packed[bound[row_of(me ^ k, part), 0]] = blocks[k][...]
    ph, pw = split(packed[...].reshape(ELEMS * MODES, 256))
    edges[...] = (dot(ph, take[...]) + dot(pw, take[...])).reshape(ELEMS, MODES, 128)
    lane = lax.broadcasted_iota(jnp.int32, (MODES, 128), 1)
    for e in range(ELEMS):
        total = jnp.zeros((MODES, 128), F32)
        for t in range(3):
            edge = own[e * 4 + t]
            shift = (21 * (edge - other_edge[e * 4 + t]) + 128) & 127
            turned = pltpu.roll(edges[other[e * 4 + t]], shift, 1)
            low = edge * 21
            total = jnp.where((lane >= low) & (lane < low + 21) & (edge >= 0), turned, total)
        far[e] = total
    fh, fl = split(far[...].reshape(ELEMS * MODES, 128))
    given = dot(fh, give[...]) + dot(fl, give[...])
    for e in range(ELEMS):
        keep = jnp.ones((1, 256), F32)
        for t in range(3):
            edge = own[e * 4 + t]
            row = where[pl.ds(jnp.maximum(edge, 0), 1), :]
            keep = keep - jnp.where(edge >= 0, row, 0.0)
        done = packed[e] * keep + given[e * MODES : (e + 1) * MODES]
        for c in range(3):
            out[c, :, e * 81 : e * 81 + 81] = done[:, c * 81 : c * 81 + 81]


def spec_of(space):
    return pl.BlockSpec(memory_space=space)


def call(kernel, name, scalars, arrays, outs, scratch=()):
    shapes = [jax.ShapeDtypeStruct(shape, F32) for shape in outs]
    return pl.pallas_call(
        kernel,
        out_shape=shapes,
        in_specs=[spec_of(pltpu.SMEM)] * len(scalars) + [spec_of(pltpu.VMEM)] * len(arrays),
        out_specs=[spec_of(pltpu.VMEM)] * len(outs),
        scratch_shapes=list(scratch),
        compiler_params=pltpu.CompilerParams(vmem_limit_bytes=LIMIT),
        name=name,
    )(*scalars, *arrays)


def pair_scratch():
    return [pltpu.SMEM((n,), jnp.int32) for n in (ELEMS, ELEMS * 4, ELEMS * 4, ELEMS * 4)]


def exchange(blocks):
    return [blocks[0]] + [
        lax.ppermute(blocks[k], "span", [(s, s ^ k) for s in range(SPAN)])
        for k in range(1, SPAN)
    ]


def side_swap(block, parts):
    def device(part, row, side):
        return ((row ^ (3 * (part & 1))) * 2 + side) * parts + part

    perm = []
    for part in range(parts):
        before = (part - 1) % parts
        for row in range(ROWS):
            perm.append((device(part, row, 0), device(before, row, 1)))
            perm.append((device(before, row, 1), device(part, row, 0)))
    return lax.ppermute(block, ("span", "dom"), perm)


def on_device(velocity_modes, metric, pair_table, bound_table):
    value, slope = span_tables()
    th, tl = halves(value)
    dh, dl = halves(slope)
    gh, gl = halves(gradient_table())
    edge_values, edge_pick = edge_tables()
    ah, al = halves(edge_values)
    pick = halves(edge_pick)[0]
    take, give, where = settle_tables()
    block, edge_block = (MODES, 256), (MODES, 128)

    packed, *blocks = call(
        pack_kernel, "pack", [bound_table], [velocity_modes], [(ELEMS, MODES, 256)] + [block] * SPAN
    )
    blocks = exchange(blocks)
    columns, *edge_blocks = call(
        edge_kernel,
        "edges",
        [bound_table, pair_table],
        [packed, metric, ah, al, pick],
        [(128, 128)] + [edge_block] * SPAN,
        [pltpu.VMEM((ELEMS, 4, MODES, 128), F32), pltpu.VMEM((16, 256), F32), pltpu.VMEM((16, 1, 256), F32), pltpu.VMEM((128, 128), F32)]
        + pair_scratch(),
    )
    edge_blocks = exchange(edge_blocks)
    send, mine, u, q, g = call(
        element_kernel,
        "element",
        [bound_table],
        [*blocks, columns, th, tl, dh, dl, gh, gl],
        [(88, NZ), (88, NZ), (3, 88, NZ), (3, 88, NZ), (6, 88, NZ)],
        [pltpu.VMEM((NZ, 256), F32), pltpu.VMEM((264, NZ), F32), pltpu.VMEM((264, NZ), F32), pltpu.VMEM((8, NZ), F32)],
    )
    other = side_swap(send, lax.axis_size("dom"))
    (term,) = call(
        term_kernel,
        "term",
        [bound_table, pair_table],
        [*edge_blocks, th, tl, u, q, g],
        [(256, NZ)],
        [pltpu.VMEM((NZ, 128), F32)] + pair_scratch(),
    )
    blocks = call(
        spectra_kernel,
        "spectra",
        [bound_table],
        [term, mine, other, th, tl],
        [block] * SPAN,
        [pltpu.VMEM((256, NZ), F32), pltpu.VMEM((NZ, 256), F32)],
    )
    blocks = exchange(blocks)
    (out,) = call(
        settle_kernel,
        "settle",
        [bound_table, pair_table],
        [*blocks, halves(take)[0], halves(give)[0], where.astype(np.float32)],
        [(3, MODES, ELEMS * PTS)],
        [pltpu.VMEM((ELEMS, MODES, 256), F32), pltpu.VMEM((ELEMS, MODES, 128), F32), pltpu.VMEM((ELEMS, MODES, 128), F32)]
        + pair_scratch(),
    )
    return out


def solution(mesh):
    return jax.shard_map(
        on_device,
        mesh=mesh,
        in_specs=(P(None, "span", "dom"), P(None, "dom"), P("dom", None), P("dom", None)),
        out_specs=P(None, "span", "dom"),
        check_vma=False,
    )
```

time: 213 us -> 67.7 us (0.32); the launches traced: 209 us -> 67.2 us
  local copies, waits for them, and re-layouts: 70.4 us -> 6.37 us
  waiting for transfers between devices: 52.3 us -> 8.66 us
  matrix products: 19.6 us -> 0 us
  blocking collectives: 17.1 us -> 0 us
  other arithmetic: 16.6 us -> 0 us
  Pallas kernels: 0 us -> 11.8 us
  starting transfers between devices: 32 us -> 40.1 us
    all_to_all x3 -> x0, waiting for transfers between devices: 47.8 us -> none  [the longest x1 21.3 us: on_device(): lax.all_to_all(jnp.concatenate([physical, span_slope], 0), 'span', split_...]
    ppermute x4 -> x22, starting transfers between devices: 15.1 us -> 40.1 us  [the longest x21 36.2 us: exchange(): lax.ppermute(blocks[k], 'span', [(s, s ^ k) for s in range(SPAN)])]
    scatter x9 -> x0, local copies, waits for them, and re-layouts: 19.9 us -> none  [the longest x4 11.9 us: settle(): signal.at[..., first_side].set(average).at[..., second_side].set(average)]
    dot_general x4 -> x0, matrix products: 19.6 us -> none  [the longest x1 6.68 us: on_device(): jnp.einsum('mz,fzp->fmp', forward_table, lax.all_to_all(advect, 'span', s...]
    all_to_all x1 -> x0, blocking collectives: 17.1 us -> none  [on_device(): lax.all_to_all(spectra, 'span', split_axis=1, concat_axis=2, tiled=True)]
    all_to_all x3 -> x0, starting transfers between devices: 16.9 us -> none  [the longest x1 7.4 us: on_device(): lax.all_to_all(velocity_modes, 'span', split_axis=2, concat_axis=1, tiled...]
    pallas_call x0 -> x6, Pallas kernels: none -> 11.8 us  [call(): pl.pallas_call(kernel, out_shape=shapes, in_specs=[spec_of(pltpu.SMEM)] *...]
    mul x10 -> x0, local copies, waits for them, and re-layouts: 11 us -> none  [the longest x2 3.59 us: on_device(): plane_data[1] * gradient[3:6]]
  transfers between devices with their start and end apart: 7 -> 22, of which waited for: 4 -> 4; matrix products, arithmetic and copies ran while one was open for 16% -> 1% of each run, Pallas kernels for 0% -> 7%
where the time goes in v1:
time: 67.7 us; the launch traced here: 67.2 us
  starting transfers between devices  40.1 us (59%)
  Pallas kernels  11.8 us (17%)
  waiting for transfers between devices  8.66 us (13%)
  local copies, waits for them, and re-layouts  6.37 us (9%)
    ppermute x21, starting transfers between devices, exchange(): lax.ppermute(blocks[k], 'span', [(s, s ^ k) for s in range(SPAN)])  36.2 us
    pallas_call x6, Pallas kernels, call(): pl.pallas_call(kernel, out_shape=shapes, in_specs=[spec_of(pltpu.SMEM)] *...  11.8 us
    ppermute x21, waiting for transfers between devices, exchange(): lax.ppermute(blocks[k], 'span', [(s, s ^ k) for s in range(SPAN)])  8.66 us
    unnamed x30, local copies, waits for them, and re-layouts  6.37 us
    ppermute x1, starting transfers between devices, side_swap(): return lax.ppermute(block, ('span', 'dom'), perm)  3.98 us
  transfers between devices with their start and end apart: 22, of which 4 were waited for; matrix products, arithmetic and copies ran while one was open for 1% of the time, Pallas kernels for 7%

profile of v1, /device:TPU:1, one launch (start us, length us, event | category | flops | bytes accessed | tf_op | source)
XLA Modules:
  0.0 67.2 jit_solution(4177619272816440319)
XLA Ops:
  0.0 0.8 %copy.24.bound = s32[8,2]{1,0:T(8,128)S(1)} copy(s32[8,2]{0,1:T(2,128)} %param.19) | data formatting | bytes 128 | tf_op args[3]
  0.8 1.1 %copy-done.2 = f32[3,64,648]{2,1,0:T(8,128)S(1)} copy-done((f32[3,64,648]{2,1,0:T(8,128)S(1)}, f32[3,64,648]{2,1,0:T(8,128)}, u32[]{:S(2)}) %copy-start.2) | copy-done | bytes 497688
  1.8 1.0 %pack.1 = (f32[8,64,256]{2,1,0:T(8,128)S(1)}, f32[64,256]{1,0:T(8,128)S(1)}, f32[64,256]{1,0:T(8,128)S(1)}, f32[64,256]{1,0:T(8,128)S(1)}, f32[64,256]{1,0:T(8,1...) custom-call(s32[8,2]{1,0:T(8,128)S(1)} %copy.24.bound, ...), custom_call_target="tpu_custom_call" | custom-call | tf_op jit(solution)/shard_map/pack/pallas_call | solution.py:349
  2.8 0.0 copy-start
  2.8 0.0 copy-start.1
  2.8 3.3 %collective-permute-start.7 = (f32[64,256]{1,0:T(8,128)S(1)}, f32[64,256]{1,0:T(8,128)S(1)}, u32[]{:S(2)}, u32[]{:S(2)}) collective-permute-start(f32[64,256]{1,0:T(8,128)S(1)} %get-tuple-element.46), channel_id=1, source_target_pairs={{0,32},{32,0},{64,96},{96,64},{128,160},{160,128},{192,224},{224,1... | collective-permute-start | bytes 196616 | tf_op jit(solution)/shard_map/ppermute | solution.py:366
  6.2 1.7 %collective-permute-start.9 = (f32[64,256]{1,0:T(8,128)S(1)}, f32[64,256]{1,0:T(8,128)S(1)}, u32[]{:S(2)}, u32[]{:S(2)}) collective-permute-start(f32[64,256]{1,0:T(8,128)S(1)} %get-tuple-element.48), channel_id=1, source_target_pairs={{0,96},{32,64},{64,32},{96,0},{128,224},{160,192},{192,160},{224,1... | collective-permute-start | bytes 196616 | tf_op jit(solution)/shard_map/ppermute | solution.py:366
  7.9 1.3 %collective-permute-start.10 = (f32[64,256]{1,0:T(8,128)S(1)}, f32[64,256]{1,0:T(8,128)S(1)}, u32[]{:S(2)}, u32[]{:S(2)}) collective-permute-start(f32[64,256]{1,0:T(8,128)S(1)} %get-tuple-element.49), channel_id=1, source_target_pairs={{0,128},{32,160},{64,192},{96,224},{128,0},{160,32},{192,64},{224,... | collective-permute-start | bytes 196616 | tf_op jit(solution)/shard_map/ppermute | solution.py:366
  9.2 1.4 %collective-permute-start.11 = (f32[64,256]{1,0:T(8,128)S(1)}, f32[64,256]{1,0:T(8,128)S(1)}, u32[]{:S(2)}, u32[]{:S(2)}) collective-permute-start(f32[64,256]{1,0:T(8,128)S(1)} %get-tuple-element.50), channel_id=1, source_target_pairs={{0,160},{32,128},{64,224},{96,192},{128,32},{160,0},{192,96},{224,... | collective-permute-start | bytes 196616 | tf_op jit(solution)/shard_map/ppermute | solution.py:366
  10.6 0.0 collective-permute-done.7.rest_1_
  10.6 2.6 %collective-permute-start.12 = (f32[64,256]{1,0:T(8,128)S(1)}, f32[64,256]{1,0:T(8,128)S(1)}, u32[]{:S(2)}, u32[]{:S(2)}) collective-permute-start(f32[64,256]{1,0:T(8,128)S(1)} %get-tuple-element.51), channel_id=1, source_target_pairs={{0,192},{32,224},{64,128},{96,160},{128,64},{160,96},{192,0},{224,... | collective-permute-start | bytes 196616 | tf_op jit(solution)/shard_map/ppermute | solution.py:366
  13.2 0.0 collective-permute-done.8.rest_2_
  13.2 0.9 %collective-permute-start.13 = (f32[64,256]{1,0:T(8,128)S(1)}, f32[64,256]{1,0:T(8,128)S(1)}, u32[]{:S(2)}, u32[]{:S(2)}) collective-permute-start(f32[64,256]{1,0:T(8,128)S(1)} %get-tuple-element.52), channel_id=1, source_target_pairs={{0,224},{32,192},{64,160},{96,128},{128,96},{160,64},{192,32},{224... | collective-permute-start | bytes 196616 | tf_op jit(solution)/shard_map/ppermute | solution.py:366
  14.1 0.8 %copy.25.pair = s32[10,4]{1,0:T(8,128)S(1)} copy(s32[10,4]{0,1:T(4,128)} %param.18) | data formatting | bytes 320 | tf_op args[2]
  14.9 1.0 %copy-done.3 = bf16[256,1024]{1,0:T(8,128)(2,1)S(1)} copy-done((bf16[256,1024]{1,0:T(8,128)(2,1)S(1)}, bf16[256,1024]{1,0:T(8,128)(2,1)}, u32[]{:S(2)}) %copy-start.3) | copy-done | bytes 524312
  15.9 1.0 %copy-done.4 = bf16[256,1024]{1,0:T(8,128)(2,1)S(1)} copy-done((bf16[256,1024]{1,0:T(8,128)(2,1)S(1)}, bf16[256,1024]{1,0:T(8,128)(2,1)}, u32[]{:S(2)}) %copy-start.4) | copy-done | bytes 524312
  17.0 0.9 %copy-done.7 = bf16[256,512]{1,0:T(8,128)(2,1)S(1)} copy-done((bf16[256,512]{1,0:T(8,128)(2,1)S(1)}, bf16[256,512]{1,0:T(8,128)(2,1)}, u32[]{:S(2)}) %copy-start.7) | copy-done | bytes 262168
  17.9 0.7 %copy-done.12 = f32[4,648]{1,0:T(4,128)S(1)} copy-done((f32[4,648]{1,0:T(4,128)S(1)}, f32[4,648]{1,0:T(4,128)}, u32[]{:S(2)}) %copy-start.12) | copy-done | bytes 10392
  18.6 2.7 %edges.1 = (f32[128,128]{1,0:T(8,128)S(1)}, f32[64,128]{1,0:T(8,128)S(1)}, f32[64,128]{1,0:T(8,128)S(1)}, f32[64,128]{1,0:T(8,128)S(1)}, f32[64,128]{1,0:T(8,128...) custom-call(s32[8,2]{1,0:T(8,128)S(1)} %copy.24.bound, ...), custom_call_target="tpu_custom_call" | custom-call | tf_op jit(solution)/shard_map/edges/pallas_call | solution.py:349
  21.4 0.0 collective-permute-done.10.rest_4_
  21.4 0.0 collective-permute-done.11.rest_5_
  21.4 0.0 collective-permute-done.13.rest_7_
  21.5 2.2 %element.1 = (f32[88,512]{1,0:T(8,128)S(1)}, f32[88,512]{1,0:T(8,128)S(1)}, f32[3,88,512]{2,1,0:T(8,128)S(1)}, f32[3,88,512]{2,1,0:T(8,128)S(1)}, f32[6,88,512]{2,1,0:T(8,128)S(1)}) custom-call(s32[8,2]{1,0:T(8,128)S(1)} %copy.24.bound, f32[64,256]{1,0:T(8,128)S(1)} %get-tuple-element.45.rest_0_, f32[64,256]{1,0:T(8,128)S(1)} %collective-permute-done.7.rest_1_, ...), custom_call_target="tpu_custom_call" | custom-call | tf_op jit(solution)/shard_map/element/pallas_call | solution.py:349
  23.7 4.0 %collective-permute-start.14 = (f32[88,512]{1,0:T(8,128)S(1)}, f32[88,512]{1,0:T(8,128)S(1)}, u32[]{:S(2)}, u32[]{:S(2)}) collective-permute-start(f32[88,512]{1,0:T(8,128)S(1)} %get-tuple-element.58), channel_id=1, source_target_pairs={{0,255},{255,0},{64,191},{191,64},{128,127},{127,128},{192,63},{63... | collective-permute-start | bytes 540680 | tf_op jit(solution)/shard_map/ppermute | solution.py:381
  27.7 5.0 %collective-permute-start = (f32[64,128]{1,0:T(8,128)S(1)}, f32[64,128]{1,0:T(8,128)S(1)}, u32[]{:S(2)}, u32[]{:S(2)}) collective-permute-start(f32[64,128]{1,0:T(8,128)S(1)} %get-tuple-element.38), channel_id=1, source_target_pairs={{0,32},{32,0},{64,96},{96,64},{128,160},{160,128},{192,224},{224,1... | collective-permute-start | bytes 98312 | tf_op jit(solution)/shard_map/ppermute | solution.py:366
  32.7 2.2 %collective-permute-start.1 = (f32[64,128]{1,0:T(8,128)S(1)}, f32[64,128]{1,0:T(8,128)S(1)}, u32[]{:S(2)}, u32[]{:S(2)}) collective-permute-start(f32[64,128]{1,0:T(8,128)S(1)} %get-tuple-element.39), channel_id=1, source_target_pairs={{0,64},{32,96},{64,0},{96,32},{128,192},{160,224},{192,128},{224,1... | collective-permute-start | bytes 98312 | tf_op jit(solution)/shard_map/ppermute | solution.py:366
  34.9 0.0 collective-permute-start.2
  34.9 2.1 %collective-permute-start.3 = (f32[64,128]{1,0:T(8,128)S(1)}, f32[64,128]{1,0:T(8,128)S(1)}, u32[]{:S(2)}, u32[]{:S(2)}) collective-permute-start(f32[64,128]{1,0:T(8,128)S(1)} %get-tuple-element.41), channel_id=1, source_target_pairs={{0,128},{32,160},{64,192},{96,224},{128,0},{160,32},{192,64},{224,... | collective-permute-start | bytes 98312 | tf_op jit(solution)/shard_map/ppermute | solution.py:366
  37.0 0.9 %collective-permute-start.4 = (f32[64,128]{1,0:T(8,128)S(1)}, f32[64,128]{1,0:T(8,128)S(1)}, u32[]{:S(2)}, u32[]{:S(2)}) collective-permute-start(f32[64,128]{1,0:T(8,128)S(1)} %get-tuple-element.42), channel_id=1, source_target_pairs={{0,160},{32,128},{64,224},{96,192},{128,32},{160,0},{192,96},{224,... | collective-permute-start | bytes 98312 | tf_op jit(solution)/shard_map/ppermute | solution.py:366
  37.9 0.0 collective-permute-done.1.rest_2_
  37.9 1.6 %collective-permute-start.5 = (f32[64,128]{1,0:T(8,128)S(1)}, f32[64,128]{1,0:T(8,128)S(1)}, u32[]{:S(2)}, u32[]{:S(2)}) collective-permute-start(f32[64,128]{1,0:T(8,128)S(1)} %get-tuple-element.43), channel_id=1, source_target_pairs={{0,192},{32,224},{64,128},{96,160},{128,64},{160,96},{192,0},{224,... | collective-permute-start | bytes 98312 | tf_op jit(solution)/shard_map/ppermute | solution.py:366
  39.5 0.7 %collective-permute-done.2.rest_3_ = f32[64,128]{1,0:T(8,128)S(1)} collective-permute-done((f32[64,128]{1,0:T(8,128)S(1)}, f32[64,128]{1,0:T(8,128)S(1)}, u32[]{:S(2)}, u32[]{:S(2)}) %collective-permute-start.2) | collective-permute-done | bytes 32800 | tf_op jit(solution)/shard_map/ppermute | solution.py:366
  40.2 3.5 %collective-permute-start.6 = (f32[64,128]{1,0:T(8,128)S(1)}, f32[64,128]{1,0:T(8,128)S(1)}, u32[]{:S(2)}, u32[]{:S(2)}) collective-permute-start(f32[64,128]{1,0:T(8,128)S(1)} %get-tuple-element.44), channel_id=1, source_target_pairs={{0,224},{32,192},{64,160},{96,128},{128,96},{160,64},{192,32},{224... | collective-permute-start | bytes 98312 | tf_op jit(solution)/shard_map/ppermute | solution.py:366
  43.7 1.9 %collective-permute-done.6.rest_7_ = f32[64,128]{1,0:T(8,128)S(1)} collective-permute-done((f32[64,128]{1,0:T(8,128)S(1)}, f32[64,128]{1,0:T(8,128)S(1)}, u32[]{:S(2)}, u32[]{:S(2)}) %collective-permute-start.6) | collective-permute-done | bytes 32800 | tf_op jit(solution)/shard_map/ppermute | solution.py:366
  45.6 1.8 %term.1 = f32[256,512]{1,0:T(8,128)S(1)} custom-call(s32[8,2]{1,0:T(8,128)S(1)} %copy.24.bound, s32[10,4]{1,0:T(8,128)S(1)} %copy.25.pair, f32[64,128]{1,0:T(8,128)S(1)} %get-tuple-element.37.rest_0_, f32[64,128]{1,0:T(8,128)S(1)} %collective-permute-done.rest_1_, f32[64,128]{1,0:T(8,128)S(1)} %collective-permute-done.1.rest_2_, ...), custom_call_target="tpu_custom_call" | custom-call | tf_op jit(solution)/shard_map/term/pallas_call | solution.py:349
  47.4 0.0 copy-start.8
  47.4 0.0 copy-start.9
  47.4 0.0 copy-start.13
  47.4 1.3 %spectra.1 = (f32[64,256]{1,0:T(8,128)S(1)}, f32[64,256]{1,0:T(8,128)S(1)}, f32[64,256]{1,0:T(8,128)S(1)}, f32[64,256]{1,0:T(8,128)S(1)}, f32[64,256]{1,0:T(8,12...) custom-call(s32[8,2]{1,0:T(8,128)S(1)} %copy.24.bound, f32[256,512]{1,0:T(8,128)S(1)} %term.1, ...), custom_call_target="tpu_custom_call" | custom-call | tf_op jit(solution)/shard_map/spectra/pallas_call | solution.py:349
  48.8 1.8 %collective-permute-start.15 = (f32[64,256]{1,0:T(8,128)S(1)}, f32[64,256]{1,0:T(8,128)S(1)}, u32[]{:S(2)}, u32[]{:S(2)}) collective-permute-start(f32[64,256]{1,0:T(8,128)S(1)} %get-tuple-element.60), channel_id=1, source_target_pairs={{0,32},{32,0},{64,96},{96,64},{128,160},{160,128},{192,224},{224,1... | collective-permute-start | bytes 196616 | tf_op jit(solution)/shard_map/ppermute | solution.py:366
  50.5 1.7 %collective-permute-start.17 = (f32[64,256]{1,0:T(8,128)S(1)}, f32[64,256]{1,0:T(8,128)S(1)}, u32[]{:S(2)}, u32[]{:S(2)}) collective-permute-start(f32[64,256]{1,0:T(8,128)S(1)} %get-tuple-element.62), channel_id=1, source_target_pairs={{0,96},{32,64},{64,32},{96,0},{128,224},{160,192},{192,160},{224,1... | collective-permute-start | bytes 196616 | tf_op jit(solution)/shard_map/ppermute | solution.py:366
  52.3 0.3 collective-permute-start.18
  52.5 2.4 %collective-permute-start.19 = (f32[64,256]{1,0:T(8,128)S(1)}, f32[64,256]{1,0:T(8,128)S(1)}, u32[]{:S(2)}, u32[]{:S(2)}) collective-permute-start(f32[64,256]{1,0:T(8,128)S(1)} %get-tuple-element.64), channel_id=1, source_target_pairs={{0,160},{32,128},{64,224},{96,192},{128,32},{160,0},{192,96},{224,... | collective-permute-start | bytes 196616 | tf_op jit(solution)/shard_map/ppermute | solution.py:366
  55.0 1.7 %collective-permute-start.20 = (f32[64,256]{1,0:T(8,128)S(1)}, f32[64,256]{1,0:T(8,128)S(1)}, u32[]{:S(2)}, u32[]{:S(2)}) collective-permute-start(f32[64,256]{1,0:T(8,128)S(1)} %get-tuple-element.65), channel_id=1, source_target_pairs={{0,192},{32,224},{64,128},{96,160},{128,64},{160,96},{192,0},{224,... | collective-permute-start | bytes 196616 | tf_op jit(solution)/shard_map/ppermute | solution.py:366
  56.6 1.8 %collective-permute-start.21 = (f32[64,256]{1,0:T(8,128)S(1)}, f32[64,256]{1,0:T(8,128)S(1)}, u32[]{:S(2)}, u32[]{:S(2)}) collective-permute-start(f32[64,256]{1,0:T(8,128)S(1)} %get-tuple-element.66), channel_id=1, source_target_pairs={{0,224},{32,192},{64,160},{96,128},{128,96},{160,64},{192,32},{224... | collective-permute-start | bytes 196616 | tf_op jit(solution)/shard_map/ppermute | solution.py:366
  58.5 2.6 %collective-permute-done.18.rest_4_ = f32[64,256]{1,0:T(8,128)S(1)} collective-permute-done((f32[64,256]{1,0:T(8,128)S(1)}, f32[64,256]{1,0:T(8,128)S(1)}, u32[]{:S(2)}, u32[]{:S(2)}) %collective-permute-start.18) | collective-permute-done | bytes 65568 | tf_op jit(solution)/shard_map/ppermute | solution.py:366
  61.0 3.4 %collective-permute-done.19.rest_5_ = f32[64,256]{1,0:T(8,128)S(1)} collective-permute-done((f32[64,256]{1,0:T(8,128)S(1)}, f32[64,256]{1,0:T(8,128)S(1)}, u32[]{:S(2)}, u32[]{:S(2)}) %collective-permute-start.19) | collective-permute-done | bytes 65568 | tf_op jit(solution)/shard_map/ppermute | solution.py:366
  64.5 2.7 %settle.1 = f32[3,64,648]{2,1,0:T(8,128)} custom-call(s32[8,2]{1,0:T(8,128)S(1)} %copy.24.bound, s32[10,4]{1,0:T(8,128)S(1)} %copy.25.pair, f32[64,256]{1,0:T(8,128)S(1)} %get-tuple-element.59.rest_0_, f32[64,256]{1,0:T(8,128)S(1)} %collective-permute-done.15.rest_1_, f32[64,256]{1,0:T(8,128)S(1)} %collective-permute-done.16.rest_2_, ...), custom_call_target="tpu_custom_call" | custom-call | tf_op jit(solution)/shard_map/settle/pallas_call | solution.py:349
  (32 shorter events, 0.1 us)
Async XLA Ops:
  0.8 1.1 %copy-start.2 = (f32[3,64,648]{2,1,0:T(8,128)S(1)}, f32[3,64,648]{2,1,0:T(8,128)}, u32[]{:S(2)}) copy-start(f32[3,64,648]{2,1,0:T(8,128)} %v.1) | copy-start | bytes 1492996
  1.8 19.6 %copy-start.5 = (bf16[512,512]{1,0:T(8,128)(2,1)S(1)}, bf16[512,512]{1,0:T(8,128)(2,1)}, u32[]{:S(2)}) copy-start(bf16[512,512]{1,0:T(8,128)(2,1)} %constant.30.clone.rest_12_) | copy-start | bytes 1572868
  1.8 19.6 %copy-start.10 = (bf16[176,96]{1,0:T(8,128)(2,1)S(1)}, bf16[176,96]{1,0:T(8,128)(2,1)}, u32[]{:S(2)}) copy-start(bf16[176,96]{1,0:T(8,128)(2,1)} %constant.32.clone.rest_14_) | copy-start | bytes 101380
  2.8 18.6 %copy-start = (bf16[512,512]{1,0:T(8,128)(2,1)S(1)}, bf16[512,512]{1,0:T(8,128)(2,1)}, u32[]{:S(2)}) copy-start(bf16[512,512]{1,0:T(8,128)(2,1)} %constant.28.clone.rest_10_.rest_9_.tl) | copy-start | bytes 1572868
  2.8 18.6 %copy-start.1 = (bf16[512,512]{1,0:T(8,128)(2,1)S(1)}, bf16[512,512]{1,0:T(8,128)(2,1)}, u32[]{:S(2)}) copy-start(bf16[512,512]{1,0:T(8,128)(2,1)} %constant.27.clone.rest_9_.rest_8_.th) | copy-start | bytes 1572868
  2.8 7.8 %collective-permute-start.7 = (f32[64,256]{1,0:T(8,128)S(1)}, f32[64,256]{1,0:T(8,128)S(1)}, u32[]{:S(2)}, u32[]{:S(2)}) collective-permute-start(f32[64,256]{1,0:T(8,128)S(1)} %get-tuple-element.46), channel_id=1, source_target_pairs={{0,32},{32,0},{64,96},{96,64},{128,160},{160,128},{192,224},{224,1... | collective-permute-start | bytes 196616 | tf_op jit(solution)/shard_map/ppermute | solution.py:366
  6.2 7.0 %collective-permute-start.8 = (f32[64,256]{1,0:T(8,128)S(1)}, f32[64,256]{1,0:T(8,128)S(1)}, u32[]{:S(2)}, u32[]{:S(2)}) collective-permute-start(f32[64,256]{1,0:T(8,128)S(1)} %get-tuple-element.47), channel_id=1, source_target_pairs={{0,64},{32,96},{64,0},{96,32},{128,192},{160,224},{192,128},{224,1... | collective-permute-start | bytes 196616 | tf_op jit(solution)/shard_map/ppermute | solution.py:366
  6.2 15.2 %collective-permute-start.9 = (f32[64,256]{1,0:T(8,128)S(1)}, f32[64,256]{1,0:T(8,128)S(1)}, u32[]{:S(2)}, u32[]{:S(2)}) collective-permute-start(f32[64,256]{1,0:T(8,128)S(1)} %get-tuple-element.48), channel_id=1, source_target_pairs={{0,96},{32,64},{64,32},{96,0},{128,224},{160,192},{192,160},{224,1... | collective-permute-start | bytes 196616 | tf_op jit(solution)/shard_map/ppermute | solution.py:366
  7.9 13.5 %collective-permute-start.10 = (f32[64,256]{1,0:T(8,128)S(1)}, f32[64,256]{1,0:T(8,128)S(1)}, u32[]{:S(2)}, u32[]{:S(2)}) collective-permute-start(f32[64,256]{1,0:T(8,128)S(1)} %get-tuple-element.49), channel_id=1, source_target_pairs={{0,128},{32,160},{64,192},{96,224},{128,0},{160,32},{192,64},{224,... | collective-permute-start | bytes 196616 | tf_op jit(solution)/shard_map/ppermute | solution.py:366
  9.2 12.2 %collective-permute-start.11 = (f32[64,256]{1,0:T(8,128)S(1)}, f32[64,256]{1,0:T(8,128)S(1)}, u32[]{:S(2)}, u32[]{:S(2)}) collective-permute-start(f32[64,256]{1,0:T(8,128)S(1)} %get-tuple-element.50), channel_id=1, source_target_pairs={{0,160},{32,128},{64,224},{96,192},{128,32},{160,0},{192,96},{224,... | collective-permute-start | bytes 196616 | tf_op jit(solution)/shard_map/ppermute | solution.py:366
  10.6 10.8 %collective-permute-start.12 = (f32[64,256]{1,0:T(8,128)S(1)}, f32[64,256]{1,0:T(8,128)S(1)}, u32[]{:S(2)}, u32[]{:S(2)}) collective-permute-start(f32[64,256]{1,0:T(8,128)S(1)} %get-tuple-element.51), channel_id=1, source_target_pairs={{0,192},{32,224},{64,128},{96,160},{128,64},{160,96},{192,0},{224,... | collective-permute-start | bytes 196616 | tf_op jit(solution)/shard_map/ppermute | solution.py:366
  13.2 8.2 %collective-permute-start.13 = (f32[64,256]{1,0:T(8,128)S(1)}, f32[64,256]{1,0:T(8,128)S(1)}, u32[]{:S(2)}, u32[]{:S(2)}) collective-permute-start(f32[64,256]{1,0:T(8,128)S(1)} %get-tuple-element.52), channel_id=1, source_target_pairs={{0,224},{32,192},{64,160},{96,128},{128,96},{160,64},{192,32},{224... | collective-permute-start | bytes 196616 | tf_op jit(solution)/shard_map/ppermute | solution.py:366
  14.9 1.0 %copy-start.3 = (bf16[256,1024]{1,0:T(8,128)(2,1)S(1)}, bf16[256,1024]{1,0:T(8,128)(2,1)}, u32[]{:S(2)}) copy-start(bf16[256,1024]{1,0:T(8,128)(2,1)} %constant.25.clone.low) | copy-start | bytes 1572868
  15.9 1.0 %copy-start.4 = (bf16[256,1024]{1,0:T(8,128)(2,1)S(1)}, bf16[256,1024]{1,0:T(8,128)(2,1)}, u32[]{:S(2)}) copy-start(bf16[256,1024]{1,0:T(8,128)(2,1)} %constant.24.clone.high) | copy-start | bytes 1572868
  17.0 0.9 %copy-start.7 = (bf16[256,512]{1,0:T(8,128)(2,1)S(1)}, bf16[256,512]{1,0:T(8,128)(2,1)}, u32[]{:S(2)}) copy-start(bf16[256,512]{1,0:T(8,128)(2,1)} %constant.26.clone.pick) | copy-start | bytes 786436
  17.9 0.7 %copy-start.12 = (f32[4,648]{1,0:T(4,128)S(1)}, f32[4,648]{1,0:T(4,128)}, u32[]{:S(2)}) copy-start(f32[4,648]{1,0:T(4,128)} %metric.1) | copy-start | bytes 31108
  18.6 2.8 %copy-start.6 = (bf16[512,512]{1,0:T(8,128)(2,1)S(1)}, bf16[512,512]{1,0:T(8,128)(2,1)}, u32[]{:S(2)}) copy-start(bf16[512,512]{1,0:T(8,128)(2,1)} %constant.29.clone.rest_11_) | copy-start | bytes 1572868
  18.6 2.9 %copy-start.11 = (bf16[176,96]{1,0:T(8,128)(2,1)S(1)}, bf16[176,96]{1,0:T(8,128)(2,1)}, u32[]{:S(2)}) copy-start(bf16[176,96]{1,0:T(8,128)(2,1)} %constant.31.clone.rest_13_) | copy-start | bytes 101380
  23.7 23.7 %collective-permute-start.14 = (f32[88,512]{1,0:T(8,128)S(1)}, f32[88,512]{1,0:T(8,128)S(1)}, u32[]{:S(2)}, u32[]{:S(2)}) collective-permute-start(f32[88,512]{1,0:T(8,128)S(1)} %get-tuple-element.58), channel_id=1, source_target_pairs={{0,255},{255,0},{64,191},{191,64},{128,127},{127,128},{192,63},{63... | collective-permute-start | bytes 540680 | tf_op jit(solution)/shard_map/ppermute | solution.py:381
  27.7 9.3 %collective-permute-start = (f32[64,128]{1,0:T(8,128)S(1)}, f32[64,128]{1,0:T(8,128)S(1)}, u32[]{:S(2)}, u32[]{:S(2)}) collective-permute-start(f32[64,128]{1,0:T(8,128)S(1)} %get-tuple-element.38), channel_id=1, source_target_pairs={{0,32},{32,0},{64,96},{96,64},{128,160},{160,128},{192,224},{224,1... | collective-permute-start | bytes 98312 | tf_op jit(solution)/shard_map/ppermute | solution.py:366
  32.7 5.2 %collective-permute-start.1 = (f32[64,128]{1,0:T(8,128)S(1)}, f32[64,128]{1,0:T(8,128)S(1)}, u32[]{:S(2)}, u32[]{:S(2)}) collective-permute-start(f32[64,128]{1,0:T(8,128)S(1)} %get-tuple-element.39), channel_id=1, source_target_pairs={{0,64},{32,96},{64,0},{96,32},{128,192},{160,224},{192,128},{224,1... | collective-permute-start | bytes 98312 | tf_op jit(solution)/shard_map/ppermute | solution.py:366
  34.9 5.3 %collective-permute-start.2 = (f32[64,128]{1,0:T(8,128)S(1)}, f32[64,128]{1,0:T(8,128)S(1)}, u32[]{:S(2)}, u32[]{:S(2)}) collective-permute-start(f32[64,128]{1,0:T(8,128)S(1)} %get-tuple-element.40), channel_id=1, source_target_pairs={{0,96},{32,64},{64,32},{96,0},{128,224},{160,192},{192,160},{224,1... | collective-permute-start | bytes 98312 | tf_op jit(solution)/shard_map/ppermute | solution.py:366
  34.9 8.8 %collective-permute-start.3 = (f32[64,128]{1,0:T(8,128)S(1)}, f32[64,128]{1,0:T(8,128)S(1)}, u32[]{:S(2)}, u32[]{:S(2)}) collective-permute-start(f32[64,128]{1,0:T(8,128)S(1)} %get-tuple-element.41), channel_id=1, source_target_pairs={{0,128},{32,160},{64,192},{96,224},{128,0},{160,32},{192,64},{224,... | collective-permute-start | bytes 98312 | tf_op jit(solution)/shard_map/ppermute | solution.py:366
  37.0 6.7 %collective-permute-start.4 = (f32[64,128]{1,0:T(8,128)S(1)}, f32[64,128]{1,0:T(8,128)S(1)}, u32[]{:S(2)}, u32[]{:S(2)}) collective-permute-start(f32[64,128]{1,0:T(8,128)S(1)} %get-tuple-element.42), channel_id=1, source_target_pairs={{0,160},{32,128},{64,224},{96,192},{128,32},{160,0},{192,96},{224,... | collective-permute-start | bytes 98312 | tf_op jit(solution)/shard_map/ppermute | solution.py:366
  37.9 5.8 %collective-permute-start.5 = (f32[64,128]{1,0:T(8,128)S(1)}, f32[64,128]{1,0:T(8,128)S(1)}, u32[]{:S(2)}, u32[]{:S(2)}) collective-permute-start(f32[64,128]{1,0:T(8,128)S(1)} %get-tuple-element.43), channel_id=1, source_target_pairs={{0,192},{32,224},{64,128},{96,160},{128,64},{160,96},{192,0},{224,... | collective-permute-start | bytes 98312 | tf_op jit(solution)/shard_map/ppermute | solution.py:366
  40.2 5.4 %collective-permute-start.6 = (f32[64,128]{1,0:T(8,128)S(1)}, f32[64,128]{1,0:T(8,128)S(1)}, u32[]{:S(2)}, u32[]{:S(2)}) collective-permute-start(f32[64,128]{1,0:T(8,128)S(1)} %get-tuple-element.44), channel_id=1, source_target_pairs={{0,224},{32,192},{64,160},{96,128},{128,96},{160,64},{192,32},{224... | collective-permute-start | bytes 98312 | tf_op jit(solution)/shard_map/ppermute | solution.py:366
  47.4 17.1 %copy-start.8 = (bf16[128,256]{1,0:T(8,128)(2,1)S(1)}, bf16[128,256]{1,0:T(8,128)(2,1)}, u32[]{:S(2)}) copy-start(bf16[128,256]{1,0:T(8,128)(2,1)} %constant.34.clone.rest_9_) | copy-start | bytes 196612
  47.4 17.1 %copy-start.9 = (bf16[256,128]{1,0:T(8,128)(2,1)S(1)}, bf16[256,128]{1,0:T(8,128)(2,1)}, u32[]{:S(2)}) copy-start(bf16[256,128]{1,0:T(8,128)(2,1)} %constant.33.clone.rest_8_) | copy-start | bytes 196612
  47.4 17.0 %copy-start.13 = (f32[8,256]{1,0:T(8,128)S(1)}, f32[8,256]{1,0:T(8,128)}, u32[]{:S(2)}) copy-start(f32[8,256]{1,0:T(8,128)} %constant.35.clone.rest_10_) | copy-start | bytes 24580
  48.8 6.2 %collective-permute-start.15 = (f32[64,256]{1,0:T(8,128)S(1)}, f32[64,256]{1,0:T(8,128)S(1)}, u32[]{:S(2)}, u32[]{:S(2)}) collective-permute-start(f32[64,256]{1,0:T(8,128)S(1)} %get-tuple-element.60), channel_id=1, source_target_pairs={{0,32},{32,0},{64,96},{96,64},{128,160},{160,128},{192,224},{224,1... | collective-permute-start | bytes 196616 | tf_op jit(solution)/shard_map/ppermute | solution.py:366
  50.5 6.1 %collective-permute-start.16 = (f32[64,256]{1,0:T(8,128)S(1)}, f32[64,256]{1,0:T(8,128)S(1)}, u32[]{:S(2)}, u32[]{:S(2)}) collective-permute-start(f32[64,256]{1,0:T(8,128)S(1)} %get-tuple-element.61), channel_id=1, source_target_pairs={{0,64},{32,96},{64,0},{96,32},{128,192},{160,224},{192,128},{224,1... | collective-permute-start | bytes 196616 | tf_op jit(solution)/shard_map/ppermute | solution.py:366
  50.5 7.9 %collective-permute-start.17 = (f32[64,256]{1,0:T(8,128)S(1)}, f32[64,256]{1,0:T(8,128)S(1)}, u32[]{:S(2)}, u32[]{:S(2)}) collective-permute-start(f32[64,256]{1,0:T(8,128)S(1)} %get-tuple-element.62), channel_id=1, source_target_pairs={{0,96},{32,64},{64,32},{96,0},{128,224},{160,192},{192,160},{224,1... | collective-permute-start | bytes 196616 | tf_op jit(solution)/shard_map/ppermute | solution.py:366
  52.3 8.8 %collective-permute-start.18 = (f32[64,256]{1,0:T(8,128)S(1)}, f32[64,256]{1,0:T(8,128)S(1)}, u32[]{:S(2)}, u32[]{:S(2)}) collective-permute-start(f32[64,256]{1,0:T(8,128)S(1)} %get-tuple-element.63), channel_id=1, source_target_pairs={{0,128},{32,160},{64,192},{96,224},{128,0},{160,32},{192,64},{224,... | collective-permute-start | bytes 196616 | tf_op jit(solution)/shard_map/ppermute | solution.py:366
  52.5 11.9 %collective-permute-start.19 = (f32[64,256]{1,0:T(8,128)S(1)}, f32[64,256]{1,0:T(8,128)S(1)}, u32[]{:S(2)}, u32[]{:S(2)}) collective-permute-start(f32[64,256]{1,0:T(8,128)S(1)} %get-tuple-element.64), channel_id=1, source_target_pairs={{0,160},{32,128},{64,224},{96,192},{128,32},{160,0},{192,96},{224,... | collective-permute-start | bytes 196616 | tf_op jit(solution)/shard_map/ppermute | solution.py:366
  55.0 9.5 %collective-permute-start.20 = (f32[64,256]{1,0:T(8,128)S(1)}, f32[64,256]{1,0:T(8,128)S(1)}, u32[]{:S(2)}, u32[]{:S(2)}) collective-permute-start(f32[64,256]{1,0:T(8,128)S(1)} %get-tuple-element.65), channel_id=1, source_target_pairs={{0,192},{32,224},{64,128},{96,160},{128,64},{160,96},{192,0},{224,... | collective-permute-start | bytes 196616 | tf_op jit(solution)/shard_map/ppermute | solution.py:366
  56.6 7.8 %collective-permute-start.21 = (f32[64,256]{1,0:T(8,128)S(1)}, f32[64,256]{1,0:T(8,128)S(1)}, u32[]{:S(2)}, u32[]{:S(2)}) collective-permute-start(f32[64,256]{1,0:T(8,128)S(1)} %get-tuple-element.66), channel_id=1, source_target_pairs={{0,224},{32,192},{64,160},{96,128},{128,96},{160,64},{192,32},{224... | collective-permute-start | bytes 196616 | tf_op jit(solution)/shard_map/ppermute | solution.py:366

commit v2 on v1

--- a/solution.py
+++ b/solution.py
@@ -101,7 +101,16 @@
                         for h in range(2):
                             table[c * 81 : c * 81 + 81, h * 512 + lane] = mats[h][edges[s, i]]
                         pick[xy * 128 + edges[s, i], lane] = 1.0
-    return table, pick
+    high, low = halves(table)
+    pick = halves(pick)[0]
+    lanes = [slice(s * 128, s * 128 + 128) for s in range(4)]
+    later = [slice(512 + s * 128, 640 + s * 128) for s in range(4)]
+    return np.stack(
+        [
+            np.concatenate([high[:, n], high[:, m], low[:, n], low[:, m]], axis=1)
+            for n, m in zip(lanes, later)
+        ]
+    ), pick
 
 
 def settle_tables():
@@ -109,6 +118,7 @@
     take = np.zeros((256, 128))
     give = np.zeros((128, 256))
     where = np.zeros((8, 256))
+    put = np.zeros((4, 32, 256))
     for s in range(4):
         for c in range(3):
             for i in range(7):
@@ -116,7 +126,8 @@
                 take[c * 81 + edges[s, 6 - i], lane] = 1.0
                 give[lane, c * 81 + edges[s, i]] = 0.5
                 where[s, c * 81 + edges[s, i]] = 0.5
-    return take, give, where
+                put[s, c * 8 + i, c * 81 + edges[s, i]] = 1.0
+    return take, give, where, put
 
 
 def row_of(place, part):
@@ -147,29 +158,21 @@
         other_edge[n] = 0
     for row in range(PAIRS):
         for first, second in ((0, 2), (2, 0)):
-            e = pair[row, first]
+            e = pair[first, row]
             slot = e * 4 + count[e]
-            own[slot] = pair[row, first + 1]
-            other[slot] = pair[row, second]
-            other_edge[slot] = pair[row, second + 1]
+            own[slot] = pair[first + 1, row]
+            other[slot] = pair[second, row]
+            other_edge[slot] = pair[second + 1, row]
             count[e] = count[e] + 1
 
 
-def pack_kernel(bound, v, packed, *outs):
-    me, part = lax.axis_index("span"), lax.axis_index("dom")
-    for e in range(ELEMS):
-        for c in range(3):
-            packed[e, :, c * 81 : c * 81 + 81] = v[c, :, e * 81 : e * 81 + 81]
-        packed[e, :, 243:256] = jnp.zeros((MODES, 13), F32)
-    for k in range(SPAN):
-        outs[k][...] = packed[bound[row_of(me ^ k, part), 0]]
-
-
-def edge_kernel(bound, pair, packed, metric, high, low, pick, columns, *rest):
-    outs = rest[:SPAN]
-    grads, rows, lines, square, count, own, other, other_edge = rest[SPAN:]
-    me, part = lax.axis_index("span"), lax.axis_index("dom")
-    list_pairs(pair, count, own, other, other_edge)
+def chip_modes(j):
+    chip = (lax.axis_index("span") >> 1) ^ j
+    return pl.ds(pl.multiple_of(chip * 2 * MODES, 2 * MODES), 2 * MODES)
+
+
+def metric_kernel(bound, pair, metric, pick, scale, columns, ready, rows, lines, square):
+    me, part = lax.axis_index("span"), lax.axis_index("dom")
     rows[...] = jnp.zeros((16, 256), F32)
     for e in range(ELEMS):
         for j in range(4):
@@ -177,46 +180,86 @@
             lane = 128 * (j % 2)
             rows[at : at + 1, lane : lane + 81] = metric[j : j + 1, e * 81 : e * 81 + 81]
     rows_high, rows_low = split(rows[...])
-    scale = dot(rows_high, pick[...]) + dot(rows_low, pick[...])
-    values_high, values_low = split(packed[...].reshape(ELEMS * MODES, 256))
     for s in range(4):
-        lanes = pl.ds(s * 128, 128)
-        parts = []
-        for h in range(2):
-            at = pl.ds(h * 512 + s * 128, 128)
-            parts.append(
-                dot(values_high, high[:, at])
-                + dot(values_low, high[:, at])
-                + dot(values_high, low[:, at])
-            )
-        for e in range(ELEMS):
-            span = slice(e * MODES, (e + 1) * MODES)
-            grads[e, s] = (
-                parts[0][span] * scale[e : e + 1, s * 128 : s * 128 + 128]
-                + parts[1][span] * scale[8 + e : 9 + e, s * 128 : s * 128 + 128]
-            )
-    lane = lax.broadcasted_iota(jnp.int32, (MODES, 128), 1)
-    for k in range(SPAN):
-        e = bound[row_of(me ^ k, part), 0]
-        picked = [grads[other[e * 4 + t], other_edge[e * 4 + t]] for t in range(3)]
-        outs[k][...] = jnp.where(lane < 42, picked[0], jnp.where(lane < 84, picked[1], picked[2]))
-    mine = bound[row_of(me, part), 0]
+        here = pick[:, s * 128 : s * 128 + 128]
+        size = dot(rows_high, here) + dot(rows_low, here)
+        for n in range(16):
+            scale[n * 4 + s] = size[n : n + 1, :]
     for n in range(16):
         lines[n] = rows[n : n + 1, :]
     square[...] = jnp.zeros((128, 128), F32)
+    mine = bound[0, row_of(me, part)]
     for j in range(4):
         line = lines[mine + 8 * (j // 2)]
         square[j : j + 1, :] = line[:, 128 * (j % 2) : 128 * (j % 2) + 128]
     columns[...] = square[...].T
+    ready[...] = jnp.full((8, 128), pair[0, 0], jnp.int32).astype(F32)
+
+
+def pack_element(packed, e, core, here, there):
+    for at, v in ((core, here), (1 - core, there)):
+        rows = pl.ds(pl.multiple_of(at * MODES, MODES), MODES)
+        for c in range(3):
+            packed[e, rows, c * 81 : c * 81 + 81] = v[c, :, e * 81 : e * 81 + 81]
+        packed[e, rows, 243:256] = jnp.zeros((MODES, 13), F32)
+
+
+def column_flags(bound, core, flags):
+    for e in range(ELEMS):
+        flags[e] = 0
+    for row in range(ROWS):
+        flags[bound[0, core * ROWS + row]] = 1
+
+
+def pack_kernel(bound, here, there, ready, packed, *rest):
+    outs, flags = rest[:4], rest[4]
+    me, part = lax.axis_index("span"), lax.axis_index("dom")
+    core = me & 1
+    column_flags(bound, core, flags)
+    for e in range(ELEMS):
+        pl.when(flags[e] == 1)(lambda e=e: pack_element(packed, e, core, here, there))
+    for j in range(4):
+        outs[j][...] = packed[bound[0, row_of(me ^ (2 * j), part)]]
+
+
+def edge_kernel(bound, pair, done, here, there, scale, table, *rest):
+    outs = rest[:4]
+    packed, flags, count, own, other, other_edge = rest[4:]
+    me, part = lax.axis_index("span"), lax.axis_index("dom")
+    core = me & 1
+    column_flags(bound, core, flags)
+    list_pairs(pair, count, own, other, other_edge)
+
+    def copy_element(e):
+        packed[e] = done[e]
+
+    for e in range(ELEMS):
+        pl.when(flags[e] == 1)(lambda e=e: copy_element(e))
+        pl.when(flags[e] == 0)(lambda e=e: pack_element(packed, e, core, here, there))
+    lane = lax.broadcasted_iota(jnp.int32, (2 * MODES, 128), 1)
+    for j in range(4):
+        e = bound[0, row_of(me ^ (2 * j), part)]
+        total = jnp.zeros((2 * MODES, 128), F32)
+        for t in range(3):
+            far, edge = other[e * 4 + t], other_edge[e * 4 + t]
+            vh, vl = split(packed[far])
+            high = table[edge, :, 0:256]
+            value = dot(vh, high) + dot(vl, high) + dot(vh, table[edge, :, 256:512])
+            value = (
+                value[:, :128] * scale[far * 4 + edge]
+                + value[:, 128:] * scale[(8 + far) * 4 + edge]
+            )
+            total = jnp.where((lane >= t * 42) & (lane < t * 42 + 42), value, total)
+        outs[j][...] = total
 
 
 def element_kernel(bound, *rest):
-    blocks = rest[:SPAN]
-    columns, th, tl, dh, dl, gh, gl = rest[SPAN : SPAN + 7]
-    send, mine, u, q, g, modes, value, slope, fields = rest[SPAN + 7 :]
-    me, part = lax.axis_index("span"), lax.axis_index("dom")
-    for k in range(SPAN):
-        modes[pl.ds(pl.multiple_of((me ^ k) * MODES, MODES), MODES), :] = blocks[k][...]
+    blocks = rest[:4]
+    columns, th, tl, dh, dl, gh, gl = rest[4:11]
+    send, mine, u, q, g, modes, value, slope = rest[11:]
+    me, part = lax.axis_index("span"), lax.axis_index("dom")
+    for j in range(4):
+        modes[chip_modes(j), :] = blocks[j][...]
     vh, vl = split(modes[...].T)
     value[0:256] = dot(vh, th[...]) + dot(vl, th[...]) + dot(vh, tl[...])
     slope[0:256] = dot(vh, dh[...]) + dot(vl, dh[...]) + dot(vh, dl[...])
@@ -231,28 +274,28 @@
         g[3 + c] = columns[0:88, 1:2] * fx + columns[0:88, 3:4] * fe
         u[c] = value[81 * c : 81 * c + 88]
         q[c] = third * slope[81 * c : 81 * c + 88]
-    base, step = edge_start(bound[row_of(me, part), 1])
-    send[...] = jnp.zeros((88, NZ), F32)
-    mine[...] = jnp.zeros((88, NZ), F32)
+    base, step = edge_start(bound[1, row_of(me, part)])
+    send[77:80] = jnp.zeros((3, NZ), F32)
+    mine[77:80] = jnp.zeros((3, NZ), F32)
     order = [(g, f) for f in range(6)] + [(u, 0), (u, 1)] + [(q, c) for c in range(3)]
     for f, (ref, at) in enumerate(order):
         for i in range(7):
             line = ref[at, pl.ds(base + step * i, 1), :]
-            mine[f * 8 + i : f * 8 + i + 1, :] = line
-            send[f * 8 + 6 - i : f * 8 + 7 - i, :] = line
+            mine[f * 7 + i : f * 7 + i + 1, :] = line
+            send[f * 7 + 6 - i : f * 7 + 7 - i, :] = line
 
 
 def term_kernel(bound, pair, *rest):
-    blocks = rest[:SPAN]
-    th, tl, u, q, g, term, modes, count, own, other, other_edge = rest[SPAN:]
+    blocks = rest[:4]
+    th, tl, u, q, g, term, modes, count, own, other, other_edge = rest[4:]
     me, part = lax.axis_index("span"), lax.axis_index("dom")
     list_pairs(pair, count, own, other, other_edge)
-    for k in range(SPAN):
-        modes[pl.ds(pl.multiple_of((me ^ k) * MODES, MODES), MODES), :] = blocks[k][...]
+    for j in range(4):
+        modes[chip_modes(j), :] = blocks[j][...]
     eh, el = split(modes[...].T)
     planes = dot(eh, th[...]) + dot(el, th[...]) + dot(eh, tl[...])
     ph, pw = split(planes)
-    e = bound[row_of(me, part), 0]
+    e = bound[0, row_of(me, part)]
     lane = lax.broadcasted_iota(jnp.int32, (88, 128), 1)
     point = lax.broadcasted_iota(jnp.int32, (88, 128), 0)
     slot = jnp.where(lane < 42, 0, jnp.where(lane < 84, 1, 2))
@@ -283,38 +326,70 @@
     term[243:256, :] = jnp.zeros((13, NZ), F32)
 
 
-def spectra_kernel(bound, term, mine, other, th, tl, *rest):
-    outs = rest[:SPAN]
-    work, spec = rest[SPAN:]
-    me, part = lax.axis_index("span"), lax.axis_index("dom")
-    work[...] = term[...]
-    m = [mine[f * 8 : f * 8 + 8, :] for f in range(11)]
-    r = [other[f * 8 : f * 8 + 8, :] for f in range(11)]
-    base, step = edge_start(bound[row_of(me, part), 1])
-    for c in range(3):
-        gx = (m[c] + r[c]) * 0.5
-        gy = (m[3 + c] + r[3 + c]) * 0.5
-        value = (
-            (m[6] * gx + m[7] * gy + m[8 + c]) + (r[6] * gx + r[7] * gy + r[8 + c])
-        ) * 0.5
-        for i in range(7):
-            work[pl.ds(81 * c + base + step * i, 1), :] = value[i : i + 1, :]
-    wh, wl = split(work[...])
+def spectra_kernel(term, th, tl, *rest):
+    outs = rest[:4]
+    (spec,) = rest[4:]
+    wh, wl = split(term[...])
     along = ((1,), (1,))
     total = dot(th[...], wh, along) + dot(th[...], wl, along) + dot(tl[...], wh, along)
     slot = lax.broadcasted_iota(jnp.int32, (NZ, 256), 0)
     spec[...] = total * jnp.where(slot < 2, 1.0 / NZ, 2.0 / NZ)
-    for k in range(SPAN):
-        outs[k][...] = spec[pl.ds(pl.multiple_of((me ^ k) * MODES, MODES), MODES), :]
-
-
-def settle_kernel(bound, pair, *rest):
-    blocks = rest[:SPAN]
-    take, give, where, out, packed, edges, far, count, own, other, other_edge = rest[SPAN:]
+    for j in range(4):
+        outs[j][...] = spec[chip_modes(j), :]
+
+
+def side_kernel(mine, other, th, tl, *rest):
+    outs = rest[:4]
+    value, spec = rest[4:]
+    chip = lax.axis_index("span") >> 1
+    m = [mine[f * 7 : f * 7 + 7, :] for f in range(11)]
+    r = [other[f * 7 : f * 7 + 7, :] for f in range(11)]
+    value[...] = jnp.zeros((32, NZ), F32)
+    for c in range(3):
+        gx = (m[c] + r[c]) * 0.5
+        gy = (m[3 + c] + r[3 + c]) * 0.5
+        value[c * 8 : c * 8 + 7, :] = (
+            (m[6] * gx + m[7] * gy + m[8 + c]) + (r[6] * gx + r[7] * gy + r[8 + c])
+        ) * 0.5
+    vh, vl = split(value[...])
+    along = ((1,), (1,))
+    total = dot(vh, th[...], along) + dot(vl, th[...], along) + dot(vh, tl[...], along)
+    slot = lax.broadcasted_iota(jnp.int32, (32, NZ), 1)
+    total = total * jnp.where(slot < 2, 1.0 / NZ, 2.0 / NZ)
+    for z in range(4):
+        spec[z] = total[:, z * 128 : z * 128 + 128]
+    for j in range(4):
+        outs[j][...] = spec[chip ^ j]
+
+
+def merge_kernel(bound, *rest):
+    blocks, sides = rest[:4], rest[4:8]
+    where, put, keep, cross, both = rest[8:]
+    me, part = lax.axis_index("span"), lax.axis_index("dom")
+    core = me & 1
+    mine = pl.ds(pl.multiple_of(core * MODES, MODES), MODES)
+    others = pl.ds(pl.multiple_of((1 - core) * MODES, MODES), MODES)
+    across = ((0,), (0,))
+    for j in range(4):
+        edge = bound[1, row_of(me ^ (2 * j), part)]
+        sh, sl = split(sides[j][...])
+        place = put[edge]
+        both[...] = (
+            blocks[j][...] * (1.0 - 2.0 * where[pl.ds(edge, 1), :])
+            + dot(sh, place, across)
+            + dot(sl, place, across)
+        )
+        keep[j] = both[mine, :]
+        cross[j] = both[others, :]
+
+
+def settle_kernel(bound, pair, keep_blocks, cross_blocks, take, give, where, out, *rest):
+    packed, edges, far, count, own, other, other_edge = rest
     me, part = lax.axis_index("span"), lax.axis_index("dom")
     list_pairs(pair, count, own, other, other_edge)
-    for k in range(SPAN):
-        packed[bound[row_of(me ^ k, part), 0]] = blocks[k][...]
+    for j in range(4):
+        packed[bound[0, row_of(me ^ (2 * j), part)]] = keep_blocks[j]
+        packed[bound[0, row_of(me ^ (2 * j + 1), part)]] = cross_blocks[j]
     ph, pw = split(packed[...].reshape(ELEMS * MODES, 256))
     edges[...] = (dot(ph, take[...]) + dot(pw, take[...])).reshape(ELEMS, MODES, 128)
     lane = lax.broadcasted_iota(jnp.int32, (MODES, 128), 1)
@@ -344,15 +419,17 @@
     return pl.BlockSpec(memory_space=space)
 
 
-def call(kernel, name, scalars, arrays, outs, scratch=()):
+def call(kernel, name, scalars, arrays, outs, scratch=(), weight=1000):
     shapes = [jax.ShapeDtypeStruct(shape, F32) for shape in outs]
     return pl.pallas_call(
         kernel,
         out_shape=shapes,
-        in_specs=[spec_of(pltpu.SMEM)] * len(scalars) + [spec_of(pltpu.VMEM)] * len(arrays),
+        in_specs=[spec_of(pltpu.SMEM)] * len(scalars)
+        + [spec_of(pltpu.VMEM)] * len(arrays),
         out_specs=[spec_of(pltpu.VMEM)] * len(outs),
         scratch_shapes=list(scratch),
         compiler_params=pltpu.CompilerParams(vmem_limit_bytes=LIMIT),
+        cost_estimate=pl.CostEstimate(flops=weight, bytes_accessed=weight, transcendentals=0),
         name=name,
     )(*scalars, *arrays)
 
@@ -361,11 +438,16 @@
     return [pltpu.SMEM((n,), jnp.int32) for n in (ELEMS, ELEMS * 4, ELEMS * 4, ELEMS * 4)]
 
 
-def exchange(blocks):
-    return [blocks[0]] + [
-        lax.ppermute(blocks[k], "span", [(s, s ^ k) for s in range(SPAN)])
-        for k in range(1, SPAN)
-    ]
+def between_chips(blocks):
+    far = {
+        j: lax.ppermute(blocks[j], "span", [(s, s ^ (2 * j)) for s in range(SPAN)])
+        for j in (1, 2, 3)
+    }
+    return [blocks[0], far[1], far[2], far[3]]
+
+
+def between_cores(block):
+    return lax.ppermute(block, "span", [(s, s ^ 1) for s in range(SPAN)])
 
 
 def side_swap(block, parts):
@@ -386,33 +468,52 @@
     th, tl = halves(value)
     dh, dl = halves(slope)
     gh, gl = halves(gradient_table())
-    edge_values, edge_pick = edge_tables()
-    ah, al = halves(edge_values)
-    pick = halves(edge_pick)[0]
-    take, give, where = settle_tables()
-    block, edge_block = (MODES, 256), (MODES, 128)
-
+    edge_table, pick = edge_tables()
+    take, give, where, put = settle_tables()
+    chip, edge_chip = (2 * MODES, 256), (2 * MODES, 128)
+    pair_table, bound_table = pair_table.T, bound_table.T
+    flags = [pltpu.SMEM((ELEMS,), jnp.int32)]
+
+    there = between_cores(velocity_modes)
+    scale, columns, ready = call(
+        metric_kernel,
+        "metric",
+        [bound_table, pair_table],
+        [metric, pick],
+        [(64, 1, 128), (128, 128), (8, 128)],
+        [pltpu.VMEM((16, 256), F32), pltpu.VMEM((16, 1, 256), F32), pltpu.VMEM((128, 128), F32)],
+        weight=8_000_000,
+    )
+    there, ready = lax.optimization_barrier((there, ready))
     packed, *blocks = call(
-        pack_kernel, "pack", [bound_table], [velocity_modes], [(ELEMS, MODES, 256)] + [block] * SPAN
-    )
-    blocks = exchange(blocks)
-    columns, *edge_blocks = call(
+        pack_kernel,
+        "pack",
+        [bound_table],
+        [velocity_modes, there, ready],
+        [(ELEMS, 2 * MODES, 256)] + [chip] * 4,
+        flags,
+        weight=8_000_000,
+    )
+    blocks = between_chips(blocks)
+    blocks[1], packed = lax.optimization_barrier((blocks[1], packed))
+    edge_blocks = call(
         edge_kernel,
         "edges",
         [bound_table, pair_table],
-        [packed, metric, ah, al, pick],
-        [(128, 128)] + [edge_block] * SPAN,
-        [pltpu.VMEM((ELEMS, 4, MODES, 128), F32), pltpu.VMEM((16, 256), F32), pltpu.VMEM((16, 1, 256), F32), pltpu.VMEM((128, 128), F32)]
-        + pair_scratch(),
-    )
-    edge_blocks = exchange(edge_blocks)
+        [packed, velocity_modes, there, scale, edge_table],
+        [edge_chip] * 4,
+        [pltpu.VMEM((ELEMS, 2 * MODES, 256), F32)] + flags + pair_scratch(),
+        weight=8_000_000,
+    )
+    edge_blocks = between_chips(edge_blocks)
+    blocks, edge_blocks[1] = lax.optimization_barrier((blocks, edge_blocks[1]))
     send, mine, u, q, g = call(
         element_kernel,
         "element",
         [bound_table],
         [*blocks, columns, th, tl, dh, dl, gh, gl],
-        [(88, NZ), (88, NZ), (3, 88, NZ), (3, 88, NZ), (6, 88, NZ)],
-        [pltpu.VMEM((NZ, 256), F32), pltpu.VMEM((264, NZ), F32), pltpu.VMEM((264, NZ), F32), pltpu.VMEM((8, NZ), F32)],
+        [(80, NZ), (80, NZ), (3, 88, NZ), (3, 88, NZ), (6, 88, NZ)],
+        [pltpu.VMEM((NZ, 256), F32), pltpu.VMEM((264, NZ), F32), pltpu.VMEM((264, NZ), F32)],
     )
     other = side_swap(send, lax.axis_size("dom"))
     (term,) = call(
@@ -424,21 +525,38 @@
         [pltpu.VMEM((NZ, 128), F32)] + pair_scratch(),
     )
     blocks = call(
-        spectra_kernel,
-        "spectra",
+        spectra_kernel, "spectra", [], [term, th, tl], [chip] * 4, [pltpu.VMEM((NZ, 256), F32)]
+    )
+    blocks = between_chips(blocks)
+    sides = call(
+        side_kernel,
+        "side",
+        [],
+        [mine, other, th, tl],
+        [(32, 128)] * 4,
+        [pltpu.VMEM((32, NZ), F32), pltpu.VMEM((4, 32, 128), F32)],
+    )
+    sides = between_chips(sides)
+    where = where.astype(np.float32)
+    keep, cross = call(
+        merge_kernel,
+        "merge",
         [bound_table],
-        [term, mine, other, th, tl],
-        [block] * SPAN,
-        [pltpu.VMEM((256, NZ), F32), pltpu.VMEM((NZ, 256), F32)],
-    )
-    blocks = exchange(blocks)
+        [*blocks, *sides, where, halves(put)[0]],
+        [(4, MODES, 256)] * 2,
+        [pltpu.VMEM((2 * MODES, 256), F32)],
+    )
     (out,) = call(
         settle_kernel,
         "settle",
         [bound_table, pair_table],
-        [*blocks, halves(take)[0], halves(give)[0], where.astype(np.float32)],
+        [keep, between_cores(cross), halves(take)[0], halves(give)[0], where],
         [(3, MODES, ELEMS * PTS)],
-        [pltpu.VMEM((ELEMS, MODES, 256), F32), pltpu.VMEM((ELEMS, MODES, 128), F32), pltpu.VMEM((ELEMS, MODES, 128), F32)]
+        [
+            pltpu.VMEM((ELEMS, MODES, 256), F32),
+            pltpu.VMEM((ELEMS, MODES, 128), F32),
+            pltpu.VMEM((ELEMS, MODES, 128), F32),
+        ]
         + pair_scratch(),
     )
     return out

time: 67.7 us -> 58.3 us (0.86)
  starting transfers between devices: 40.1 us -> 27 us
  waiting for transfers between devices: 8.66 us -> 12.5 us
  local copies, waits for them, and re-layouts: 6.37 us -> 5.36 us
  Pallas kernels: 11.8 us -> 12.8 us
    ppermute x21 -> x14, starting transfers between devices: 36.2 us -> 21.7 us  [the longest x12 15.8 us: between_chips(): lax.ppermute(blocks[j], 'span', [(s, s ^ 2 * j) for s in range(SPAN)])]
    ppermute x21 -> x14, waiting for transfers between devices: 8.66 us -> 12.5 us  [the longest x12 11.3 us: between_chips(): lax.ppermute(blocks[j], 'span', [(s, s ^ 2 * j) for s in range(SPAN)])]
    ppermute x1, starting transfers between devices: 3.98 us -> 5.32 us  [side_swap(): return lax.ppermute(block, ('span', 'dom'), perm)]
    pallas_call x6 -> x9, Pallas kernels: 11.8 us -> 12.8 us  [call(): pl.pallas_call(kernel, out_shape=shapes, in_specs=[spec_of(pltpu.SMEM)] *...]
    unnamed x30 -> x36, local copies, waits for them, and re-layouts: 6.37 us -> 5.36 us
  transfers between devices with their start and end apart: 22 -> 15, of which waited for: 4 -> 4; matrix products, arithmetic and copies ran while one was open for 1% -> 0% of each run, Pallas kernels for 7% -> 14%
where the time goes in v2:
time: 58.3 us; the launch traced here: 57.9 us
  starting transfers between devices  27 us (46%)
  Pallas kernels  12.8 us (22%)
  waiting for transfers between devices  12.5 us (21%)
  local copies, waits for them, and re-layouts  5.36 us (9%)
    ppermute x12, starting transfers between devices, between_chips(): lax.ppermute(blocks[j], 'span', [(s, s ^ 2 * j) for s in range(SPAN)])  15.8 us
    pallas_call x9, Pallas kernels, call(): pl.pallas_call(kernel, out_shape=shapes, in_specs=[spec_of(pltpu.SMEM)] *...  12.8 us
    ppermute x12, waiting for transfers between devices, between_chips(): lax.ppermute(blocks[j], 'span', [(s, s ^ 2 * j) for s in range(SPAN)])  11.3 us
    ppermute x2, starting transfers between devices, between_cores(): return lax.ppermute(block, 'span', [(s, s ^ 1) for s in range(SPAN)])  5.92 us
    unnamed x36, local copies, waits for them, and re-layouts  5.36 us
    ppermute x1, starting transfers between devices, side_swap(): return lax.ppermute(block, ('span', 'dom'), perm)  5.32 us
  transfers between devices with their start and end apart: 15, of which 4 were waited for; matrix products, arithmetic and copies ran while one was open for 0% of the time, Pallas kernels for 14%

profile of v2, /device:TPU:1, one launch (start us, length us, event | category | flops | bytes accessed | tf_op | source)
XLA Modules:
  0.0 57.9 jit_solution(2195519576684776582)
XLA Ops:
  0.0 3.2 %collective-permute-start = (f32[3,64,648]{2,1,0:T(8,128)}, f32[3,64,648]{2,1,0:T(8,128)S(1)}, u32[]{:S(2)}, u32[]{:S(2)}) collective-permute-start(f32[3,64,648]{2,1,0:T(8,128)} %here.3), channel_id=1, source_target_pairs={{0,32},{32,0},{64,96},{96,64},{128,160},{160,128},{192,224},{224,1... | collective-permute-start | bytes 1493000 | tf_op jit(solution)/shard_map/ppermute | solution.py:450
  3.2 0.9 %copy-done.7 = bf16[256,512]{1,0:T(8,128)(2,1)S(1)} copy-done((bf16[256,512]{1,0:T(8,128)(2,1)S(1)}, bf16[256,512]{1,0:T(8,128)(2,1)}, u32[]{:S(2)}) %copy-start.7) | copy-done | bytes 262168
  4.2 0.7 %copy-done.11 = s32[8,2]{0,1:T(2,128)S(1)} copy-done((s32[8,2]{0,1:T(2,128)S(1)}, s32[8,2]{0,1:T(2,128)}, u32[]{:S(2)}) %copy-start.11) | copy-done | bytes 88
  4.9 0.7 %copy-done.15 = s32[10,4]{0,1:T(4,128)S(1)} copy-done((s32[10,4]{0,1:T(4,128)S(1)}, s32[10,4]{0,1:T(4,128)}, u32[]{:S(2)}) %copy-start.15) | copy-done | bytes 184
  5.6 0.7 %copy-done.17 = f32[4,648]{1,0:T(4,128)S(1)} copy-done((f32[4,648]{1,0:T(4,128)S(1)}, f32[4,648]{1,0:T(4,128)}, u32[]{:S(2)}) %copy-start.17) | copy-done | bytes 10392
  6.3 0.9 %metric.2 = (f32[64,1,128]{2,1,0:T(1,128)S(1)}, f32[128,128]{1,0:T(8,128)S(1)}, f32[8,128]{1,0:T(8,128)S(1)}) custom-call(s32[2,8]{1,0:T(2,128)S(1)} %bitcast.2, s32[4,10]{1,0:T(4,128)S(1)} %bitcast.9, f32[4,648]{1,0:T(4,128)S(1)} %copy-done.17, bf16[256,512]{1,0:T(8,128)(2,1)S(1)} %copy-done.7), custom_call_target="tpu_custom_call" | custom-call | flops 8000000 | bytes 8000000 | tf_op jit(solution)/shard_map/metric/pallas_call | solution.py:424
  7.1 0.0 collective-permute-done.there
  7.2 0.0 copy-start.2
  7.2 1.1 %copy-done.2 = f32[3,64,648]{2,1,0:T(8,128)S(1)} copy-done((f32[3,64,648]{2,1,0:T(8,128)S(1)}, f32[3,64,648]{2,1,0:T(8,128)}, u32[]{:S(2)}) %copy-start.2) | copy-done | bytes 497688
  8.2 1.2 %pack.1 = (f32[8,128,256]{2,1,0:T(8,128)S(1)}, f32[128,256]{1,0:T(8,128)S(1)}, f32[128,256]{1,0:T(8,128)S(1)}, f32[128,256]{1,0:T(8,128)S(1)}, f32[128,256]{1,0:T(8,128)S(1)}) custom-call(s32[2,8]{1,0:T(2,128)S(1)} %bitcast.3, f32[3,64,648]{2,1,0:T(8,128)S(1)} %copy-done.2, f32[3,64,648]{2,1,0:T(8,128)S(1)} %collective-permute-done.there, ...), custom_call_target="tpu_custom_call" | custom-call | flops 8000000 | bytes 8000000 | tf_op jit(solution)/shard_map/pack/pallas_call | solution.py:424
  9.4 0.1 collective-permute-start.1
  9.5 2.9 %collective-permute-start.2 = (f32[128,256]{1,0:T(8,128)S(1)}, f32[128,256]{1,0:T(8,128)S(1)}, u32[]{:S(2)}, u32[]{:S(2)}) collective-permute-start(f32[128,256]{1,0:T(8,128)S(1)} %get-tuple-element.51), channel_id=1, source_target_pairs={{0,128},{32,160},{64,192},{96,224},{128,0},{160,32},{192,64},{224,... | collective-permute-start | bytes 393224 | tf_op jit(solution)/shard_map/ppermute | solution.py:443
  12.4 0.7 %collective-permute-start.3 = (f32[128,256]{1,0:T(8,128)S(1)}, f32[128,256]{1,0:T(8,128)S(1)}, u32[]{:S(2)}, u32[]{:S(2)}) collective-permute-start(f32[128,256]{1,0:T(8,128)S(1)} %get-tuple-element.52), channel_id=1, source_target_pairs={{0,192},{32,224},{64,128},{96,160},{128,64},{160,96},{192,0},{224,... | collective-permute-start | bytes 393224 | tf_op jit(solution)/shard_map/ppermute | solution.py:443
  13.0 4.0 %collective-permute-done.1.rest_1_ = f32[128,256]{1,0:T(8,128)S(1)} collective-permute-done((f32[128,256]{1,0:T(8,128)S(1)}, f32[128,256]{1,0:T(8,128)S(1)}, u32[]{:S(2)}, u32[]{:S(2)}) %collective-permute-start.1) | collective-permute-done | bytes 131104 | tf_op jit(solution)/shard_map/ppermute | solution.py:443
  17.0 1.2 %copy-done.4 = bf16[4,256,512]{2,1,0:T(8,128)(2,1)S(1)} copy-done((bf16[4,256,512]{2,1,0:T(8,128)(2,1)S(1)}, bf16[4,256,512]{2,1,0:T(8,128)(2,1)}, u32[]{:S(2)}) %copy-start.4) | copy-done | bytes 1048600
  18.3 0.0 copy-start.12
  18.3 0.0 copy-start.13
  18.3 2.3 %edges.1 = (f32[128,128]{1,0:T(8,128)S(1)}, f32[128,128]{1,0:T(8,128)S(1)}, f32[128,128]{1,0:T(8,128)S(1)}, f32[128,128]{1,0:T(8,128)S(1)}) custom-call(s32[2,8]{1,0:T(2,128)S(1)} %bitcast.4, s32[4,10]{1,0:T(4,128)S(1)} %bitcast.10, f32[8,128,256]{2,1,0:T(8,128)S(1)} %get-tuple-element.46.done, f32[3,64,648]{2,1,0:T(8,128)S(1)} %copy-done.3, ...), custom_call_target="tpu_custom_call" | custom-call | flops 8000000 | bytes 8000000 | tf_op jit(solution)/shard_map/edges/pallas_call | solution.py:424
  20.6 0.1 collective-permute-start.4
  20.7 1.5 %collective-permute-start.5 = (f32[128,128]{1,0:T(8,128)S(1)}, f32[128,128]{1,0:T(8,128)S(1)}, u32[]{:S(2)}, u32[]{:S(2)}) collective-permute-start(f32[128,128]{1,0:T(8,128)S(1)} %get-tuple-element.55), channel_id=1, source_target_pairs={{0,128},{32,160},{64,192},{96,224},{128,0},{160,32},{192,64},{224,... | collective-permute-start | bytes 196616 | tf_op jit(solution)/shard_map/ppermute | solution.py:443
  22.2 2.0 %collective-permute-start.6 = (f32[128,128]{1,0:T(8,128)S(1)}, f32[128,128]{1,0:T(8,128)S(1)}, u32[]{:S(2)}, u32[]{:S(2)}) collective-permute-start(f32[128,128]{1,0:T(8,128)S(1)} %get-tuple-element.56), channel_id=1, source_target_pairs={{0,192},{32,224},{64,128},{96,160},{128,64},{160,96},{192,0},{224,... | collective-permute-start | bytes 196616 | tf_op jit(solution)/shard_map/ppermute | solution.py:443
  24.2 0.0 collective-permute-done.2.rest_2_
  24.2 0.0 collective-permute-done.3.rest_3_
  24.2 0.0 collective-permute-done.4.rest_1_
  24.3 2.2 %element.1 = (f32[80,512]{1,0:T(8,128)S(1)}, f32[80,512]{1,0:T(8,128)S(1)}, f32[3,88,512]{2,1,0:T(8,128)S(1)}, f32[3,88,512]{2,1,0:T(8,128)S(1)}, f32[6,88,512]{2,1,0:T(8,128)S(1)}) custom-call(s32[2,8]{1,0:T(2,128)S(1)} %bitcast.5, f32[128,256]{1,0:T(8,128)S(1)} %get-tuple-element.57.rest_0_, f32[128,256]{1,0:T(8,128)S(1)} %collective-permute-done.1.rest_1_, ...), custom_call_target="tpu_custom_call" | custom-call | flops 1000 | bytes 1000 | tf_op jit(solution)/shard_map/element/pallas_call | solution.py:424
  26.5 5.3 %collective-permute-start.10 = (f32[80,512]{1,0:T(8,128)S(1)}, f32[80,512]{1,0:T(8,128)S(1)}, u32[]{:S(2)}, u32[]{:S(2)}) collective-permute-start(f32[80,512]{1,0:T(8,128)S(1)} %get-tuple-element.70), channel_id=1, source_target_pairs={{0,255},{255,0},{64,191},{191,64},{128,127},{127,128},{192,63},{63... | collective-permute-start | bytes 491528 | tf_op jit(solution)/shard_map/ppermute | solution.py:463
  31.8 0.0 collective-permute-done.5.rest_2_
  31.8 0.0 collective-permute-done.6.rest_3_
  31.8 1.6 %term.1 = f32[256,512]{1,0:T(8,128)S(1)} custom-call(s32[2,8]{1,0:T(2,128)S(1)} %bitcast.6, s32[4,10]{1,0:T(4,128)S(1)} %bitcast.11, f32[128,128]{1,0:T(8,128)S(1)} %get-tuple-element.48.rest_0_, f32[128,128]{1,0:T(8,128)S(1)} %collective-permute-done.4.rest_1_, f32[128,128]{1,0:T(8,128)S(1)} %collective-permute-done.5.rest_2_, ...), custom_call_target="tpu_custom_call" | custom-call | flops 1000 | bytes 1000 | tf_op jit(solution)/shard_map/term/pallas_call | solution.py:424
  33.4 0.7 %spectra.1 = (f32[128,256]{1,0:T(8,128)S(1)}, f32[128,256]{1,0:T(8,128)S(1)}, f32[128,256]{1,0:T(8,128)S(1)}, f32[128,256]{1,0:T(8,128)S(1)}) custom-call(f32[256,512]{1,0:T(8,128)S(1)} %term.1, bf16[512,512]{1,0:T(8,128)(2,1)S(1)} %copy-done.1, bf16[512,512]{1,0:T(8,128)(2,1)S(1)} %copy-done), custom_call_target="tpu_custom_call" | custom-call | flops 1000 | bytes 1000 | tf_op jit(solution)/shard_map/spectra/pallas_call | solution.py:424
  34.1 0.0 copy-start.10
  34.1 0.0 copy-start.14
  34.1 0.0 copy-start.8
  34.1 0.0 copy-start.9
  34.1 2.5 %collective-permute-start.7 = (f32[128,256]{1,0:T(8,128)S(1)}, f32[128,256]{1,0:T(8,128)S(1)}, u32[]{:S(2)}, u32[]{:S(2)}) collective-permute-start(f32[128,256]{1,0:T(8,128)S(1)} %get-tuple-element.66), channel_id=1, source_target_pairs={{0,64},{32,96},{64,0},{96,32},{128,192},{160,224},{192,128},{224,1... | collective-permute-start | bytes 393224 | tf_op jit(solution)/shard_map/ppermute | solution.py:443
  36.6 0.5 collective-permute-start.8
  37.2 1.6 %collective-permute-start.9 = (f32[128,256]{1,0:T(8,128)S(1)}, f32[128,256]{1,0:T(8,128)S(1)}, u32[]{:S(2)}, u32[]{:S(2)}) collective-permute-start(f32[128,256]{1,0:T(8,128)S(1)} %get-tuple-element.68), channel_id=1, source_target_pairs={{0,192},{32,224},{64,128},{96,160},{128,64},{160,96},{192,0},{224,... | collective-permute-start | bytes 393224 | tf_op jit(solution)/shard_map/ppermute | solution.py:443
  38.8 0.0 collective-permute-done.10.other
  38.8 0.6 %side.1 = (f32[32,128]{1,0:T(8,128)S(1)}, f32[32,128]{1,0:T(8,128)S(1)}, f32[32,128]{1,0:T(8,128)S(1)}, f32[32,128]{1,0:T(8,128)S(1)}) custom-call(f32[80,512]{1,0:T(8,128)S(1)} %get-tuple-element.69.mine, f32[80,512]{1,0:T(8,128)S(1)} %collective-permute-done.10.other, bf16[512,512]{1,0:T(8,128)(2,1)S(1)} %copy-done.1, bf16[512,512]{1,0:T(8,128)(2,1)S(1)} %copy-done), custom_call_target="tpu_custom_call" | custom-call | flops 1000 | bytes 1000 | tf_op jit(solution)/shard_map/side/pallas_call | solution.py:424
  39.4 0.7 %collective-permute-start.11 = (f32[32,128]{1,0:T(8,128)S(1)}, f32[32,128]{1,0:T(8,128)S(1)}, u32[]{:S(2)}, u32[]{:S(2)}) collective-permute-start(f32[32,128]{1,0:T(8,128)S(1)} %get-tuple-element.72), channel_id=1, source_target_pairs={{0,64},{32,96},{64,0},{96,32},{128,192},{160,224},{192,128},{224,1... | collective-permute-start | bytes 49160 | tf_op jit(solution)/shard_map/ppermute | solution.py:443
  40.2 2.1 %collective-permute-start.12 = (f32[32,128]{1,0:T(8,128)S(1)}, f32[32,128]{1,0:T(8,128)S(1)}, u32[]{:S(2)}, u32[]{:S(2)}) collective-permute-start(f32[32,128]{1,0:T(8,128)S(1)} %get-tuple-element.73), channel_id=1, source_target_pairs={{0,128},{32,160},{64,192},{96,224},{128,0},{160,32},{192,64},{224,... | collective-permute-start | bytes 49160 | tf_op jit(solution)/shard_map/ppermute | solution.py:443
  42.3 0.9 %collective-permute-start.13 = (f32[32,128]{1,0:T(8,128)S(1)}, f32[32,128]{1,0:T(8,128)S(1)}, u32[]{:S(2)}, u32[]{:S(2)}) collective-permute-start(f32[32,128]{1,0:T(8,128)S(1)} %get-tuple-element.74), channel_id=1, source_target_pairs={{0,192},{32,224},{64,128},{96,160},{128,64},{160,96},{192,0},{224,... | collective-permute-start | bytes 49160 | tf_op jit(solution)/shard_map/ppermute | solution.py:443
  43.2 2.7 %collective-permute-done.9.rest_3_ = f32[128,256]{1,0:T(8,128)S(1)} collective-permute-done((f32[128,256]{1,0:T(8,128)S(1)}, f32[128,256]{1,0:T(8,128)S(1)}, u32[]{:S(2)}, u32[]{:S(2)}) %collective-permute-start.9) | collective-permute-done | bytes 131104 | tf_op jit(solution)/shard_map/ppermute | solution.py:443
  46.0 4.6 %collective-permute-done.12.rest_6_ = f32[32,128]{1,0:T(8,128)S(1)} collective-permute-done((f32[32,128]{1,0:T(8,128)S(1)}, f32[32,128]{1,0:T(8,128)S(1)}, u32[]{:S(2)}, u32[]{:S(2)}) %collective-permute-start.12) | collective-permute-done | bytes 16416 | tf_op jit(solution)/shard_map/ppermute | solution.py:443
  50.6 0.9 %merge.1 = (f32[4,64,256]{2,1,0:T(8,128)S(1)}, f32[4,64,256]{2,1,0:T(8,128)S(1)}) custom-call(s32[2,8]{1,0:T(2,128)S(1)} %bitcast.7, f32[128,256]{1,0:T(8,128)S(1)} %get-tuple-element.65.rest_0_, f32[128,256]{1,0:T(8,128)S(1)} %collective-permute-done.7.rest_1_, f32[128,256]{1,0:T(8,128)S(1)} %collective-permute-done.8.rest_2_, ...), custom_call_target="tpu_custom_call" | custom-call | flops 1000 | bytes 1000 | tf_op jit(solution)/shard_map/merge/pallas_call | solution.py:424
  51.5 2.7 %collective-permute-start.14 = (f32[4,64,256]{2,1,0:T(8,128)S(1)}, f32[4,64,256]{2,1,0:T(8,128)S(1)}, u32[]{:S(2)}, u32[]{:S(2)}) collective-permute-start(f32[4,64,256]{2,1,0:T(8,128)S(1)} %get-tuple-element.76), channel_id=1, source_target_pairs={{0,32},{32,0},{64,96},{96,64},{128,160},{160,128},{192,224},{224,1... | collective-permute-start | bytes 786440 | tf_op jit(solution)/shard_map/ppermute | solution.py:450
  54.2 1.2 %collective-permute-done.14.cross_blocks = f32[4,64,256]{2,1,0:T(8,128)S(1)} collective-permute-done((f32[4,64,256]{2,1,0:T(8,128)S(1)}, f32[4,64,256]{2,1,0:T(8,128)S(1)}, u32[]{:S(2)}, u32[]{:S(2)}) %collective-permute-start.14) | collective-permute-done | bytes 262176 | tf_op jit(solution)/shard_map/ppermute | solution.py:450
  55.4 2.5 %settle.1 = f32[3,64,648]{2,1,0:T(8,128)} custom-call(s32[2,8]{1,0:T(2,128)S(1)} %bitcast.8, s32[4,10]{1,0:T(4,128)S(1)} %bitcast.12, f32[4,64,256]{2,1,0:T(8,128)S(1)} %get-tuple-element.75.keep_blocks, f32[4,64,256]{2,1,0:T(8,128)S(1)} %collective-permute-done.14.cross_blocks, bf16[256,128]{1,0:T(8,128)(2,1)S(1)} %copy-done.9, ...), custom_call_target="tpu_custom_call" | custom-call | flops 1000 | bytes 1000 | tf_op jit(solution)/shard_map/settle/pallas_call | solution.py:424
  (27 shorter events, 0.1 us)
Async XLA Ops:
  0.0 17.0 %copy-start.16 = (s32[10,4]{0,1:T(4,128)S(1)}, s32[10,4]{0,1:T(4,128)}, u32[]{:S(2)}) copy-start(s32[10,4]{0,1:T(4,128)} %param.18) | copy-start | bytes 484
  0.0 7.1 %collective-permute-start = (f32[3,64,648]{2,1,0:T(8,128)}, f32[3,64,648]{2,1,0:T(8,128)S(1)}, u32[]{:S(2)}, u32[]{:S(2)}) collective-permute-start(f32[3,64,648]{2,1,0:T(8,128)} %here.3), channel_id=1, source_target_pairs={{0,32},{32,0},{64,96},{96,64},{128,160},{160,128},{192,224},{224,1... | collective-permute-start | bytes 1493000 | tf_op jit(solution)/shard_map/ppermute | solution.py:450
  3.2 0.9 %copy-start.7 = (bf16[256,512]{1,0:T(8,128)(2,1)S(1)}, bf16[256,512]{1,0:T(8,128)(2,1)}, u32[]{:S(2)}) copy-start(bf16[256,512]{1,0:T(8,128)(2,1)} %constant.24.clone.pick) | copy-start | bytes 786436
  4.2 0.7 %copy-start.11 = (s32[8,2]{0,1:T(2,128)S(1)}, s32[8,2]{0,1:T(2,128)}, u32[]{:S(2)}) copy-start(s32[8,2]{0,1:T(2,128)} %param.19) | copy-start | bytes 196
  4.9 0.7 %copy-start.15 = (s32[10,4]{0,1:T(4,128)S(1)}, s32[10,4]{0,1:T(4,128)}, u32[]{:S(2)}) copy-start(s32[10,4]{0,1:T(4,128)} %param.18) | copy-start | bytes 484
  5.6 0.7 %copy-start.17 = (f32[4,648]{1,0:T(4,128)S(1)}, f32[4,648]{1,0:T(4,128)}, u32[]{:S(2)}) copy-start(f32[4,648]{1,0:T(4,128)} %metric.3) | copy-start | bytes 31108
  7.2 1.1 %copy-start.2 = (f32[3,64,648]{2,1,0:T(8,128)S(1)}, f32[3,64,648]{2,1,0:T(8,128)}, u32[]{:S(2)}) copy-start(f32[3,64,648]{2,1,0:T(8,128)} %here.3) | copy-start | bytes 1492996
  8.2 8.8 %copy-start.3 = (f32[3,64,648]{2,1,0:T(8,128)S(1)}, f32[3,64,648]{2,1,0:T(8,128)}, u32[]{:S(2)}) copy-start(f32[3,64,648]{2,1,0:T(8,128)} %here.3) | copy-start | bytes 1492996
  9.4 7.6 %collective-permute-start.1 = (f32[128,256]{1,0:T(8,128)S(1)}, f32[128,256]{1,0:T(8,128)S(1)}, u32[]{:S(2)}, u32[]{:S(2)}) collective-permute-start(f32[128,256]{1,0:T(8,128)S(1)} %get-tuple-element.44), channel_id=1, source_target_pairs={{0,64},{32,96},{64,0},{96,32},{128,192},{160,224},{192,128},{224,1... | collective-permute-start | bytes 393224 | tf_op jit(solution)/shard_map/ppermute | solution.py:443
  9.5 14.7 %collective-permute-start.2 = (f32[128,256]{1,0:T(8,128)S(1)}, f32[128,256]{1,0:T(8,128)S(1)}, u32[]{:S(2)}, u32[]{:S(2)}) collective-permute-start(f32[128,256]{1,0:T(8,128)S(1)} %get-tuple-element.51), channel_id=1, source_target_pairs={{0,128},{32,160},{64,192},{96,224},{128,0},{160,32},{192,64},{224,... | collective-permute-start | bytes 393224 | tf_op jit(solution)/shard_map/ppermute | solution.py:443
  12.4 11.8 %collective-permute-start.3 = (f32[128,256]{1,0:T(8,128)S(1)}, f32[128,256]{1,0:T(8,128)S(1)}, u32[]{:S(2)}, u32[]{:S(2)}) collective-permute-start(f32[128,256]{1,0:T(8,128)S(1)} %get-tuple-element.52), channel_id=1, source_target_pairs={{0,192},{32,224},{64,128},{96,160},{128,64},{160,96},{192,0},{224,... | collective-permute-start | bytes 393224 | tf_op jit(solution)/shard_map/ppermute | solution.py:443
  17.0 1.2 %copy-start.4 = (bf16[4,256,512]{2,1,0:T(8,128)(2,1)S(1)}, bf16[4,256,512]{2,1,0:T(8,128)(2,1)}, u32[]{:S(2)}) copy-start(bf16[4,256,512]{2,1,0:T(8,128)(2,1)} %constant.25.clone.table) | copy-start | bytes 3145732
  18.3 6.0 %copy-start = (bf16[512,512]{1,0:T(8,128)(2,1)S(1)}, bf16[512,512]{1,0:T(8,128)(2,1)}, u32[]{:S(2)}) copy-start(bf16[512,512]{1,0:T(8,128)(2,1)} %constant.27.clone.rest_6_.rest_5_.tl) | copy-start | bytes 1572868
  18.3 6.0 %copy-start.1 = (bf16[512,512]{1,0:T(8,128)(2,1)S(1)}, bf16[512,512]{1,0:T(8,128)(2,1)}, u32[]{:S(2)}) copy-start(bf16[512,512]{1,0:T(8,128)(2,1)} %constant.26.clone.rest_5_.rest_4_.th) | copy-start | bytes 1572868
  18.3 6.0 %copy-start.5 = (bf16[512,512]{1,0:T(8,128)(2,1)S(1)}, bf16[512,512]{1,0:T(8,128)(2,1)}, u32[]{:S(2)}) copy-start(bf16[512,512]{1,0:T(8,128)(2,1)} %constant.29.clone.rest_8_) | copy-start | bytes 1572868
  18.3 6.0 %copy-start.6 = (bf16[512,512]{1,0:T(8,128)(2,1)S(1)}, bf16[512,512]{1,0:T(8,128)(2,1)}, u32[]{:S(2)}) copy-start(bf16[512,512]{1,0:T(8,128)(2,1)} %constant.28.clone.rest_7_) | copy-start | bytes 1572868
  18.3 6.0 %copy-start.12 = (bf16[176,96]{1,0:T(8,128)(2,1)S(1)}, bf16[176,96]{1,0:T(8,128)(2,1)}, u32[]{:S(2)}) copy-start(bf16[176,96]{1,0:T(8,128)(2,1)} %constant.31.clone.rest_10_) | copy-start | bytes 101380
  18.3 6.0 %copy-start.13 = (bf16[176,96]{1,0:T(8,128)(2,1)S(1)}, bf16[176,96]{1,0:T(8,128)(2,1)}, u32[]{:S(2)}) copy-start(bf16[176,96]{1,0:T(8,128)(2,1)} %constant.30.clone.rest_9_) | copy-start | bytes 101380
  20.6 3.6 %collective-permute-start.4 = (f32[128,128]{1,0:T(8,128)S(1)}, f32[128,128]{1,0:T(8,128)S(1)}, u32[]{:S(2)}, u32[]{:S(2)}) collective-permute-start(f32[128,128]{1,0:T(8,128)S(1)} %get-tuple-element.53), channel_id=1, source_target_pairs={{0,64},{32,96},{64,0},{96,32},{128,192},{160,224},{192,128},{224,1... | collective-permute-start | bytes 196616 | tf_op jit(solution)/shard_map/ppermute | solution.py:443
  20.7 11.1 %collective-permute-start.5 = (f32[128,128]{1,0:T(8,128)S(1)}, f32[128,128]{1,0:T(8,128)S(1)}, u32[]{:S(2)}, u32[]{:S(2)}) collective-permute-start(f32[128,128]{1,0:T(8,128)S(1)} %get-tuple-element.55), channel_id=1, source_target_pairs={{0,128},{32,160},{64,192},{96,224},{128,0},{160,32},{192,64},{224,... | collective-permute-start | bytes 196616 | tf_op jit(solution)/shard_map/ppermute | solution.py:443
  22.2 9.6 %collective-permute-start.6 = (f32[128,128]{1,0:T(8,128)S(1)}, f32[128,128]{1,0:T(8,128)S(1)}, u32[]{:S(2)}, u32[]{:S(2)}) collective-permute-start(f32[128,128]{1,0:T(8,128)S(1)} %get-tuple-element.56), channel_id=1, source_target_pairs={{0,192},{32,224},{64,128},{96,160},{128,64},{160,96},{192,0},{224,... | collective-permute-start | bytes 196616 | tf_op jit(solution)/shard_map/ppermute | solution.py:443
  26.5 12.4 %collective-permute-start.10 = (f32[80,512]{1,0:T(8,128)S(1)}, f32[80,512]{1,0:T(8,128)S(1)}, u32[]{:S(2)}, u32[]{:S(2)}) collective-permute-start(f32[80,512]{1,0:T(8,128)S(1)} %get-tuple-element.70), channel_id=1, source_target_pairs={{0,255},{255,0},{64,191},{191,64},{128,127},{127,128},{192,63},{63... | collective-permute-start | bytes 491528 | tf_op jit(solution)/shard_map/ppermute | solution.py:463
  34.1 16.5 %copy-start.10 = (bf16[4,32,256]{2,1,0:T(8,128)(2,1)S(1)}, bf16[4,32,256]{2,1,0:T(8,128)(2,1)}, u32[]{:S(2)}) copy-start(bf16[4,32,256]{2,1,0:T(8,128)(2,1)} %constant.33.clone.rest_9_) | copy-start | bytes 196612
  34.1 16.5 %copy-start.14 = (f32[8,256]{1,0:T(8,128)S(1)}, f32[8,256]{1,0:T(8,128)}, u32[]{:S(2)}) copy-start(f32[8,256]{1,0:T(8,128)} %constant.32.clone.rest_8_.where) | copy-start | bytes 24580
  34.1 21.3 %copy-start.8 = (bf16[128,256]{1,0:T(8,128)(2,1)S(1)}, bf16[128,256]{1,0:T(8,128)(2,1)}, u32[]{:S(2)}) copy-start(bf16[128,256]{1,0:T(8,128)(2,1)} %constant.35.clone.give) | copy-start | bytes 196612
  34.1 21.2 %copy-start.9 = (bf16[256,128]{1,0:T(8,128)(2,1)S(1)}, bf16[256,128]{1,0:T(8,128)(2,1)}, u32[]{:S(2)}) copy-start(bf16[256,128]{1,0:T(8,128)(2,1)} %constant.34.clone.take) | copy-start | bytes 196612
  34.1 8.2 %collective-permute-start.7 = (f32[128,256]{1,0:T(8,128)S(1)}, f32[128,256]{1,0:T(8,128)S(1)}, u32[]{:S(2)}, u32[]{:S(2)}) collective-permute-start(f32[128,256]{1,0:T(8,128)S(1)} %get-tuple-element.66), channel_id=1, source_target_pairs={{0,64},{32,96},{64,0},{96,32},{128,192},{160,224},{192,128},{224,1... | collective-permute-start | bytes 393224 | tf_op jit(solution)/shard_map/ppermute | solution.py:443
  36.6 6.6 %collective-permute-start.8 = (f32[128,256]{1,0:T(8,128)S(1)}, f32[128,256]{1,0:T(8,128)S(1)}, u32[]{:S(2)}, u32[]{:S(2)}) collective-permute-start(f32[128,256]{1,0:T(8,128)S(1)} %get-tuple-element.67), channel_id=1, source_target_pairs={{0,128},{32,160},{64,192},{96,224},{128,0},{160,32},{192,64},{224,... | collective-permute-start | bytes 393224 | tf_op jit(solution)/shard_map/ppermute | solution.py:443
  37.2 8.8 %collective-permute-start.9 = (f32[128,256]{1,0:T(8,128)S(1)}, f32[128,256]{1,0:T(8,128)S(1)}, u32[]{:S(2)}, u32[]{:S(2)}) collective-permute-start(f32[128,256]{1,0:T(8,128)S(1)} %get-tuple-element.68), channel_id=1, source_target_pairs={{0,192},{32,224},{64,128},{96,160},{128,64},{160,96},{192,0},{224,... | collective-permute-start | bytes 393224 | tf_op jit(solution)/shard_map/ppermute | solution.py:443
  39.4 6.6 %collective-permute-start.11 = (f32[32,128]{1,0:T(8,128)S(1)}, f32[32,128]{1,0:T(8,128)S(1)}, u32[]{:S(2)}, u32[]{:S(2)}) collective-permute-start(f32[32,128]{1,0:T(8,128)S(1)} %get-tuple-element.72), channel_id=1, source_target_pairs={{0,64},{32,96},{64,0},{96,32},{128,192},{160,224},{192,128},{224,1... | collective-permute-start | bytes 49160 | tf_op jit(solution)/shard_map/ppermute | solution.py:443
  40.2 10.4 %collective-permute-start.12 = (f32[32,128]{1,0:T(8,128)S(1)}, f32[32,128]{1,0:T(8,128)S(1)}, u32[]{:S(2)}, u32[]{:S(2)}) collective-permute-start(f32[32,128]{1,0:T(8,128)S(1)} %get-tuple-element.73), channel_id=1, source_target_pairs={{0,128},{32,160},{64,192},{96,224},{128,0},{160,32},{192,64},{224,... | collective-permute-start | bytes 49160 | tf_op jit(solution)/shard_map/ppermute | solution.py:443
  42.3 8.3 %collective-permute-start.13 = (f32[32,128]{1,0:T(8,128)S(1)}, f32[32,128]{1,0:T(8,128)S(1)}, u32[]{:S(2)}, u32[]{:S(2)}) collective-permute-start(f32[32,128]{1,0:T(8,128)S(1)} %get-tuple-element.74), channel_id=1, source_target_pairs={{0,192},{32,224},{64,128},{96,160},{128,64},{160,96},{192,0},{224,... | collective-permute-start | bytes 49160 | tf_op jit(solution)/shard_map/ppermute | solution.py:443
  51.5 3.8 %collective-permute-start.14 = (f32[4,64,256]{2,1,0:T(8,128)S(1)}, f32[4,64,256]{2,1,0:T(8,128)S(1)}, u32[]{:S(2)}, u32[]{:S(2)}) collective-permute-start(f32[4,64,256]{2,1,0:T(8,128)S(1)} %get-tuple-element.76), channel_id=1, source_target_pairs={{0,32},{32,0},{64,96},{96,64},{128,160},{160,128},{192,224},{224,1... | collective-permute-start | bytes 786440 | tf_op jit(solution)/shard_map/ppermute | solution.py:450

commit v3 on v2

v3 whole, which is shorter than its diff:
```python
import jax
import jax.numpy as jnp
import ml_dtypes
import numpy as np
from jax import lax
from jax.experimental import pallas as pl
from jax.experimental.pallas import tpu as pltpu
from jax.sharding import PartitionSpec as P

NZ = 512
PTS = 81
ELEMS = 8
ROWS = 4
PAIRS = 10
SPAN = 8
MODES = NZ // SPAN
SPAN_RATE = 1.0 / 32.0
BF = jnp.bfloat16
F32 = jnp.float32
LIMIT = 48 * 1024 * 1024
LONG = 200_000_000


def legendre_rows(abscissa, node_count):
    legendre = np.zeros((node_count, node_count))
    legendre[:, 0] = 1.0
    legendre[:, 1] = abscissa
    for degree in range(2, node_count):
        legendre[:, degree] = (
            (2 * degree - 1) * abscissa * legendre[:, degree - 1]
            - (degree - 1) * legendre[:, degree - 2]
        ) / degree
    return legendre


def lobatto_matrix(order):
    node_count = order + 1
    abscissa = -np.cos(np.pi * np.arange(node_count) / order)
    for _ in range(60):
        legendre = legendre_rows(abscissa, node_count)
        abscissa = abscissa - (abscissa * legendre[:, order] - legendre[:, order - 1]) / (
            node_count * legendre[:, order]
        )
    legendre = legendre_rows(abscissa, node_count)
    end_values = legendre[:, order]
    spacing = abscissa[:, None] - abscissa[None, :] + np.eye(node_count)
    matrix = end_values[:, None] / (end_values[None, :] * spacing)
    matrix = matrix * (1.0 - np.eye(node_count))
    matrix[0, 0] = -order * node_count / 4.0
    matrix[order, order] = order * node_count / 4.0
    return matrix


def edge_points():
    positions = np.arange(9)
    outline = [positions, positions * 9 + 8, 72 + (8 - positions), (8 - positions) * 9]
    return np.stack(outline)[:, 1:8]


INSIDE = 53


def point_order():
    edges = edge_points().reshape(-1)
    inside = [point for point in range(PTS) if point not in set(edges.tolist())]
    return np.concatenate([inside, edges]).astype(int)


def lane_of(c, place):
    if place >= INSIDE:
        return 128 + 31 + 28 * c + place - INSIDE
    return 53 * c + place


def halves(table):
    high = table.astype(np.float32).astype(ml_dtypes.bfloat16)
    low = (table - high.astype(np.float64)).astype(np.float32).astype(ml_dtypes.bfloat16)
    return high, low


def span_tables():
    planes = np.arange(NZ)[None, :]
    slots = np.arange(NZ)[:, None]
    waves = np.where(slots == 1, NZ // 2, slots // 2)
    angles = (planes * waves % NZ) * (2.0 * np.pi / NZ)
    sine = (slots % 2 == 1) & (slots > 1)
    value = np.where(sine, np.sin(angles), np.cos(angles))
    rate = np.where(slots == 1, 0, waves) * SPAN_RATE
    slope = rate * np.where(sine, np.cos(angles), -np.sin(angles))
    return value, slope


def point_matrices():
    lobatto = lobatto_matrix(8)
    return np.kron(np.eye(9), lobatto), np.kron(lobatto, np.eye(9))


def gradient_table():
    along_xi, along_eta = point_matrices()
    order = point_order()
    table = np.zeros((176, 96))
    table[:81, :81] = along_xi[np.ix_(order, order)]
    table[88:169, :81] = along_eta[np.ix_(order, order)]
    return table


def order_table():
    order = point_order()
    table = np.zeros((288, 256))
    for c in range(3):
        for place in range(PTS):
            table[c * 96 + place, c * 81 + order[place]] = 1.0
    return table


def edge_tables():
    edges = edge_points()
    mats = point_matrices()
    table = np.zeros((256, 1024))
    pick = np.zeros((256, 512))
    for s in range(4):
        for t in range(3):
            for c in range(3):
                for xy in range(2):
                    for i in range(7):
                        lane = s * 128 + t * 42 + c * 14 + xy * 7 + i
                        for h in range(2):
                            table[c * 81 : c * 81 + 81, h * 512 + lane] = mats[h][edges[s, i]]
                        pick[xy * 128 + edges[s, i], lane] = 1.0
    high, low = halves(table)
    pick = halves(pick)[0]
    lanes = [slice(s * 128, s * 128 + 128) for s in range(4)]
    later = [slice(512 + s * 128, 640 + s * 128) for s in range(4)]
    return np.stack(
        [
            np.concatenate([high[:, n], high[:, m], low[:, n], low[:, m]], axis=1)
            for n, m in zip(lanes, later)
        ]
    ), pick


def settle_tables():
    order = point_order()
    take = np.zeros((128, 128))
    give = np.zeros((128, 384))
    where = np.zeros((8, 128))
    back = np.zeros((256, 384))
    for c in range(3):
        for place in range(PTS):
            back[lane_of(c, place), c * 128 + order[place]] = 1.0
        for s in range(4):
            for i in range(7):
                lane = s * 21 + c * 7 + i
                place = INSIDE + s * 7 + i
                take[lane_of(c, INSIDE + s * 7 + 6 - i) - 128, lane] = 1.0
                give[lane, c * 128 + order[place]] = 0.5
                where[s, lane_of(c, place) - 128] = 0.5
    return take, give, where, back


def row_of(place, part):
    return (place & 1) * ROWS + ((place >> 1) ^ (3 * (part & 1)))


def split(x):
    high = x.astype(BF)
    return high, (x - high.astype(F32)).astype(BF)


def dot(a, b, dims=((1,), (0,))):
    return lax.dot_general(a, b, (dims, ((), ())), preferred_element_type=F32)


def list_pairs(pair, count, own, other, other_edge):
    for e in range(ELEMS):
        count[e] = 0
    for n in range(ELEMS * 4):
        own[n] = -1
        other[n] = 0
        other_edge[n] = 0
    for row in range(PAIRS):
        for first, second in ((0, 2), (2, 0)):
            e = pair[first, row]
            slot = e * 4 + count[e]
            own[slot] = pair[first + 1, row]
            other[slot] = pair[second, row]
            other_edge[slot] = pair[second + 1, row]
            count[e] = count[e] + 1


def chip_modes(j):
    chip = (lax.axis_index("span") >> 1) ^ j
    return pl.ds(pl.multiple_of(chip * 2 * MODES, 2 * MODES), 2 * MODES)


def ready_kernel(bound, here, out):
    out[...] = here[0, 0:8, 0:128] + jnp.full((8, 128), bound[0, 0], jnp.int32).astype(F32)


def pack_element(packed, e, core, here, there):
    for at, v in ((core, here), (1 - core, there)):
        rows = pl.ds(pl.multiple_of(at * MODES, MODES), MODES)
        for c in range(3):
            packed[e, rows, c * 81 : c * 81 + 81] = v[c, :, e * 81 : e * 81 + 81]
        packed[e, rows, 243:256] = jnp.zeros((MODES, 13), F32)


def column_flags(bound, core, flags):
    for e in range(ELEMS):
        flags[e] = 0
    for row in range(ROWS):
        flags[bound[0, core * ROWS + row]] = 1


def pack_kernel(bound, here, there, ready, packed, *rest):
    outs, flags = rest[:4], rest[4]
    me, part = lax.axis_index("span"), lax.axis_index("dom")
    core = me & 1
    column_flags(bound, core, flags)
    for e in range(ELEMS):
        pl.when(flags[e] == 1)(lambda e=e: pack_element(packed, e, core, here, there))
    for j in range(4):
        outs[j][...] = packed[bound[0, row_of(me ^ (2 * j), part)]]


def edge_kernel(bound, pair, done, here, there, metric, pick, table, turn, columns, *rest):
    outs = rest[:4]
    packed, rows, lines, scale, square, flags, count, own, other, other_edge = rest[4:]
    me, part = lax.axis_index("span"), lax.axis_index("dom")
    core = me & 1
    column_flags(bound, core, flags)
    list_pairs(pair, count, own, other, other_edge)

    def copy_element(e):
        packed[e] = done[e]

    for e in range(ELEMS):
        pl.when(flags[e] == 1)(lambda e=e: copy_element(e))
        pl.when(flags[e] == 0)(lambda e=e: pack_element(packed, e, core, here, there))
    rows[...] = jnp.zeros((16, 256), F32)
    for e in range(ELEMS):
        for j in range(4):
            at = e + 8 * (j // 2)
            lane = 128 * (j % 2)
            rows[at : at + 1, lane : lane + 81] = metric[j : j + 1, e * 81 : e * 81 + 81]
    rows_high, rows_low = split(rows[...])
    for s in range(4):
        here_lanes = pick[:, s * 128 : s * 128 + 128]
        size = dot(rows_high, here_lanes) + dot(rows_low, here_lanes)
        for n in range(16):
            scale[n * 4 + s] = size[n : n + 1, :]
    for n in range(16):
        lines[n] = rows[n : n + 1, :]
    square[...] = jnp.zeros((128, 128), F32)
    mine = bound[0, row_of(me, part)]
    for j in range(4):
        line = lines[mine + 8 * (j // 2)]
        square[j : j + 1, :] = line[:, 128 * (j % 2) : 128 * (j % 2) + 128]
    high, low = split(square[...].T)
    columns[...] = dot(turn[0:96, 0:128], high) + dot(turn[0:96, 0:128], low)
    lane = lax.broadcasted_iota(jnp.int32, (2 * MODES, 128), 1)
    for j in range(4):
        e = bound[0, row_of(me ^ (2 * j), part)]
        total = jnp.zeros((2 * MODES, 128), F32)
        for t in range(3):
            far, edge = other[e * 4 + t], other_edge[e * 4 + t]
            vh, vl = split(packed[far])
            high = table[edge, :, 0:256]
            value = dot(vh, high) + dot(vl, high) + dot(vh, table[edge, :, 256:512])
            value = (
                value[:, :128] * scale[far * 4 + edge]
                + value[:, 128:] * scale[(8 + far) * 4 + edge]
            )
            total = jnp.where((lane >= t * 42) & (lane < t * 42 + 42), value, total)
        outs[j][...] = total


def element_kernel(bound, *rest):
    blocks = rest[:4]
    columns, turn, th, tl, dh, dl, gh, gl = rest[4:12]
    send, mine, u, q, g, modes = rest[12:]
    me, part = lax.axis_index("span"), lax.axis_index("dom")
    for j in range(4):
        modes[chip_modes(j), :] = blocks[j][...]
    vh, vl = split(modes[...].T)
    vh, vl = dot(turn[...], vh).astype(BF), dot(turn[...], vl).astype(BF)
    value = dot(vh, th[...]) + dot(vl, th[...]) + dot(vh, tl[...])
    slope = dot(vh, dh[...]) + dot(vl, dh[...]) + dot(vh, dl[...])
    uh, ul = split(value)
    third = value[192:280]
    for c in range(3):
        rows = slice(96 * c, 96 * c + 96)
        both = dot(gh[...], uh[rows]) + dot(gh[...], ul[rows]) + dot(gl[...], uh[rows])
        fx, fe = both[:88], both[88:]
        g[c] = columns[0:88, 0:1] * fx + columns[0:88, 2:3] * fe
        g[3 + c] = columns[0:88, 1:2] * fx + columns[0:88, 3:4] * fe
        u[c] = value[96 * c : 96 * c + 88]
        q[c] = third * slope[96 * c : 96 * c + 88]
    base = INSIDE + 7 * bound[1, row_of(me, part)]
    send[77:80] = jnp.zeros((3, NZ), F32)
    mine[77:80] = jnp.zeros((3, NZ), F32)
    order = [(g, f) for f in range(6)] + [(u, 0), (u, 1)] + [(q, c) for c in range(3)]
    for f, (ref, at) in enumerate(order):
        for i in range(7):
            line = ref[at, pl.ds(base + i, 1), :]
            mine[f * 7 + i : f * 7 + i + 1, :] = line
            send[f * 7 + 6 - i : f * 7 + 7 - i, :] = line


def to_modes(term, th, tl):
    wh, wl = split(term)
    along = ((1,), (1,))
    total = dot(th[...], wh, along) + dot(th[...], wl, along) + dot(tl[...], wh, along)
    slot = lax.broadcasted_iota(jnp.int32, total.shape, 0)
    return total * jnp.where(slot < 2, 1.0 / NZ, 2.0 / NZ)


def inside_kernel(u, q, g, th, tl, *rest):
    outs = rest[:4]
    term, spec = rest[4:]
    for c, count in ((0, 53), (1, 53), (2, 22)):
        value = u[0, 0:56] * g[c, 0:56] + u[1, 0:56] * g[3 + c, 0:56] + q[c, 0:56]
        term[53 * c : 53 * c + count, :] = value[:count]
    spec[...] = to_modes(term[...], th, tl)
    for j in range(4):
        outs[j][...] = spec[chip_modes(j), :]


def edge_term_kernel(bound, pair, *rest):
    blocks = rest[:4]
    th, tl, u, q, g, term, modes, count, own, other, other_edge = rest[4:]
    me, part = lax.axis_index("span"), lax.axis_index("dom")
    list_pairs(pair, count, own, other, other_edge)
    for j in range(4):
        modes[chip_modes(j), :] = blocks[j][...]
    eh, el = split(modes[...].T)
    planes = dot(eh, th[...]) + dot(el, th[...]) + dot(eh, tl[...])
    ph, pw = split(planes)
    e = bound[0, row_of(me, part)]
    lane = lax.broadcasted_iota(jnp.int32, (32, 128), 1)
    point = lax.broadcasted_iota(jnp.int32, (32, 128), 0)
    slot = jnp.where(lane < 42, 0, jnp.where(lane < 84, 1, 2))
    starts = []
    for t in range(3):
        edge = own[e * 4 + t]
        starts.append(jnp.where(edge < 0, -1000, 7 * edge))
    base = jnp.where(slot == 0, starts[0], jnp.where(slot == 1, starts[1], starts[2]))
    place = lane - slot * 42
    takes = []
    for f in range(6):
        xy, c = f // 3, f % 3
        i = 6 - (place - (c * 14 + xy * 7))
        hit = (i >= 0) & (i <= 6) & (lane < 126) & (point == base + i)
        takes.append(jnp.where(hit, 0.5, 0.0))
    keep = 1.0 - jnp.sum(takes[0], axis=1, keepdims=True)[:28]
    take = jnp.concatenate(takes, axis=0).astype(BF)
    far = dot(take, ph) + dot(take, pw)
    for c in range(3):
        u0, u1 = u[0, 53:81], u[1, 53:81]
        term[31 + 28 * c : 59 + 28 * c, :] = (
            u0 * (g[c, 53:81] * keep + far[c * 32 : c * 32 + 28])
            + u1 * (g[3 + c, 53:81] * keep + far[(3 + c) * 32 : (3 + c) * 32 + 28])
            + q[c, 53:81]
        )
    term[0:31, :] = u[0, 22:53] * g[2, 22:53] + u[1, 22:53] * g[5, 22:53] + q[2, 22:53]
    term[115:128, :] = jnp.zeros((13, NZ), F32)


def side_kernel(bound, term, mine, other, th, tl, *rest):
    outs = rest[:4]
    work, spec = rest[4:]
    me, part = lax.axis_index("span"), lax.axis_index("dom")
    work[...] = term[...]
    m = [mine[f * 7 : f * 7 + 7, :] for f in range(11)]
    r = [other[f * 7 : f * 7 + 7, :] for f in range(11)]
    base = 31 + 7 * bound[1, row_of(me, part)]
    for c in range(3):
        gx = (m[c] + r[c]) * 0.5
        gy = (m[3 + c] + r[3 + c]) * 0.5
        value = (
            (m[6] * gx + m[7] * gy + m[8 + c]) + (r[6] * gx + r[7] * gy + r[8 + c])
        ) * 0.5
        for i in range(7):
            work[pl.ds(base + 28 * c + i, 1), :] = value[i : i + 1, :]
    spec[...] = to_modes(work[...], th, tl)
    for j in range(4):
        outs[j][...] = spec[chip_modes(j), :]


def cut_kernel(*rest):
    blocks, cross = rest[:4], rest[4]
    others = pl.ds(pl.multiple_of((1 - (lax.axis_index("span") & 1)) * MODES, MODES), MODES)
    for j in range(4):
        cross[j] = blocks[j][others, :]


def settle_kernel(bound, pair, *rest):
    inside, edge = rest[:4], rest[4:8]
    cross, edge_cross, take, give, where, back, out = rest[8:15]
    packed, edges, far, count, own, other, other_edge = rest[15:]
    me, part = lax.axis_index("span"), lax.axis_index("dom")
    list_pairs(pair, count, own, other, other_edge)
    mine = pl.ds(pl.multiple_of((me & 1) * MODES, MODES), MODES)
    for j in range(4):
        e = bound[0, row_of(me ^ (2 * j), part)]
        packed[e, :, 0:128] = inside[j][mine, :]
        packed[e, :, 128:256] = edge[j][mine, :]
        e = bound[0, row_of(me ^ (2 * j + 1), part)]
        packed[e, :, 0:128] = cross[j]
        packed[e, :, 128:256] = edge_cross[j]
    ph, pw = split(packed[:, :, 128:256].reshape(ELEMS * MODES, 128))
    edges[...] = (dot(ph, take[...]) + dot(pw, take[...])).reshape(ELEMS, MODES, 128)
    lane = lax.broadcasted_iota(jnp.int32, (MODES, 128), 1)
    for e in range(ELEMS):
        total = jnp.zeros((MODES, 128), F32)
        keep = jnp.ones((1, 128), F32)
        for t in range(3):
            edge = own[e * 4 + t]
            shift = (21 * (edge - other_edge[e * 4 + t]) + 128) & 127
            turned = pltpu.roll(edges[other[e * 4 + t]], shift, 1)
            low = edge * 21
            total = jnp.where((lane >= low) & (lane < low + 21) & (edge >= 0), turned, total)
            row = where[pl.ds(jnp.maximum(edge, 0), 1), :]
            keep = keep - jnp.where(edge >= 0, row, 0.0)
        far[e] = total
        packed[e, :, 128:256] = packed[e, :, 128:256] * keep
    fh, fl = split(far[...].reshape(ELEMS * MODES, 128))
    ph, pw = split(packed[...].reshape(ELEMS * MODES, 256))
    done = (
        dot(ph, back[...]) + dot(pw, back[...]) + dot(fh, give[...]) + dot(fl, give[...])
    )
    for e in range(ELEMS):
        for c in range(3):
            out[c, :, e * 81 : e * 81 + 81] = done[e * MODES : (e + 1) * MODES, c * 128 : c * 128 + 81]


def spec_of(space):
    return pl.BlockSpec(memory_space=space)


def call(kernel, name, scalars, arrays, outs, scratch=(), weight=1000):
    shapes = [jax.ShapeDtypeStruct(shape, F32) for shape in outs]
    return pl.pallas_call(
        kernel,
        out_shape=shapes,
        in_specs=[spec_of(pltpu.SMEM)] * len(scalars)
        + [spec_of(pltpu.VMEM)] * len(arrays),
        out_specs=[spec_of(pltpu.VMEM)] * len(outs),
        scratch_shapes=list(scratch),
        compiler_params=pltpu.CompilerParams(vmem_limit_bytes=LIMIT),
        cost_estimate=pl.CostEstimate(flops=weight, bytes_accessed=weight, transcendentals=0),
        name=name,
    )(*scalars, *arrays)


def pair_scratch():
    return [pltpu.SMEM((n,), jnp.int32) for n in (ELEMS, ELEMS * 4, ELEMS * 4, ELEMS * 4)]


def between_chips(blocks, order=(3, 2, 1)):
    far = {
        j: lax.ppermute(blocks[j], "span", [(s, s ^ (2 * j)) for s in range(SPAN)])
        for j in order
    }
    return [blocks[0], far[1], far[2], far[3]]


def between_cores(block):
    return lax.ppermute(block, "span", [(s, s ^ 1) for s in range(SPAN)])


def side_swap(block, parts):
    def device(part, row, side):
        return ((row ^ (3 * (part & 1))) * 2 + side) * parts + part

    perm = []
    for part in range(parts):
        before = (part - 1) % parts
        for row in range(ROWS):
            perm.append((device(part, row, 0), device(before, row, 1)))
            perm.append((device(before, row, 1), device(part, row, 0)))
    return lax.ppermute(block, ("span", "dom"), perm)


def on_device(velocity_modes, metric, pair_table, bound_table):
    value, slope = span_tables()
    th, tl = halves(value)
    dh, dl = halves(slope)
    gh, gl = halves(gradient_table())
    edge_table, pick = edge_tables()
    take, give, where, back = settle_tables()
    turn = halves(order_table())[0]
    chip, edge_chip = (2 * MODES, 256), (2 * MODES, 128)
    pair_table, bound_table = pair_table.T, bound_table.T
    flags = [pltpu.SMEM((ELEMS,), jnp.int32)]

    there = between_cores(velocity_modes)
    (ready,) = call(
        ready_kernel, "ready", [bound_table], [velocity_modes], [(8, 128)], weight=LONG
    )
    there, ready = lax.optimization_barrier((there, ready))
    packed, *blocks = call(
        pack_kernel,
        "pack",
        [bound_table],
        [velocity_modes, there, ready],
        [(ELEMS, 2 * MODES, 256)] + [chip] * 4,
        flags,
        weight=LONG,
    )
    blocks = between_chips(blocks)
    blocks[3], packed = lax.optimization_barrier((blocks[3], packed))
    columns, *edge_blocks = call(
        edge_kernel,
        "edges",
        [bound_table, pair_table],
        [packed, velocity_modes, there, metric, pick, edge_table, turn],
        [(96, 128)] + [edge_chip] * 4,
        [
            pltpu.VMEM((ELEMS, 2 * MODES, 256), F32),
            pltpu.VMEM((16, 256), F32),
            pltpu.VMEM((16, 1, 256), F32),
            pltpu.VMEM((64, 1, 128), F32),
            pltpu.VMEM((128, 128), F32),
        ]
        + flags
        + pair_scratch(),
        weight=LONG,
    )
    edge_blocks = between_chips(edge_blocks)
    send, mine, u, q, g = call(
        element_kernel,
        "element",
        [bound_table],
        [*blocks, columns, turn, th, tl, dh, dl, gh, gl],
        [(80, NZ), (80, NZ), (3, 88, NZ), (3, 88, NZ), (6, 88, NZ)],
        [pltpu.VMEM((NZ, 256), F32)],
    )
    send, edge_blocks[1:3] = lax.optimization_barrier((send, edge_blocks[1:3]))
    other = side_swap(send, lax.axis_size("dom"))
    modes_scratch = pltpu.VMEM((NZ, 128), F32)
    term_scratch = pltpu.VMEM((128, NZ), F32)
    inside = call(
        inside_kernel, "inside", [], [u, q, g, th, tl], [edge_chip] * 4, [term_scratch, modes_scratch]
    )
    inside = between_chips(inside)
    (term,) = call(
        edge_term_kernel,
        "term",
        [bound_table, pair_table],
        [*edge_blocks, th, tl, u, q, g],
        [(128, NZ)],
        [modes_scratch] + pair_scratch(),
    )
    edge = call(
        side_kernel,
        "side",
        [bound_table],
        [term, mine, other, th, tl],
        [edge_chip] * 4,
        [term_scratch, modes_scratch],
    )
    edge = between_chips(edge)
    (cross,) = call(cut_kernel, "cut", [], inside, [(4, MODES, 128)])
    (edge_cross,) = call(cut_kernel, "cut_edge", [], edge, [(4, MODES, 128)])
    (out,) = call(
        settle_kernel,
        "settle",
        [bound_table, pair_table],
        [
            *inside,
            *edge,
            between_cores(cross),
            between_cores(edge_cross),
            *(halves(table)[0] for table in (take, give)),
            where.astype(np.float32),
            halves(back)[0],
        ],
        [(3, MODES, ELEMS * PTS)],
        [
            pltpu.VMEM((ELEMS, MODES, 256), F32),
            pltpu.VMEM((ELEMS, MODES, 128), F32),
            pltpu.VMEM((ELEMS, MODES, 128), F32),
        ]
        + pair_scratch(),
    )
    return out


def solution(mesh):
    return jax.shard_map(
        on_device,
        mesh=mesh,
        in_specs=(P(None, "span", "dom"), P(None, "dom"), P("dom", None), P("dom", None)),
        out_specs=P(None, "span", "dom"),
        check_vma=False,
    )
```

time: 58.3 us -> 54.3 us (0.931)
  waiting for transfers between devices: 12.5 us -> 5.72 us
  starting transfers between devices: 27 us -> 33.7 us
  local copies, waits for them, and re-layouts: 5.36 us -> 1.83 us
    ppermute x12, waiting for transfers between devices: 11.3 us -> 4.73 us  [between_chips(): lax.ppermute(blocks[j], 'span', [(s, s ^ 2 * j) for s in range(SPAN)])]
    ppermute x2 -> x3, starting transfers between devices: 5.92 us -> 12 us  [between_cores(): return lax.ppermute(block, 'span', [(s, s ^ 1) for s in range(SPAN)])]
    unnamed x36 -> x34, local copies, waits for them, and re-layouts: 5.36 us -> 1.83 us
    ppermute x1, starting transfers between devices: 5.32 us -> 6.25 us  [side_swap(): return lax.ppermute(block, ('span', 'dom'), perm)]
    pallas_call x9 -> x10, Pallas kernels: 12.8 us -> 12.5 us  [call(): pl.pallas_call(kernel, out_shape=shapes, in_specs=[spec_of(pltpu.SMEM)] *...]
  transfers between devices with their start and end apart: 15 -> 16, of which waited for: 4 -> 4; matrix products, arithmetic and copies ran while one was open for 0% -> 0% of each run, Pallas kernels for 14% -> 17%
where the time goes in v3:
time: 54.3 us; the launch traced here: 54.1 us
  starting transfers between devices  33.7 us (62%)
  Pallas kernels  12.5 us (23%)
  waiting for transfers between devices  5.72 us (11%)
  local copies, waits for them, and re-layouts  1.83 us (3%)
    ppermute x12, starting transfers between devices, between_chips(): lax.ppermute(blocks[j], 'span', [(s, s ^ 2 * j) for s in range(SPAN)])  15.5 us
    pallas_call x10, Pallas kernels, call(): pl.pallas_call(kernel, out_shape=shapes, in_specs=[spec_of(pltpu.SMEM)] *...  12.5 us
    ppermute x3, starting transfers between devices, between_cores(): return lax.ppermute(block, 'span', [(s, s ^ 1) for s in range(SPAN)])  12 us
    ppermute x1, starting transfers between devices, side_swap(): return lax.ppermute(block, ('span', 'dom'), perm)  6.25 us
    ppermute x12, waiting for transfers between devices, between_chips(): lax.ppermute(blocks[j], 'span', [(s, s ^ 2 * j) for s in range(SPAN)])  4.73 us
    unnamed x34, local copies, waits for them, and re-layouts  1.83 us
  transfers between devices with their start and end apart: 16, of which 4 were waited for; matrix products, arithmetic and copies ran while one was open for 0% of the time, Pallas kernels for 17%

profile of v3, /device:TPU:1, one launch (start us, length us, event | category | flops | bytes accessed | tf_op | source)
XLA Modules:
  0.0 54.1 jit_solution(13532188598322213565)
XLA Ops:
  0.0 3.2 %collective-permute-start = (f32[3,64,648]{2,1,0:T(8,128)}, f32[3,64,648]{2,1,0:T(8,128)S(1)}, u32[]{:S(2)}, u32[]{:S(2)}) collective-permute-start(f32[3,64,648]{2,1,0:T(8,128)} %here.5), channel_id=1, source_target_pairs={{0,32},{32,0},{64,96},{96,64},{128,160},{160,128},{192,224},{224,1... | collective-permute-start | bytes 1493000 | tf_op jit(solution)/shard_map/ppermute | solution.py:469
  3.2 1.1 %copy-done.2 = f32[3,64,648]{2,1,0:T(8,128)S(1)} copy-done((f32[3,64,648]{2,1,0:T(8,128)S(1)}, f32[3,64,648]{2,1,0:T(8,128)}, u32[]{:S(2)}) %copy-start.2) | copy-done | bytes 497688
  4.3 0.7 %copy-done.12 = s32[8,2]{0,1:T(2,128)S(1)} copy-done((s32[8,2]{0,1:T(2,128)S(1)}, s32[8,2]{0,1:T(2,128)}, u32[]{:S(2)}) %copy-start.12) | copy-done | bytes 88
  5.0 0.6 %ready.1 = f32[8,128]{1,0:T(8,128)S(1)} custom-call(s32[2,8]{1,0:T(2,128)S(1)} %bitcast.2, f32[3,64,648]{2,1,0:T(8,128)S(1)} %copy-done.2), custom_call_target="tpu_custom_call" | custom-call | flops 200000000 | bytes 200000000 | tf_op jit(solution)/shard_map/ready/pallas_call | solution.py:443
  5.6 0.0 collective-permute-done.there
  5.6 1.1 %pack.1 = (f32[8,128,256]{2,1,0:T(8,128)S(1)}, f32[128,256]{1,0:T(8,128)S(1)}, f32[128,256]{1,0:T(8,128)S(1)}, f32[128,256]{1,0:T(8,128)S(1)}, f32[128,256]{1,0:T(8,128)S(1)}) custom-call(s32[2,8]{1,0:T(2,128)S(1)} %bitcast.3, f32[3,64,648]{2,1,0:T(8,128)S(1)} %copy-done.2, f32[3,64,648]{2,1,0:T(8,128)S(1)} %collective-permute-done.there, f32[8,128]{1,0:T(8,128)S(1)} %ready.1), custom_call_target="tpu_custom_call" | custom-call | flops 200000000 | bytes 200000000 | tf_op jit(solution)/shard_map/pack/pallas_call | solution.py:443
  6.7 2.7 %collective-permute-start.3 = (f32[128,256]{1,0:T(8,128)S(1)}, f32[128,256]{1,0:T(8,128)S(1)}, u32[]{:S(2)}, u32[]{:S(2)}) collective-permute-start(f32[128,256]{1,0:T(8,128)S(1)} %get-tuple-element.40), channel_id=1, source_target_pairs={{0,192},{32,224},{64,128},{96,160},{128,64},{160,96},{192,0},{224,... | collective-permute-start | bytes 393224 | tf_op jit(solution)/shard_map/ppermute | solution.py:462
  9.4 0.9 %collective-permute-start.2 = (f32[128,256]{1,0:T(8,128)S(1)}, f32[128,256]{1,0:T(8,128)S(1)}, u32[]{:S(2)}, u32[]{:S(2)}) collective-permute-start(f32[128,256]{1,0:T(8,128)S(1)} %get-tuple-element.39), channel_id=1, source_target_pairs={{0,128},{32,160},{64,192},{96,224},{128,0},{160,32},{192,64},{224,... | collective-permute-start | bytes 393224 | tf_op jit(solution)/shard_map/ppermute | solution.py:462
  10.4 3.3 %collective-permute-done.3.rest_3_ = f32[128,256]{1,0:T(8,128)S(1)} collective-permute-done((f32[128,256]{1,0:T(8,128)S(1)}, f32[128,256]{1,0:T(8,128)S(1)}, u32[]{:S(2)}, u32[]{:S(2)}) %collective-permute-start.3) | collective-permute-done | bytes 131104 | tf_op jit(solution)/shard_map/ppermute | solution.py:462
  13.7 0.0 copy-start
  13.7 0.0 copy-start.1
  13.7 0.0 copy-start.5
  13.7 0.0 copy-start.6
  13.7 0.0 copy-start.10
  13.7 0.0 copy-start.11
  13.7 2.6 %edges.1 = (f32[96,128]{1,0:T(8,128)S(1)}, f32[128,128]{1,0:T(8,128)S(1)}, f32[128,128]{1,0:T(8,128)S(1)}, f32[128,128]{1,0:T(8,128)S(1)}, f32[128,128]{1,0:T(8,128)S(1)}) custom-call(s32[2,8]{1,0:T(2,128)S(1)} %bitcast.4, s32[4,10]{1,0:T(4,128)S(1)} %bitcast.9, f32[8,128,256]{2,1,0:T(8,128)S(1)} %get-tuple-element.43.done, f32[3,64,648]{2,1,0:T(8,128)S(1)} %copy-done.2, ...), custom_call_target="tpu_custom_call" | custom-call | flops 200000000 | bytes 200000000 | tf_op jit(solution)/shard_map/edges/pallas_call | solution.py:443
  16.4 1.2 %collective-permute-start.7 = (f32[128,128]{1,0:T(8,128)S(1)}, f32[128,128]{1,0:T(8,128)S(1)}, u32[]{:S(2)}, u32[]{:S(2)}) collective-permute-start(f32[128,128]{1,0:T(8,128)S(1)} %get-tuple-element.54), channel_id=1, source_target_pairs={{0,64},{32,96},{64,0},{96,32},{128,192},{160,224},{192,128},{224,1... | collective-permute-start | bytes 196616 | tf_op jit(solution)/shard_map/ppermute | solution.py:462
  17.6 1.8 %collective-permute-start.8 = (f32[128,128]{1,0:T(8,128)S(1)}, f32[128,128]{1,0:T(8,128)S(1)}, u32[]{:S(2)}, u32[]{:S(2)}) collective-permute-start(f32[128,128]{1,0:T(8,128)S(1)} %get-tuple-element.55), channel_id=1, source_target_pairs={{0,128},{32,160},{64,192},{96,224},{128,0},{160,32},{192,64},{224,... | collective-permute-start | bytes 196616 | tf_op jit(solution)/shard_map/ppermute | solution.py:462
  19.3 0.0 collective-permute-done.1.rest_1_
  19.3 0.9 %collective-permute-done.2.rest_2_ = f32[128,256]{1,0:T(8,128)S(1)} collective-permute-done((f32[128,256]{1,0:T(8,128)S(1)}, f32[128,256]{1,0:T(8,128)S(1)}, u32[]{:S(2)}, u32[]{:S(2)}) %collective-permute-start.2) | collective-permute-done | bytes 131104 | tf_op jit(solution)/shard_map/ppermute | solution.py:462
  20.2 2.5 %element.1 = (f32[80,512]{1,0:T(8,128)S(1)}, f32[80,512]{1,0:T(8,128)S(1)}, f32[3,88,512]{2,1,0:T(8,128)S(1)}, f32[3,88,512]{2,1,0:T(8,128)S(1)}, f32[6,88,512]{2,1,0:T(8,128)S(1)}) custom-call(s32[2,8]{1,0:T(2,128)S(1)} %bitcast.5, f32[128,256]{1,0:T(8,128)S(1)} %get-tuple-element.37.rest_0_, f32[128,256]{1,0:T(8,128)S(1)} %collective-permute-done.1.rest_1_, ...), custom_call_target="tpu_custom_call" | custom-call | flops 1000 | bytes 1000 | tf_op jit(solution)/shard_map/element/pallas_call | solution.py:443
  22.8 0.0 collective-permute-done.8.rest_2_
  22.8 6.3 %collective-permute-start.10 = (f32[80,512]{1,0:T(8,128)S(1)}, f32[80,512]{1,0:T(8,128)S(1)}, u32[]{:S(2)}, u32[]{:S(2)}) collective-permute-start(f32[80,512]{1,0:T(8,128)S(1)} %get-tuple-element.60), channel_id=1, source_target_pairs={{0,255},{255,0},{64,191},{191,64},{128,127},{127,128},{192,63},{63... | collective-permute-start | bytes 491528 | tf_op jit(solution)/shard_map/ppermute | solution.py:482
  29.0 1.6 %collective-permute-start.9 = (f32[128,128]{1,0:T(8,128)S(1)}, f32[128,128]{1,0:T(8,128)S(1)}, u32[]{:S(2)}, u32[]{:S(2)}) collective-permute-start(f32[128,128]{1,0:T(8,128)S(1)} %get-tuple-element.58), channel_id=1, source_target_pairs={{0,192},{32,224},{64,128},{96,160},{128,64},{160,96},{192,0},{224,... | collective-permute-start | bytes 196616 | tf_op jit(solution)/shard_map/ppermute | solution.py:462
  30.7 0.7 %inside.1 = (f32[128,128]{1,0:T(8,128)S(1)}, f32[128,128]{1,0:T(8,128)S(1)}, f32[128,128]{1,0:T(8,128)S(1)}, f32[128,128]{1,0:T(8,128)S(1)}) custom-call(f32[3,88,512]{2,1,0:T(8,128)S(1)} %get-tuple-element.45.u.rest_6_, f32[3,88,512]{2,1,0:T(8,128)S(1)} %get-tuple-element.46.q.rest_7_, f32[6,88,512]{2,1,0:T(8,128)S(1)} %get-tuple-element.47.g.rest_8_, ...), custom_call_target="tpu_custom_call" | custom-call | flops 1000 | bytes 1000 | tf_op jit(solution)/shard_map/inside/pallas_call | solution.py:443
  31.3 0.1 collective-permute-start.4
  31.4 1.9 %collective-permute-start.5 = (f32[128,128]{1,0:T(8,128)S(1)}, f32[128,128]{1,0:T(8,128)S(1)}, u32[]{:S(2)}, u32[]{:S(2)}) collective-permute-start(f32[128,128]{1,0:T(8,128)S(1)} %get-tuple-element.50), channel_id=1, source_target_pairs={{0,128},{32,160},{64,192},{96,224},{128,0},{160,32},{192,64},{224,... | collective-permute-start | bytes 196616 | tf_op jit(solution)/shard_map/ppermute | solution.py:462
  33.3 1.6 %collective-permute-start.6 = (f32[128,128]{1,0:T(8,128)S(1)}, f32[128,128]{1,0:T(8,128)S(1)}, u32[]{:S(2)}, u32[]{:S(2)}) collective-permute-start(f32[128,128]{1,0:T(8,128)S(1)} %get-tuple-element.51), channel_id=1, source_target_pairs={{0,192},{32,224},{64,128},{96,160},{128,64},{160,96},{192,0},{224,... | collective-permute-start | bytes 196616 | tf_op jit(solution)/shard_map/ppermute | solution.py:462
  35.0 0.6 %collective-permute-done.9.rest_3_ = f32[128,128]{1,0:T(8,128)S(1)} collective-permute-done((f32[128,128]{1,0:T(8,128)S(1)}, f32[128,128]{1,0:T(8,128)S(1)}, u32[]{:S(2)}, u32[]{:S(2)}) %collective-permute-start.9) | collective-permute-done | bytes 65568 | tf_op jit(solution)/shard_map/ppermute | solution.py:462
  35.6 1.4 %term.1 = f32[128,512]{1,0:T(8,128)S(1)} custom-call(s32[2,8]{1,0:T(2,128)S(1)} %bitcast.6, s32[4,10]{1,0:T(4,128)S(1)} %bitcast.10, f32[128,128]{1,0:T(8,128)S(1)} %get-tuple-element.52.rest_0_, f32[128,128]{1,0:T(8,128)S(1)} %collective-permute-done.7.rest_1_, f32[128,128]{1,0:T(8,128)S(1)} %collective-permute-done.8.rest_2_, ...), custom_call_target="tpu_custom_call" | custom-call | flops 1000 | bytes 1000 | tf_op jit(solution)/shard_map/term/pallas_call | solution.py:443
  36.9 0.0 collective-permute-done.10.other
  36.9 0.0 copy-start.8
  36.9 0.0 copy-start.9
  37.0 0.0 copy-start.13
  37.0 0.0 copy-start.16
  37.0 1.3 %side.1 = (f32[128,128]{1,0:T(8,128)S(1)}, f32[128,128]{1,0:T(8,128)S(1)}, f32[128,128]{1,0:T(8,128)S(1)}, f32[128,128]{1,0:T(8,128)S(1)}) custom-call(s32[2,8]{1,0:T(2,128)S(1)} %bitcast.7, f32[128,512]{1,0:T(8,128)S(1)} %term.1, f32[80,512]{1,0:T(8,128)S(1)} %get-tuple-element.59.mine, f32[80,512]{1,0:T(8,128)S(1)} %collective-permute-done.10.other, ...), custom_call_target="tpu_custom_call" | custom-call | flops 1000 | bytes 1000 | tf_op jit(solution)/shard_map/side/pallas_call | solution.py:443
  38.3 0.1 collective-permute-start.11
  38.4 1.9 %collective-permute-start.12 = (f32[128,128]{1,0:T(8,128)S(1)}, f32[128,128]{1,0:T(8,128)S(1)}, u32[]{:S(2)}, u32[]{:S(2)}) collective-permute-start(f32[128,128]{1,0:T(8,128)S(1)} %get-tuple-element.63), channel_id=1, source_target_pairs={{0,128},{32,160},{64,192},{96,224},{128,0},{160,32},{192,64},{224,... | collective-permute-start | bytes 196616 | tf_op jit(solution)/shard_map/ppermute | solution.py:462
  40.2 0.0 collective-permute-done.4.rest_1_
  40.2 1.7 %collective-permute-start.13 = (f32[128,128]{1,0:T(8,128)S(1)}, f32[128,128]{1,0:T(8,128)S(1)}, u32[]{:S(2)}, u32[]{:S(2)}) collective-permute-start(f32[128,128]{1,0:T(8,128)S(1)} %get-tuple-element.64), channel_id=1, source_target_pairs={{0,192},{32,224},{64,128},{96,160},{128,64},{160,96},{192,0},{224,... | collective-permute-start | bytes 196616 | tf_op jit(solution)/shard_map/ppermute | solution.py:462
  41.9 0.0 collective-permute-done.5.rest_2_
  41.9 0.0 collective-permute-done.6.rest_3_
  41.9 4.6 %collective-permute-start.14 = (f32[4,64,128]{2,1,0:T(8,128)S(1)}, f32[4,64,128]{2,1,0:T(8,128)S(1)}, u32[]{:S(2)}, u32[]{:S(2)}) collective-permute-start(f32[4,64,128]{2,1,0:T(8,128)S(1)} %cut.1), channel_id=1, source_target_pairs={{0,32},{32,0},{64,96},{96,64},{128,160},{160,128},{192,224},{224,1... | collective-permute-start | bytes 393224 | tf_op jit(solution)/shard_map/ppermute | solution.py:469
  46.5 0.0 collective-permute-done.11.rest_1_.rest_5_
  46.5 0.0 collective-permute-done.12.rest_2_.rest_6_
  46.6 4.1 %collective-permute-start.15 = (f32[4,64,128]{2,1,0:T(8,128)S(1)}, f32[4,64,128]{2,1,0:T(8,128)S(1)}, u32[]{:S(2)}, u32[]{:S(2)}) collective-permute-start(f32[4,64,128]{2,1,0:T(8,128)S(1)} %cut_edge.1), channel_id=1, source_target_pairs={{0,32},{32,0},{64,96},{96,64},{128,160},{160,128},{192,224},{224,1... | collective-permute-start | bytes 393224 | tf_op jit(solution)/shard_map/ppermute | solution.py:469
  50.7 1.0 %collective-permute-done.15.rest_9_ = f32[4,64,128]{2,1,0:T(8,128)S(1)} collective-permute-done((f32[4,64,128]{2,1,0:T(8,128)S(1)}, f32[4,64,128]{2,1,0:T(8,128)S(1)}, u32[]{:S(2)}, u32[]{:S(2)}) %collective-permute-start.15) | collective-permute-done | bytes 131104 | tf_op jit(solution)/shard_map/ppermute | solution.py:469
  51.7 2.4 %settle.1 = f32[3,64,648]{2,1,0:T(8,128)} custom-call(s32[2,8]{1,0:T(2,128)S(1)} %bitcast.8, s32[4,10]{1,0:T(4,128)S(1)} %bitcast.11, f32[128,128]{1,0:T(8,128)S(1)} %get-tuple-element.48.rest_0_, f32[128,128]{1,0:T(8,128)S(1)} %collective-permute-done.4.rest_1_, f32[128,128]{1,0:T(8,128)S(1)} %collective-permute-done.5.rest_2_, ...), custom_call_target="tpu_custom_call" | custom-call | flops 1000 | bytes 1000 | tf_op jit(solution)/shard_map/settle/pallas_call | solution.py:443
  (28 shorter events, 0.1 us)
Async XLA Ops:
  0.0 5.6 %collective-permute-start = (f32[3,64,648]{2,1,0:T(8,128)}, f32[3,64,648]{2,1,0:T(8,128)S(1)}, u32[]{:S(2)}, u32[]{:S(2)}) collective-permute-start(f32[3,64,648]{2,1,0:T(8,128)} %here.5), channel_id=1, source_target_pairs={{0,32},{32,0},{64,96},{96,64},{128,160},{160,128},{192,224},{224,1... | collective-permute-start | bytes 1493000 | tf_op jit(solution)/shard_map/ppermute | solution.py:469
  3.2 1.1 %copy-start.2 = (f32[3,64,648]{2,1,0:T(8,128)S(1)}, f32[3,64,648]{2,1,0:T(8,128)}, u32[]{:S(2)}) copy-start(f32[3,64,648]{2,1,0:T(8,128)} %here.5) | copy-start | bytes 1492996
  4.3 0.7 %copy-start.12 = (s32[8,2]{0,1:T(2,128)S(1)}, s32[8,2]{0,1:T(2,128)}, u32[]{:S(2)}) copy-start(s32[8,2]{0,1:T(2,128)} %param.20) | copy-start | bytes 196
  5.0 8.6 %copy-start.3 = (bf16[4,256,512]{2,1,0:T(8,128)(2,1)S(1)}, bf16[4,256,512]{2,1,0:T(8,128)(2,1)}, u32[]{:S(2)}) copy-start(bf16[4,256,512]{2,1,0:T(8,128)(2,1)} %constant.27.clone.table) | copy-start | bytes 3145732
  5.0 8.6 %copy-start.4 = (bf16[288,256]{1,0:T(8,128)(2,1)S(1)}, bf16[288,256]{1,0:T(8,128)(2,1)}, u32[]{:S(2)}) copy-start(bf16[288,256]{1,0:T(8,128)(2,1)} %constant.28.clone.turn.rest_5_) | copy-start | bytes 442372
  5.0 8.6 %copy-start.7 = (bf16[256,512]{1,0:T(8,128)(2,1)S(1)}, bf16[256,512]{1,0:T(8,128)(2,1)}, u32[]{:S(2)}) copy-start(bf16[256,512]{1,0:T(8,128)(2,1)} %constant.26.clone.pick) | copy-start | bytes 786436
  5.0 8.7 %copy-start.14 = (s32[10,4]{0,1:T(4,128)S(1)}, s32[10,4]{0,1:T(4,128)}, u32[]{:S(2)}) copy-start(s32[10,4]{0,1:T(4,128)} %param.19) | copy-start | bytes 484
  5.0 8.7 %copy-start.15 = (f32[4,648]{1,0:T(4,128)S(1)}, f32[4,648]{1,0:T(4,128)}, u32[]{:S(2)}) copy-start(f32[4,648]{1,0:T(4,128)} %metric.1) | copy-start | bytes 31108
  6.7 6.9 %collective-permute-start.3 = (f32[128,256]{1,0:T(8,128)S(1)}, f32[128,256]{1,0:T(8,128)S(1)}, u32[]{:S(2)}, u32[]{:S(2)}) collective-permute-start(f32[128,256]{1,0:T(8,128)S(1)} %get-tuple-element.40), channel_id=1, source_target_pairs={{0,192},{32,224},{64,128},{96,160},{128,64},{160,96},{192,0},{224,... | collective-permute-start | bytes 393224 | tf_op jit(solution)/shard_map/ppermute | solution.py:462
  9.4 9.9 %collective-permute-start.1 = (f32[128,256]{1,0:T(8,128)S(1)}, f32[128,256]{1,0:T(8,128)S(1)}, u32[]{:S(2)}, u32[]{:S(2)}) collective-permute-start(f32[128,256]{1,0:T(8,128)S(1)} %get-tuple-element.38), channel_id=1, source_target_pairs={{0,64},{32,96},{64,0},{96,32},{128,192},{160,224},{192,128},{224,1... | collective-permute-start | bytes 393224 | tf_op jit(solution)/shard_map/ppermute | solution.py:462
  9.4 10.8 %collective-permute-start.2 = (f32[128,256]{1,0:T(8,128)S(1)}, f32[128,256]{1,0:T(8,128)S(1)}, u32[]{:S(2)}, u32[]{:S(2)}) collective-permute-start(f32[128,256]{1,0:T(8,128)S(1)} %get-tuple-element.39), channel_id=1, source_target_pairs={{0,128},{32,160},{64,192},{96,224},{128,0},{160,32},{192,64},{224,... | collective-permute-start | bytes 393224 | tf_op jit(solution)/shard_map/ppermute | solution.py:462
  13.7 6.6 %copy-start = (bf16[512,512]{1,0:T(8,128)(2,1)S(1)}, bf16[512,512]{1,0:T(8,128)(2,1)}, u32[]{:S(2)}) copy-start(bf16[512,512]{1,0:T(8,128)(2,1)} %constant.30.clone.rest_7_.tl.rest_5_) | copy-start | bytes 1572868
  13.7 6.5 %copy-start.1 = (bf16[512,512]{1,0:T(8,128)(2,1)S(1)}, bf16[512,512]{1,0:T(8,128)(2,1)}, u32[]{:S(2)}) copy-start(bf16[512,512]{1,0:T(8,128)(2,1)} %constant.29.clone.rest_6_.th.rest_4_) | copy-start | bytes 1572868
  13.7 6.5 %copy-start.5 = (bf16[512,512]{1,0:T(8,128)(2,1)S(1)}, bf16[512,512]{1,0:T(8,128)(2,1)}, u32[]{:S(2)}) copy-start(bf16[512,512]{1,0:T(8,128)(2,1)} %constant.32.clone.rest_9_) | copy-start | bytes 1572868
  13.7 6.5 %copy-start.6 = (bf16[512,512]{1,0:T(8,128)(2,1)S(1)}, bf16[512,512]{1,0:T(8,128)(2,1)}, u32[]{:S(2)}) copy-start(bf16[512,512]{1,0:T(8,128)(2,1)} %constant.31.clone.rest_8_) | copy-start | bytes 1572868
  13.7 6.5 %copy-start.10 = (bf16[176,96]{1,0:T(8,128)(2,1)S(1)}, bf16[176,96]{1,0:T(8,128)(2,1)}, u32[]{:S(2)}) copy-start(bf16[176,96]{1,0:T(8,128)(2,1)} %constant.34.clone.rest_11_) | copy-start | bytes 101380
  13.7 6.5 %copy-start.11 = (bf16[176,96]{1,0:T(8,128)(2,1)S(1)}, bf16[176,96]{1,0:T(8,128)(2,1)}, u32[]{:S(2)}) copy-start(bf16[176,96]{1,0:T(8,128)(2,1)} %constant.33.clone.rest_10_) | copy-start | bytes 101380
  16.4 6.4 %collective-permute-start.7 = (f32[128,128]{1,0:T(8,128)S(1)}, f32[128,128]{1,0:T(8,128)S(1)}, u32[]{:S(2)}, u32[]{:S(2)}) collective-permute-start(f32[128,128]{1,0:T(8,128)S(1)} %get-tuple-element.54), channel_id=1, source_target_pairs={{0,64},{32,96},{64,0},{96,32},{128,192},{160,224},{192,128},{224,1... | collective-permute-start | bytes 196616 | tf_op jit(solution)/shard_map/ppermute | solution.py:462
  17.6 5.2 %collective-permute-start.8 = (f32[128,128]{1,0:T(8,128)S(1)}, f32[128,128]{1,0:T(8,128)S(1)}, u32[]{:S(2)}, u32[]{:S(2)}) collective-permute-start(f32[128,128]{1,0:T(8,128)S(1)} %get-tuple-element.55), channel_id=1, source_target_pairs={{0,128},{32,160},{64,192},{96,224},{128,0},{160,32},{192,64},{224,... | collective-permute-start | bytes 196616 | tf_op jit(solution)/shard_map/ppermute | solution.py:462
  22.8 14.2 %collective-permute-start.10 = (f32[80,512]{1,0:T(8,128)S(1)}, f32[80,512]{1,0:T(8,128)S(1)}, u32[]{:S(2)}, u32[]{:S(2)}) collective-permute-start(f32[80,512]{1,0:T(8,128)S(1)} %get-tuple-element.60), channel_id=1, source_target_pairs={{0,255},{255,0},{64,191},{191,64},{128,127},{127,128},{192,63},{63... | collective-permute-start | bytes 491528 | tf_op jit(solution)/shard_map/ppermute | solution.py:482
  29.0 6.5 %collective-permute-start.9 = (f32[128,128]{1,0:T(8,128)S(1)}, f32[128,128]{1,0:T(8,128)S(1)}, u32[]{:S(2)}, u32[]{:S(2)}) collective-permute-start(f32[128,128]{1,0:T(8,128)S(1)} %get-tuple-element.58), channel_id=1, source_target_pairs={{0,192},{32,224},{64,128},{96,160},{128,64},{160,96},{192,0},{224,... | collective-permute-start | bytes 196616 | tf_op jit(solution)/shard_map/ppermute | solution.py:462
  31.3 8.9 %collective-permute-start.4 = (f32[128,128]{1,0:T(8,128)S(1)}, f32[128,128]{1,0:T(8,128)S(1)}, u32[]{:S(2)}, u32[]{:S(2)}) collective-permute-start(f32[128,128]{1,0:T(8,128)S(1)} %get-tuple-element.49), channel_id=1, source_target_pairs={{0,64},{32,96},{64,0},{96,32},{128,192},{160,224},{192,128},{224,1... | collective-permute-start | bytes 196616 | tf_op jit(solution)/shard_map/ppermute | solution.py:462
  31.4 10.5 %collective-permute-start.5 = (f32[128,128]{1,0:T(8,128)S(1)}, f32[128,128]{1,0:T(8,128)S(1)}, u32[]{:S(2)}, u32[]{:S(2)}) collective-permute-start(f32[128,128]{1,0:T(8,128)S(1)} %get-tuple-element.50), channel_id=1, source_target_pairs={{0,128},{32,160},{64,192},{96,224},{128,0},{160,32},{192,64},{224,... | collective-permute-start | bytes 196616 | tf_op jit(solution)/shard_map/ppermute | solution.py:462
  33.3 8.6 %collective-permute-start.6 = (f32[128,128]{1,0:T(8,128)S(1)}, f32[128,128]{1,0:T(8,128)S(1)}, u32[]{:S(2)}, u32[]{:S(2)}) collective-permute-start(f32[128,128]{1,0:T(8,128)S(1)} %get-tuple-element.51), channel_id=1, source_target_pairs={{0,192},{32,224},{64,128},{96,160},{128,64},{160,96},{192,0},{224,... | collective-permute-start | bytes 196616 | tf_op jit(solution)/shard_map/ppermute | solution.py:462
  36.9 14.8 %copy-start.8 = (bf16[256,384]{1,0:T(8,128)(2,1)S(1)}, bf16[256,384]{1,0:T(8,128)(2,1)}, u32[]{:S(2)}) copy-start(bf16[256,384]{1,0:T(8,128)(2,1)} %constant.38.clone.rest_13_) | copy-start | bytes 589828
  36.9 14.8 %copy-start.9 = (bf16[128,384]{1,0:T(8,128)(2,1)S(1)}, bf16[128,384]{1,0:T(8,128)(2,1)}, u32[]{:S(2)}) copy-start(bf16[128,384]{1,0:T(8,128)(2,1)} %constant.36.clone.rest_11_) | copy-start | bytes 294916
  37.0 14.7 %copy-start.13 = (bf16[128,128]{1,0:T(8,128)(2,1)S(1)}, bf16[128,128]{1,0:T(8,128)(2,1)}, u32[]{:S(2)}) copy-start(bf16[128,128]{1,0:T(8,128)(2,1)} %constant.35.clone.rest_10_) | copy-start | bytes 98308
  37.0 14.7 %copy-start.16 = (f32[8,128]{1,0:T(8,128)S(1)}, f32[8,128]{1,0:T(8,128)}, u32[]{:S(2)}) copy-start(f32[8,128]{1,0:T(8,128)} %constant.37.clone.rest_12_) | copy-start | bytes 12292
  38.3 8.3 %collective-permute-start.11 = (f32[128,128]{1,0:T(8,128)S(1)}, f32[128,128]{1,0:T(8,128)S(1)}, u32[]{:S(2)}, u32[]{:S(2)}) collective-permute-start(f32[128,128]{1,0:T(8,128)S(1)} %get-tuple-element.62), channel_id=1, source_target_pairs={{0,64},{32,96},{64,0},{96,32},{128,192},{160,224},{192,128},{224,1... | collective-permute-start | bytes 196616 | tf_op jit(solution)/shard_map/ppermute | solution.py:462
  38.4 8.2 %collective-permute-start.12 = (f32[128,128]{1,0:T(8,128)S(1)}, f32[128,128]{1,0:T(8,128)S(1)}, u32[]{:S(2)}, u32[]{:S(2)}) collective-permute-start(f32[128,128]{1,0:T(8,128)S(1)} %get-tuple-element.63), channel_id=1, source_target_pairs={{0,128},{32,160},{64,192},{96,224},{128,0},{160,32},{192,64},{224,... | collective-permute-start | bytes 196616 | tf_op jit(solution)/shard_map/ppermute | solution.py:462
  40.2 6.3 %collective-permute-start.13 = (f32[128,128]{1,0:T(8,128)S(1)}, f32[128,128]{1,0:T(8,128)S(1)}, u32[]{:S(2)}, u32[]{:S(2)}) collective-permute-start(f32[128,128]{1,0:T(8,128)S(1)} %get-tuple-element.64), channel_id=1, source_target_pairs={{0,192},{32,224},{64,128},{96,160},{128,64},{160,96},{192,0},{224,... | collective-permute-start | bytes 196616 | tf_op jit(solution)/shard_map/ppermute | solution.py:462
  41.9 8.8 %collective-permute-start.14 = (f32[4,64,128]{2,1,0:T(8,128)S(1)}, f32[4,64,128]{2,1,0:T(8,128)S(1)}, u32[]{:S(2)}, u32[]{:S(2)}) collective-permute-start(f32[4,64,128]{2,1,0:T(8,128)S(1)} %cut.1), channel_id=1, source_target_pairs={{0,32},{32,0},{64,96},{96,64},{128,160},{160,128},{192,224},{224,1... | collective-permute-start | bytes 393224 | tf_op jit(solution)/shard_map/ppermute | solution.py:469
  46.6 5.1 %collective-permute-start.15 = (f32[4,64,128]{2,1,0:T(8,128)S(1)}, f32[4,64,128]{2,1,0:T(8,128)S(1)}, u32[]{:S(2)}, u32[]{:S(2)}) collective-permute-start(f32[4,64,128]{2,1,0:T(8,128)S(1)} %cut_edge.1), channel_id=1, source_target_pairs={{0,32},{32,0},{64,96},{96,64},{128,160},{160,128},{192,224},{224,1... | collective-permute-start | bytes 393224 | tf_op jit(solution)/shard_map/ppermute | solution.py:469

commit v4 on v3

--- a/solution.py
+++ b/solution.py
@@ -110,6 +110,29 @@
     for c in range(3):
         for place in range(PTS):
             table[c * 96 + place, c * 81 + order[place]] = 1.0
+    return table
+
+
+def rim_table():
+    edges = edge_points()
+    mats = point_matrices()
+    table = np.zeros((4, 64, 256), ml_dtypes.bfloat16)
+    for s in range(4):
+        rows = np.zeros((32, 256))
+        for c in range(3):
+            rows[c * 8 : c * 8 + 7, c * 81 : c * 81 + 81] = mats[(s + 1) % 2][edges[s]]
+        table[s, :32], table[s, 32:] = halves(rows)
+    return table
+
+
+def far_table():
+    lobatto = lobatto_matrix(8)
+    table = np.zeros((80, 64))
+    for c in range(3):
+        for i in range(7):
+            table[c * 8 + i, c * 9 + i + 1] = 1.0
+            table[24 + c * 8 + i, c * 9 : c * 9 + 9] = lobatto[i + 1]
+            table[48 + c * 8 + i, 27 + c * 7 + i] = 1.0
     return table
 
 
@@ -223,7 +246,7 @@
         outs[j][...] = packed[bound[0, row_of(me ^ (2 * j), part)]]
 
 
-def edge_kernel(bound, pair, done, here, there, metric, pick, table, turn, columns, *rest):
+def edge_kernel(bound, pair, done, here, there, metric, pick, table, turn, columns, terms, *rest):
     outs = rest[:4]
     packed, rows, lines, scale, square, flags, count, own, other, other_edge = rest[4:]
     me, part = lax.axis_index("span"), lax.axis_index("dom")
@@ -258,6 +281,12 @@
         square[j : j + 1, :] = line[:, 128 * (j % 2) : 128 * (j % 2) + 128]
     high, low = split(square[...].T)
     columns[...] = dot(turn[0:96, 0:128], high) + dot(turn[0:96, 0:128], low)
+    side = bound[1, row_of(me, part)]
+    along, across = scale[mine * 4 + side], scale[(8 + mine) * 4 + side]
+    even = (side & 1) == 0
+    terms[...] = jnp.zeros((8, 128), F32)
+    terms[0:1, :] = jnp.where(side < 2, 1.0, -1.0) * jnp.where(even, along, across)
+    terms[1:2, :] = jnp.where(even, across, along)
     lane = lax.broadcasted_iota(jnp.int32, (2 * MODES, 128), 1)
     for j in range(4):
         e = bound[0, row_of(me ^ (2 * j), part)]
@@ -275,15 +304,32 @@
         outs[j][...] = total
 
 
-def element_kernel(bound, *rest):
+def rim_kernel(bound, *rest):
     blocks = rest[:4]
-    columns, turn, th, tl, dh, dl, gh, gl = rest[4:12]
-    send, mine, u, q, g, modes = rest[12:]
+    terms, table, send, high, low, modes, points = rest[4:]
     me, part = lax.axis_index("span"), lax.axis_index("dom")
     for j in range(4):
         modes[chip_modes(j), :] = blocks[j][...]
-    vh, vl = split(modes[...].T)
-    vh, vl = dot(turn[...], vh).astype(BF), dot(turn[...], vl).astype(BF)
+    points[...] = modes[...].T
+    vh, vl = split(points[...])
+    high[...] = vh
+    low[...] = vl
+    side = bound[1, row_of(me, part)]
+    rows = dot(table[side], vh)
+    across = rows[:32] + rows[32:] + dot(table[side, 0:32], vl)
+    base = jnp.where(side == 0, 0, jnp.where(side == 1, 8, jnp.where(side == 2, 80, 72)))
+    step = jnp.where(side == 0, 1, jnp.where(side == 1, 9, jnp.where(side == 2, -1, -9)))
+    for c in range(3):
+        for i in range(9):
+            send[c * 9 + i : c * 9 + i + 1, :] = points[pl.ds(c * 81 + base + step * i, 1), :]
+        send[27 + c * 7 : 34 + c * 7, :] = across[c * 8 : c * 8 + 7]
+    send[48:56, :] = jnp.zeros((8, NZ), F32)
+    send[48:56, 0:128] = terms[...]
+
+
+def element_kernel(bound, high, low, columns, turn, th, tl, dh, dl, gh, gl, mine, u, q, g):
+    me, part = lax.axis_index("span"), lax.axis_index("dom")
+    vh, vl = dot(turn[...], high[...]).astype(BF), dot(turn[...], low[...]).astype(BF)
     value = dot(vh, th[...]) + dot(vl, th[...]) + dot(vh, tl[...])
     slope = dot(vh, dh[...]) + dot(vl, dh[...]) + dot(vh, dl[...])
     uh, ul = split(value)
@@ -297,14 +343,11 @@
         u[c] = value[96 * c : 96 * c + 88]
         q[c] = third * slope[96 * c : 96 * c + 88]
     base = INSIDE + 7 * bound[1, row_of(me, part)]
-    send[77:80] = jnp.zeros((3, NZ), F32)
-    mine[77:80] = jnp.zeros((3, NZ), F32)
+    mine[...] = jnp.zeros((88, NZ), F32)
     order = [(g, f) for f in range(6)] + [(u, 0), (u, 1)] + [(q, c) for c in range(3)]
     for f, (ref, at) in enumerate(order):
         for i in range(7):
-            line = ref[at, pl.ds(base + i, 1), :]
-            mine[f * 7 + i : f * 7 + i + 1, :] = line
-            send[f * 7 + 6 - i : f * 7 + 7 - i, :] = line
+            mine[f * 8 + 6 - i : f * 8 + 7 - i, :] = ref[at, pl.ds(base + i, 1), :]
 
 
 def to_modes(term, th, tl):
@@ -366,22 +409,45 @@
     term[115:128, :] = jnp.zeros((13, NZ), F32)
 
 
-def side_kernel(bound, term, mine, other, th, tl, *rest):
+def whole_kernel(bound, pair, *rest):
+    blocks = rest[:4]
+    high, low, columns, turn, th, tl, dh, dl, gh, gl = rest[4:14]
+    outs, term, mine = rest[14:18], rest[18], rest[19]
+    u, q, g, inside_term, spec, modes = rest[20:26]
+    pairs = rest[26:]
+    element_kernel(bound, high, low, columns, turn, th, tl, dh, dl, gh, gl, mine, u, q, g)
+    inside_kernel(u, q, g, th, tl, *outs, inside_term, spec)
+    edge_term_kernel(bound, pair, *blocks, th, tl, u, q, g, term, modes, *pairs)
+
+
+def side_kernel(bound, term, mine, other, table, th, tl, dh, dl, *rest):
     outs = rest[:4]
-    work, spec = rest[4:]
+    work, spec, rows, square, turned = rest[4:]
     me, part = lax.axis_index("span"), lax.axis_index("dom")
     work[...] = term[...]
-    m = [mine[f * 7 : f * 7 + 7, :] for f in range(11)]
-    r = [other[f * 7 : f * 7 + 7, :] for f in range(11)]
+    rows[0:56] = other[...]
+    rows[56:64] = jnp.zeros((8, NZ), F32)
+    rh, rl = split(rows[...])
+    xh, xl = split(dot(table[0], rh) + dot(table[0], rl) + dot(table[1], rh))
+    value = dot(xh, th[...]) + dot(xl, th[...]) + dot(xh, tl[...])
+    xh, xl = xh[:32], xl[:32]
+    slope = dot(xh, dh[...]) + dot(xl, dh[...]) + dot(xh, dl[...])
+    square[...] = jnp.zeros((128, 128), F32)
+    square[0:8, :] = other[48:56, 0:128]
+    turned[...] = square[...].T
     base = 31 + 7 * bound[1, row_of(me, part)]
+    u0 = mine[48:56, :] + value[0:8]
+    u1 = mine[56:64, :] + value[8:16]
     for c in range(3):
-        gx = (m[c] + r[c]) * 0.5
-        gy = (m[3 + c] + r[3 + c]) * 0.5
-        value = (
-            (m[6] * gx + m[7] * gy + m[8 + c]) + (r[6] * gx + r[7] * gy + r[8 + c])
-        ) * 0.5
+        along, across = value[24 + 8 * c : 32 + 8 * c], value[48 + 8 * c : 56 + 8 * c]
+        gx = mine[8 * c : 8 * c + 8, :] + (turned[0:8, 0:1] * along + turned[0:8, 1:2] * across)
+        gy = mine[24 + 8 * c : 32 + 8 * c, :] + (
+            turned[7:15, 0:1] * along + turned[7:15, 1:2] * across
+        )
+        q = mine[64 + 8 * c : 72 + 8 * c, :] + value[16:24] * slope[8 * c : 8 * c + 8]
+        mean = (u0 * gx + u1 * gy) * 0.25 + q * 0.5
         for i in range(7):
-            work[pl.ds(base + 28 * c + i, 1), :] = value[i : i + 1, :]
+            work[pl.ds(base + 28 * c + 6 - i, 1), :] = mean[i : i + 1, :]
     spec[...] = to_modes(work[...], th, tl)
     for j in range(4):
         outs[j][...] = spec[chip_modes(j), :]
@@ -439,7 +505,10 @@
 
 
 def call(kernel, name, scalars, arrays, outs, scratch=(), weight=1000):
-    shapes = [jax.ShapeDtypeStruct(shape, F32) for shape in outs]
+    shapes = [
+        shape if isinstance(shape, jax.ShapeDtypeStruct) else jax.ShapeDtypeStruct(shape, F32)
+        for shape in outs
+    ]
     return pl.pallas_call(
         kernel,
         out_shape=shapes,
@@ -510,12 +579,12 @@
     )
     blocks = between_chips(blocks)
     blocks[3], packed = lax.optimization_barrier((blocks[3], packed))
-    columns, *edge_blocks = call(
+    columns, terms, *edge_blocks = call(
         edge_kernel,
         "edges",
         [bound_table, pair_table],
         [packed, velocity_modes, there, metric, pick, edge_table, turn],
-        [(96, 128)] + [edge_chip] * 4,
+        [(96, 128), (8, 128)] + [edge_chip] * 4,
         [
             pltpu.VMEM((ELEMS, 2 * MODES, 256), F32),
             pltpu.VMEM((16, 256), F32),
@@ -528,37 +597,48 @@
         weight=LONG,
     )
     edge_blocks = between_chips(edge_blocks)
-    send, mine, u, q, g = call(
-        element_kernel,
-        "element",
+    half = jax.ShapeDtypeStruct((256, NZ), BF)
+    send, high, low = call(
+        rim_kernel,
+        "rim",
         [bound_table],
-        [*blocks, columns, turn, th, tl, dh, dl, gh, gl],
-        [(80, NZ), (80, NZ), (3, 88, NZ), (3, 88, NZ), (6, 88, NZ)],
-        [pltpu.VMEM((NZ, 256), F32)],
-    )
-    send, edge_blocks[1:3] = lax.optimization_barrier((send, edge_blocks[1:3]))
+        [*blocks, terms, rim_table()],
+        [(56, NZ), half, half],
+        [pltpu.VMEM((NZ, 256), F32), pltpu.VMEM((256, NZ), F32)],
+    )
     other = side_swap(send, lax.axis_size("dom"))
     modes_scratch = pltpu.VMEM((NZ, 128), F32)
     term_scratch = pltpu.VMEM((128, NZ), F32)
-    inside = call(
-        inside_kernel, "inside", [], [u, q, g, th, tl], [edge_chip] * 4, [term_scratch, modes_scratch]
+    *inside, term, mine = call(
+        whole_kernel,
+        "whole",
+        [bound_table, pair_table],
+        [*edge_blocks, high, low, columns, turn, th, tl, dh, dl, gh, gl],
+        [edge_chip] * 4 + [(128, NZ), (88, NZ)],
+        [
+            pltpu.VMEM((3, 88, NZ), F32),
+            pltpu.VMEM((3, 88, NZ), F32),
+            pltpu.VMEM((6, 88, NZ), F32),
+            term_scratch,
+            modes_scratch,
+            modes_scratch,
+        ]
+        + pair_scratch(),
     )
     inside = between_chips(inside)
-    (term,) = call(
-        edge_term_kernel,
-        "term",
-        [bound_table, pair_table],
-        [*edge_blocks, th, tl, u, q, g],
-        [(128, NZ)],
-        [modes_scratch] + pair_scratch(),
-    )
     edge = call(
         side_kernel,
         "side",
         [bound_table],
-        [term, mine, other, th, tl],
+        [term, mine, other, np.stack(halves(far_table())), th, tl, dh, dl],
         [edge_chip] * 4,
-        [term_scratch, modes_scratch],
+        [
+            term_scratch,
+            modes_scratch,
+            pltpu.VMEM((64, NZ), F32),
+            pltpu.VMEM((128, 128), F32),
+            pltpu.VMEM((128, 128), F32),
+        ],
     )
     edge = between_chips(edge)
     (cross,) = call(cut_kernel, "cut", [], inside, [(4, MODES, 128)])

time: 54.3 us -> 52.1 us (0.959)
  waiting for transfers between devices: 5.72 us -> 4.47 us
  local copies, waits for them, and re-layouts: 1.83 us -> 1.17 us
  starting transfers between devices: 33.7 us -> 33.1 us
    ppermute x12, waiting for transfers between devices: 4.73 us -> 3.29 us  [between_chips(): lax.ppermute(blocks[j], 'span', [(s, s ^ 2 * j) for s in range(SPAN)])]
    ppermute x1, starting transfers between devices: 6.25 us -> 7.6 us  [side_swap(): return lax.ppermute(block, ('span', 'dom'), perm)]
    ppermute x3, starting transfers between devices: 12 us -> 11 us  [between_cores(): return lax.ppermute(block, 'span', [(s, s ^ 1) for s in range(SPAN)])]
    ppermute x12, starting transfers between devices: 15.5 us -> 14.5 us  [between_chips(): lax.ppermute(blocks[j], 'span', [(s, s ^ 2 * j) for s in range(SPAN)])]
    unnamed x34 -> x38, local copies, waits for them, and re-layouts: 1.83 us -> 1.17 us
    pallas_call x10 -> x9, Pallas kernels: 12.5 us -> 13 us  [call(): pl.pallas_call(kernel, out_shape=shapes, in_specs=[spec_of(pltpu.SMEM)] *...]
  transfers between devices with their start and end apart: 16 -> 16, of which waited for: 4 -> 4; matrix products, arithmetic and copies ran while one was open for 0% -> 0% of each run, Pallas kernels for 17% -> 18%
where the time goes in v4:
time: 52.1 us; the launch traced here: 52 us
  starting transfers between devices  33.1 us (64%)
  Pallas kernels  13 us (25%)
  waiting for transfers between devices  4.47 us (9%)
  local copies, waits for them, and re-layouts  1.17 us (2%)
    ppermute x12, starting transfers between devices, between_chips(): lax.ppermute(blocks[j], 'span', [(s, s ^ 2 * j) for s in range(SPAN)])  14.5 us
    pallas_call x9, Pallas kernels, call(): pl.pallas_call(kernel, out_shape=shapes, in_specs=[spec_of(pltpu.SMEM)] *...  13 us
    ppermute x3, starting transfers between devices, between_cores(): return lax.ppermute(block, 'span', [(s, s ^ 1) for s in range(SPAN)])  11 us
    ppermute x1, starting transfers between devices, side_swap(): return lax.ppermute(block, ('span', 'dom'), perm)  7.6 us
    ppermute x12, waiting for transfers between devices, between_chips(): lax.ppermute(blocks[j], 'span', [(s, s ^ 2 * j) for s in range(SPAN)])  3.29 us
    ppermute x3, waiting for transfers between devices, between_cores(): return lax.ppermute(block, 'span', [(s, s ^ 1) for s in range(SPAN)])  1.17 us
    unnamed x38, local copies, waits for them, and re-layouts  1.17 us
  transfers between devices with their start and end apart: 16, of which 4 were waited for; matrix products, arithmetic and copies ran while one was open for 0% of the time, Pallas kernels for 18%

profile of v4, /device:TPU:1, one launch (start us, length us, event | category | flops | bytes accessed | tf_op | source)
XLA Modules:
  0.0 52.0 jit_solution(11829569410206264301)
XLA Ops:
  0.0 3.2 %collective-permute-start = (f32[3,64,648]{2,1,0:T(8,128)}, f32[3,64,648]{2,1,0:T(8,128)S(1)}, u32[]{:S(2)}, u32[]{:S(2)}) collective-permute-start(f32[3,64,648]{2,1,0:T(8,128)} %here.5), channel_id=1, source_target_pairs={{0,32},{32,0},{64,96},{96,64},{128,160},{160,128},{192,224},{224,1... | collective-permute-start | bytes 1493000 | tf_op jit(solution)/shard_map/ppermute | solution.py:538
  3.2 1.1 %copy-done = f32[3,64,648]{2,1,0:T(8,128)S(1)} copy-done((f32[3,64,648]{2,1,0:T(8,128)S(1)}, f32[3,64,648]{2,1,0:T(8,128)}, u32[]{:S(2)}) %copy-start) | copy-done | bytes 497688
  4.3 0.6 %ready.1 = f32[8,128]{1,0:T(8,128)S(1)} custom-call(s32[2,8]{1,0:T(2,128)S(1)} %bitcast.2, f32[3,64,648]{2,1,0:T(8,128)S(1)} %copy-done), custom_call_target="tpu_custom_call" | custom-call | flops 200000000 | bytes 200000000 | tf_op jit(solution)/shard_map/ready/pallas_call | solution.py:512
  4.9 0.0 copy-start.6
  4.9 0.0 copy-start.7
  4.9 0.2 collective-permute-done.there
  5.1 1.2 %pack.1 = (f32[8,128,256]{2,1,0:T(8,128)S(1)}, f32[128,256]{1,0:T(8,128)S(1)}, f32[128,256]{1,0:T(8,128)S(1)}, f32[128,256]{1,0:T(8,128)S(1)}, f32[128,256]{1,0:T(8,128)S(1)}) custom-call(s32[2,8]{1,0:T(2,128)S(1)} %bitcast.3, f32[3,64,648]{2,1,0:T(8,128)S(1)} %copy-done, f32[3,64,648]{2,1,0:T(8,128)S(1)} %collective-permute-done.there, f32[8,128]{1,0:T(8,128)S(1)} %ready.1), custom_call_target="tpu_custom_call" | custom-call | flops 200000000 | bytes 200000000 | tf_op jit(solution)/shard_map/pack/pallas_call | solution.py:512
  6.3 2.7 %collective-permute-start.1 = (f32[128,256]{1,0:T(8,128)S(1)}, f32[128,256]{1,0:T(8,128)S(1)}, u32[]{:S(2)}, u32[]{:S(2)}) collective-permute-start(f32[128,256]{1,0:T(8,128)S(1)} %get-tuple-element.35), channel_id=1, source_target_pairs={{0,192},{32,224},{64,128},{96,160},{128,64},{160,96},{192,0},{224,... | collective-permute-start | bytes 393224 | tf_op jit(solution)/shard_map/ppermute | solution.py:531
  9.0 0.0 collective-permute-start.5
  9.0 0.9 %collective-permute-start.6 = (f32[128,256]{1,0:T(8,128)S(1)}, f32[128,256]{1,0:T(8,128)S(1)}, u32[]{:S(2)}, u32[]{:S(2)}) collective-permute-start(f32[128,256]{1,0:T(8,128)S(1)} %get-tuple-element.44), channel_id=1, source_target_pairs={{0,128},{32,160},{64,192},{96,224},{128,0},{160,32},{192,64},{224,... | collective-permute-start | bytes 393224 | tf_op jit(solution)/shard_map/ppermute | solution.py:531
  9.9 2.8 %collective-permute-done.1.rest_3_ = f32[128,256]{1,0:T(8,128)S(1)} collective-permute-done((f32[128,256]{1,0:T(8,128)S(1)}, f32[128,256]{1,0:T(8,128)S(1)}, u32[]{:S(2)}, u32[]{:S(2)}) %collective-permute-start.1) | collective-permute-done | bytes 131104 | tf_op jit(solution)/shard_map/ppermute | solution.py:531
  12.7 0.0 copy-start.9
  12.7 0.0 copy-start.2
  12.7 0.0 copy-start.3
  12.8 0.0 copy-start.4
  12.8 2.5 %edges.1 = (f32[96,128]{1,0:T(8,128)S(1)}, f32[8,128]{1,0:T(8,128)S(1)}, f32[128,128]{1,0:T(8,128)S(1)}, f32[128,128]{1,0:T(8,128)S(1)}, f32[128,128]{1,0:T(8,128)S(1)}, /*index=5*/f32[128,128]{1,0:T(8,128)S(1)}) custom-call(s32[2,8]{1,0:T(2,128)S(1)} %bitcast.4, s32[4,10]{1,0:T(4,128)S(1)} %bitcast.9, f32[8,128,256]{2,1,0:T(8,128)S(1)} %get-tuple-element.37.done, ...), custom_call_target="tpu_custom_call" | custom-call | flops 200000000 | bytes 200000000 | tf_op jit(solution)/shard_map/edges/pallas_call | solution.py:512
  15.3 0.0 copy-start.1
  15.3 0.1 collective-permute-start.2
  15.4 2.9 %collective-permute-start.3 = (f32[128,128]{1,0:T(8,128)S(1)}, f32[128,128]{1,0:T(8,128)S(1)}, u32[]{:S(2)}, u32[]{:S(2)}) collective-permute-start(f32[128,128]{1,0:T(8,128)S(1)} %get-tuple-element.40), channel_id=1, source_target_pairs={{0,128},{32,160},{64,192},{96,224},{128,0},{160,32},{192,64},{224,... | collective-permute-start | bytes 196616 | tf_op jit(solution)/shard_map/ppermute | solution.py:531
  18.3 0.7 %collective-permute-start.4 = (f32[128,128]{1,0:T(8,128)S(1)}, f32[128,128]{1,0:T(8,128)S(1)}, u32[]{:S(2)}, u32[]{:S(2)}) collective-permute-start(f32[128,128]{1,0:T(8,128)S(1)} %get-tuple-element.41), channel_id=1, source_target_pairs={{0,192},{32,224},{64,128},{96,160},{128,64},{160,96},{192,0},{224,... | collective-permute-start | bytes 196616 | tf_op jit(solution)/shard_map/ppermute | solution.py:531
  19.0 0.0 collective-permute-done.5.rest_1_
  19.0 0.5 collective-permute-done.6.rest_2_
  19.4 1.0 %rim.1 = (f32[56,512]{1,0:T(8,128)S(1)}, bf16[256,512]{1,0:T(8,128)(2,1)S(1)}, bf16[256,512]{1,0:T(8,128)(2,1)S(1)}) custom-call(s32[2,8]{1,0:T(2,128)S(1)} %bitcast.5, f32[128,256]{1,0:T(8,128)S(1)} %get-tuple-element.42.rest_0_, f32[128,256]{1,0:T(8,128)S(1)} %collective-permute-done.5.rest_1_, f32[128,256]{1,0:T(8,128)S(1)} %collective-permute-done.6.rest_2_, ...), custom_call_target="tpu_custom_call" | custom-call | flops 1000 | bytes 1000 | tf_op jit(solution)/shard_map/rim/pallas_call | solution.py:512
  20.4 7.6 %collective-permute-start.10 = (f32[56,512]{1,0:T(8,128)S(1)}, f32[56,512]{1,0:T(8,128)S(1)}, u32[]{:S(2)}, u32[]{:S(2)}) collective-permute-start(f32[56,512]{1,0:T(8,128)S(1)} %get-tuple-element.56), channel_id=1, source_target_pairs={{0,255},{255,0},{64,191},{191,64},{128,127},{127,128},{192,63},{63... | collective-permute-start | bytes 344072 | tf_op jit(solution)/shard_map/ppermute | solution.py:551
  28.0 0.0 collective-permute-done.2.rest_1_
  28.0 0.0 collective-permute-done.3.rest_2_
  28.0 0.0 collective-permute-done.4.rest_3_
  28.1 0.0 copy-start.13
  28.1 3.4 %whole.1 = (f32[128,128]{1,0:T(8,128)S(1)}, f32[128,128]{1,0:T(8,128)S(1)}, f32[128,128]{1,0:T(8,128)S(1)}, f32[128,128]{1,0:T(8,128)S(1)}, f32[128,512]{1,0:T(8,128)S(1)}, /*index=5*/f32[88,512]{1,0:T(8,128)S(1)}) custom-call(s32[2,8]{1,0:T(2,128)S(1)} %bitcast.6, s32[4,10]{1,0:T(4,128)S(1)} %bitcast.10, f32[128,128]{1,0:T(8,128)S(1)} %get-tuple-element.38.rest_0_, ...), custom_call_target="tpu_custom_call" | custom-call | flops 1000 | bytes 1000 | tf_op jit(solution)/shard_map/whole/pallas_call | solution.py:512
  31.5 1.4 %collective-permute-start.7 = (f32[128,128]{1,0:T(8,128)S(1)}, f32[128,128]{1,0:T(8,128)S(1)}, u32[]{:S(2)}, u32[]{:S(2)}) collective-permute-start(f32[128,128]{1,0:T(8,128)S(1)} %get-tuple-element.51), channel_id=1, source_target_pairs={{0,64},{32,96},{64,0},{96,32},{128,192},{160,224},{192,128},{224,1... | collective-permute-start | bytes 196616 | tf_op jit(solution)/shard_map/ppermute | solution.py:531
  32.9 0.6 %collective-permute-start.8 = (f32[128,128]{1,0:T(8,128)S(1)}, f32[128,128]{1,0:T(8,128)S(1)}, u32[]{:S(2)}, u32[]{:S(2)}) collective-permute-start(f32[128,128]{1,0:T(8,128)S(1)} %get-tuple-element.52), channel_id=1, source_target_pairs={{0,128},{32,160},{64,192},{96,224},{128,0},{160,32},{192,64},{224,... | collective-permute-start | bytes 196616 | tf_op jit(solution)/shard_map/ppermute | solution.py:531
  33.5 1.6 %collective-permute-start.9 = (f32[128,128]{1,0:T(8,128)S(1)}, f32[128,128]{1,0:T(8,128)S(1)}, u32[]{:S(2)}, u32[]{:S(2)}) collective-permute-start(f32[128,128]{1,0:T(8,128)S(1)} %get-tuple-element.53), channel_id=1, source_target_pairs={{0,192},{32,224},{64,128},{96,160},{128,64},{160,96},{192,0},{224,... | collective-permute-start | bytes 196616 | tf_op jit(solution)/shard_map/ppermute | solution.py:531
  35.2 0.0 collective-permute-done.10.other
  35.2 2.0 %side.1 = (f32[128,128]{1,0:T(8,128)S(1)}, f32[128,128]{1,0:T(8,128)S(1)}, f32[128,128]{1,0:T(8,128)S(1)}, f32[128,128]{1,0:T(8,128)S(1)}) custom-call(s32[2,8]{1,0:T(2,128)S(1)} %bitcast.7, f32[128,512]{1,0:T(8,128)S(1)} %get-tuple-element.54.term, f32[88,512]{1,0:T(8,128)S(1)} %get-tuple-element.55.mine, f32[56,512]{1,0:T(8,128)S(1)} %collective-permute-done.10.other, ...), custom_call_target="tpu_custom_call" | custom-call | flops 1000 | bytes 1000 | tf_op jit(solution)/shard_map/side/pallas_call | solution.py:512
  37.2 0.5 collective-permute-start.11
  37.6 1.5 %collective-permute-start.12 = (f32[128,128]{1,0:T(8,128)S(1)}, f32[128,128]{1,0:T(8,128)S(1)}, u32[]{:S(2)}, u32[]{:S(2)}) collective-permute-start(f32[128,128]{1,0:T(8,128)S(1)} %get-tuple-element.59), channel_id=1, source_target_pairs={{0,128},{32,160},{64,192},{96,224},{128,0},{160,32},{192,64},{224,... | collective-permute-start | bytes 196616 | tf_op jit(solution)/shard_map/ppermute | solution.py:531
  39.2 0.0 collective-permute-done.7.rest_1_
  39.2 1.6 %collective-permute-start.13 = (f32[128,128]{1,0:T(8,128)S(1)}, f32[128,128]{1,0:T(8,128)S(1)}, u32[]{:S(2)}, u32[]{:S(2)}) collective-permute-start(f32[128,128]{1,0:T(8,128)S(1)} %get-tuple-element.60), channel_id=1, source_target_pairs={{0,192},{32,224},{64,128},{96,160},{128,64},{160,96},{192,0},{224,... | collective-permute-start | bytes 196616 | tf_op jit(solution)/shard_map/ppermute | solution.py:531
  40.8 3.6 %collective-permute-start.14 = (f32[4,64,128]{2,1,0:T(8,128)S(1)}, f32[4,64,128]{2,1,0:T(8,128)S(1)}, u32[]{:S(2)}, u32[]{:S(2)}) collective-permute-start(f32[4,64,128]{2,1,0:T(8,128)S(1)} %cut.1), channel_id=1, source_target_pairs={{0,32},{32,0},{64,96},{96,64},{128,160},{160,128},{192,224},{224,1... | collective-permute-start | bytes 393224 | tf_op jit(solution)/shard_map/ppermute | solution.py:538
  44.4 0.0 collective-permute-done.12.rest_2_.rest_6_
  44.4 0.0 collective-permute-done.13.rest_3_.rest_7_
  44.4 0.0 copy-start.8
  44.5 0.0 copy-start.10
  44.5 0.0 copy-start.15
  44.5 0.0 copy-start.18
  44.5 4.1 %collective-permute-start.15 = (f32[4,64,128]{2,1,0:T(8,128)S(1)}, f32[4,64,128]{2,1,0:T(8,128)S(1)}, u32[]{:S(2)}, u32[]{:S(2)}) collective-permute-start(f32[4,64,128]{2,1,0:T(8,128)S(1)} %cut_edge.1), channel_id=1, source_target_pairs={{0,32},{32,0},{64,96},{96,64},{128,160},{160,128},{192,224},{224,1... | collective-permute-start | bytes 393224 | tf_op jit(solution)/shard_map/ppermute | solution.py:538
  48.6 1.0 %collective-permute-done.15.rest_9_ = f32[4,64,128]{2,1,0:T(8,128)S(1)} collective-permute-done((f32[4,64,128]{2,1,0:T(8,128)S(1)}, f32[4,64,128]{2,1,0:T(8,128)S(1)}, u32[]{:S(2)}, u32[]{:S(2)}) %collective-permute-start.15) | collective-permute-done | bytes 131104 | tf_op jit(solution)/shard_map/ppermute | solution.py:538
  49.6 2.4 %settle.1 = f32[3,64,648]{2,1,0:T(8,128)} custom-call(s32[2,8]{1,0:T(2,128)S(1)} %bitcast.8, s32[4,10]{1,0:T(4,128)S(1)} %bitcast.11, f32[128,128]{1,0:T(8,128)S(1)} %get-tuple-element.50.rest_0_, f32[128,128]{1,0:T(8,128)S(1)} %collective-permute-done.7.rest_1_, f32[128,128]{1,0:T(8,128)S(1)} %collective-permute-done.8.rest_2_, ...), custom_call_target="tpu_custom_call" | custom-call | flops 1000 | bytes 1000 | tf_op jit(solution)/shard_map/settle/pallas_call | solution.py:512
  (31 shorter events, 0.1 us)
Async XLA Ops:
  0.0 3.2 %copy-start.14 = (s32[8,2]{0,1:T(2,128)S(1)}, s32[8,2]{0,1:T(2,128)}, u32[]{:S(2)}) copy-start(s32[8,2]{0,1:T(2,128)} %param.22) | copy-start | bytes 196
  0.0 5.1 %collective-permute-start = (f32[3,64,648]{2,1,0:T(8,128)}, f32[3,64,648]{2,1,0:T(8,128)S(1)}, u32[]{:S(2)}, u32[]{:S(2)}) collective-permute-start(f32[3,64,648]{2,1,0:T(8,128)} %here.5), channel_id=1, source_target_pairs={{0,32},{32,0},{64,96},{96,64},{128,160},{160,128},{192,224},{224,1... | collective-permute-start | bytes 1493000 | tf_op jit(solution)/shard_map/ppermute | solution.py:538
  3.2 1.1 %copy-start = (f32[3,64,648]{2,1,0:T(8,128)S(1)}, f32[3,64,648]{2,1,0:T(8,128)}, u32[]{:S(2)}) copy-start(f32[3,64,648]{2,1,0:T(8,128)} %here.5) | copy-start | bytes 1492996
  4.3 8.4 %copy-start.5 = (bf16[4,256,512]{2,1,0:T(8,128)(2,1)S(1)}, bf16[4,256,512]{2,1,0:T(8,128)(2,1)}, u32[]{:S(2)}) copy-start(bf16[4,256,512]{2,1,0:T(8,128)(2,1)} %constant.31.clone.table) | copy-start | bytes 3145732
  4.9 7.8 %copy-start.6 = (bf16[288,256]{1,0:T(8,128)(2,1)S(1)}, bf16[288,256]{1,0:T(8,128)(2,1)}, u32[]{:S(2)}) copy-start(bf16[288,256]{1,0:T(8,128)(2,1)} %constant.32.clone.turn.rest_7_) | copy-start | bytes 442372
  4.9 7.8 %copy-start.7 = (bf16[256,512]{1,0:T(8,128)(2,1)S(1)}, bf16[256,512]{1,0:T(8,128)(2,1)}, u32[]{:S(2)}) copy-start(bf16[256,512]{1,0:T(8,128)(2,1)} %constant.30.clone.pick) | copy-start | bytes 786436
  5.1 7.6 %copy-start.17 = (f32[4,648]{1,0:T(4,128)S(1)}, f32[4,648]{1,0:T(4,128)}, u32[]{:S(2)}) copy-start(f32[4,648]{1,0:T(4,128)} %metric.1) | copy-start | bytes 31108
  6.3 6.4 %collective-permute-start.1 = (f32[128,256]{1,0:T(8,128)S(1)}, f32[128,256]{1,0:T(8,128)S(1)}, u32[]{:S(2)}, u32[]{:S(2)}) collective-permute-start(f32[128,256]{1,0:T(8,128)S(1)} %get-tuple-element.35), channel_id=1, source_target_pairs={{0,192},{32,224},{64,128},{96,160},{128,64},{160,96},{192,0},{224,... | collective-permute-start | bytes 393224 | tf_op jit(solution)/shard_map/ppermute | solution.py:531
  9.0 10.0 %collective-permute-start.5 = (f32[128,256]{1,0:T(8,128)S(1)}, f32[128,256]{1,0:T(8,128)S(1)}, u32[]{:S(2)}, u32[]{:S(2)}) collective-permute-start(f32[128,256]{1,0:T(8,128)S(1)} %get-tuple-element.43), channel_id=1, source_target_pairs={{0,64},{32,96},{64,0},{96,32},{128,192},{160,224},{192,128},{224,1... | collective-permute-start | bytes 393224 | tf_op jit(solution)/shard_map/ppermute | solution.py:531
  9.0 3.8 %copy-start.16 = (s32[10,4]{0,1:T(4,128)S(1)}, s32[10,4]{0,1:T(4,128)}, u32[]{:S(2)}) copy-start(s32[10,4]{0,1:T(4,128)} %param.21) | copy-start | bytes 484
  9.0 10.5 %collective-permute-start.6 = (f32[128,256]{1,0:T(8,128)S(1)}, f32[128,256]{1,0:T(8,128)S(1)}, u32[]{:S(2)}, u32[]{:S(2)}) collective-permute-start(f32[128,256]{1,0:T(8,128)S(1)} %get-tuple-element.44), channel_id=1, source_target_pairs={{0,128},{32,160},{64,192},{96,224},{128,0},{160,32},{192,64},{224,... | collective-permute-start | bytes 393224 | tf_op jit(solution)/shard_map/ppermute | solution.py:531
  12.7 6.7 %copy-start.9 = (bf16[4,64,256]{2,1,0:T(8,128)(2,1)S(1)}, bf16[4,64,256]{2,1,0:T(8,128)(2,1)}, u32[]{:S(2)}) copy-start(bf16[4,64,256]{2,1,0:T(8,128)(2,1)} %constant.33.clone.rest_5_) | copy-start | bytes 393220
  12.7 15.3 %copy-start.2 = (bf16[512,512]{1,0:T(8,128)(2,1)S(1)}, bf16[512,512]{1,0:T(8,128)(2,1)}, u32[]{:S(2)}) copy-start(bf16[512,512]{1,0:T(8,128)(2,1)} %constant.36.clone.rest_10_.dh) | copy-start | bytes 1572868
  12.7 15.3 %copy-start.3 = (bf16[512,512]{1,0:T(8,128)(2,1)S(1)}, bf16[512,512]{1,0:T(8,128)(2,1)}, u32[]{:S(2)}) copy-start(bf16[512,512]{1,0:T(8,128)(2,1)} %constant.35.clone.rest_9_.tl) | copy-start | bytes 1572868
  12.8 15.3 %copy-start.4 = (bf16[512,512]{1,0:T(8,128)(2,1)S(1)}, bf16[512,512]{1,0:T(8,128)(2,1)}, u32[]{:S(2)}) copy-start(bf16[512,512]{1,0:T(8,128)(2,1)} %constant.34.clone.rest_8_.th) | copy-start | bytes 1572868
  15.3 12.7 %copy-start.1 = (bf16[512,512]{1,0:T(8,128)(2,1)S(1)}, bf16[512,512]{1,0:T(8,128)(2,1)}, u32[]{:S(2)}) copy-start(bf16[512,512]{1,0:T(8,128)(2,1)} %constant.37.clone.rest_11_.dl) | copy-start | bytes 1572868
  15.3 12.7 %collective-permute-start.2 = (f32[128,128]{1,0:T(8,128)S(1)}, f32[128,128]{1,0:T(8,128)S(1)}, u32[]{:S(2)}, u32[]{:S(2)}) collective-permute-start(f32[128,128]{1,0:T(8,128)S(1)} %get-tuple-element.39), channel_id=1, source_target_pairs={{0,64},{32,96},{64,0},{96,32},{128,192},{160,224},{192,128},{224,1... | collective-permute-start | bytes 196616 | tf_op jit(solution)/shard_map/ppermute | solution.py:531
  15.4 12.6 %collective-permute-start.3 = (f32[128,128]{1,0:T(8,128)S(1)}, f32[128,128]{1,0:T(8,128)S(1)}, u32[]{:S(2)}, u32[]{:S(2)}) collective-permute-start(f32[128,128]{1,0:T(8,128)S(1)} %get-tuple-element.40), channel_id=1, source_target_pairs={{0,128},{32,160},{64,192},{96,224},{128,0},{160,32},{192,64},{224,... | collective-permute-start | bytes 196616 | tf_op jit(solution)/shard_map/ppermute | solution.py:531
  18.3 9.7 %collective-permute-start.4 = (f32[128,128]{1,0:T(8,128)S(1)}, f32[128,128]{1,0:T(8,128)S(1)}, u32[]{:S(2)}, u32[]{:S(2)}) collective-permute-start(f32[128,128]{1,0:T(8,128)S(1)} %get-tuple-element.41), channel_id=1, source_target_pairs={{0,192},{32,224},{64,128},{96,160},{128,64},{160,96},{192,0},{224,... | collective-permute-start | bytes 196616 | tf_op jit(solution)/shard_map/ppermute | solution.py:531
  19.4 8.6 %copy-start.11 = (bf16[176,96]{1,0:T(8,128)(2,1)S(1)}, bf16[176,96]{1,0:T(8,128)(2,1)}, u32[]{:S(2)}) copy-start(bf16[176,96]{1,0:T(8,128)(2,1)} %constant.39.clone.rest_13_) | copy-start | bytes 101380
  19.4 8.6 %copy-start.12 = (bf16[176,96]{1,0:T(8,128)(2,1)S(1)}, bf16[176,96]{1,0:T(8,128)(2,1)}, u32[]{:S(2)}) copy-start(bf16[176,96]{1,0:T(8,128)(2,1)} %constant.38.clone.rest_12_) | copy-start | bytes 101380
  20.4 14.7 %collective-permute-start.10 = (f32[56,512]{1,0:T(8,128)S(1)}, f32[56,512]{1,0:T(8,128)S(1)}, u32[]{:S(2)}, u32[]{:S(2)}) collective-permute-start(f32[56,512]{1,0:T(8,128)S(1)} %get-tuple-element.56), channel_id=1, source_target_pairs={{0,255},{255,0},{64,191},{191,64},{128,127},{127,128},{192,63},{63... | collective-permute-start | bytes 344072 | tf_op jit(solution)/shard_map/ppermute | solution.py:551
  28.1 7.1 %copy-start.13 = (bf16[2,80,64]{2,1,0:T(8,128)(2,1)S(1)}, bf16[2,80,64]{2,1,0:T(8,128)(2,1)}, u32[]{:S(2)}) copy-start(bf16[2,80,64]{2,1,0:T(8,128)(2,1)} %constant.40.clone.table) | copy-start | bytes 61444
  31.5 7.6 %collective-permute-start.7 = (f32[128,128]{1,0:T(8,128)S(1)}, f32[128,128]{1,0:T(8,128)S(1)}, u32[]{:S(2)}, u32[]{:S(2)}) collective-permute-start(f32[128,128]{1,0:T(8,128)S(1)} %get-tuple-element.51), channel_id=1, source_target_pairs={{0,64},{32,96},{64,0},{96,32},{128,192},{160,224},{192,128},{224,1... | collective-permute-start | bytes 196616 | tf_op jit(solution)/shard_map/ppermute | solution.py:531
  32.9 7.9 %collective-permute-start.8 = (f32[128,128]{1,0:T(8,128)S(1)}, f32[128,128]{1,0:T(8,128)S(1)}, u32[]{:S(2)}, u32[]{:S(2)}) collective-permute-start(f32[128,128]{1,0:T(8,128)S(1)} %get-tuple-element.52), channel_id=1, source_target_pairs={{0,128},{32,160},{64,192},{96,224},{128,0},{160,32},{192,64},{224,... | collective-permute-start | bytes 196616 | tf_op jit(solution)/shard_map/ppermute | solution.py:531
  33.5 7.3 %collective-permute-start.9 = (f32[128,128]{1,0:T(8,128)S(1)}, f32[128,128]{1,0:T(8,128)S(1)}, u32[]{:S(2)}, u32[]{:S(2)}) collective-permute-start(f32[128,128]{1,0:T(8,128)S(1)} %get-tuple-element.53), channel_id=1, source_target_pairs={{0,192},{32,224},{64,128},{96,160},{128,64},{160,96},{192,0},{224,... | collective-permute-start | bytes 196616 | tf_op jit(solution)/shard_map/ppermute | solution.py:531
  37.2 7.3 %collective-permute-start.11 = (f32[128,128]{1,0:T(8,128)S(1)}, f32[128,128]{1,0:T(8,128)S(1)}, u32[]{:S(2)}, u32[]{:S(2)}) collective-permute-start(f32[128,128]{1,0:T(8,128)S(1)} %get-tuple-element.58), channel_id=1, source_target_pairs={{0,64},{32,96},{64,0},{96,32},{128,192},{160,224},{192,128},{224,1... | collective-permute-start | bytes 196616 | tf_op jit(solution)/shard_map/ppermute | solution.py:531
  37.6 6.8 %collective-permute-start.12 = (f32[128,128]{1,0:T(8,128)S(1)}, f32[128,128]{1,0:T(8,128)S(1)}, u32[]{:S(2)}, u32[]{:S(2)}) collective-permute-start(f32[128,128]{1,0:T(8,128)S(1)} %get-tuple-element.59), channel_id=1, source_target_pairs={{0,128},{32,160},{64,192},{96,224},{128,0},{160,32},{192,64},{224,... | collective-permute-start | bytes 196616 | tf_op jit(solution)/shard_map/ppermute | solution.py:531
  39.2 5.3 %collective-permute-start.13 = (f32[128,128]{1,0:T(8,128)S(1)}, f32[128,128]{1,0:T(8,128)S(1)}, u32[]{:S(2)}, u32[]{:S(2)}) collective-permute-start(f32[128,128]{1,0:T(8,128)S(1)} %get-tuple-element.60), channel_id=1, source_target_pairs={{0,192},{32,224},{64,128},{96,160},{128,64},{160,96},{192,0},{224,... | collective-permute-start | bytes 196616 | tf_op jit(solution)/shard_map/ppermute | solution.py:531
  40.8 7.8 %collective-permute-start.14 = (f32[4,64,128]{2,1,0:T(8,128)S(1)}, f32[4,64,128]{2,1,0:T(8,128)S(1)}, u32[]{:S(2)}, u32[]{:S(2)}) collective-permute-start(f32[4,64,128]{2,1,0:T(8,128)S(1)} %cut.1), channel_id=1, source_target_pairs={{0,32},{32,0},{64,96},{96,64},{128,160},{160,128},{192,224},{224,1... | collective-permute-start | bytes 393224 | tf_op jit(solution)/shard_map/ppermute | solution.py:538
  44.4 5.2 %copy-start.8 = (bf16[256,384]{1,0:T(8,128)(2,1)S(1)}, bf16[256,384]{1,0:T(8,128)(2,1)}, u32[]{:S(2)}) copy-start(bf16[256,384]{1,0:T(8,128)(2,1)} %constant.44.clone.rest_13_) | copy-start | bytes 589828
  44.5 5.2 %copy-start.10 = (bf16[128,384]{1,0:T(8,128)(2,1)S(1)}, bf16[128,384]{1,0:T(8,128)(2,1)}, u32[]{:S(2)}) copy-start(bf16[128,384]{1,0:T(8,128)(2,1)} %constant.42.clone.rest_11_) | copy-start | bytes 294916
  44.5 5.1 %copy-start.15 = (bf16[128,128]{1,0:T(8,128)(2,1)S(1)}, bf16[128,128]{1,0:T(8,128)(2,1)}, u32[]{:S(2)}) copy-start(bf16[128,128]{1,0:T(8,128)(2,1)} %constant.41.clone.rest_10_) | copy-start | bytes 98308
  44.5 5.1 %copy-start.18 = (f32[8,128]{1,0:T(8,128)S(1)}, f32[8,128]{1,0:T(8,128)}, u32[]{:S(2)}) copy-start(f32[8,128]{1,0:T(8,128)} %constant.43.clone.rest_12_) | copy-start | bytes 12292
  44.5 5.1 %collective-permute-start.15 = (f32[4,64,128]{2,1,0:T(8,128)S(1)}, f32[4,64,128]{2,1,0:T(8,128)S(1)}, u32[]{:S(2)}, u32[]{:S(2)}) collective-permute-start(f32[4,64,128]{2,1,0:T(8,128)S(1)} %cut_edge.1), channel_id=1, source_target_pairs={{0,32},{32,0},{64,96},{96,64},{128,160},{160,128},{192,224},{224,1... | collective-permute-start | bytes 393224 | tf_op jit(solution)/shard_map/ppermute | solution.py:538

commit v5 on v4

--- a/solution.py
+++ b/solution.py
@@ -8,6 +8,7 @@
 from jax.sharding import PartitionSpec as P
 
 NZ = 512
+HALF = 256
 PTS = 81
 ELEMS = 8
 ROWS = 4
@@ -79,15 +80,12 @@
 
 
 def span_tables():
-    planes = np.arange(NZ)[None, :]
-    slots = np.arange(NZ)[:, None]
-    waves = np.where(slots == 1, NZ // 2, slots // 2)
+    planes = np.arange(HALF)[None, :]
+    waves = np.arange(HALF + 16)[:, None]
     angles = (planes * waves % NZ) * (2.0 * np.pi / NZ)
-    sine = (slots % 2 == 1) & (slots > 1)
-    value = np.where(sine, np.sin(angles), np.cos(angles))
-    rate = np.where(slots == 1, 0, waves) * SPAN_RATE
-    slope = rate * np.where(sine, np.cos(angles), -np.sin(angles))
-    return value, slope
+    cosines, sines = np.cos(angles), np.sin(angles)[:HALF]
+    sines[0] = 1.0 - 2.0 * (np.arange(HALF) % 2)
+    return cosines, sines
 
 
 def point_matrices():
@@ -194,6 +192,50 @@
     return lax.dot_general(a, b, (dims, ((), ())), preferred_element_type=F32)
 
 
+def pick_slots(modes):
+    even, odd = modes[pl.ds(0, HALF, stride=2), :], modes[pl.ds(1, HALF, stride=2), :]
+    return even.T, odd.T
+
+
+def to_planes(x, tables):
+    ch, cl, sh, sl = tables
+    high, low = split(x)
+    ch, cl = ch[0:HALF], cl[0:HALF]
+    sh, sl = sh[...], sl[...]
+    even = dot(high[:, :HALF], ch) + dot(low[:, :HALF], ch) + dot(high[:, :HALF], cl)
+    odd = dot(high[:, HALF:], sh) + dot(low[:, HALF:], sh) + dot(high[:, HALF:], sl)
+    lane = lax.broadcasted_iota(jnp.int32, even.shape, 1)
+    sign = jnp.where((lane & 1) == 0, 1.0, -1.0)
+    lone = x[:, HALF : HALF + 1]
+    middle = jnp.sum(x[:, :HALF] * sign, axis=1, keepdims=True) + lone
+    mirror = jnp.where(lane == 0, middle, even - odd + (lone + lone) * sign)
+    return jnp.concatenate([even + odd, mirror], axis=1)
+
+
+def slope_slots(x):
+    lane = lax.broadcasted_iota(jnp.int32, (x.shape[0], HALF), 1)
+    rate = lane.astype(F32) * SPAN_RATE
+    return jnp.concatenate([x[:, HALF:] * rate, -x[:, :HALF] * rate], axis=1)
+
+
+def to_slots(term, tables, spec):
+    ch, cl, sh, sl = tables
+    first, mirror = term[:, :HALF], term[:, HALF:]
+    lane = lax.broadcasted_iota(jnp.int32, first.shape, 1)
+    eh, el = split(jnp.where(lane == 0, first, first + mirror))
+    oh, ol = split(first - mirror)
+    along = ((1,), (1,))
+    even = dot(ch[...], eh, along) + dot(ch[...], el, along) + dot(cl[...], eh, along)
+    odd = dot(sh[...], oh, along) + dot(sh[...], ol, along) + dot(sl[...], oh, along)
+    row = lax.broadcasted_iota(jnp.int32, even.shape, 0)
+    middle = mirror[:, 0:128].T[0:1, :]
+    even = even + jnp.where((row & 1) == 0, 1.0, -1.0) * middle
+    row = row[:HALF]
+    lone = even[HALF : HALF + 1] * (1.0 / NZ)
+    spec[pl.ds(0, HALF, stride=2), :] = even[:HALF] * jnp.where(row == 0, 1.0 / NZ, 2.0 / NZ)
+    spec[pl.ds(1, HALF, stride=2), :] = jnp.where(row == 0, lone, odd * (2.0 / NZ))
+
+
 def list_pairs(pair, count, own, other, other_edge):
     for e in range(ELEMS):
         count[e] = 0
@@ -309,8 +351,11 @@
     terms, table, send, high, low, modes, points = rest[4:]
     me, part = lax.axis_index("span"), lax.axis_index("dom")
     for j in range(4):
-        modes[chip_modes(j), :] = blocks[j][...]
-    points[...] = modes[...].T
+        for t in range(2):
+            modes[t, chip_modes(j), :] = blocks[j][:, t * 128 : t * 128 + 128]
+    for t in range(2):
+        rows = slice(t * 128, t * 128 + 128)
+        points[rows, 0:HALF], points[rows, HALF:] = pick_slots(modes.at[t])
     vh, vl = split(points[...])
     high[...] = vh
     low[...] = vl
@@ -327,11 +372,11 @@
     send[48:56, 0:128] = terms[...]
 
 
-def element_kernel(bound, high, low, columns, turn, th, tl, dh, dl, gh, gl, mine, u, q, g):
+def element_kernel(bound, high, low, columns, turn, tables, gh, gl, mine, u, q, g):
     me, part = lax.axis_index("span"), lax.axis_index("dom")
-    vh, vl = dot(turn[...], high[...]).astype(BF), dot(turn[...], low[...]).astype(BF)
-    value = dot(vh, th[...]) + dot(vl, th[...]) + dot(vh, tl[...])
-    slope = dot(vh, dh[...]) + dot(vl, dh[...]) + dot(vh, dl[...])
+    slots = dot(turn[...], high[...]) + dot(turn[...], low[...])
+    both = to_planes(jnp.concatenate([slots, slope_slots(slots)], axis=0), tables)
+    value, slope = both[:288], both[288:]
     uh, ul = split(value)
     third = value[192:280]
     for c in range(3):
@@ -350,35 +395,25 @@
             mine[f * 8 + 6 - i : f * 8 + 7 - i, :] = ref[at, pl.ds(base + i, 1), :]
 
 
-def to_modes(term, th, tl):
-    wh, wl = split(term)
-    along = ((1,), (1,))
-    total = dot(th[...], wh, along) + dot(th[...], wl, along) + dot(tl[...], wh, along)
-    slot = lax.broadcasted_iota(jnp.int32, total.shape, 0)
-    return total * jnp.where(slot < 2, 1.0 / NZ, 2.0 / NZ)
-
-
-def inside_kernel(u, q, g, th, tl, *rest):
+def inside_kernel(u, q, g, tables, *rest):
     outs = rest[:4]
     term, spec = rest[4:]
     for c, count in ((0, 53), (1, 53), (2, 22)):
         value = u[0, 0:56] * g[c, 0:56] + u[1, 0:56] * g[3 + c, 0:56] + q[c, 0:56]
         term[53 * c : 53 * c + count, :] = value[:count]
-    spec[...] = to_modes(term[...], th, tl)
+    to_slots(term[...], tables, spec)
     for j in range(4):
         outs[j][...] = spec[chip_modes(j), :]
 
 
-def edge_term_kernel(bound, pair, *rest):
+def edge_term_kernel(bound, pair, tables, *rest):
     blocks = rest[:4]
-    th, tl, u, q, g, term, modes, count, own, other, other_edge = rest[4:]
+    u, q, g, term, modes, count, own, other, other_edge = rest[4:]
     me, part = lax.axis_index("span"), lax.axis_index("dom")
     list_pairs(pair, count, own, other, other_edge)
     for j in range(4):
         modes[chip_modes(j), :] = blocks[j][...]
-    eh, el = split(modes[...].T)
-    planes = dot(eh, th[...]) + dot(el, th[...]) + dot(eh, tl[...])
-    ph, pw = split(planes)
+    ph, pw = split(to_planes(jnp.concatenate(pick_slots(modes), axis=1), tables))
     e = bound[0, row_of(me, part)]
     lane = lax.broadcasted_iota(jnp.int32, (32, 128), 1)
     point = lax.broadcasted_iota(jnp.int32, (32, 128), 0)
@@ -411,27 +446,27 @@
 
 def whole_kernel(bound, pair, *rest):
     blocks = rest[:4]
-    high, low, columns, turn, th, tl, dh, dl, gh, gl = rest[4:14]
+    high, low, columns, turn = rest[4:8]
+    tables, (gh, gl) = rest[8:12], rest[12:14]
     outs, term, mine = rest[14:18], rest[18], rest[19]
     u, q, g, inside_term, spec, modes = rest[20:26]
     pairs = rest[26:]
-    element_kernel(bound, high, low, columns, turn, th, tl, dh, dl, gh, gl, mine, u, q, g)
-    inside_kernel(u, q, g, th, tl, *outs, inside_term, spec)
-    edge_term_kernel(bound, pair, *blocks, th, tl, u, q, g, term, modes, *pairs)
-
-
-def side_kernel(bound, term, mine, other, table, th, tl, dh, dl, *rest):
-    outs = rest[:4]
-    work, spec, rows, square, turned = rest[4:]
+    element_kernel(bound, high, low, columns, turn, tables, gh, gl, mine, u, q, g)
+    inside_kernel(u, q, g, tables, *outs, inside_term, spec)
+    edge_term_kernel(bound, pair, tables, *blocks, u, q, g, term, modes, *pairs)
+
+
+def side_kernel(bound, term, mine, other, table, *rest):
+    tables, outs = rest[:4], rest[4:8]
+    work, spec, rows, square, turned = rest[8:]
     me, part = lax.axis_index("span"), lax.axis_index("dom")
     work[...] = term[...]
     rows[0:56] = other[...]
     rows[56:64] = jnp.zeros((8, NZ), F32)
     rh, rl = split(rows[...])
-    xh, xl = split(dot(table[0], rh) + dot(table[0], rl) + dot(table[1], rh))
-    value = dot(xh, th[...]) + dot(xl, th[...]) + dot(xh, tl[...])
-    xh, xl = xh[:32], xl[:32]
-    slope = dot(xh, dh[...]) + dot(xl, dh[...]) + dot(xh, dl[...])
+    near = dot(table[0], rh) + dot(table[0], rl) + dot(table[1], rh)
+    value = to_planes(jnp.concatenate([near[0:72], slope_slots(near[0:24])], axis=0), tables)
+    slope = value[72:96]
     square[...] = jnp.zeros((128, 128), F32)
     square[0:8, :] = other[48:56, 0:128]
     turned[...] = square[...].T
@@ -448,7 +483,7 @@
         mean = (u0 * gx + u1 * gy) * 0.25 + q * 0.5
         for i in range(7):
             work[pl.ds(base + 28 * c + 6 - i, 1), :] = mean[i : i + 1, :]
-    spec[...] = to_modes(work[...], th, tl)
+    to_slots(work[...], tables, spec)
     for j in range(4):
         outs[j][...] = spec[chip_modes(j), :]
 
@@ -552,9 +587,8 @@
 
 
 def on_device(velocity_modes, metric, pair_table, bound_table):
-    value, slope = span_tables()
-    th, tl = halves(value)
-    dh, dl = halves(slope)
+    cosines, sines = span_tables()
+    tables = [*halves(cosines), *halves(sines)]
     gh, gl = halves(gradient_table())
     edge_table, pick = edge_tables()
     take, give, where, back = settle_tables()
@@ -604,7 +638,7 @@
         [bound_table],
         [*blocks, terms, rim_table()],
         [(56, NZ), half, half],
-        [pltpu.VMEM((NZ, 256), F32), pltpu.VMEM((256, NZ), F32)],
+        [pltpu.VMEM((2, NZ, 128), F32), pltpu.VMEM((256, NZ), F32)],
     )
     other = side_swap(send, lax.axis_size("dom"))
     modes_scratch = pltpu.VMEM((NZ, 128), F32)
@@ -613,7 +647,7 @@
         whole_kernel,
         "whole",
         [bound_table, pair_table],
-        [*edge_blocks, high, low, columns, turn, th, tl, dh, dl, gh, gl],
+        [*edge_blocks, high, low, columns, turn, *tables, gh, gl],
         [edge_chip] * 4 + [(128, NZ), (88, NZ)],
         [
             pltpu.VMEM((3, 88, NZ), F32),
@@ -630,7 +664,7 @@
         side_kernel,
         "side",
         [bound_table],
-        [term, mine, other, np.stack(halves(far_table())), th, tl, dh, dl],
+        [term, mine, other, np.stack(halves(far_table())), *tables],
         [edge_chip] * 4,
         [
             term_scratch,

time: 52.1 us -> 51.2 us (0.983)
  Pallas kernels: 13 us -> 12.2 us
    pallas_call x9, Pallas kernels: 13 us -> 12.2 us  [call(): pl.pallas_call(kernel, out_shape=shapes, in_specs=[spec_of(pltpu.SMEM)] *...]
  transfers between devices with their start and end apart: 16 -> 16, of which waited for: 4 -> 5; matrix products, arithmetic and copies ran while one was open for 0% -> 0% of each run, Pallas kernels for 18% -> 17%
where the time goes in v5:
time: 51.2 us; the launch traced here: 51.1 us
  starting transfers between devices  32.6 us (64%)
  Pallas kernels  12.2 us (24%)
  waiting for transfers between devices  4.95 us (10%)
  local copies, waits for them, and re-layouts  1.16 us (2%)
    ppermute x12, starting transfers between devices, between_chips(): lax.ppermute(blocks[j], 'span', [(s, s ^ 2 * j) for s in range(SPAN)])  14.5 us
    pallas_call x9, Pallas kernels, call(): pl.pallas_call(kernel, out_shape=shapes, in_specs=[spec_of(pltpu.SMEM)] *...  12.2 us
    ppermute x3, starting transfers between devices, between_cores(): return lax.ppermute(block, 'span', [(s, s ^ 1) for s in range(SPAN)])  10.6 us
    ppermute x1, starting transfers between devices, side_swap(): return lax.ppermute(block, ('span', 'dom'), perm)  7.53 us
    ppermute x12, waiting for transfers between devices, between_chips(): lax.ppermute(blocks[j], 'span', [(s, s ^ 2 * j) for s in range(SPAN)])  3.77 us
    ppermute x3, waiting for transfers between devices, between_cores(): return lax.ppermute(block, 'span', [(s, s ^ 1) for s in range(SPAN)])  1.17 us
    unnamed x38, local copies, waits for them, and re-layouts  1.16 us
  transfers between devices with their start and end apart: 16, of which 5 were waited for; matrix products, arithmetic and copies ran while one was open for 0% of the time, Pallas kernels for 17%

profile of v5, /device:TPU:1, one launch (start us, length us, event | category | flops | bytes accessed | tf_op | source)
XLA Modules:
  0.0 51.1 jit_solution(2846995570586037047)
XLA Ops:
  0.0 3.2 %collective-permute-start = (f32[3,64,648]{2,1,0:T(8,128)}, f32[3,64,648]{2,1,0:T(8,128)S(1)}, u32[]{:S(2)}, u32[]{:S(2)}) collective-permute-start(f32[3,64,648]{2,1,0:T(8,128)} %here.5), channel_id=1, source_target_pairs={{0,32},{32,0},{64,96},{96,64},{128,160},{160,128},{192,224},{224,1... | collective-permute-start | bytes 1493000 | tf_op jit(solution)/shard_map/ppermute | solution.py:573
  3.2 1.1 %copy-done = f32[3,64,648]{2,1,0:T(8,128)S(1)} copy-done((f32[3,64,648]{2,1,0:T(8,128)S(1)}, f32[3,64,648]{2,1,0:T(8,128)}, u32[]{:S(2)}) %copy-start) | copy-done | bytes 497688
  4.3 0.6 %ready.1 = f32[8,128]{1,0:T(8,128)S(1)} custom-call(s32[2,8]{1,0:T(2,128)S(1)} %bitcast.2, f32[3,64,648]{2,1,0:T(8,128)S(1)} %copy-done), custom_call_target="tpu_custom_call" | custom-call | flops 200000000 | bytes 200000000 | tf_op jit(solution)/shard_map/ready/pallas_call | solution.py:547
  4.9 0.0 copy-start.2
  4.9 0.0 copy-start.7
  4.9 0.2 collective-permute-done.there
  5.1 1.2 %pack.1 = (f32[8,128,256]{2,1,0:T(8,128)S(1)}, f32[128,256]{1,0:T(8,128)S(1)}, f32[128,256]{1,0:T(8,128)S(1)}, f32[128,256]{1,0:T(8,128)S(1)}, f32[128,256]{1,0:T(8,128)S(1)}) custom-call(s32[2,8]{1,0:T(2,128)S(1)} %bitcast.3, f32[3,64,648]{2,1,0:T(8,128)S(1)} %copy-done, f32[3,64,648]{2,1,0:T(8,128)S(1)} %collective-permute-done.there, f32[8,128]{1,0:T(8,128)S(1)} %ready.1), custom_call_target="tpu_custom_call" | custom-call | flops 200000000 | bytes 200000000 | tf_op jit(solution)/shard_map/pack/pallas_call | solution.py:547
  6.3 2.7 %collective-permute-start.1 = (f32[128,256]{1,0:T(8,128)S(1)}, f32[128,256]{1,0:T(8,128)S(1)}, u32[]{:S(2)}, u32[]{:S(2)}) collective-permute-start(f32[128,256]{1,0:T(8,128)S(1)} %get-tuple-element.35), channel_id=1, source_target_pairs={{0,192},{32,224},{64,128},{96,160},{128,64},{160,96},{192,0},{224,... | collective-permute-start | bytes 393224 | tf_op jit(solution)/shard_map/ppermute | solution.py:566
  9.0 0.0 collective-permute-start.5
  9.0 0.9 %collective-permute-start.6 = (f32[128,256]{1,0:T(8,128)S(1)}, f32[128,256]{1,0:T(8,128)S(1)}, u32[]{:S(2)}, u32[]{:S(2)}) collective-permute-start(f32[128,256]{1,0:T(8,128)S(1)} %get-tuple-element.44), channel_id=1, source_target_pairs={{0,128},{32,160},{64,192},{96,224},{128,0},{160,32},{192,64},{224,... | collective-permute-start | bytes 393224 | tf_op jit(solution)/shard_map/ppermute | solution.py:566
  9.9 2.9 %collective-permute-done.1.rest_3_ = f32[128,256]{1,0:T(8,128)S(1)} collective-permute-done((f32[128,256]{1,0:T(8,128)S(1)}, f32[128,256]{1,0:T(8,128)S(1)}, u32[]{:S(2)}, u32[]{:S(2)}) %collective-permute-start.1) | collective-permute-done | bytes 131104 | tf_op jit(solution)/shard_map/ppermute | solution.py:566
  12.8 0.0 copy-start.9
  12.8 2.5 %edges.1 = (f32[96,128]{1,0:T(8,128)S(1)}, f32[8,128]{1,0:T(8,128)S(1)}, f32[128,128]{1,0:T(8,128)S(1)}, f32[128,128]{1,0:T(8,128)S(1)}, f32[128,128]{1,0:T(8,128)S(1)}, /*index=5*/f32[128,128]{1,0:T(8,128)S(1)}) custom-call(s32[2,8]{1,0:T(2,128)S(1)} %bitcast.4, s32[4,10]{1,0:T(4,128)S(1)} %bitcast.9, f32[8,128,256]{2,1,0:T(8,128)S(1)} %get-tuple-element.37.done, ...), custom_call_target="tpu_custom_call" | custom-call | flops 200000000 | bytes 200000000 | tf_op jit(solution)/shard_map/edges/pallas_call | solution.py:547
  15.3 0.1 collective-permute-start.2
  15.4 2.9 %collective-permute-start.3 = (f32[128,128]{1,0:T(8,128)S(1)}, f32[128,128]{1,0:T(8,128)S(1)}, u32[]{:S(2)}, u32[]{:S(2)}) collective-permute-start(f32[128,128]{1,0:T(8,128)S(1)} %get-tuple-element.40), channel_id=1, source_target_pairs={{0,128},{32,160},{64,192},{96,224},{128,0},{160,32},{192,64},{224,... | collective-permute-start | bytes 196616 | tf_op jit(solution)/shard_map/ppermute | solution.py:566
  18.3 0.7 %collective-permute-start.4 = (f32[128,128]{1,0:T(8,128)S(1)}, f32[128,128]{1,0:T(8,128)S(1)}, u32[]{:S(2)}, u32[]{:S(2)}) collective-permute-start(f32[128,128]{1,0:T(8,128)S(1)} %get-tuple-element.41), channel_id=1, source_target_pairs={{0,192},{32,224},{64,128},{96,160},{128,64},{160,96},{192,0},{224,... | collective-permute-start | bytes 196616 | tf_op jit(solution)/shard_map/ppermute | solution.py:566
  19.0 0.0 collective-permute-done.5.rest_1_
  19.0 0.5 collective-permute-done.6.rest_2_
  19.5 0.0 copy-start.6
  19.5 0.0 copy-start.11
  19.5 0.0 copy-start.12
  19.5 1.0 %rim.1 = (f32[56,512]{1,0:T(8,128)S(1)}, bf16[256,512]{1,0:T(8,128)(2,1)S(1)}, bf16[256,512]{1,0:T(8,128)(2,1)S(1)}) custom-call(s32[2,8]{1,0:T(2,128)S(1)} %bitcast.5, f32[128,256]{1,0:T(8,128)S(1)} %get-tuple-element.42.rest_0_, f32[128,256]{1,0:T(8,128)S(1)} %collective-permute-done.5.rest_1_, f32[128,256]{1,0:T(8,128)S(1)} %collective-permute-done.6.rest_2_, ...), custom_call_target="tpu_custom_call" | custom-call | flops 1000 | bytes 1000 | tf_op jit(solution)/shard_map/rim/pallas_call | solution.py:547
  20.5 7.5 %collective-permute-start.10 = (f32[56,512]{1,0:T(8,128)S(1)}, f32[56,512]{1,0:T(8,128)S(1)}, u32[]{:S(2)}, u32[]{:S(2)}) collective-permute-start(f32[56,512]{1,0:T(8,128)S(1)} %get-tuple-element.56), channel_id=1, source_target_pairs={{0,255},{255,0},{64,191},{191,64},{128,127},{127,128},{192,63},{63... | collective-permute-start | bytes 344072 | tf_op jit(solution)/shard_map/ppermute | solution.py:586
  28.0 0.0 collective-permute-done.2.rest_1_
  28.0 0.0 collective-permute-done.3.rest_2_
  28.0 0.0 collective-permute-done.4.rest_3_
  28.1 0.0 copy-start.13
  28.1 3.1 %whole.1 = (f32[128,128]{1,0:T(8,128)S(1)}, f32[128,128]{1,0:T(8,128)S(1)}, f32[128,128]{1,0:T(8,128)S(1)}, f32[128,128]{1,0:T(8,128)S(1)}, f32[128,512]{1,0:T(8,128)S(1)}, /*index=5*/f32[88,512]{1,0:T(8,128)S(1)}) custom-call(s32[2,8]{1,0:T(2,128)S(1)} %bitcast.6, s32[4,10]{1,0:T(4,128)S(1)} %bitcast.10, f32[128,128]{1,0:T(8,128)S(1)} %get-tuple-element.38.rest_0_, ...), custom_call_target="tpu_custom_call" | custom-call | flops 1000 | bytes 1000 | tf_op jit(solution)/shard_map/whole/pallas_call | solution.py:547
  31.2 1.3 %collective-permute-start.7 = (f32[128,128]{1,0:T(8,128)S(1)}, f32[128,128]{1,0:T(8,128)S(1)}, u32[]{:S(2)}, u32[]{:S(2)}) collective-permute-start(f32[128,128]{1,0:T(8,128)S(1)} %get-tuple-element.51), channel_id=1, source_target_pairs={{0,64},{32,96},{64,0},{96,32},{128,192},{160,224},{192,128},{224,1... | collective-permute-start | bytes 196616 | tf_op jit(solution)/shard_map/ppermute | solution.py:566
  32.5 0.7 %collective-permute-start.8 = (f32[128,128]{1,0:T(8,128)S(1)}, f32[128,128]{1,0:T(8,128)S(1)}, u32[]{:S(2)}, u32[]{:S(2)}) collective-permute-start(f32[128,128]{1,0:T(8,128)S(1)} %get-tuple-element.52), channel_id=1, source_target_pairs={{0,128},{32,160},{64,192},{96,224},{128,0},{160,32},{192,64},{224,... | collective-permute-start | bytes 196616 | tf_op jit(solution)/shard_map/ppermute | solution.py:566
  33.2 1.6 %collective-permute-start.9 = (f32[128,128]{1,0:T(8,128)S(1)}, f32[128,128]{1,0:T(8,128)S(1)}, u32[]{:S(2)}, u32[]{:S(2)}) collective-permute-start(f32[128,128]{1,0:T(8,128)S(1)} %get-tuple-element.53), channel_id=1, source_target_pairs={{0,192},{32,224},{64,128},{96,160},{128,64},{160,96},{192,0},{224,... | collective-permute-start | bytes 196616 | tf_op jit(solution)/shard_map/ppermute | solution.py:566
  34.8 0.0 collective-permute-done.10.other
  34.8 1.5 %side.1 = (f32[128,128]{1,0:T(8,128)S(1)}, f32[128,128]{1,0:T(8,128)S(1)}, f32[128,128]{1,0:T(8,128)S(1)}, f32[128,128]{1,0:T(8,128)S(1)}) custom-call(s32[2,8]{1,0:T(2,128)S(1)} %bitcast.7, f32[128,512]{1,0:T(8,128)S(1)} %get-tuple-element.54.term, f32[88,512]{1,0:T(8,128)S(1)} %get-tuple-element.55.mine, f32[56,512]{1,0:T(8,128)S(1)} %collective-permute-done.10.other, ...), custom_call_target="tpu_custom_call" | custom-call | flops 1000 | bytes 1000 | tf_op jit(solution)/shard_map/side/pallas_call | solution.py:547
  36.3 0.4 collective-permute-start.11
  36.7 1.6 %collective-permute-start.12 = (f32[128,128]{1,0:T(8,128)S(1)}, f32[128,128]{1,0:T(8,128)S(1)}, u32[]{:S(2)}, u32[]{:S(2)}) collective-permute-start(f32[128,128]{1,0:T(8,128)S(1)} %get-tuple-element.59), channel_id=1, source_target_pairs={{0,128},{32,160},{64,192},{96,224},{128,0},{160,32},{192,64},{224,... | collective-permute-start | bytes 196616 | tf_op jit(solution)/shard_map/ppermute | solution.py:566
  38.3 0.0 collective-permute-done.7.rest_1_
  38.3 1.6 %collective-permute-start.13 = (f32[128,128]{1,0:T(8,128)S(1)}, f32[128,128]{1,0:T(8,128)S(1)}, u32[]{:S(2)}, u32[]{:S(2)}) collective-permute-start(f32[128,128]{1,0:T(8,128)S(1)} %get-tuple-element.60), channel_id=1, source_target_pairs={{0,192},{32,224},{64,128},{96,160},{128,64},{160,96},{192,0},{224,... | collective-permute-start | bytes 196616 | tf_op jit(solution)/shard_map/ppermute | solution.py:566
  40.0 0.0 collective-permute-done.8.rest_2_
  40.0 0.0 collective-permute-done.9.rest_3_
  40.0 3.5 %collective-permute-start.14 = (f32[4,64,128]{2,1,0:T(8,128)S(1)}, f32[4,64,128]{2,1,0:T(8,128)S(1)}, u32[]{:S(2)}, u32[]{:S(2)}) collective-permute-start(f32[4,64,128]{2,1,0:T(8,128)S(1)} %cut.1), channel_id=1, source_target_pairs={{0,32},{32,0},{64,96},{96,64},{128,160},{160,128},{192,224},{224,1... | collective-permute-start | bytes 393224 | tf_op jit(solution)/shard_map/ppermute | solution.py:573
  43.5 0.0 collective-permute-done.11.rest_1_.rest_5_
  43.5 0.4 collective-permute-done.12.rest_2_.rest_6_
  43.9 0.0 collective-permute-done.13.rest_3_.rest_7_
  43.9 0.0 copy-start.18
  43.9 3.8 %collective-permute-start.15 = (f32[4,64,128]{2,1,0:T(8,128)S(1)}, f32[4,64,128]{2,1,0:T(8,128)S(1)}, u32[]{:S(2)}, u32[]{:S(2)}) collective-permute-start(f32[4,64,128]{2,1,0:T(8,128)S(1)} %cut_edge.1), channel_id=1, source_target_pairs={{0,32},{32,0},{64,96},{96,64},{128,160},{160,128},{192,224},{224,1... | collective-permute-start | bytes 393224 | tf_op jit(solution)/shard_map/ppermute | solution.py:573
  47.8 0.0 collective-permute-done.14.rest_8_
  47.8 1.0 %collective-permute-done.15.rest_9_ = f32[4,64,128]{2,1,0:T(8,128)S(1)} collective-permute-done((f32[4,64,128]{2,1,0:T(8,128)S(1)}, f32[4,64,128]{2,1,0:T(8,128)S(1)}, u32[]{:S(2)}, u32[]{:S(2)}) %collective-permute-start.15) | collective-permute-done | bytes 131104 | tf_op jit(solution)/shard_map/ppermute | solution.py:573
  48.8 2.4 %settle.1 = f32[3,64,648]{2,1,0:T(8,128)} custom-call(s32[2,8]{1,0:T(2,128)S(1)} %bitcast.8, s32[4,10]{1,0:T(4,128)S(1)} %bitcast.11, f32[128,128]{1,0:T(8,128)S(1)} %get-tuple-element.50.rest_0_, f32[128,128]{1,0:T(8,128)S(1)} %collective-permute-done.7.rest_1_, f32[128,128]{1,0:T(8,128)S(1)} %collective-permute-done.8.rest_2_, ...), custom_call_target="tpu_custom_call" | custom-call | flops 1000 | bytes 1000 | tf_op jit(solution)/shard_map/settle/pallas_call | solution.py:547
  (31 shorter events, 0.1 us)
Async XLA Ops:
  0.0 3.2 %copy-start.14 = (s32[8,2]{0,1:T(2,128)S(1)}, s32[8,2]{0,1:T(2,128)}, u32[]{:S(2)}) copy-start(s32[8,2]{0,1:T(2,128)} %param.22) | copy-start | bytes 196
  0.0 5.1 %collective-permute-start = (f32[3,64,648]{2,1,0:T(8,128)}, f32[3,64,648]{2,1,0:T(8,128)S(1)}, u32[]{:S(2)}, u32[]{:S(2)}) collective-permute-start(f32[3,64,648]{2,1,0:T(8,128)} %here.5), channel_id=1, source_target_pairs={{0,32},{32,0},{64,96},{96,64},{128,160},{160,128},{192,224},{224,1... | collective-permute-start | bytes 1493000 | tf_op jit(solution)/shard_map/ppermute | solution.py:573
  3.2 1.1 %copy-start = (f32[3,64,648]{2,1,0:T(8,128)S(1)}, f32[3,64,648]{2,1,0:T(8,128)}, u32[]{:S(2)}) copy-start(f32[3,64,648]{2,1,0:T(8,128)} %here.5) | copy-start | bytes 1492996
  4.3 8.5 %copy-start.1 = (bf16[4,256,512]{2,1,0:T(8,128)(2,1)S(1)}, bf16[4,256,512]{2,1,0:T(8,128)(2,1)}, u32[]{:S(2)}) copy-start(bf16[4,256,512]{2,1,0:T(8,128)(2,1)} %constant.31.clone.table) | copy-start | bytes 3145732
  4.9 7.9 %copy-start.2 = (bf16[288,256]{1,0:T(8,128)(2,1)S(1)}, bf16[288,256]{1,0:T(8,128)(2,1)}, u32[]{:S(2)}) copy-start(bf16[288,256]{1,0:T(8,128)(2,1)} %constant.32.clone.turn.rest_7_) | copy-start | bytes 442372
  4.9 7.9 %copy-start.7 = (bf16[256,512]{1,0:T(8,128)(2,1)S(1)}, bf16[256,512]{1,0:T(8,128)(2,1)}, u32[]{:S(2)}) copy-start(bf16[256,512]{1,0:T(8,128)(2,1)} %constant.30.clone.pick) | copy-start | bytes 786436
  5.1 7.7 %copy-start.17 = (f32[4,648]{1,0:T(4,128)S(1)}, f32[4,648]{1,0:T(4,128)}, u32[]{:S(2)}) copy-start(f32[4,648]{1,0:T(4,128)} %metric.1) | copy-start | bytes 31108
  6.3 6.5 %collective-permute-start.1 = (f32[128,256]{1,0:T(8,128)S(1)}, f32[128,256]{1,0:T(8,128)S(1)}, u32[]{:S(2)}, u32[]{:S(2)}) collective-permute-start(f32[128,256]{1,0:T(8,128)S(1)} %get-tuple-element.35), channel_id=1, source_target_pairs={{0,192},{32,224},{64,128},{96,160},{128,64},{160,96},{192,0},{224,... | collective-permute-start | bytes 393224 | tf_op jit(solution)/shard_map/ppermute | solution.py:566
  9.0 10.0 %collective-permute-start.5 = (f32[128,256]{1,0:T(8,128)S(1)}, f32[128,256]{1,0:T(8,128)S(1)}, u32[]{:S(2)}, u32[]{:S(2)}) collective-permute-start(f32[128,256]{1,0:T(8,128)S(1)} %get-tuple-element.43), channel_id=1, source_target_pairs={{0,64},{32,96},{64,0},{96,32},{128,192},{160,224},{192,128},{224,1... | collective-permute-start | bytes 393224 | tf_op jit(solution)/shard_map/ppermute | solution.py:566
  9.0 3.8 %copy-start.16 = (s32[10,4]{0,1:T(4,128)S(1)}, s32[10,4]{0,1:T(4,128)}, u32[]{:S(2)}) copy-start(s32[10,4]{0,1:T(4,128)} %param.21) | copy-start | bytes 484
  9.0 10.5 %collective-permute-start.6 = (f32[128,256]{1,0:T(8,128)S(1)}, f32[128,256]{1,0:T(8,128)S(1)}, u32[]{:S(2)}, u32[]{:S(2)}) collective-permute-start(f32[128,256]{1,0:T(8,128)S(1)} %get-tuple-element.44), channel_id=1, source_target_pairs={{0,128},{32,160},{64,192},{96,224},{128,0},{160,32},{192,64},{224,... | collective-permute-start | bytes 393224 | tf_op jit(solution)/shard_map/ppermute | solution.py:566
  12.8 6.7 %copy-start.9 = (bf16[4,64,256]{2,1,0:T(8,128)(2,1)S(1)}, bf16[4,64,256]{2,1,0:T(8,128)(2,1)}, u32[]{:S(2)}) copy-start(bf16[4,64,256]{2,1,0:T(8,128)(2,1)} %constant.33.clone.rest_5_) | copy-start | bytes 393220
  15.3 12.7 %collective-permute-start.2 = (f32[128,128]{1,0:T(8,128)S(1)}, f32[128,128]{1,0:T(8,128)S(1)}, u32[]{:S(2)}, u32[]{:S(2)}) collective-permute-start(f32[128,128]{1,0:T(8,128)S(1)} %get-tuple-element.39), channel_id=1, source_target_pairs={{0,64},{32,96},{64,0},{96,32},{128,192},{160,224},{192,128},{224,1... | collective-permute-start | bytes 196616 | tf_op jit(solution)/shard_map/ppermute | solution.py:566
  15.4 12.6 %collective-permute-start.3 = (f32[128,128]{1,0:T(8,128)S(1)}, f32[128,128]{1,0:T(8,128)S(1)}, u32[]{:S(2)}, u32[]{:S(2)}) collective-permute-start(f32[128,128]{1,0:T(8,128)S(1)} %get-tuple-element.40), channel_id=1, source_target_pairs={{0,128},{32,160},{64,192},{96,224},{128,0},{160,32},{192,64},{224,... | collective-permute-start | bytes 196616 | tf_op jit(solution)/shard_map/ppermute | solution.py:566
  18.3 9.7 %collective-permute-start.4 = (f32[128,128]{1,0:T(8,128)S(1)}, f32[128,128]{1,0:T(8,128)S(1)}, u32[]{:S(2)}, u32[]{:S(2)}) collective-permute-start(f32[128,128]{1,0:T(8,128)S(1)} %get-tuple-element.41), channel_id=1, source_target_pairs={{0,192},{32,224},{64,128},{96,160},{128,64},{160,96},{192,0},{224,... | collective-permute-start | bytes 196616 | tf_op jit(solution)/shard_map/ppermute | solution.py:566
  19.5 8.6 %copy-start.3 = (bf16[272,256]{1,0:T(8,128)(2,1)S(1)}, bf16[272,256]{1,0:T(8,128)(2,1)}, u32[]{:S(2)}) copy-start(bf16[272,256]{1,0:T(8,128)(2,1)} %constant.35.clone.rest_9_.rest_1_) | copy-start | bytes 417796
  19.5 8.6 %copy-start.4 = (bf16[272,256]{1,0:T(8,128)(2,1)S(1)}, bf16[272,256]{1,0:T(8,128)(2,1)}, u32[]{:S(2)}) copy-start(bf16[272,256]{1,0:T(8,128)(2,1)} %constant.34.clone.rest_8_.rest_0_) | copy-start | bytes 417796
  19.5 8.6 %copy-start.5 = (bf16[256,256]{1,0:T(8,128)(2,1)S(1)}, bf16[256,256]{1,0:T(8,128)(2,1)}, u32[]{:S(2)}) copy-start(bf16[256,256]{1,0:T(8,128)(2,1)} %constant.37.clone.rest_11_.rest_3_) | copy-start | bytes 393220
  19.5 8.6 %copy-start.6 = (bf16[256,256]{1,0:T(8,128)(2,1)S(1)}, bf16[256,256]{1,0:T(8,128)(2,1)}, u32[]{:S(2)}) copy-start(bf16[256,256]{1,0:T(8,128)(2,1)} %constant.36.clone.rest_10_.rest_2_) | copy-start | bytes 393220
  19.5 8.6 %copy-start.11 = (bf16[176,96]{1,0:T(8,128)(2,1)S(1)}, bf16[176,96]{1,0:T(8,128)(2,1)}, u32[]{:S(2)}) copy-start(bf16[176,96]{1,0:T(8,128)(2,1)} %constant.39.clone.rest_13_) | copy-start | bytes 101380
  19.5 8.6 %copy-start.12 = (bf16[176,96]{1,0:T(8,128)(2,1)S(1)}, bf16[176,96]{1,0:T(8,128)(2,1)}, u32[]{:S(2)}) copy-start(bf16[176,96]{1,0:T(8,128)(2,1)} %constant.38.clone.rest_12_) | copy-start | bytes 101380
  20.5 14.3 %collective-permute-start.10 = (f32[56,512]{1,0:T(8,128)S(1)}, f32[56,512]{1,0:T(8,128)S(1)}, u32[]{:S(2)}, u32[]{:S(2)}) collective-permute-start(f32[56,512]{1,0:T(8,128)S(1)} %get-tuple-element.56), channel_id=1, source_target_pairs={{0,255},{255,0},{64,191},{191,64},{128,127},{127,128},{192,63},{63... | collective-permute-start | bytes 344072 | tf_op jit(solution)/shard_map/ppermute | solution.py:586
  28.1 6.7 %copy-start.13 = (bf16[2,80,64]{2,1,0:T(8,128)(2,1)S(1)}, bf16[2,80,64]{2,1,0:T(8,128)(2,1)}, u32[]{:S(2)}) copy-start(bf16[2,80,64]{2,1,0:T(8,128)(2,1)} %constant.40.clone.table) | copy-start | bytes 61444
  31.2 7.1 %collective-permute-start.7 = (f32[128,128]{1,0:T(8,128)S(1)}, f32[128,128]{1,0:T(8,128)S(1)}, u32[]{:S(2)}, u32[]{:S(2)}) collective-permute-start(f32[128,128]{1,0:T(8,128)S(1)} %get-tuple-element.51), channel_id=1, source_target_pairs={{0,64},{32,96},{64,0},{96,32},{128,192},{160,224},{192,128},{224,1... | collective-permute-start | bytes 196616 | tf_op jit(solution)/shard_map/ppermute | solution.py:566
  32.5 7.5 %collective-permute-start.8 = (f32[128,128]{1,0:T(8,128)S(1)}, f32[128,128]{1,0:T(8,128)S(1)}, u32[]{:S(2)}, u32[]{:S(2)}) collective-permute-start(f32[128,128]{1,0:T(8,128)S(1)} %get-tuple-element.52), channel_id=1, source_target_pairs={{0,128},{32,160},{64,192},{96,224},{128,0},{160,32},{192,64},{224,... | collective-permute-start | bytes 196616 | tf_op jit(solution)/shard_map/ppermute | solution.py:566
  33.2 6.8 %collective-permute-start.9 = (f32[128,128]{1,0:T(8,128)S(1)}, f32[128,128]{1,0:T(8,128)S(1)}, u32[]{:S(2)}, u32[]{:S(2)}) collective-permute-start(f32[128,128]{1,0:T(8,128)S(1)} %get-tuple-element.53), channel_id=1, source_target_pairs={{0,192},{32,224},{64,128},{96,160},{128,64},{160,96},{192,0},{224,... | collective-permute-start | bytes 196616 | tf_op jit(solution)/shard_map/ppermute | solution.py:566
  36.3 7.2 %collective-permute-start.11 = (f32[128,128]{1,0:T(8,128)S(1)}, f32[128,128]{1,0:T(8,128)S(1)}, u32[]{:S(2)}, u32[]{:S(2)}) collective-permute-start(f32[128,128]{1,0:T(8,128)S(1)} %get-tuple-element.58), channel_id=1, source_target_pairs={{0,64},{32,96},{64,0},{96,32},{128,192},{160,224},{192,128},{224,1... | collective-permute-start | bytes 196616 | tf_op jit(solution)/shard_map/ppermute | solution.py:566
  36.7 7.2 %collective-permute-start.12 = (f32[128,128]{1,0:T(8,128)S(1)}, f32[128,128]{1,0:T(8,128)S(1)}, u32[]{:S(2)}, u32[]{:S(2)}) collective-permute-start(f32[128,128]{1,0:T(8,128)S(1)} %get-tuple-element.59), channel_id=1, source_target_pairs={{0,128},{32,160},{64,192},{96,224},{128,0},{160,32},{192,64},{224,... | collective-permute-start | bytes 196616 | tf_op jit(solution)/shard_map/ppermute | solution.py:566
  38.3 5.6 %collective-permute-start.13 = (f32[128,128]{1,0:T(8,128)S(1)}, f32[128,128]{1,0:T(8,128)S(1)}, u32[]{:S(2)}, u32[]{:S(2)}) collective-permute-start(f32[128,128]{1,0:T(8,128)S(1)} %get-tuple-element.60), channel_id=1, source_target_pairs={{0,192},{32,224},{64,128},{96,160},{128,64},{160,96},{192,0},{224,... | collective-permute-start | bytes 196616 | tf_op jit(solution)/shard_map/ppermute | solution.py:566
  40.0 7.8 %collective-permute-start.14 = (f32[4,64,128]{2,1,0:T(8,128)S(1)}, f32[4,64,128]{2,1,0:T(8,128)S(1)}, u32[]{:S(2)}, u32[]{:S(2)}) collective-permute-start(f32[4,64,128]{2,1,0:T(8,128)S(1)} %cut.1), channel_id=1, source_target_pairs={{0,32},{32,0},{64,96},{96,64},{128,160},{160,128},{192,224},{224,1... | collective-permute-start | bytes 393224 | tf_op jit(solution)/shard_map/ppermute | solution.py:573
  43.9 4.9 %copy-start.8 = (bf16[256,384]{1,0:T(8,128)(2,1)S(1)}, bf16[256,384]{1,0:T(8,128)(2,1)}, u32[]{:S(2)}) copy-start(bf16[256,384]{1,0:T(8,128)(2,1)} %constant.44.clone.rest_13_) | copy-start | bytes 589828
  43.9 4.9 %copy-start.10 = (bf16[128,384]{1,0:T(8,128)(2,1)S(1)}, bf16[128,384]{1,0:T(8,128)(2,1)}, u32[]{:S(2)}) copy-start(bf16[128,384]{1,0:T(8,128)(2,1)} %constant.42.clone.rest_11_) | copy-start | bytes 294916
  43.9 4.9 %copy-start.15 = (bf16[128,128]{1,0:T(8,128)(2,1)S(1)}, bf16[128,128]{1,0:T(8,128)(2,1)}, u32[]{:S(2)}) copy-start(bf16[128,128]{1,0:T(8,128)(2,1)} %constant.41.clone.rest_10_) | copy-start | bytes 98308
  43.9 4.9 %copy-start.18 = (f32[8,128]{1,0:T(8,128)S(1)}, f32[8,128]{1,0:T(8,128)}, u32[]{:S(2)}) copy-start(f32[8,128]{1,0:T(8,128)} %constant.43.clone.rest_12_) | copy-start | bytes 12292
  43.9 4.8 %collective-permute-start.15 = (f32[4,64,128]{2,1,0:T(8,128)S(1)}, f32[4,64,128]{2,1,0:T(8,128)S(1)}, u32[]{:S(2)}, u32[]{:S(2)}) collective-permute-start(f32[4,64,128]{2,1,0:T(8,128)S(1)} %cut_edge.1), channel_id=1, source_target_pairs={{0,32},{32,0},{64,96},{96,64},{128,160},{160,128},{192,224},{224,1... | collective-permute-start | bytes 393224 | tf_op jit(solution)/shard_map/ppermute | solution.py:573

commit v6 on v5

--- a/solution.py
+++ b/solution.py
@@ -288,13 +288,12 @@
         outs[j][...] = packed[bound[0, row_of(me ^ (2 * j), part)]]
 
 
-def edge_kernel(bound, pair, done, here, there, metric, pick, table, turn, columns, terms, *rest):
-    outs = rest[:4]
-    packed, rows, lines, scale, square, flags, count, own, other, other_edge = rest[4:]
+def metric_kernel(
+    bound, done, here, there, metric, pick, turn, packed, scale, columns, terms, rows, lines, square, flags
+):
     me, part = lax.axis_index("span"), lax.axis_index("dom")
     core = me & 1
     column_flags(bound, core, flags)
-    list_pairs(pair, count, own, other, other_edge)
 
     def copy_element(e):
         packed[e] = done[e]
@@ -329,6 +328,13 @@
     terms[...] = jnp.zeros((8, 128), F32)
     terms[0:1, :] = jnp.where(side < 2, 1.0, -1.0) * jnp.where(even, along, across)
     terms[1:2, :] = jnp.where(even, across, along)
+
+
+def edge_kernel(bound, pair, packed, scale, table, *rest):
+    outs = rest[:4]
+    count, own, other, other_edge = rest[4:]
+    me, part = lax.axis_index("span"), lax.axis_index("dom")
+    list_pairs(pair, count, own, other, other_edge)
     lane = lax.broadcasted_iota(jnp.int32, (2 * MODES, 128), 1)
     for j in range(4):
         e = bound[0, row_of(me ^ (2 * j), part)]
@@ -612,22 +618,24 @@
         weight=LONG,
     )
     blocks = between_chips(blocks)
+    packed, scale, columns, terms = call(
+        metric_kernel,
+        "metric",
+        [bound_table],
+        [packed, velocity_modes, there, metric, pick, turn],
+        [(ELEMS, 2 * MODES, 256), (64, 1, 128), (96, 128), (8, 128)],
+        [pltpu.VMEM((16, 256), F32), pltpu.VMEM((16, 1, 256), F32), pltpu.VMEM((128, 128), F32)]
+        + flags,
+        weight=LONG,
+    )
     blocks[3], packed = lax.optimization_barrier((blocks[3], packed))
-    columns, terms, *edge_blocks = call(
+    edge_blocks = call(
         edge_kernel,
         "edges",
         [bound_table, pair_table],
-        [packed, velocity_modes, there, metric, pick, edge_table, turn],
-        [(96, 128), (8, 128)] + [edge_chip] * 4,
-        [
-            pltpu.VMEM((ELEMS, 2 * MODES, 256), F32),
-            pltpu.VMEM((16, 256), F32),
-            pltpu.VMEM((16, 1, 256), F32),
-            pltpu.VMEM((64, 1, 128), F32),
-            pltpu.VMEM((128, 128), F32),
-        ]
-        + flags
-        + pair_scratch(),
+        [packed, scale, edge_table],
+        [edge_chip] * 4,
+        pair_scratch(),
         weight=LONG,
     )
     edge_blocks = between_chips(edge_blocks)

time: 51.2 us -> 51.3 us (level)
  waiting for transfers between devices: 4.95 us -> 2.94 us
  starting transfers between devices: 32.6 us -> 33.4 us
  Pallas kernels: 12.2 us -> 12.9 us
  local copies, waits for them, and re-layouts: 1.16 us -> 1.84 us
    ppermute x12, waiting for transfers between devices: 3.77 us -> 1.76 us  [between_chips(): lax.ppermute(blocks[j], 'span', [(s, s ^ 2 * j) for s in range(SPAN)])]
    unnamed x38, local copies, waits for them, and re-layouts: 1.16 us -> 1.84 us
    pallas_call x9 -> x10, Pallas kernels: 12.2 us -> 12.9 us  [call(): pl.pallas_call(kernel, out_shape=shapes, in_specs=[spec_of(pltpu.SMEM)] *...]
  transfers between devices with their start and end apart: 16 -> 16, of which waited for: 5 -> 4; matrix products, arithmetic and copies ran while one was open for 0% -> 0% of each run, Pallas kernels for 17% -> 18%
where the time goes in v6:
time: 51.3 us
  starting transfers between devices  33.4 us (65%)
  Pallas kernels  12.9 us (25%)
  waiting for transfers between devices  2.94 us (6%)
  local copies, waits for them, and re-layouts  1.84 us (4%)
    ppermute x12, starting transfers between devices, between_chips(): lax.ppermute(blocks[j], 'span', [(s, s ^ 2 * j) for s in range(SPAN)])  14.5 us
    pallas_call x10, Pallas kernels, call(): pl.pallas_call(kernel, out_shape=shapes, in_specs=[spec_of(pltpu.SMEM)] *...  12.9 us
    ppermute x3, starting transfers between devices, between_cores(): return lax.ppermute(block, 'span', [(s, s ^ 1) for s in range(SPAN)])  10.8 us
    ppermute x1, starting transfers between devices, side_swap(): return lax.ppermute(block, ('span', 'dom'), perm)  8.01 us
    unnamed x38, local copies, waits for them, and re-layouts  1.84 us
    ppermute x12, waiting for transfers between devices, between_chips(): lax.ppermute(blocks[j], 'span', [(s, s ^ 2 * j) for s in range(SPAN)])  1.76 us
    ppermute x3, waiting for transfers between devices, between_cores(): return lax.ppermute(block, 'span', [(s, s ^ 1) for s in range(SPAN)])  1.18 us
  transfers between devices with their start and end apart: 16, of which 4 were waited for; matrix products, arithmetic and copies ran while one was open for 0% of the time, Pallas kernels for 18%

profile of v6, /device:TPU:1, one launch (start us, length us, event | category | flops | bytes accessed | tf_op | source)
XLA Modules:
  0.0 51.3 jit_solution(2462166284729057000)
XLA Ops:
  0.0 3.2 %collective-permute-start = (f32[3,64,648]{2,1,0:T(8,128)}, f32[3,64,648]{2,1,0:T(8,128)S(1)}, u32[]{:S(2)}, u32[]{:S(2)}) collective-permute-start(f32[3,64,648]{2,1,0:T(8,128)} %here.5), channel_id=1, source_target_pairs={{0,32},{32,0},{64,96},{96,64},{128,160},{160,128},{192,224},{224,1... | collective-permute-start | bytes 1493000 | tf_op jit(solution)/shard_map/ppermute | solution.py:579
  3.2 1.1 %copy-done = f32[3,64,648]{2,1,0:T(8,128)S(1)} copy-done((f32[3,64,648]{2,1,0:T(8,128)S(1)}, f32[3,64,648]{2,1,0:T(8,128)}, u32[]{:S(2)}) %copy-start) | copy-done | bytes 497688
  4.3 0.6 %ready.1 = f32[8,128]{1,0:T(8,128)S(1)} custom-call(s32[2,8]{1,0:T(2,128)S(1)} %bitcast.2, f32[3,64,648]{2,1,0:T(8,128)S(1)} %copy-done), custom_call_target="tpu_custom_call" | custom-call | flops 200000000 | bytes 200000000 | tf_op jit(solution)/shard_map/ready/pallas_call | solution.py:553
  4.9 0.0 copy-start.2
  4.9 0.0 copy-start.7
  4.9 0.2 collective-permute-done.there
  5.1 1.2 %pack.1 = (f32[8,128,256]{2,1,0:T(8,128)S(1)}, f32[128,256]{1,0:T(8,128)S(1)}, f32[128,256]{1,0:T(8,128)S(1)}, f32[128,256]{1,0:T(8,128)S(1)}, f32[128,256]{1,0:T(8,128)S(1)}) custom-call(s32[2,8]{1,0:T(2,128)S(1)} %bitcast.3, f32[3,64,648]{2,1,0:T(8,128)S(1)} %copy-done, f32[3,64,648]{2,1,0:T(8,128)S(1)} %collective-permute-done.there, f32[8,128]{1,0:T(8,128)S(1)} %ready.1), custom_call_target="tpu_custom_call" | custom-call | flops 200000000 | bytes 200000000 | tf_op jit(solution)/shard_map/pack/pallas_call | solution.py:553
  6.3 2.7 %collective-permute-start.1 = (f32[128,256]{1,0:T(8,128)S(1)}, f32[128,256]{1,0:T(8,128)S(1)}, u32[]{:S(2)}, u32[]{:S(2)}) collective-permute-start(f32[128,256]{1,0:T(8,128)S(1)} %get-tuple-element.37), channel_id=1, source_target_pairs={{0,192},{32,224},{64,128},{96,160},{128,64},{160,96},{192,0},{224,... | collective-permute-start | bytes 393224 | tf_op jit(solution)/shard_map/ppermute | solution.py:572
  9.0 0.0 collective-permute-start.5
  9.0 0.9 %collective-permute-start.6 = (f32[128,256]{1,0:T(8,128)S(1)}, f32[128,256]{1,0:T(8,128)S(1)}, u32[]{:S(2)}, u32[]{:S(2)}) collective-permute-start(f32[128,256]{1,0:T(8,128)S(1)} %get-tuple-element.48), channel_id=1, source_target_pairs={{0,128},{32,160},{64,192},{96,224},{128,0},{160,32},{192,64},{224,... | collective-permute-start | bytes 393224 | tf_op jit(solution)/shard_map/ppermute | solution.py:572
  10.0 1.6 %metric.2 = (f32[8,128,256]{2,1,0:T(8,128)S(1)}, f32[64,1,128]{2,1,0:T(1,128)S(1)}, f32[96,128]{1,0:T(8,128)S(1)}, f32[8,128]{1,0:T(8,128)S(1)}) custom-call(s32[2,8]{1,0:T(2,128)S(1)} %bitcast.4, f32[8,128,256]{2,1,0:T(8,128)S(1)} %get-tuple-element.38.done, f32[3,64,648]{2,1,0:T(8,128)S(1)} %copy-done, f32[3,64,648]{2,1,0:T(8,128)S(1)} %collective-permute-done.there, ...), custom_call_target="tpu_custom_call" | custom-call | flops 200000000 | bytes 200000000 | tf_op jit(solution)/shard_map/metric/pallas_call | solution.py:553
  11.6 1.2 %collective-permute-done.1.rest_3_ = f32[128,256]{1,0:T(8,128)S(1)} collective-permute-done((f32[128,256]{1,0:T(8,128)S(1)}, f32[128,256]{1,0:T(8,128)S(1)}, u32[]{:S(2)}, u32[]{:S(2)}) %collective-permute-start.1) | collective-permute-done | bytes 131104 | tf_op jit(solution)/shard_map/ppermute | solution.py:572
  12.8 0.7 %copy-done.16 = s32[10,4]{0,1:T(4,128)S(1)} copy-done((s32[10,4]{0,1:T(4,128)S(1)}, s32[10,4]{0,1:T(4,128)}, u32[]{:S(2)}) %copy-start.16) | copy-done | bytes 184
  13.5 1.6 %edges.1 = (f32[128,128]{1,0:T(8,128)S(1)}, f32[128,128]{1,0:T(8,128)S(1)}, f32[128,128]{1,0:T(8,128)S(1)}, f32[128,128]{1,0:T(8,128)S(1)}) custom-call(s32[2,8]{1,0:T(2,128)S(1)} %bitcast.5, s32[4,10]{1,0:T(4,128)S(1)} %bitcast.10, f32[8,128,256]{2,1,0:T(8,128)S(1)} %get-tuple-element.40.packed, f32[64,1,128]{2,1,0:T(1,128)S(1)} %get-tuple-element.41.scale, ...), custom_call_target="tpu_custom_call" | custom-call | flops 200000000 | bytes 200000000 | tf_op jit(solution)/shard_map/edges/pallas_call | solution.py:553
  15.1 0.1 collective-permute-start.2
  15.2 2.9 %collective-permute-start.3 = (f32[128,128]{1,0:T(8,128)S(1)}, f32[128,128]{1,0:T(8,128)S(1)}, u32[]{:S(2)}, u32[]{:S(2)}) collective-permute-start(f32[128,128]{1,0:T(8,128)S(1)} %get-tuple-element.44), channel_id=1, source_target_pairs={{0,128},{32,160},{64,192},{96,224},{128,0},{160,32},{192,64},{224,... | collective-permute-start | bytes 196616 | tf_op jit(solution)/shard_map/ppermute | solution.py:572
  18.0 0.7 %collective-permute-start.4 = (f32[128,128]{1,0:T(8,128)S(1)}, f32[128,128]{1,0:T(8,128)S(1)}, u32[]{:S(2)}, u32[]{:S(2)}) collective-permute-start(f32[128,128]{1,0:T(8,128)S(1)} %get-tuple-element.45), channel_id=1, source_target_pairs={{0,192},{32,224},{64,128},{96,160},{128,64},{160,96},{192,0},{224,... | collective-permute-start | bytes 196616 | tf_op jit(solution)/shard_map/ppermute | solution.py:572
  18.7 0.0 collective-permute-done.5.rest_1_
  18.7 0.5 collective-permute-done.6.rest_2_
  19.2 0.0 copy-start.6
  19.2 0.0 copy-start.12
  19.3 0.0 copy-start.13
  19.3 1.0 %rim.1 = (f32[56,512]{1,0:T(8,128)S(1)}, bf16[256,512]{1,0:T(8,128)(2,1)S(1)}, bf16[256,512]{1,0:T(8,128)(2,1)S(1)}) custom-call(s32[2,8]{1,0:T(2,128)S(1)} %bitcast.6, f32[128,256]{1,0:T(8,128)S(1)} %get-tuple-element.46.rest_0_, f32[128,256]{1,0:T(8,128)S(1)} %collective-permute-done.5.rest_1_, f32[128,256]{1,0:T(8,128)S(1)} %collective-permute-done.6.rest_2_, ...), custom_call_target="tpu_custom_call" | custom-call | flops 1000 | bytes 1000 | tf_op jit(solution)/shard_map/rim/pallas_call | solution.py:553
  20.2 8.0 %collective-permute-start.10 = (f32[56,512]{1,0:T(8,128)S(1)}, f32[56,512]{1,0:T(8,128)S(1)}, u32[]{:S(2)}, u32[]{:S(2)}) collective-permute-start(f32[56,512]{1,0:T(8,128)S(1)} %get-tuple-element.60), channel_id=1, source_target_pairs={{0,255},{255,0},{64,191},{191,64},{128,127},{127,128},{192,63},{63... | collective-permute-start | bytes 344072 | tf_op jit(solution)/shard_map/ppermute | solution.py:592
  28.3 0.0 collective-permute-done.2.rest_1_
  28.3 0.0 collective-permute-done.3.rest_2_
  28.3 0.0 collective-permute-done.4.rest_3_
  28.3 0.0 copy-start.14
  28.3 3.1 %whole.1 = (f32[128,128]{1,0:T(8,128)S(1)}, f32[128,128]{1,0:T(8,128)S(1)}, f32[128,128]{1,0:T(8,128)S(1)}, f32[128,128]{1,0:T(8,128)S(1)}, f32[128,512]{1,0:T(8,128)S(1)}, /*index=5*/f32[88,512]{1,0:T(8,128)S(1)}) custom-call(s32[2,8]{1,0:T(2,128)S(1)} %bitcast.7, s32[4,10]{1,0:T(4,128)S(1)} %bitcast.11, f32[128,128]{1,0:T(8,128)S(1)} %get-tuple-element.42.rest_0_, ...), custom_call_target="tpu_custom_call" | custom-call | flops 1000 | bytes 1000 | tf_op jit(solution)/shard_map/whole/pallas_call | solution.py:553
  31.4 1.0 %collective-permute-start.7 = (f32[128,128]{1,0:T(8,128)S(1)}, f32[128,128]{1,0:T(8,128)S(1)}, u32[]{:S(2)}, u32[]{:S(2)}) collective-permute-start(f32[128,128]{1,0:T(8,128)S(1)} %get-tuple-element.55), channel_id=1, source_target_pairs={{0,64},{32,96},{64,0},{96,32},{128,192},{160,224},{192,128},{224,1... | collective-permute-start | bytes 196616 | tf_op jit(solution)/shard_map/ppermute | solution.py:572
  32.4 1.0 %collective-permute-start.8 = (f32[128,128]{1,0:T(8,128)S(1)}, f32[128,128]{1,0:T(8,128)S(1)}, u32[]{:S(2)}, u32[]{:S(2)}) collective-permute-start(f32[128,128]{1,0:T(8,128)S(1)} %get-tuple-element.56), channel_id=1, source_target_pairs={{0,128},{32,160},{64,192},{96,224},{128,0},{160,32},{192,64},{224,... | collective-permute-start | bytes 196616 | tf_op jit(solution)/shard_map/ppermute | solution.py:572
  33.4 1.6 %collective-permute-start.9 = (f32[128,128]{1,0:T(8,128)S(1)}, f32[128,128]{1,0:T(8,128)S(1)}, u32[]{:S(2)}, u32[]{:S(2)}) collective-permute-start(f32[128,128]{1,0:T(8,128)S(1)} %get-tuple-element.57), channel_id=1, source_target_pairs={{0,192},{32,224},{64,128},{96,160},{128,64},{160,96},{192,0},{224,... | collective-permute-start | bytes 196616 | tf_op jit(solution)/shard_map/ppermute | solution.py:572
  35.1 0.0 collective-permute-done.10.other
  35.1 1.5 %side.1 = (f32[128,128]{1,0:T(8,128)S(1)}, f32[128,128]{1,0:T(8,128)S(1)}, f32[128,128]{1,0:T(8,128)S(1)}, f32[128,128]{1,0:T(8,128)S(1)}) custom-call(s32[2,8]{1,0:T(2,128)S(1)} %bitcast.8, f32[128,512]{1,0:T(8,128)S(1)} %get-tuple-element.58.term, f32[88,512]{1,0:T(8,128)S(1)} %get-tuple-element.59.mine, f32[56,512]{1,0:T(8,128)S(1)} %collective-permute-done.10.other, ...), custom_call_target="tpu_custom_call" | custom-call | flops 1000 | bytes 1000 | tf_op jit(solution)/shard_map/side/pallas_call | solution.py:553
  36.5 0.1 collective-permute-start.11
  36.6 1.9 %collective-permute-start.12 = (f32[128,128]{1,0:T(8,128)S(1)}, f32[128,128]{1,0:T(8,128)S(1)}, u32[]{:S(2)}, u32[]{:S(2)}) collective-permute-start(f32[128,128]{1,0:T(8,128)S(1)} %get-tuple-element.63), channel_id=1, source_target_pairs={{0,128},{32,160},{64,192},{96,224},{128,0},{160,32},{192,64},{224,... | collective-permute-start | bytes 196616 | tf_op jit(solution)/shard_map/ppermute | solution.py:572
  38.5 0.0 collective-permute-done.7.rest_1_
  38.6 1.6 %collective-permute-start.13 = (f32[128,128]{1,0:T(8,128)S(1)}, f32[128,128]{1,0:T(8,128)S(1)}, u32[]{:S(2)}, u32[]{:S(2)}) collective-permute-start(f32[128,128]{1,0:T(8,128)S(1)} %get-tuple-element.64), channel_id=1, source_target_pairs={{0,192},{32,224},{64,128},{96,160},{128,64},{160,96},{192,0},{224,... | collective-permute-start | bytes 196616 | tf_op jit(solution)/shard_map/ppermute | solution.py:572
  40.2 0.0 collective-permute-done.8.rest_2_
  40.2 3.5 %collective-permute-start.14 = (f32[4,64,128]{2,1,0:T(8,128)S(1)}, f32[4,64,128]{2,1,0:T(8,128)S(1)}, u32[]{:S(2)}, u32[]{:S(2)}) collective-permute-start(f32[4,64,128]{2,1,0:T(8,128)S(1)} %cut.1), channel_id=1, source_target_pairs={{0,32},{32,0},{64,96},{96,64},{128,160},{160,128},{192,224},{224,1... | collective-permute-start | bytes 393224 | tf_op jit(solution)/shard_map/ppermute | solution.py:579
  43.7 0.0 collective-permute-done.13.rest_3_.rest_7_
  43.7 0.0 copy-start.8
  43.7 0.0 copy-start.10
  43.7 0.0 copy-start.15
  43.8 0.0 copy-start.18
  43.8 4.1 %collective-permute-start.15 = (f32[4,64,128]{2,1,0:T(8,128)S(1)}, f32[4,64,128]{2,1,0:T(8,128)S(1)}, u32[]{:S(2)}, u32[]{:S(2)}) collective-permute-start(f32[4,64,128]{2,1,0:T(8,128)S(1)} %cut_edge.1), channel_id=1, source_target_pairs={{0,32},{32,0},{64,96},{96,64},{128,160},{160,128},{192,224},{224,1... | collective-permute-start | bytes 393224 | tf_op jit(solution)/shard_map/ppermute | solution.py:579
  47.9 1.0 %collective-permute-done.15.rest_9_ = f32[4,64,128]{2,1,0:T(8,128)S(1)} collective-permute-done((f32[4,64,128]{2,1,0:T(8,128)S(1)}, f32[4,64,128]{2,1,0:T(8,128)S(1)}, u32[]{:S(2)}, u32[]{:S(2)}) %collective-permute-start.15) | collective-permute-done | bytes 131104 | tf_op jit(solution)/shard_map/ppermute | solution.py:579
  48.9 2.4 %settle.1 = f32[3,64,648]{2,1,0:T(8,128)} custom-call(s32[2,8]{1,0:T(2,128)S(1)} %bitcast.9, s32[4,10]{1,0:T(4,128)S(1)} %bitcast.12, f32[128,128]{1,0:T(8,128)S(1)} %get-tuple-element.54.rest_0_, f32[128,128]{1,0:T(8,128)S(1)} %collective-permute-done.7.rest_1_, f32[128,128]{1,0:T(8,128)S(1)} %collective-permute-done.8.rest_2_, ...), custom_call_target="tpu_custom_call" | custom-call | flops 1000 | bytes 1000 | tf_op jit(solution)/shard_map/settle/pallas_call | solution.py:553
  (32 shorter events, 0.1 us)
Async XLA Ops:
  0.0 3.2 %copy-start.11 = (s32[8,2]{0,1:T(2,128)S(1)}, s32[8,2]{0,1:T(2,128)}, u32[]{:S(2)}) copy-start(s32[8,2]{0,1:T(2,128)} %param.22) | copy-start | bytes 196
  0.0 5.1 %collective-permute-start = (f32[3,64,648]{2,1,0:T(8,128)}, f32[3,64,648]{2,1,0:T(8,128)S(1)}, u32[]{:S(2)}, u32[]{:S(2)}) collective-permute-start(f32[3,64,648]{2,1,0:T(8,128)} %here.5), channel_id=1, source_target_pairs={{0,32},{32,0},{64,96},{96,64},{128,160},{160,128},{192,224},{224,1... | collective-permute-start | bytes 1493000 | tf_op jit(solution)/shard_map/ppermute | solution.py:579
  3.2 1.1 %copy-start = (f32[3,64,648]{2,1,0:T(8,128)S(1)}, f32[3,64,648]{2,1,0:T(8,128)}, u32[]{:S(2)}) copy-start(f32[3,64,648]{2,1,0:T(8,128)} %here.5) | copy-start | bytes 1492996
  4.9 5.1 %copy-start.2 = (bf16[288,256]{1,0:T(8,128)(2,1)S(1)}, bf16[288,256]{1,0:T(8,128)(2,1)}, u32[]{:S(2)}) copy-start(bf16[288,256]{1,0:T(8,128)(2,1)} %constant.31.clone.turn.rest_7_) | copy-start | bytes 442372
  4.9 5.1 %copy-start.7 = (bf16[256,512]{1,0:T(8,128)(2,1)S(1)}, bf16[256,512]{1,0:T(8,128)(2,1)}, u32[]{:S(2)}) copy-start(bf16[256,512]{1,0:T(8,128)(2,1)} %constant.30.clone.pick) | copy-start | bytes 786436
  5.1 4.9 %copy-start.17 = (f32[4,648]{1,0:T(4,128)S(1)}, f32[4,648]{1,0:T(4,128)}, u32[]{:S(2)}) copy-start(f32[4,648]{1,0:T(4,128)} %metric.3) | copy-start | bytes 31108
  6.3 6.5 %collective-permute-start.1 = (f32[128,256]{1,0:T(8,128)S(1)}, f32[128,256]{1,0:T(8,128)S(1)}, u32[]{:S(2)}, u32[]{:S(2)}) collective-permute-start(f32[128,256]{1,0:T(8,128)S(1)} %get-tuple-element.37), channel_id=1, source_target_pairs={{0,192},{32,224},{64,128},{96,160},{128,64},{160,96},{192,0},{224,... | collective-permute-start | bytes 393224 | tf_op jit(solution)/shard_map/ppermute | solution.py:572
  9.0 9.7 %collective-permute-start.5 = (f32[128,256]{1,0:T(8,128)S(1)}, f32[128,256]{1,0:T(8,128)S(1)}, u32[]{:S(2)}, u32[]{:S(2)}) collective-permute-start(f32[128,256]{1,0:T(8,128)S(1)} %get-tuple-element.47), channel_id=1, source_target_pairs={{0,64},{32,96},{64,0},{96,32},{128,192},{160,224},{192,128},{224,1... | collective-permute-start | bytes 393224 | tf_op jit(solution)/shard_map/ppermute | solution.py:572
  9.0 10.2 %collective-permute-start.6 = (f32[128,256]{1,0:T(8,128)S(1)}, f32[128,256]{1,0:T(8,128)S(1)}, u32[]{:S(2)}, u32[]{:S(2)}) collective-permute-start(f32[128,256]{1,0:T(8,128)S(1)} %get-tuple-element.48), channel_id=1, source_target_pairs={{0,128},{32,160},{64,192},{96,224},{128,0},{160,32},{192,64},{224,... | collective-permute-start | bytes 393224 | tf_op jit(solution)/shard_map/ppermute | solution.py:572
  9.9 2.9 %copy-start.1 = (bf16[4,256,512]{2,1,0:T(8,128)(2,1)S(1)}, bf16[4,256,512]{2,1,0:T(8,128)(2,1)}, u32[]{:S(2)}) copy-start(bf16[4,256,512]{2,1,0:T(8,128)(2,1)} %constant.32.clone.table) | copy-start | bytes 3145732
  12.8 0.7 %copy-start.16 = (s32[10,4]{0,1:T(4,128)S(1)}, s32[10,4]{0,1:T(4,128)}, u32[]{:S(2)}) copy-start(s32[10,4]{0,1:T(4,128)} %param.21) | copy-start | bytes 484
  13.5 5.7 %copy-start.9 = (bf16[4,64,256]{2,1,0:T(8,128)(2,1)S(1)}, bf16[4,64,256]{2,1,0:T(8,128)(2,1)}, u32[]{:S(2)}) copy-start(bf16[4,64,256]{2,1,0:T(8,128)(2,1)} %constant.33.clone.rest_5_) | copy-start | bytes 393220
  15.1 13.2 %collective-permute-start.2 = (f32[128,128]{1,0:T(8,128)S(1)}, f32[128,128]{1,0:T(8,128)S(1)}, u32[]{:S(2)}, u32[]{:S(2)}) collective-permute-start(f32[128,128]{1,0:T(8,128)S(1)} %get-tuple-element.43), channel_id=1, source_target_pairs={{0,64},{32,96},{64,0},{96,32},{128,192},{160,224},{192,128},{224,1... | collective-permute-start | bytes 196616 | tf_op jit(solution)/shard_map/ppermute | solution.py:572
  15.2 13.1 %collective-permute-start.3 = (f32[128,128]{1,0:T(8,128)S(1)}, f32[128,128]{1,0:T(8,128)S(1)}, u32[]{:S(2)}, u32[]{:S(2)}) collective-permute-start(f32[128,128]{1,0:T(8,128)S(1)} %get-tuple-element.44), channel_id=1, source_target_pairs={{0,128},{32,160},{64,192},{96,224},{128,0},{160,32},{192,64},{224,... | collective-permute-start | bytes 196616 | tf_op jit(solution)/shard_map/ppermute | solution.py:572
  18.0 10.2 %collective-permute-start.4 = (f32[128,128]{1,0:T(8,128)S(1)}, f32[128,128]{1,0:T(8,128)S(1)}, u32[]{:S(2)}, u32[]{:S(2)}) collective-permute-start(f32[128,128]{1,0:T(8,128)S(1)} %get-tuple-element.45), channel_id=1, source_target_pairs={{0,192},{32,224},{64,128},{96,160},{128,64},{160,96},{192,0},{224,... | collective-permute-start | bytes 196616 | tf_op jit(solution)/shard_map/ppermute | solution.py:572
  19.2 9.1 %copy-start.3 = (bf16[272,256]{1,0:T(8,128)(2,1)S(1)}, bf16[272,256]{1,0:T(8,128)(2,1)}, u32[]{:S(2)}) copy-start(bf16[272,256]{1,0:T(8,128)(2,1)} %constant.35.clone.rest_9_.rest_1_) | copy-start | bytes 417796
  19.2 9.1 %copy-start.4 = (bf16[272,256]{1,0:T(8,128)(2,1)S(1)}, bf16[272,256]{1,0:T(8,128)(2,1)}, u32[]{:S(2)}) copy-start(bf16[272,256]{1,0:T(8,128)(2,1)} %constant.34.clone.rest_8_.rest_0_) | copy-start | bytes 417796
  19.2 9.1 %copy-start.5 = (bf16[256,256]{1,0:T(8,128)(2,1)S(1)}, bf16[256,256]{1,0:T(8,128)(2,1)}, u32[]{:S(2)}) copy-start(bf16[256,256]{1,0:T(8,128)(2,1)} %constant.37.clone.rest_11_.rest_3_) | copy-start | bytes 393220
  19.2 9.1 %copy-start.6 = (bf16[256,256]{1,0:T(8,128)(2,1)S(1)}, bf16[256,256]{1,0:T(8,128)(2,1)}, u32[]{:S(2)}) copy-start(bf16[256,256]{1,0:T(8,128)(2,1)} %constant.36.clone.rest_10_.rest_2_) | copy-start | bytes 393220
  19.2 9.1 %copy-start.12 = (bf16[176,96]{1,0:T(8,128)(2,1)S(1)}, bf16[176,96]{1,0:T(8,128)(2,1)}, u32[]{:S(2)}) copy-start(bf16[176,96]{1,0:T(8,128)(2,1)} %constant.39.clone.rest_13_) | copy-start | bytes 101380
  19.3 9.1 %copy-start.13 = (bf16[176,96]{1,0:T(8,128)(2,1)S(1)}, bf16[176,96]{1,0:T(8,128)(2,1)}, u32[]{:S(2)}) copy-start(bf16[176,96]{1,0:T(8,128)(2,1)} %constant.38.clone.rest_12_) | copy-start | bytes 101380
  20.2 14.8 %collective-permute-start.10 = (f32[56,512]{1,0:T(8,128)S(1)}, f32[56,512]{1,0:T(8,128)S(1)}, u32[]{:S(2)}, u32[]{:S(2)}) collective-permute-start(f32[56,512]{1,0:T(8,128)S(1)} %get-tuple-element.60), channel_id=1, source_target_pairs={{0,255},{255,0},{64,191},{191,64},{128,127},{127,128},{192,63},{63... | collective-permute-start | bytes 344072 | tf_op jit(solution)/shard_map/ppermute | solution.py:592
  28.3 6.7 %copy-start.14 = (bf16[2,80,64]{2,1,0:T(8,128)(2,1)S(1)}, bf16[2,80,64]{2,1,0:T(8,128)(2,1)}, u32[]{:S(2)}) copy-start(bf16[2,80,64]{2,1,0:T(8,128)(2,1)} %constant.40.clone.table) | copy-start | bytes 61444
  31.4 7.1 %collective-permute-start.7 = (f32[128,128]{1,0:T(8,128)S(1)}, f32[128,128]{1,0:T(8,128)S(1)}, u32[]{:S(2)}, u32[]{:S(2)}) collective-permute-start(f32[128,128]{1,0:T(8,128)S(1)} %get-tuple-element.55), channel_id=1, source_target_pairs={{0,64},{32,96},{64,0},{96,32},{128,192},{160,224},{192,128},{224,1... | collective-permute-start | bytes 196616 | tf_op jit(solution)/shard_map/ppermute | solution.py:572
  32.4 7.8 %collective-permute-start.8 = (f32[128,128]{1,0:T(8,128)S(1)}, f32[128,128]{1,0:T(8,128)S(1)}, u32[]{:S(2)}, u32[]{:S(2)}) collective-permute-start(f32[128,128]{1,0:T(8,128)S(1)} %get-tuple-element.56), channel_id=1, source_target_pairs={{0,128},{32,160},{64,192},{96,224},{128,0},{160,32},{192,64},{224,... | collective-permute-start | bytes 196616 | tf_op jit(solution)/shard_map/ppermute | solution.py:572
  33.4 6.8 %collective-permute-start.9 = (f32[128,128]{1,0:T(8,128)S(1)}, f32[128,128]{1,0:T(8,128)S(1)}, u32[]{:S(2)}, u32[]{:S(2)}) collective-permute-start(f32[128,128]{1,0:T(8,128)S(1)} %get-tuple-element.57), channel_id=1, source_target_pairs={{0,192},{32,224},{64,128},{96,160},{128,64},{160,96},{192,0},{224,... | collective-permute-start | bytes 196616 | tf_op jit(solution)/shard_map/ppermute | solution.py:572
  36.5 7.2 %collective-permute-start.11 = (f32[128,128]{1,0:T(8,128)S(1)}, f32[128,128]{1,0:T(8,128)S(1)}, u32[]{:S(2)}, u32[]{:S(2)}) collective-permute-start(f32[128,128]{1,0:T(8,128)S(1)} %get-tuple-element.62), channel_id=1, source_target_pairs={{0,64},{32,96},{64,0},{96,32},{128,192},{160,224},{192,128},{224,1... | collective-permute-start | bytes 196616 | tf_op jit(solution)/shard_map/ppermute | solution.py:572
  36.6 7.1 %collective-permute-start.12 = (f32[128,128]{1,0:T(8,128)S(1)}, f32[128,128]{1,0:T(8,128)S(1)}, u32[]{:S(2)}, u32[]{:S(2)}) collective-permute-start(f32[128,128]{1,0:T(8,128)S(1)} %get-tuple-element.63), channel_id=1, source_target_pairs={{0,128},{32,160},{64,192},{96,224},{128,0},{160,32},{192,64},{224,... | collective-permute-start | bytes 196616 | tf_op jit(solution)/shard_map/ppermute | solution.py:572
  38.6 5.2 %collective-permute-start.13 = (f32[128,128]{1,0:T(8,128)S(1)}, f32[128,128]{1,0:T(8,128)S(1)}, u32[]{:S(2)}, u32[]{:S(2)}) collective-permute-start(f32[128,128]{1,0:T(8,128)S(1)} %get-tuple-element.64), channel_id=1, source_target_pairs={{0,192},{32,224},{64,128},{96,160},{128,64},{160,96},{192,0},{224,... | collective-permute-start | bytes 196616 | tf_op jit(solution)/shard_map/ppermute | solution.py:572
  40.2 7.7 %collective-permute-start.14 = (f32[4,64,128]{2,1,0:T(8,128)S(1)}, f32[4,64,128]{2,1,0:T(8,128)S(1)}, u32[]{:S(2)}, u32[]{:S(2)}) collective-permute-start(f32[4,64,128]{2,1,0:T(8,128)S(1)} %cut.1), channel_id=1, source_target_pairs={{0,32},{32,0},{64,96},{96,64},{128,160},{160,128},{192,224},{224,1... | collective-permute-start | bytes 393224 | tf_op jit(solution)/shard_map/ppermute | solution.py:579
  43.7 5.2 %copy-start.8 = (bf16[256,384]{1,0:T(8,128)(2,1)S(1)}, bf16[256,384]{1,0:T(8,128)(2,1)}, u32[]{:S(2)}) copy-start(bf16[256,384]{1,0:T(8,128)(2,1)} %constant.44.clone.rest_13_) | copy-start | bytes 589828
  43.7 5.1 %copy-start.10 = (bf16[128,384]{1,0:T(8,128)(2,1)S(1)}, bf16[128,384]{1,0:T(8,128)(2,1)}, u32[]{:S(2)}) copy-start(bf16[128,384]{1,0:T(8,128)(2,1)} %constant.42.clone.rest_11_) | copy-start | bytes 294916
  43.7 5.1 %copy-start.15 = (bf16[128,128]{1,0:T(8,128)(2,1)S(1)}, bf16[128,128]{1,0:T(8,128)(2,1)}, u32[]{:S(2)}) copy-start(bf16[128,128]{1,0:T(8,128)(2,1)} %constant.41.clone.rest_10_) | copy-start | bytes 98308
  43.8 5.1 %copy-start.18 = (f32[8,128]{1,0:T(8,128)S(1)}, f32[8,128]{1,0:T(8,128)}, u32[]{:S(2)}) copy-start(f32[8,128]{1,0:T(8,128)} %constant.43.clone.rest_12_) | copy-start | bytes 12292
  43.8 5.1 %collective-permute-start.15 = (f32[4,64,128]{2,1,0:T(8,128)S(1)}, f32[4,64,128]{2,1,0:T(8,128)S(1)}, u32[]{:S(2)}, u32[]{:S(2)}) collective-permute-start(f32[4,64,128]{2,1,0:T(8,128)S(1)} %cut_edge.1), channel_id=1, source_target_pairs={{0,32},{32,0},{64,96},{96,64},{128,160},{160,128},{192,224},{224,1... | collective-permute-start | bytes 393224 | tf_op jit(solution)/shard_map/ppermute | solution.py:579

commit v7 on v6

--- a/solution.py
+++ b/solution.py
@@ -244,7 +244,7 @@
         other[n] = 0
         other_edge[n] = 0
     for row in range(PAIRS):
-        for first, second in ((0, 2), (2, 0)):
+        for first, second in ((2, 4), (4, 2)):
             e = pair[first, row]
             slot = e * 4 + count[e]
             own[slot] = pair[first + 1, row]
@@ -600,7 +600,8 @@
     take, give, where, back = settle_tables()
     turn = halves(order_table())[0]
     chip, edge_chip = (2 * MODES, 256), (2 * MODES, 128)
-    pair_table, bound_table = pair_table.T, bound_table.T
+    side_rows = jnp.pad(bound_table.T, ((0, 0), (0, PAIRS - 2 * ROWS)))
+    bound_table = pair_table = jnp.concatenate([side_rows, pair_table.T], axis=0)
     flags = [pltpu.SMEM((ELEMS,), jnp.int32)]
 
     there = between_cores(velocity_modes)

time: 51.3 us -> 52.6 us (1.025)
  waiting for transfers between devices: 2.94 us -> 3.99 us
    ppermute x1, starting transfers between devices: 8.01 us -> 6.12 us  [side_swap(): return lax.ppermute(block, ('span', 'dom'), perm)]
    ppermute x3, starting transfers between devices: 10.8 us -> 12.5 us  [between_cores(): return lax.ppermute(block, 'span', [(s, s ^ 1) for s in range(SPAN)])]
    ppermute x12, waiting for transfers between devices: 1.76 us -> 2.99 us  [between_chips(): lax.ppermute(blocks[j], 'span', [(s, s ^ 2 * j) for s in range(SPAN)])]
  transfers between devices with their start and end apart: 16 -> 16, of which waited for: 4 -> 3; matrix products, arithmetic and copies ran while one was open for 0% -> 0% of each run, Pallas kernels for 18% -> 18%
where the time goes in v7:
time: 52.6 us; the launch traced here: 52.7 us
  starting transfers between devices  33.2 us (63%)
  Pallas kernels  13.4 us (25%)
  waiting for transfers between devices  3.99 us (8%)
  local copies, waits for them, and re-layouts  1.83 us (3%)
    ppermute x12, starting transfers between devices, between_chips(): lax.ppermute(blocks[j], 'span', [(s, s ^ 2 * j) for s in range(SPAN)])  14.5 us
    pallas_call x10, Pallas kernels, call(): pl.pallas_call(kernel, out_shape=shapes, in_specs=[spec_of(pltpu.SMEM)] *...  13.4 us
    ppermute x3, starting transfers between devices, between_cores(): return lax.ppermute(block, 'span', [(s, s ^ 1) for s in range(SPAN)])  12.5 us
    ppermute x1, starting transfers between devices, side_swap(): return lax.ppermute(block, ('span', 'dom'), perm)  6.12 us
    ppermute x12, waiting for transfers between devices, between_chips(): lax.ppermute(blocks[j], 'span', [(s, s ^ 2 * j) for s in range(SPAN)])  2.99 us
    unnamed x38, local copies, waits for them, and re-layouts  1.83 us
  transfers between devices with their start and end apart: 16, of which 3 were waited for; matrix products, arithmetic and copies ran while one was open for 0% of the time, Pallas kernels for 18%

profile of v7, /device:TPU:1, one launch (start us, length us, event | category | flops | bytes accessed | tf_op | source)
XLA Modules:
  0.0 52.7 jit_solution(11302821081198790841)
XLA Ops:
  0.0 3.2 %collective-permute-start = (f32[3,64,648]{2,1,0:T(8,128)}, f32[3,64,648]{2,1,0:T(8,128)S(1)}, u32[]{:S(2)}, u32[]{:S(2)}) collective-permute-start(f32[3,64,648]{2,1,0:T(8,128)} %here.5), channel_id=1, source_target_pairs={{0,32},{32,0},{64,96},{96,64},{128,160},{160,128},{192,224},{224,1... | collective-permute-start | bytes 1493000 | tf_op jit(solution)/shard_map/ppermute | solution.py:579
  3.2 0.7 %copy-done.18 = s32[8,2]{0,1:T(2,128)S(1)} copy-done((s32[8,2]{0,1:T(2,128)S(1)}, s32[8,2]{0,1:T(2,128)}, u32[]{:S(2)}) %copy-start.18) | copy-done | bytes 88
  3.9 1.1 %copy-done = f32[3,64,648]{2,1,0:T(8,128)S(1)} copy-done((f32[3,64,648]{2,1,0:T(8,128)S(1)}, f32[3,64,648]{2,1,0:T(8,128)}, u32[]{:S(2)}) %copy-start) | copy-done | bytes 497688
  5.0 0.6 %ready.1 = f32[8,128]{1,0:T(8,128)S(1)} custom-call(s32[6,10]{1,0:T(8,128)S(1)} %pad_add_fusion.bound.pair, f32[3,64,648]{2,1,0:T(8,128)S(1)} %copy-done), custom_call_target="tpu_custom_call" | custom-call | flops 200000000 | bytes 200000000 | tf_op jit(solution)/shard_map/ready/pallas_call | solution.py:553
  5.6 0.0 copy-start.2
  5.6 0.0 copy-start.7
  5.6 0.0 collective-permute-done.there
  5.6 0.0 copy-start.15
  5.7 1.3 %pack.1 = (f32[8,128,256]{2,1,0:T(8,128)S(1)}, f32[128,256]{1,0:T(8,128)S(1)}, f32[128,256]{1,0:T(8,128)S(1)}, f32[128,256]{1,0:T(8,128)S(1)}, f32[128,256]{1,0:T(8,128)S(1)}) custom-call(s32[6,10]{1,0:T(8,128)S(1)} %pad_add_fusion.bound.pair, f32[3,64,648]{2,1,0:T(8,128)S(1)} %copy-done, f32[3,64,648]{2,1,0:T(8,128)S(1)} %collective-permute-done.there, ...), custom_call_target="tpu_custom_call" | custom-call | flops 200000000 | bytes 200000000 | tf_op jit(solution)/shard_map/pack/pallas_call | solution.py:553
  6.9 2.7 %collective-permute-start.1 = (f32[128,256]{1,0:T(8,128)S(1)}, f32[128,256]{1,0:T(8,128)S(1)}, u32[]{:S(2)}, u32[]{:S(2)}) collective-permute-start(f32[128,256]{1,0:T(8,128)S(1)} %get-tuple-element.37), channel_id=1, source_target_pairs={{0,192},{32,224},{64,128},{96,160},{128,64},{160,96},{192,0},{224,... | collective-permute-start | bytes 393224 | tf_op jit(solution)/shard_map/ppermute | solution.py:572
  9.6 0.0 collective-permute-start.5
  9.6 0.9 %collective-permute-start.6 = (f32[128,256]{1,0:T(8,128)S(1)}, f32[128,256]{1,0:T(8,128)S(1)}, u32[]{:S(2)}, u32[]{:S(2)}) collective-permute-start(f32[128,256]{1,0:T(8,128)S(1)} %get-tuple-element.48), channel_id=1, source_target_pairs={{0,128},{32,160},{64,192},{96,224},{128,0},{160,32},{192,64},{224,... | collective-permute-start | bytes 393224 | tf_op jit(solution)/shard_map/ppermute | solution.py:572
  10.6 1.7 %metric.2 = (f32[8,128,256]{2,1,0:T(8,128)S(1)}, f32[64,1,128]{2,1,0:T(1,128)S(1)}, f32[96,128]{1,0:T(8,128)S(1)}, f32[8,128]{1,0:T(8,128)S(1)}) custom-call(s32[6,10]{1,0:T(8,128)S(1)} %pad_add_fusion.bound.pair, f32[8,128,256]{2,1,0:T(8,128)S(1)} %get-tuple-element.38.done, f32[3,64,648]{2,1,0:T(8,128)S(1)} %copy-done, ...), custom_call_target="tpu_custom_call" | custom-call | flops 200000000 | bytes 200000000 | tf_op jit(solution)/shard_map/metric/pallas_call | solution.py:553
  12.3 1.8 %collective-permute-done.1.rest_3_ = f32[128,256]{1,0:T(8,128)S(1)} collective-permute-done((f32[128,256]{1,0:T(8,128)S(1)}, f32[128,256]{1,0:T(8,128)S(1)}, u32[]{:S(2)}, u32[]{:S(2)}) %collective-permute-start.1) | collective-permute-done | bytes 131104 | tf_op jit(solution)/shard_map/ppermute | solution.py:572
  14.1 1.6 %edges.1 = (f32[128,128]{1,0:T(8,128)S(1)}, f32[128,128]{1,0:T(8,128)S(1)}, f32[128,128]{1,0:T(8,128)S(1)}, f32[128,128]{1,0:T(8,128)S(1)}) custom-call(s32[6,10]{1,0:T(8,128)S(1)} %pad_add_fusion.bound.pair, s32[6,10]{1,0:T(8,128)S(1)} %pad_add_fusion.bound.pair, f32[8,128,256]{2,1,0:T(8,128)S(1)} %get-tuple-element.40.packed, ...), custom_call_target="tpu_custom_call" | custom-call | flops 200000000 | bytes 200000000 | tf_op jit(solution)/shard_map/edges/pallas_call | solution.py:553
  15.7 1.2 %collective-permute-start.2 = (f32[128,128]{1,0:T(8,128)S(1)}, f32[128,128]{1,0:T(8,128)S(1)}, u32[]{:S(2)}, u32[]{:S(2)}) collective-permute-start(f32[128,128]{1,0:T(8,128)S(1)} %get-tuple-element.43), channel_id=1, source_target_pairs={{0,64},{32,96},{64,0},{96,32},{128,192},{160,224},{192,128},{224,1... | collective-permute-start | bytes 196616 | tf_op jit(solution)/shard_map/ppermute | solution.py:572
  16.9 1.8 %collective-permute-start.3 = (f32[128,128]{1,0:T(8,128)S(1)}, f32[128,128]{1,0:T(8,128)S(1)}, u32[]{:S(2)}, u32[]{:S(2)}) collective-permute-start(f32[128,128]{1,0:T(8,128)S(1)} %get-tuple-element.44), channel_id=1, source_target_pairs={{0,128},{32,160},{64,192},{96,224},{128,0},{160,32},{192,64},{224,... | collective-permute-start | bytes 196616 | tf_op jit(solution)/shard_map/ppermute | solution.py:572
  18.7 0.7 %collective-permute-start.4 = (f32[128,128]{1,0:T(8,128)S(1)}, f32[128,128]{1,0:T(8,128)S(1)}, u32[]{:S(2)}, u32[]{:S(2)}) collective-permute-start(f32[128,128]{1,0:T(8,128)S(1)} %get-tuple-element.45), channel_id=1, source_target_pairs={{0,192},{32,224},{64,128},{96,160},{128,64},{160,96},{192,0},{224,... | collective-permute-start | bytes 196616 | tf_op jit(solution)/shard_map/ppermute | solution.py:572
  19.3 0.0 collective-permute-done.5.rest_1_
  19.4 1.2 %collective-permute-done.6.rest_2_ = f32[128,256]{1,0:T(8,128)S(1)} collective-permute-done((f32[128,256]{1,0:T(8,128)S(1)}, f32[128,256]{1,0:T(8,128)S(1)}, u32[]{:S(2)}, u32[]{:S(2)}) %collective-permute-start.6) | collective-permute-done | bytes 131104 | tf_op jit(solution)/shard_map/ppermute | solution.py:572
  20.5 0.0 copy-start.6
  20.6 0.0 copy-start.11
  20.6 0.0 copy-start.12
  20.6 1.0 %rim.1 = (f32[56,512]{1,0:T(8,128)S(1)}, bf16[256,512]{1,0:T(8,128)(2,1)S(1)}, bf16[256,512]{1,0:T(8,128)(2,1)S(1)}) custom-call(s32[6,10]{1,0:T(8,128)S(1)} %pad_add_fusion.bound.pair, f32[128,256]{1,0:T(8,128)S(1)} %get-tuple-element.46.rest_0_, f32[128,256]{1,0:T(8,128)S(1)} %collective-permute-done.5.rest_1_, ...), custom_call_target="tpu_custom_call" | custom-call | flops 1000 | bytes 1000 | tf_op jit(solution)/shard_map/rim/pallas_call | solution.py:553
  21.6 6.1 %collective-permute-start.10 = (f32[56,512]{1,0:T(8,128)S(1)}, f32[56,512]{1,0:T(8,128)S(1)}, u32[]{:S(2)}, u32[]{:S(2)}) collective-permute-start(f32[56,512]{1,0:T(8,128)S(1)} %get-tuple-element.60), channel_id=1, source_target_pairs={{0,255},{255,0},{64,191},{191,64},{128,127},{127,128},{192,63},{63... | collective-permute-start | bytes 344072 | tf_op jit(solution)/shard_map/ppermute | solution.py:592
  27.7 0.0 collective-permute-done.2.rest_1_
  27.7 0.0 collective-permute-done.3.rest_2_
  27.7 0.0 collective-permute-done.4.rest_3_
  27.8 0.0 copy-start.13
  27.8 3.2 %whole.1 = (f32[128,128]{1,0:T(8,128)S(1)}, f32[128,128]{1,0:T(8,128)S(1)}, f32[128,128]{1,0:T(8,128)S(1)}, f32[128,128]{1,0:T(8,128)S(1)}, f32[128,512]{1,0:T(8,128)S(1)}, /*index=5*/f32[88,512]{1,0:T(8,128)S(1)}) custom-call(s32[6,10]{1,0:T(8,128)S(1)} %pad_add_fusion.bound.pair, s32[6,10]{1,0:T(8,128)S(1)} %pad_add_fusion.bound.pair, ...), custom_call_target="tpu_custom_call" | custom-call | flops 1000 | bytes 1000 | tf_op jit(solution)/shard_map/whole/pallas_call | solution.py:553
  31.0 0.2 collective-permute-start.7
  31.2 1.8 %collective-permute-start.8 = (f32[128,128]{1,0:T(8,128)S(1)}, f32[128,128]{1,0:T(8,128)S(1)}, u32[]{:S(2)}, u32[]{:S(2)}) collective-permute-start(f32[128,128]{1,0:T(8,128)S(1)} %get-tuple-element.56), channel_id=1, source_target_pairs={{0,128},{32,160},{64,192},{96,224},{128,0},{160,32},{192,64},{224,... | collective-permute-start | bytes 196616 | tf_op jit(solution)/shard_map/ppermute | solution.py:572
  33.0 1.6 %collective-permute-start.9 = (f32[128,128]{1,0:T(8,128)S(1)}, f32[128,128]{1,0:T(8,128)S(1)}, u32[]{:S(2)}, u32[]{:S(2)}) collective-permute-start(f32[128,128]{1,0:T(8,128)S(1)} %get-tuple-element.57), channel_id=1, source_target_pairs={{0,192},{32,224},{64,128},{96,160},{128,64},{160,96},{192,0},{224,... | collective-permute-start | bytes 196616 | tf_op jit(solution)/shard_map/ppermute | solution.py:572
  34.6 0.0 collective-permute-done.10.other
  34.6 1.5 %side.1 = (f32[128,128]{1,0:T(8,128)S(1)}, f32[128,128]{1,0:T(8,128)S(1)}, f32[128,128]{1,0:T(8,128)S(1)}, f32[128,128]{1,0:T(8,128)S(1)}) custom-call(s32[6,10]{1,0:T(8,128)S(1)} %pad_add_fusion.bound.pair, f32[128,512]{1,0:T(8,128)S(1)} %get-tuple-element.58.term, f32[88,512]{1,0:T(8,128)S(1)} %get-tuple-element.59.mine, ...), custom_call_target="tpu_custom_call" | custom-call | flops 1000 | bytes 1000 | tf_op jit(solution)/shard_map/side/pallas_call | solution.py:553
  36.2 0.1 collective-permute-start.11
  36.3 1.9 %collective-permute-start.12 = (f32[128,128]{1,0:T(8,128)S(1)}, f32[128,128]{1,0:T(8,128)S(1)}, u32[]{:S(2)}, u32[]{:S(2)}) collective-permute-start(f32[128,128]{1,0:T(8,128)S(1)} %get-tuple-element.63), channel_id=1, source_target_pairs={{0,128},{32,160},{64,192},{96,224},{128,0},{160,32},{192,64},{224,... | collective-permute-start | bytes 196616 | tf_op jit(solution)/shard_map/ppermute | solution.py:572
  38.2 0.0 collective-permute-done.7.rest_1_
  38.2 1.6 %collective-permute-start.13 = (f32[128,128]{1,0:T(8,128)S(1)}, f32[128,128]{1,0:T(8,128)S(1)}, u32[]{:S(2)}, u32[]{:S(2)}) collective-permute-start(f32[128,128]{1,0:T(8,128)S(1)} %get-tuple-element.64), channel_id=1, source_target_pairs={{0,192},{32,224},{64,128},{96,160},{128,64},{160,96},{192,0},{224,... | collective-permute-start | bytes 196616 | tf_op jit(solution)/shard_map/ppermute | solution.py:572
  39.8 5.2 %collective-permute-start.14 = (f32[4,64,128]{2,1,0:T(8,128)S(1)}, f32[4,64,128]{2,1,0:T(8,128)S(1)}, u32[]{:S(2)}, u32[]{:S(2)}) collective-permute-start(f32[4,64,128]{2,1,0:T(8,128)S(1)} %cut.1), channel_id=1, source_target_pairs={{0,32},{32,0},{64,96},{96,64},{128,160},{160,128},{192,224},{224,1... | collective-permute-start | bytes 393224 | tf_op jit(solution)/shard_map/ppermute | solution.py:579
  45.0 0.0 collective-permute-done.11.rest_1_.rest_5_
  45.0 0.0 copy-start.8
  45.0 0.0 copy-start.10
  45.0 0.0 copy-start.14
  45.1 0.0 copy-start.16
  45.1 4.1 %collective-permute-start.15 = (f32[4,64,128]{2,1,0:T(8,128)S(1)}, f32[4,64,128]{2,1,0:T(8,128)S(1)}, u32[]{:S(2)}, u32[]{:S(2)}) collective-permute-start(f32[4,64,128]{2,1,0:T(8,128)S(1)} %cut_edge.1), channel_id=1, source_target_pairs={{0,32},{32,0},{64,96},{96,64},{128,160},{160,128},{192,224},{224,1... | collective-permute-start | bytes 393224 | tf_op jit(solution)/shard_map/ppermute | solution.py:579
  49.2 1.0 %collective-permute-done.15.rest_9_ = f32[4,64,128]{2,1,0:T(8,128)S(1)} collective-permute-done((f32[4,64,128]{2,1,0:T(8,128)S(1)}, f32[4,64,128]{2,1,0:T(8,128)S(1)}, u32[]{:S(2)}, u32[]{:S(2)}) %collective-permute-start.15) | collective-permute-done | bytes 131104 | tf_op jit(solution)/shard_map/ppermute | solution.py:579
  50.2 2.5 %settle.1 = f32[3,64,648]{2,1,0:T(8,128)} custom-call(s32[6,10]{1,0:T(8,128)S(1)} %pad_add_fusion.bound.pair, s32[6,10]{1,0:T(8,128)S(1)} %pad_add_fusion.bound.pair, f32[128,128]{1,0:T(8,128)S(1)} %get-tuple-element.54.rest_0_, f32[128,128]{1,0:T(8,128)S(1)} %collective-permute-done.7.rest_1_, f32[128,128]{1,0:T(8,128)S(1)} %collective-permute-done.8.rest_2_, ...), custom_call_target="tpu_custom_call" | custom-call | flops 1000 | bytes 1000 | tf_op jit(solution)/shard_map/settle/pallas_call | solution.py:553
  (33 shorter events, 0.1 us)
Async XLA Ops:
  0.0 3.2 %copy-start.17 = (s32[10,4]{0,1:T(4,128)S(1)}, s32[10,4]{0,1:T(4,128)}, u32[]{:S(2)}) copy-start(s32[10,4]{0,1:T(4,128)} %param.21) | copy-start | bytes 484
  0.0 5.6 %collective-permute-start = (f32[3,64,648]{2,1,0:T(8,128)}, f32[3,64,648]{2,1,0:T(8,128)S(1)}, u32[]{:S(2)}, u32[]{:S(2)}) collective-permute-start(f32[3,64,648]{2,1,0:T(8,128)} %here.5), channel_id=1, source_target_pairs={{0,32},{32,0},{64,96},{96,64},{128,160},{160,128},{192,224},{224,1... | collective-permute-start | bytes 1493000 | tf_op jit(solution)/shard_map/ppermute | solution.py:579
  3.2 0.7 %copy-start.18 = (s32[8,2]{0,1:T(2,128)S(1)}, s32[8,2]{0,1:T(2,128)}, u32[]{:S(2)}) copy-start(s32[8,2]{0,1:T(2,128)} %param.22) | copy-start | bytes 196
  3.9 1.1 %copy-start = (f32[3,64,648]{2,1,0:T(8,128)S(1)}, f32[3,64,648]{2,1,0:T(8,128)}, u32[]{:S(2)}) copy-start(f32[3,64,648]{2,1,0:T(8,128)} %here.5) | copy-start | bytes 1492996
  5.6 5.0 %copy-start.2 = (bf16[288,256]{1,0:T(8,128)(2,1)S(1)}, bf16[288,256]{1,0:T(8,128)(2,1)}, u32[]{:S(2)}) copy-start(bf16[288,256]{1,0:T(8,128)(2,1)} %constant.33.clone.turn.rest_7_) | copy-start | bytes 442372
  5.6 5.0 %copy-start.7 = (bf16[256,512]{1,0:T(8,128)(2,1)S(1)}, bf16[256,512]{1,0:T(8,128)(2,1)}, u32[]{:S(2)}) copy-start(bf16[256,512]{1,0:T(8,128)(2,1)} %constant.32.clone.pick) | copy-start | bytes 786436
  5.6 4.9 %copy-start.15 = (f32[4,648]{1,0:T(4,128)S(1)}, f32[4,648]{1,0:T(4,128)}, u32[]{:S(2)}) copy-start(f32[4,648]{1,0:T(4,128)} %metric.3) | copy-start | bytes 31108
  6.9 7.1 %collective-permute-start.1 = (f32[128,256]{1,0:T(8,128)S(1)}, f32[128,256]{1,0:T(8,128)S(1)}, u32[]{:S(2)}, u32[]{:S(2)}) collective-permute-start(f32[128,256]{1,0:T(8,128)S(1)} %get-tuple-element.37), channel_id=1, source_target_pairs={{0,192},{32,224},{64,128},{96,160},{128,64},{160,96},{192,0},{224,... | collective-permute-start | bytes 393224 | tf_op jit(solution)/shard_map/ppermute | solution.py:572
  9.6 9.7 %collective-permute-start.5 = (f32[128,256]{1,0:T(8,128)S(1)}, f32[128,256]{1,0:T(8,128)S(1)}, u32[]{:S(2)}, u32[]{:S(2)}) collective-permute-start(f32[128,256]{1,0:T(8,128)S(1)} %get-tuple-element.47), channel_id=1, source_target_pairs={{0,64},{32,96},{64,0},{96,32},{128,192},{160,224},{192,128},{224,1... | collective-permute-start | bytes 393224 | tf_op jit(solution)/shard_map/ppermute | solution.py:572
  9.6 10.9 %collective-permute-start.6 = (f32[128,256]{1,0:T(8,128)S(1)}, f32[128,256]{1,0:T(8,128)S(1)}, u32[]{:S(2)}, u32[]{:S(2)}) collective-permute-start(f32[128,256]{1,0:T(8,128)S(1)} %get-tuple-element.48), channel_id=1, source_target_pairs={{0,128},{32,160},{64,192},{96,224},{128,0},{160,32},{192,64},{224,... | collective-permute-start | bytes 393224 | tf_op jit(solution)/shard_map/ppermute | solution.py:572
  10.6 3.5 %copy-start.1 = (bf16[4,256,512]{2,1,0:T(8,128)(2,1)S(1)}, bf16[4,256,512]{2,1,0:T(8,128)(2,1)}, u32[]{:S(2)}) copy-start(bf16[4,256,512]{2,1,0:T(8,128)(2,1)} %constant.34.clone.table) | copy-start | bytes 3145732
  14.1 6.5 %copy-start.9 = (bf16[4,64,256]{2,1,0:T(8,128)(2,1)S(1)}, bf16[4,64,256]{2,1,0:T(8,128)(2,1)}, u32[]{:S(2)}) copy-start(bf16[4,64,256]{2,1,0:T(8,128)(2,1)} %constant.35.clone.rest_5_) | copy-start | bytes 393220
  15.7 12.0 %collective-permute-start.2 = (f32[128,128]{1,0:T(8,128)S(1)}, f32[128,128]{1,0:T(8,128)S(1)}, u32[]{:S(2)}, u32[]{:S(2)}) collective-permute-start(f32[128,128]{1,0:T(8,128)S(1)} %get-tuple-element.43), channel_id=1, source_target_pairs={{0,64},{32,96},{64,0},{96,32},{128,192},{160,224},{192,128},{224,1... | collective-permute-start | bytes 196616 | tf_op jit(solution)/shard_map/ppermute | solution.py:572
  16.9 10.8 %collective-permute-start.3 = (f32[128,128]{1,0:T(8,128)S(1)}, f32[128,128]{1,0:T(8,128)S(1)}, u32[]{:S(2)}, u32[]{:S(2)}) collective-permute-start(f32[128,128]{1,0:T(8,128)S(1)} %get-tuple-element.44), channel_id=1, source_target_pairs={{0,128},{32,160},{64,192},{96,224},{128,0},{160,32},{192,64},{224,... | collective-permute-start | bytes 196616 | tf_op jit(solution)/shard_map/ppermute | solution.py:572
  18.7 9.0 %collective-permute-start.4 = (f32[128,128]{1,0:T(8,128)S(1)}, f32[128,128]{1,0:T(8,128)S(1)}, u32[]{:S(2)}, u32[]{:S(2)}) collective-permute-start(f32[128,128]{1,0:T(8,128)S(1)} %get-tuple-element.45), channel_id=1, source_target_pairs={{0,192},{32,224},{64,128},{96,160},{128,64},{160,96},{192,0},{224,... | collective-permute-start | bytes 196616 | tf_op jit(solution)/shard_map/ppermute | solution.py:572
  20.5 7.2 %copy-start.3 = (bf16[272,256]{1,0:T(8,128)(2,1)S(1)}, bf16[272,256]{1,0:T(8,128)(2,1)}, u32[]{:S(2)}) copy-start(bf16[272,256]{1,0:T(8,128)(2,1)} %constant.37.clone.rest_9_.rest_1_) | copy-start | bytes 417796
  20.5 7.2 %copy-start.4 = (bf16[272,256]{1,0:T(8,128)(2,1)S(1)}, bf16[272,256]{1,0:T(8,128)(2,1)}, u32[]{:S(2)}) copy-start(bf16[272,256]{1,0:T(8,128)(2,1)} %constant.36.clone.rest_8_.rest_0_) | copy-start | bytes 417796
  20.5 7.2 %copy-start.5 = (bf16[256,256]{1,0:T(8,128)(2,1)S(1)}, bf16[256,256]{1,0:T(8,128)(2,1)}, u32[]{:S(2)}) copy-start(bf16[256,256]{1,0:T(8,128)(2,1)} %constant.39.clone.rest_11_.rest_3_) | copy-start | bytes 393220
  20.5 7.2 %copy-start.6 = (bf16[256,256]{1,0:T(8,128)(2,1)S(1)}, bf16[256,256]{1,0:T(8,128)(2,1)}, u32[]{:S(2)}) copy-start(bf16[256,256]{1,0:T(8,128)(2,1)} %constant.38.clone.rest_10_.rest_2_) | copy-start | bytes 393220
  20.6 7.2 %copy-start.11 = (bf16[176,96]{1,0:T(8,128)(2,1)S(1)}, bf16[176,96]{1,0:T(8,128)(2,1)}, u32[]{:S(2)}) copy-start(bf16[176,96]{1,0:T(8,128)(2,1)} %constant.41.clone.rest_13_) | copy-start | bytes 101380
  20.6 7.2 %copy-start.12 = (bf16[176,96]{1,0:T(8,128)(2,1)S(1)}, bf16[176,96]{1,0:T(8,128)(2,1)}, u32[]{:S(2)}) copy-start(bf16[176,96]{1,0:T(8,128)(2,1)} %constant.40.clone.rest_12_) | copy-start | bytes 101380
  21.6 13.0 %collective-permute-start.10 = (f32[56,512]{1,0:T(8,128)S(1)}, f32[56,512]{1,0:T(8,128)S(1)}, u32[]{:S(2)}, u32[]{:S(2)}) collective-permute-start(f32[56,512]{1,0:T(8,128)S(1)} %get-tuple-element.60), channel_id=1, source_target_pairs={{0,255},{255,0},{64,191},{191,64},{128,127},{127,128},{192,63},{63... | collective-permute-start | bytes 344072 | tf_op jit(solution)/shard_map/ppermute | solution.py:592
  27.8 6.8 %copy-start.13 = (bf16[2,80,64]{2,1,0:T(8,128)(2,1)S(1)}, bf16[2,80,64]{2,1,0:T(8,128)(2,1)}, u32[]{:S(2)}) copy-start(bf16[2,80,64]{2,1,0:T(8,128)(2,1)} %constant.42.clone.table) | copy-start | bytes 61444
  31.0 7.2 %collective-permute-start.7 = (f32[128,128]{1,0:T(8,128)S(1)}, f32[128,128]{1,0:T(8,128)S(1)}, u32[]{:S(2)}, u32[]{:S(2)}) collective-permute-start(f32[128,128]{1,0:T(8,128)S(1)} %get-tuple-element.55), channel_id=1, source_target_pairs={{0,64},{32,96},{64,0},{96,32},{128,192},{160,224},{192,128},{224,1... | collective-permute-start | bytes 196616 | tf_op jit(solution)/shard_map/ppermute | solution.py:572
  31.2 8.6 %collective-permute-start.8 = (f32[128,128]{1,0:T(8,128)S(1)}, f32[128,128]{1,0:T(8,128)S(1)}, u32[]{:S(2)}, u32[]{:S(2)}) collective-permute-start(f32[128,128]{1,0:T(8,128)S(1)} %get-tuple-element.56), channel_id=1, source_target_pairs={{0,128},{32,160},{64,192},{96,224},{128,0},{160,32},{192,64},{224,... | collective-permute-start | bytes 196616 | tf_op jit(solution)/shard_map/ppermute | solution.py:572
  33.0 6.8 %collective-permute-start.9 = (f32[128,128]{1,0:T(8,128)S(1)}, f32[128,128]{1,0:T(8,128)S(1)}, u32[]{:S(2)}, u32[]{:S(2)}) collective-permute-start(f32[128,128]{1,0:T(8,128)S(1)} %get-tuple-element.57), channel_id=1, source_target_pairs={{0,192},{32,224},{64,128},{96,160},{128,64},{160,96},{192,0},{224,... | collective-permute-start | bytes 196616 | tf_op jit(solution)/shard_map/ppermute | solution.py:572
  36.2 8.9 %collective-permute-start.11 = (f32[128,128]{1,0:T(8,128)S(1)}, f32[128,128]{1,0:T(8,128)S(1)}, u32[]{:S(2)}, u32[]{:S(2)}) collective-permute-start(f32[128,128]{1,0:T(8,128)S(1)} %get-tuple-element.62), channel_id=1, source_target_pairs={{0,64},{32,96},{64,0},{96,32},{128,192},{160,224},{192,128},{224,1... | collective-permute-start | bytes 196616 | tf_op jit(solution)/shard_map/ppermute | solution.py:572
  36.3 8.8 %collective-permute-start.12 = (f32[128,128]{1,0:T(8,128)S(1)}, f32[128,128]{1,0:T(8,128)S(1)}, u32[]{:S(2)}, u32[]{:S(2)}) collective-permute-start(f32[128,128]{1,0:T(8,128)S(1)} %get-tuple-element.63), channel_id=1, source_target_pairs={{0,128},{32,160},{64,192},{96,224},{128,0},{160,32},{192,64},{224,... | collective-permute-start | bytes 196616 | tf_op jit(solution)/shard_map/ppermute | solution.py:572
  38.2 6.8 %collective-permute-start.13 = (f32[128,128]{1,0:T(8,128)S(1)}, f32[128,128]{1,0:T(8,128)S(1)}, u32[]{:S(2)}, u32[]{:S(2)}) collective-permute-start(f32[128,128]{1,0:T(8,128)S(1)} %get-tuple-element.64), channel_id=1, source_target_pairs={{0,192},{32,224},{64,128},{96,160},{128,64},{160,96},{192,0},{224,... | collective-permute-start | bytes 196616 | tf_op jit(solution)/shard_map/ppermute | solution.py:572
  39.8 9.4 %collective-permute-start.14 = (f32[4,64,128]{2,1,0:T(8,128)S(1)}, f32[4,64,128]{2,1,0:T(8,128)S(1)}, u32[]{:S(2)}, u32[]{:S(2)}) collective-permute-start(f32[4,64,128]{2,1,0:T(8,128)S(1)} %cut.1), channel_id=1, source_target_pairs={{0,32},{32,0},{64,96},{96,64},{128,160},{160,128},{192,224},{224,1... | collective-permute-start | bytes 393224 | tf_op jit(solution)/shard_map/ppermute | solution.py:579
  45.0 5.2 %copy-start.8 = (bf16[256,384]{1,0:T(8,128)(2,1)S(1)}, bf16[256,384]{1,0:T(8,128)(2,1)}, u32[]{:S(2)}) copy-start(bf16[256,384]{1,0:T(8,128)(2,1)} %constant.46.clone.rest_13_) | copy-start | bytes 589828
  45.0 5.2 %copy-start.10 = (bf16[128,384]{1,0:T(8,128)(2,1)S(1)}, bf16[128,384]{1,0:T(8,128)(2,1)}, u32[]{:S(2)}) copy-start(bf16[128,384]{1,0:T(8,128)(2,1)} %constant.44.clone.rest_11_) | copy-start | bytes 294916
  45.0 5.1 %copy-start.14 = (bf16[128,128]{1,0:T(8,128)(2,1)S(1)}, bf16[128,128]{1,0:T(8,128)(2,1)}, u32[]{:S(2)}) copy-start(bf16[128,128]{1,0:T(8,128)(2,1)} %constant.43.clone.rest_10_) | copy-start | bytes 98308
  45.1 5.1 %copy-start.16 = (f32[8,128]{1,0:T(8,128)S(1)}, f32[8,128]{1,0:T(8,128)}, u32[]{:S(2)}) copy-start(f32[8,128]{1,0:T(8,128)} %constant.45.clone.rest_12_) | copy-start | bytes 12292
  45.1 5.1 %collective-permute-start.15 = (f32[4,64,128]{2,1,0:T(8,128)S(1)}, f32[4,64,128]{2,1,0:T(8,128)S(1)}, u32[]{:S(2)}, u32[]{:S(2)}) collective-permute-start(f32[4,64,128]{2,1,0:T(8,128)S(1)} %cut_edge.1), channel_id=1, source_target_pairs={{0,32},{32,0},{64,96},{96,64},{128,160},{160,128},{192,224},{224,1... | collective-permute-start | bytes 393224 | tf_op jit(solution)/shard_map/ppermute | solution.py:579

commit v8 on v6

--- a/solution.py
+++ b/solution.py
@@ -378,11 +378,11 @@
     send[48:56, 0:128] = terms[...]
 
 
-def element_kernel(bound, high, low, columns, turn, tables, gh, gl, mine, u, q, g):
+def element_kernel(bound, high, low, columns, turn, tables, gh, gl, mine, u, q, g, more):
     me, part = lax.axis_index("span"), lax.axis_index("dom")
     slots = dot(turn[...], high[...]) + dot(turn[...], low[...])
-    both = to_planes(jnp.concatenate([slots, slope_slots(slots)], axis=0), tables)
-    value, slope = both[:288], both[288:]
+    every = to_planes(jnp.concatenate([slots, slope_slots(slots), more], axis=0), tables)
+    value, slope, rest = every[:288], every[288:576], every[576:]
     uh, ul = split(value)
     third = value[192:280]
     for c in range(3):
@@ -399,6 +399,7 @@
     for f, (ref, at) in enumerate(order):
         for i in range(7):
             mine[f * 8 + 6 - i : f * 8 + 7 - i, :] = ref[at, pl.ds(base + i, 1), :]
+    return rest
 
 
 def inside_kernel(u, q, g, tables, *rest):
@@ -412,14 +413,11 @@
         outs[j][...] = spec[chip_modes(j), :]
 
 
-def edge_term_kernel(bound, pair, tables, *rest):
-    blocks = rest[:4]
-    u, q, g, term, modes, count, own, other, other_edge = rest[4:]
+def edge_term_kernel(bound, pair, planes, *rest):
+    u, q, g, term, count, own, other, other_edge = rest
     me, part = lax.axis_index("span"), lax.axis_index("dom")
     list_pairs(pair, count, own, other, other_edge)
-    for j in range(4):
-        modes[chip_modes(j), :] = blocks[j][...]
-    ph, pw = split(to_planes(jnp.concatenate(pick_slots(modes), axis=1), tables))
+    ph, pw = split(planes)
     e = bound[0, row_of(me, part)]
     lane = lax.broadcasted_iota(jnp.int32, (32, 128), 1)
     point = lax.broadcasted_iota(jnp.int32, (32, 128), 0)
@@ -457,9 +455,12 @@
     outs, term, mine = rest[14:18], rest[18], rest[19]
     u, q, g, inside_term, spec, modes = rest[20:26]
     pairs = rest[26:]
-    element_kernel(bound, high, low, columns, turn, tables, gh, gl, mine, u, q, g)
+    for j in range(4):
+        modes[chip_modes(j), :] = blocks[j][...]
+    more = jnp.concatenate(pick_slots(modes), axis=1)
+    planes = element_kernel(bound, high, low, columns, turn, tables, gh, gl, mine, u, q, g, more)
     inside_kernel(u, q, g, tables, *outs, inside_term, spec)
-    edge_term_kernel(bound, pair, tables, *blocks, u, q, g, term, modes, *pairs)
+    edge_term_kernel(bound, pair, planes, u, q, g, term, *pairs)
 
 
 def side_kernel(bound, term, mine, other, table, *rest):

time: 51.3 us -> 50.8 us (level)
    ppermute x1, starting transfers between devices: 8.01 us -> 6.79 us  [side_swap(): return lax.ppermute(block, ('span', 'dom'), perm)]
    ppermute x3, starting transfers between devices: 10.8 us -> 11.6 us  [between_cores(): return lax.ppermute(block, 'span', [(s, s ^ 1) for s in range(SPAN)])]
  transfers between devices with their start and end apart: 16 -> 16, of which waited for: 4 -> 4; matrix products, arithmetic and copies ran while one was open for 0% -> 0% of each run, Pallas kernels for 18% -> 17%
where the time goes in v8:
time: 50.8 us
  starting transfers between devices  33.1 us (65%)
  Pallas kernels  12.5 us (25%)
  waiting for transfers between devices  3.12 us (6%)
  local copies, waits for them, and re-layouts  1.84 us (4%)
    ppermute x12, starting transfers between devices, between_chips(): lax.ppermute(blocks[j], 'span', [(s, s ^ 2 * j) for s in range(SPAN)])  14.7 us
    pallas_call x10, Pallas kernels, call(): pl.pallas_call(kernel, out_shape=shapes, in_specs=[spec_of(pltpu.SMEM)] *...  12.5 us
    ppermute x3, starting transfers between devices, between_cores(): return lax.ppermute(block, 'span', [(s, s ^ 1) for s in range(SPAN)])  11.6 us
    ppermute x1, starting transfers between devices, side_swap(): return lax.ppermute(block, ('span', 'dom'), perm)  6.79 us
    ppermute x12, waiting for transfers between devices, between_chips(): lax.ppermute(blocks[j], 'span', [(s, s ^ 2 * j) for s in range(SPAN)])  1.94 us
    unnamed x38, local copies, waits for them, and re-layouts  1.84 us
    ppermute x3, waiting for transfers between devices, between_cores(): return lax.ppermute(block, 'span', [(s, s ^ 1) for s in range(SPAN)])  1.18 us
  transfers between devices with their start and end apart: 16, of which 4 were waited for; matrix products, arithmetic and copies ran while one was open for 0% of the time, Pallas kernels for 17%

profile of v8, /device:TPU:1, one launch (start us, length us, event | category | flops | bytes accessed | tf_op | source)
XLA Modules:
  0.0 50.8 jit_solution(1396942597087535885)
XLA Ops:
  0.0 3.2 %collective-permute-start = (f32[3,64,648]{2,1,0:T(8,128)}, f32[3,64,648]{2,1,0:T(8,128)S(1)}, u32[]{:S(2)}, u32[]{:S(2)}) collective-permute-start(f32[3,64,648]{2,1,0:T(8,128)} %here.5), channel_id=1, source_target_pairs={{0,32},{32,0},{64,96},{96,64},{128,160},{160,128},{192,224},{224,1... | collective-permute-start | bytes 1493000 | tf_op jit(solution)/shard_map/ppermute | solution.py:580
  3.2 1.1 %copy-done = f32[3,64,648]{2,1,0:T(8,128)S(1)} copy-done((f32[3,64,648]{2,1,0:T(8,128)S(1)}, f32[3,64,648]{2,1,0:T(8,128)}, u32[]{:S(2)}) %copy-start) | copy-done | bytes 497688
  4.3 0.6 %ready.1 = f32[8,128]{1,0:T(8,128)S(1)} custom-call(s32[2,8]{1,0:T(2,128)S(1)} %bitcast.2, f32[3,64,648]{2,1,0:T(8,128)S(1)} %copy-done), custom_call_target="tpu_custom_call" | custom-call | flops 200000000 | bytes 200000000 | tf_op jit(solution)/shard_map/ready/pallas_call | solution.py:554
  4.9 0.0 copy-start.2
  4.9 0.0 copy-start.7
  4.9 0.2 collective-permute-done.there
  5.1 1.3 %pack.1 = (f32[8,128,256]{2,1,0:T(8,128)S(1)}, f32[128,256]{1,0:T(8,128)S(1)}, f32[128,256]{1,0:T(8,128)S(1)}, f32[128,256]{1,0:T(8,128)S(1)}, f32[128,256]{1,0:T(8,128)S(1)}) custom-call(s32[2,8]{1,0:T(2,128)S(1)} %bitcast.3, f32[3,64,648]{2,1,0:T(8,128)S(1)} %copy-done, f32[3,64,648]{2,1,0:T(8,128)S(1)} %collective-permute-done.there, f32[8,128]{1,0:T(8,128)S(1)} %ready.1), custom_call_target="tpu_custom_call" | custom-call | flops 200000000 | bytes 200000000 | tf_op jit(solution)/shard_map/pack/pallas_call | solution.py:554
  6.4 2.7 %collective-permute-start.1 = (f32[128,256]{1,0:T(8,128)S(1)}, f32[128,256]{1,0:T(8,128)S(1)}, u32[]{:S(2)}, u32[]{:S(2)}) collective-permute-start(f32[128,256]{1,0:T(8,128)S(1)} %get-tuple-element.37), channel_id=1, source_target_pairs={{0,192},{32,224},{64,128},{96,160},{128,64},{160,96},{192,0},{224,... | collective-permute-start | bytes 393224 | tf_op jit(solution)/shard_map/ppermute | solution.py:573
  9.1 0.0 collective-permute-start.5
  9.1 0.9 %collective-permute-start.6 = (f32[128,256]{1,0:T(8,128)S(1)}, f32[128,256]{1,0:T(8,128)S(1)}, u32[]{:S(2)}, u32[]{:S(2)}) collective-permute-start(f32[128,256]{1,0:T(8,128)S(1)} %get-tuple-element.48), channel_id=1, source_target_pairs={{0,128},{32,160},{64,192},{96,224},{128,0},{160,32},{192,64},{224,... | collective-permute-start | bytes 393224 | tf_op jit(solution)/shard_map/ppermute | solution.py:573
  10.0 1.6 %metric.2 = (f32[8,128,256]{2,1,0:T(8,128)S(1)}, f32[64,1,128]{2,1,0:T(1,128)S(1)}, f32[96,128]{1,0:T(8,128)S(1)}, f32[8,128]{1,0:T(8,128)S(1)}) custom-call(s32[2,8]{1,0:T(2,128)S(1)} %bitcast.4, f32[8,128,256]{2,1,0:T(8,128)S(1)} %get-tuple-element.38.done, f32[3,64,648]{2,1,0:T(8,128)S(1)} %copy-done, f32[3,64,648]{2,1,0:T(8,128)S(1)} %collective-permute-done.there, ...), custom_call_target="tpu_custom_call" | custom-call | flops 200000000 | bytes 200000000 | tf_op jit(solution)/shard_map/metric/pallas_call | solution.py:554
  11.6 1.4 %collective-permute-done.1.rest_3_ = f32[128,256]{1,0:T(8,128)S(1)} collective-permute-done((f32[128,256]{1,0:T(8,128)S(1)}, f32[128,256]{1,0:T(8,128)S(1)}, u32[]{:S(2)}, u32[]{:S(2)}) %collective-permute-start.1) | collective-permute-done | bytes 131104 | tf_op jit(solution)/shard_map/ppermute | solution.py:573
  13.0 0.7 %copy-done.16 = s32[10,4]{0,1:T(4,128)S(1)} copy-done((s32[10,4]{0,1:T(4,128)S(1)}, s32[10,4]{0,1:T(4,128)}, u32[]{:S(2)}) %copy-start.16) | copy-done | bytes 184
  13.7 1.6 %edges.1 = (f32[128,128]{1,0:T(8,128)S(1)}, f32[128,128]{1,0:T(8,128)S(1)}, f32[128,128]{1,0:T(8,128)S(1)}, f32[128,128]{1,0:T(8,128)S(1)}) custom-call(s32[2,8]{1,0:T(2,128)S(1)} %bitcast.5, s32[4,10]{1,0:T(4,128)S(1)} %bitcast.10, f32[8,128,256]{2,1,0:T(8,128)S(1)} %get-tuple-element.40.packed, f32[64,1,128]{2,1,0:T(1,128)S(1)} %get-tuple-element.41.scale, ...), custom_call_target="tpu_custom_call" | custom-call | flops 200000000 | bytes 200000000 | tf_op jit(solution)/shard_map/edges/pallas_call | solution.py:554
  15.2 0.6 %collective-permute-start.2 = (f32[128,128]{1,0:T(8,128)S(1)}, f32[128,128]{1,0:T(8,128)S(1)}, u32[]{:S(2)}, u32[]{:S(2)}) collective-permute-start(f32[128,128]{1,0:T(8,128)S(1)} %get-tuple-element.43), channel_id=1, source_target_pairs={{0,64},{32,96},{64,0},{96,32},{128,192},{160,224},{192,128},{224,1... | collective-permute-start | bytes 196616 | tf_op jit(solution)/shard_map/ppermute | solution.py:573
  15.9 2.3 %collective-permute-start.3 = (f32[128,128]{1,0:T(8,128)S(1)}, f32[128,128]{1,0:T(8,128)S(1)}, u32[]{:S(2)}, u32[]{:S(2)}) collective-permute-start(f32[128,128]{1,0:T(8,128)S(1)} %get-tuple-element.44), channel_id=1, source_target_pairs={{0,128},{32,160},{64,192},{96,224},{128,0},{160,32},{192,64},{224,... | collective-permute-start | bytes 196616 | tf_op jit(solution)/shard_map/ppermute | solution.py:573
  18.2 0.7 %collective-permute-start.4 = (f32[128,128]{1,0:T(8,128)S(1)}, f32[128,128]{1,0:T(8,128)S(1)}, u32[]{:S(2)}, u32[]{:S(2)}) collective-permute-start(f32[128,128]{1,0:T(8,128)S(1)} %get-tuple-element.45), channel_id=1, source_target_pairs={{0,192},{32,224},{64,128},{96,160},{128,64},{160,96},{192,0},{224,... | collective-permute-start | bytes 196616 | tf_op jit(solution)/shard_map/ppermute | solution.py:573
  18.9 0.0 collective-permute-done.5.rest_1_
  18.9 0.5 %collective-permute-done.6.rest_2_ = f32[128,256]{1,0:T(8,128)S(1)} collective-permute-done((f32[128,256]{1,0:T(8,128)S(1)}, f32[128,256]{1,0:T(8,128)S(1)}, u32[]{:S(2)}, u32[]{:S(2)}) %collective-permute-start.6) | collective-permute-done | bytes 131104 | tf_op jit(solution)/shard_map/ppermute | solution.py:573
  19.4 0.0 copy-start.6
  19.4 0.0 copy-start.12
  19.4 0.0 copy-start.13
  19.4 1.0 %rim.1 = (f32[56,512]{1,0:T(8,128)S(1)}, bf16[256,512]{1,0:T(8,128)(2,1)S(1)}, bf16[256,512]{1,0:T(8,128)(2,1)S(1)}) custom-call(s32[2,8]{1,0:T(2,128)S(1)} %bitcast.6, f32[128,256]{1,0:T(8,128)S(1)} %get-tuple-element.46.rest_0_, f32[128,256]{1,0:T(8,128)S(1)} %collective-permute-done.5.rest_1_, f32[128,256]{1,0:T(8,128)S(1)} %collective-permute-done.6.rest_2_, ...), custom_call_target="tpu_custom_call" | custom-call | flops 1000 | bytes 1000 | tf_op jit(solution)/shard_map/rim/pallas_call | solution.py:554
  20.4 6.8 %collective-permute-start.10 = (f32[56,512]{1,0:T(8,128)S(1)}, f32[56,512]{1,0:T(8,128)S(1)}, u32[]{:S(2)}, u32[]{:S(2)}) collective-permute-start(f32[56,512]{1,0:T(8,128)S(1)} %get-tuple-element.60), channel_id=1, source_target_pairs={{0,255},{255,0},{64,191},{191,64},{128,127},{127,128},{192,63},{63... | collective-permute-start | bytes 344072 | tf_op jit(solution)/shard_map/ppermute | solution.py:593
  27.2 0.0 collective-permute-done.2.rest_1_
  27.2 0.0 collective-permute-done.3.rest_2_
  27.3 0.0 copy-start.14
  27.3 2.7 %whole.1 = (f32[128,128]{1,0:T(8,128)S(1)}, f32[128,128]{1,0:T(8,128)S(1)}, f32[128,128]{1,0:T(8,128)S(1)}, f32[128,128]{1,0:T(8,128)S(1)}, f32[128,512]{1,0:T(8,128)S(1)}, /*index=5*/f32[88,512]{1,0:T(8,128)S(1)}) custom-call(s32[2,8]{1,0:T(2,128)S(1)} %bitcast.7, s32[4,10]{1,0:T(4,128)S(1)} %bitcast.11, f32[128,128]{1,0:T(8,128)S(1)} %get-tuple-element.42.rest_0_, ...), custom_call_target="tpu_custom_call" | custom-call | flops 1000 | bytes 1000 | tf_op jit(solution)/shard_map/whole/pallas_call | solution.py:554
  30.0 1.4 %collective-permute-start.7 = (f32[128,128]{1,0:T(8,128)S(1)}, f32[128,128]{1,0:T(8,128)S(1)}, u32[]{:S(2)}, u32[]{:S(2)}) collective-permute-start(f32[128,128]{1,0:T(8,128)S(1)} %get-tuple-element.55), channel_id=1, source_target_pairs={{0,64},{32,96},{64,0},{96,32},{128,192},{160,224},{192,128},{224,1... | collective-permute-start | bytes 196616 | tf_op jit(solution)/shard_map/ppermute | solution.py:573
  31.4 0.6 %collective-permute-start.8 = (f32[128,128]{1,0:T(8,128)S(1)}, f32[128,128]{1,0:T(8,128)S(1)}, u32[]{:S(2)}, u32[]{:S(2)}) collective-permute-start(f32[128,128]{1,0:T(8,128)S(1)} %get-tuple-element.56), channel_id=1, source_target_pairs={{0,128},{32,160},{64,192},{96,224},{128,0},{160,32},{192,64},{224,... | collective-permute-start | bytes 196616 | tf_op jit(solution)/shard_map/ppermute | solution.py:573
  32.0 1.6 %collective-permute-start.9 = (f32[128,128]{1,0:T(8,128)S(1)}, f32[128,128]{1,0:T(8,128)S(1)}, u32[]{:S(2)}, u32[]{:S(2)}) collective-permute-start(f32[128,128]{1,0:T(8,128)S(1)} %get-tuple-element.57), channel_id=1, source_target_pairs={{0,192},{32,224},{64,128},{96,160},{128,64},{160,96},{192,0},{224,... | collective-permute-start | bytes 196616 | tf_op jit(solution)/shard_map/ppermute | solution.py:573
  33.6 0.0 collective-permute-done.10.other
  33.6 1.5 %side.1 = (f32[128,128]{1,0:T(8,128)S(1)}, f32[128,128]{1,0:T(8,128)S(1)}, f32[128,128]{1,0:T(8,128)S(1)}, f32[128,128]{1,0:T(8,128)S(1)}) custom-call(s32[2,8]{1,0:T(2,128)S(1)} %bitcast.8, f32[128,512]{1,0:T(8,128)S(1)} %get-tuple-element.58.term, f32[88,512]{1,0:T(8,128)S(1)} %get-tuple-element.59.mine, f32[56,512]{1,0:T(8,128)S(1)} %collective-permute-done.10.other, ...), custom_call_target="tpu_custom_call" | custom-call | flops 1000 | bytes 1000 | tf_op jit(solution)/shard_map/side/pallas_call | solution.py:554
  35.1 0.7 %collective-permute-start.11 = (f32[128,128]{1,0:T(8,128)S(1)}, f32[128,128]{1,0:T(8,128)S(1)}, u32[]{:S(2)}, u32[]{:S(2)}) collective-permute-start(f32[128,128]{1,0:T(8,128)S(1)} %get-tuple-element.62), channel_id=1, source_target_pairs={{0,64},{32,96},{64,0},{96,32},{128,192},{160,224},{192,128},{224,1... | collective-permute-start | bytes 196616 | tf_op jit(solution)/shard_map/ppermute | solution.py:573
  35.8 1.5 %collective-permute-start.12 = (f32[128,128]{1,0:T(8,128)S(1)}, f32[128,128]{1,0:T(8,128)S(1)}, u32[]{:S(2)}, u32[]{:S(2)}) collective-permute-start(f32[128,128]{1,0:T(8,128)S(1)} %get-tuple-element.63), channel_id=1, source_target_pairs={{0,128},{32,160},{64,192},{96,224},{128,0},{160,32},{192,64},{224,... | collective-permute-start | bytes 196616 | tf_op jit(solution)/shard_map/ppermute | solution.py:573
  37.3 0.0 collective-permute-done.7.rest_1_
  37.3 1.6 %collective-permute-start.13 = (f32[128,128]{1,0:T(8,128)S(1)}, f32[128,128]{1,0:T(8,128)S(1)}, u32[]{:S(2)}, u32[]{:S(2)}) collective-permute-start(f32[128,128]{1,0:T(8,128)S(1)} %get-tuple-element.64), channel_id=1, source_target_pairs={{0,192},{32,224},{64,128},{96,160},{128,64},{160,96},{192,0},{224,... | collective-permute-start | bytes 196616 | tf_op jit(solution)/shard_map/ppermute | solution.py:573
  39.0 4.3 %collective-permute-start.14 = (f32[4,64,128]{2,1,0:T(8,128)S(1)}, f32[4,64,128]{2,1,0:T(8,128)S(1)}, u32[]{:S(2)}, u32[]{:S(2)}) collective-permute-start(f32[4,64,128]{2,1,0:T(8,128)S(1)} %cut.1), channel_id=1, source_target_pairs={{0,32},{32,0},{64,96},{96,64},{128,160},{160,128},{192,224},{224,1... | collective-permute-start | bytes 393224 | tf_op jit(solution)/shard_map/ppermute | solution.py:580
  43.2 0.0 collective-permute-done.11.rest_1_.rest_5_
  43.2 0.0 collective-permute-done.12.rest_2_.rest_6_
  43.2 0.0 collective-permute-done.13.rest_3_.rest_7_
  43.2 0.0 copy-start.8
  43.3 0.0 copy-start.10
  43.3 0.0 copy-start.15
  43.3 0.0 copy-start.18
  43.3 4.1 %collective-permute-start.15 = (f32[4,64,128]{2,1,0:T(8,128)S(1)}, f32[4,64,128]{2,1,0:T(8,128)S(1)}, u32[]{:S(2)}, u32[]{:S(2)}) collective-permute-start(f32[4,64,128]{2,1,0:T(8,128)S(1)} %cut_edge.1), channel_id=1, source_target_pairs={{0,32},{32,0},{64,96},{96,64},{128,160},{160,128},{192,224},{224,1... | collective-permute-start | bytes 393224 | tf_op jit(solution)/shard_map/ppermute | solution.py:580
  47.4 1.0 %collective-permute-done.15.rest_9_ = f32[4,64,128]{2,1,0:T(8,128)S(1)} collective-permute-done((f32[4,64,128]{2,1,0:T(8,128)S(1)}, f32[4,64,128]{2,1,0:T(8,128)S(1)}, u32[]{:S(2)}, u32[]{:S(2)}) %collective-permute-start.15) | collective-permute-done | bytes 131104 | tf_op jit(solution)/shard_map/ppermute | solution.py:580
  48.4 2.4 %settle.1 = f32[3,64,648]{2,1,0:T(8,128)} custom-call(s32[2,8]{1,0:T(2,128)S(1)} %bitcast.9, s32[4,10]{1,0:T(4,128)S(1)} %bitcast.12, f32[128,128]{1,0:T(8,128)S(1)} %get-tuple-element.54.rest_0_, f32[128,128]{1,0:T(8,128)S(1)} %collective-permute-done.7.rest_1_, f32[128,128]{1,0:T(8,128)S(1)} %collective-permute-done.8.rest_2_, ...), custom_call_target="tpu_custom_call" | custom-call | flops 1000 | bytes 1000 | tf_op jit(solution)/shard_map/settle/pallas_call | solution.py:554
  (32 shorter events, 0.1 us)
Async XLA Ops:
  0.0 3.2 %copy-start.11 = (s32[8,2]{0,1:T(2,128)S(1)}, s32[8,2]{0,1:T(2,128)}, u32[]{:S(2)}) copy-start(s32[8,2]{0,1:T(2,128)} %param.22) | copy-start | bytes 196
  0.0 5.1 %collective-permute-start = (f32[3,64,648]{2,1,0:T(8,128)}, f32[3,64,648]{2,1,0:T(8,128)S(1)}, u32[]{:S(2)}, u32[]{:S(2)}) collective-permute-start(f32[3,64,648]{2,1,0:T(8,128)} %here.5), channel_id=1, source_target_pairs={{0,32},{32,0},{64,96},{96,64},{128,160},{160,128},{192,224},{224,1... | collective-permute-start | bytes 1493000 | tf_op jit(solution)/shard_map/ppermute | solution.py:580
  3.2 1.1 %copy-start = (f32[3,64,648]{2,1,0:T(8,128)S(1)}, f32[3,64,648]{2,1,0:T(8,128)}, u32[]{:S(2)}) copy-start(f32[3,64,648]{2,1,0:T(8,128)} %here.5) | copy-start | bytes 1492996
  4.9 5.1 %copy-start.2 = (bf16[288,256]{1,0:T(8,128)(2,1)S(1)}, bf16[288,256]{1,0:T(8,128)(2,1)}, u32[]{:S(2)}) copy-start(bf16[288,256]{1,0:T(8,128)(2,1)} %constant.31.clone.turn.rest_7_) | copy-start | bytes 442372
  4.9 5.1 %copy-start.7 = (bf16[256,512]{1,0:T(8,128)(2,1)S(1)}, bf16[256,512]{1,0:T(8,128)(2,1)}, u32[]{:S(2)}) copy-start(bf16[256,512]{1,0:T(8,128)(2,1)} %constant.30.clone.pick) | copy-start | bytes 786436
  5.1 4.9 %copy-start.17 = (f32[4,648]{1,0:T(4,128)S(1)}, f32[4,648]{1,0:T(4,128)}, u32[]{:S(2)}) copy-start(f32[4,648]{1,0:T(4,128)} %metric.3) | copy-start | bytes 31108
  6.4 6.6 %collective-permute-start.1 = (f32[128,256]{1,0:T(8,128)S(1)}, f32[128,256]{1,0:T(8,128)S(1)}, u32[]{:S(2)}, u32[]{:S(2)}) collective-permute-start(f32[128,256]{1,0:T(8,128)S(1)} %get-tuple-element.37), channel_id=1, source_target_pairs={{0,192},{32,224},{64,128},{96,160},{128,64},{160,96},{192,0},{224,... | collective-permute-start | bytes 393224 | tf_op jit(solution)/shard_map/ppermute | solution.py:573
  9.1 9.8 %collective-permute-start.5 = (f32[128,256]{1,0:T(8,128)S(1)}, f32[128,256]{1,0:T(8,128)S(1)}, u32[]{:S(2)}, u32[]{:S(2)}) collective-permute-start(f32[128,256]{1,0:T(8,128)S(1)} %get-tuple-element.47), channel_id=1, source_target_pairs={{0,64},{32,96},{64,0},{96,32},{128,192},{160,224},{192,128},{224,1... | collective-permute-start | bytes 393224 | tf_op jit(solution)/shard_map/ppermute | solution.py:573
  9.1 10.3 %collective-permute-start.6 = (f32[128,256]{1,0:T(8,128)S(1)}, f32[128,256]{1,0:T(8,128)S(1)}, u32[]{:S(2)}, u32[]{:S(2)}) collective-permute-start(f32[128,256]{1,0:T(8,128)S(1)} %get-tuple-element.48), channel_id=1, source_target_pairs={{0,128},{32,160},{64,192},{96,224},{128,0},{160,32},{192,64},{224,... | collective-permute-start | bytes 393224 | tf_op jit(solution)/shard_map/ppermute | solution.py:573
  10.0 3.0 %copy-start.1 = (bf16[4,256,512]{2,1,0:T(8,128)(2,1)S(1)}, bf16[4,256,512]{2,1,0:T(8,128)(2,1)}, u32[]{:S(2)}) copy-start(bf16[4,256,512]{2,1,0:T(8,128)(2,1)} %constant.32.clone.table) | copy-start | bytes 3145732
  13.0 0.7 %copy-start.16 = (s32[10,4]{0,1:T(4,128)S(1)}, s32[10,4]{0,1:T(4,128)}, u32[]{:S(2)}) copy-start(s32[10,4]{0,1:T(4,128)} %param.21) | copy-start | bytes 484
  13.7 5.7 %copy-start.9 = (bf16[4,64,256]{2,1,0:T(8,128)(2,1)S(1)}, bf16[4,64,256]{2,1,0:T(8,128)(2,1)}, u32[]{:S(2)}) copy-start(bf16[4,64,256]{2,1,0:T(8,128)(2,1)} %constant.33.clone.rest_5_) | copy-start | bytes 393220
  15.2 12.0 %collective-permute-start.2 = (f32[128,128]{1,0:T(8,128)S(1)}, f32[128,128]{1,0:T(8,128)S(1)}, u32[]{:S(2)}, u32[]{:S(2)}) collective-permute-start(f32[128,128]{1,0:T(8,128)S(1)} %get-tuple-element.43), channel_id=1, source_target_pairs={{0,64},{32,96},{64,0},{96,32},{128,192},{160,224},{192,128},{224,1... | collective-permute-start | bytes 196616 | tf_op jit(solution)/shard_map/ppermute | solution.py:573
  15.9 11.4 %collective-permute-start.3 = (f32[128,128]{1,0:T(8,128)S(1)}, f32[128,128]{1,0:T(8,128)S(1)}, u32[]{:S(2)}, u32[]{:S(2)}) collective-permute-start(f32[128,128]{1,0:T(8,128)S(1)} %get-tuple-element.44), channel_id=1, source_target_pairs={{0,128},{32,160},{64,192},{96,224},{128,0},{160,32},{192,64},{224,... | collective-permute-start | bytes 196616 | tf_op jit(solution)/shard_map/ppermute | solution.py:573
  18.2 9.0 %collective-permute-start.4 = (f32[128,128]{1,0:T(8,128)S(1)}, f32[128,128]{1,0:T(8,128)S(1)}, u32[]{:S(2)}, u32[]{:S(2)}) collective-permute-start(f32[128,128]{1,0:T(8,128)S(1)} %get-tuple-element.45), channel_id=1, source_target_pairs={{0,192},{32,224},{64,128},{96,160},{128,64},{160,96},{192,0},{224,... | collective-permute-start | bytes 196616 | tf_op jit(solution)/shard_map/ppermute | solution.py:573
  19.4 7.8 %copy-start.3 = (bf16[272,256]{1,0:T(8,128)(2,1)S(1)}, bf16[272,256]{1,0:T(8,128)(2,1)}, u32[]{:S(2)}) copy-start(bf16[272,256]{1,0:T(8,128)(2,1)} %constant.35.clone.rest_9_.rest_1_) | copy-start | bytes 417796
  19.4 7.8 %copy-start.4 = (bf16[272,256]{1,0:T(8,128)(2,1)S(1)}, bf16[272,256]{1,0:T(8,128)(2,1)}, u32[]{:S(2)}) copy-start(bf16[272,256]{1,0:T(8,128)(2,1)} %constant.34.clone.rest_8_.rest_0_) | copy-start | bytes 417796
  19.4 7.8 %copy-start.5 = (bf16[256,256]{1,0:T(8,128)(2,1)S(1)}, bf16[256,256]{1,0:T(8,128)(2,1)}, u32[]{:S(2)}) copy-start(bf16[256,256]{1,0:T(8,128)(2,1)} %constant.37.clone.rest_11_.rest_3_) | copy-start | bytes 393220
  19.4 7.8 %copy-start.6 = (bf16[256,256]{1,0:T(8,128)(2,1)S(1)}, bf16[256,256]{1,0:T(8,128)(2,1)}, u32[]{:S(2)}) copy-start(bf16[256,256]{1,0:T(8,128)(2,1)} %constant.36.clone.rest_10_.rest_2_) | copy-start | bytes 393220
  19.4 7.8 %copy-start.12 = (bf16[176,96]{1,0:T(8,128)(2,1)S(1)}, bf16[176,96]{1,0:T(8,128)(2,1)}, u32[]{:S(2)}) copy-start(bf16[176,96]{1,0:T(8,128)(2,1)} %constant.39.clone.rest_13_) | copy-start | bytes 101380
  19.4 7.8 %copy-start.13 = (bf16[176,96]{1,0:T(8,128)(2,1)S(1)}, bf16[176,96]{1,0:T(8,128)(2,1)}, u32[]{:S(2)}) copy-start(bf16[176,96]{1,0:T(8,128)(2,1)} %constant.38.clone.rest_12_) | copy-start | bytes 101380
  20.4 13.2 %collective-permute-start.10 = (f32[56,512]{1,0:T(8,128)S(1)}, f32[56,512]{1,0:T(8,128)S(1)}, u32[]{:S(2)}, u32[]{:S(2)}) collective-permute-start(f32[56,512]{1,0:T(8,128)S(1)} %get-tuple-element.60), channel_id=1, source_target_pairs={{0,255},{255,0},{64,191},{191,64},{128,127},{127,128},{192,63},{63... | collective-permute-start | bytes 344072 | tf_op jit(solution)/shard_map/ppermute | solution.py:593
  27.3 6.4 %copy-start.14 = (bf16[2,80,64]{2,1,0:T(8,128)(2,1)S(1)}, bf16[2,80,64]{2,1,0:T(8,128)(2,1)}, u32[]{:S(2)}) copy-start(bf16[2,80,64]{2,1,0:T(8,128)(2,1)} %constant.40.clone.table) | copy-start | bytes 61444
  30.0 7.3 %collective-permute-start.7 = (f32[128,128]{1,0:T(8,128)S(1)}, f32[128,128]{1,0:T(8,128)S(1)}, u32[]{:S(2)}, u32[]{:S(2)}) collective-permute-start(f32[128,128]{1,0:T(8,128)S(1)} %get-tuple-element.55), channel_id=1, source_target_pairs={{0,64},{32,96},{64,0},{96,32},{128,192},{160,224},{192,128},{224,1... | collective-permute-start | bytes 196616 | tf_op jit(solution)/shard_map/ppermute | solution.py:573
  31.4 7.6 %collective-permute-start.8 = (f32[128,128]{1,0:T(8,128)S(1)}, f32[128,128]{1,0:T(8,128)S(1)}, u32[]{:S(2)}, u32[]{:S(2)}) collective-permute-start(f32[128,128]{1,0:T(8,128)S(1)} %get-tuple-element.56), channel_id=1, source_target_pairs={{0,128},{32,160},{64,192},{96,224},{128,0},{160,32},{192,64},{224,... | collective-permute-start | bytes 196616 | tf_op jit(solution)/shard_map/ppermute | solution.py:573
  32.0 7.0 %collective-permute-start.9 = (f32[128,128]{1,0:T(8,128)S(1)}, f32[128,128]{1,0:T(8,128)S(1)}, u32[]{:S(2)}, u32[]{:S(2)}) collective-permute-start(f32[128,128]{1,0:T(8,128)S(1)} %get-tuple-element.57), channel_id=1, source_target_pairs={{0,192},{32,224},{64,128},{96,160},{128,64},{160,96},{192,0},{224,... | collective-permute-start | bytes 196616 | tf_op jit(solution)/shard_map/ppermute | solution.py:573
  35.1 8.1 %collective-permute-start.11 = (f32[128,128]{1,0:T(8,128)S(1)}, f32[128,128]{1,0:T(8,128)S(1)}, u32[]{:S(2)}, u32[]{:S(2)}) collective-permute-start(f32[128,128]{1,0:T(8,128)S(1)} %get-tuple-element.62), channel_id=1, source_target_pairs={{0,64},{32,96},{64,0},{96,32},{128,192},{160,224},{192,128},{224,1... | collective-permute-start | bytes 196616 | tf_op jit(solution)/shard_map/ppermute | solution.py:573
  35.8 7.4 %collective-permute-start.12 = (f32[128,128]{1,0:T(8,128)S(1)}, f32[128,128]{1,0:T(8,128)S(1)}, u32[]{:S(2)}, u32[]{:S(2)}) collective-permute-start(f32[128,128]{1,0:T(8,128)S(1)} %get-tuple-element.63), channel_id=1, source_target_pairs={{0,128},{32,160},{64,192},{96,224},{128,0},{160,32},{192,64},{224,... | collective-permute-start | bytes 196616 | tf_op jit(solution)/shard_map/ppermute | solution.py:573
  37.3 5.9 %collective-permute-start.13 = (f32[128,128]{1,0:T(8,128)S(1)}, f32[128,128]{1,0:T(8,128)S(1)}, u32[]{:S(2)}, u32[]{:S(2)}) collective-permute-start(f32[128,128]{1,0:T(8,128)S(1)} %get-tuple-element.64), channel_id=1, source_target_pairs={{0,192},{32,224},{64,128},{96,160},{128,64},{160,96},{192,0},{224,... | collective-permute-start | bytes 196616 | tf_op jit(solution)/shard_map/ppermute | solution.py:573
  39.0 8.4 %collective-permute-start.14 = (f32[4,64,128]{2,1,0:T(8,128)S(1)}, f32[4,64,128]{2,1,0:T(8,128)S(1)}, u32[]{:S(2)}, u32[]{:S(2)}) collective-permute-start(f32[4,64,128]{2,1,0:T(8,128)S(1)} %cut.1), channel_id=1, source_target_pairs={{0,32},{32,0},{64,96},{96,64},{128,160},{160,128},{192,224},{224,1... | collective-permute-start | bytes 393224 | tf_op jit(solution)/shard_map/ppermute | solution.py:580
  43.2 5.2 %copy-start.8 = (bf16[256,384]{1,0:T(8,128)(2,1)S(1)}, bf16[256,384]{1,0:T(8,128)(2,1)}, u32[]{:S(2)}) copy-start(bf16[256,384]{1,0:T(8,128)(2,1)} %constant.44.clone.rest_13_) | copy-start | bytes 589828
  43.3 5.1 %copy-start.10 = (bf16[128,384]{1,0:T(8,128)(2,1)S(1)}, bf16[128,384]{1,0:T(8,128)(2,1)}, u32[]{:S(2)}) copy-start(bf16[128,384]{1,0:T(8,128)(2,1)} %constant.42.clone.rest_11_) | copy-start | bytes 294916
  43.3 5.1 %copy-start.15 = (bf16[128,128]{1,0:T(8,128)(2,1)S(1)}, bf16[128,128]{1,0:T(8,128)(2,1)}, u32[]{:S(2)}) copy-start(bf16[128,128]{1,0:T(8,128)(2,1)} %constant.41.clone.rest_10_) | copy-start | bytes 98308
  43.3 5.1 %copy-start.18 = (f32[8,128]{1,0:T(8,128)S(1)}, f32[8,128]{1,0:T(8,128)}, u32[]{:S(2)}) copy-start(f32[8,128]{1,0:T(8,128)} %constant.43.clone.rest_12_) | copy-start | bytes 12292
  43.3 5.1 %collective-permute-start.15 = (f32[4,64,128]{2,1,0:T(8,128)S(1)}, f32[4,64,128]{2,1,0:T(8,128)S(1)}, u32[]{:S(2)}, u32[]{:S(2)}) collective-permute-start(f32[4,64,128]{2,1,0:T(8,128)S(1)} %cut_edge.1), channel_id=1, source_target_pairs={{0,32},{32,0},{64,96},{96,64},{128,160},{160,128},{192,224},{224,1... | collective-permute-start | bytes 393224 | tf_op jit(solution)/shard_map/ppermute | solution.py:580
